TPU v7x, 32 devices: a whole 2x2x4 slice. The times are simulated.
32 devices in a mesh: dp: 4 (over x, core), fsdp: 4 (over z), sp: 2 (over y).
Axes of the slice: x: 2, y: 2, z: 4, core: 2. Of those that a mesh axis runs over, the one named last changes fastest.
Arguments:
- tokens: bfloat16 [12288, 1024], P(('dp', 'fsdp', 'sp')), may hold values from -6 to 6
- cotangent: bfloat16 [12288, 1024], P(('dp', 'fsdp', 'sp')), may hold values from -6 to 6
- doc_lengths: int32 [16, 4], P(('dp', 'fsdp')), may hold values from 1 to 576, 768 in all within a row
- input_weight: bfloat16 [1024, 6144], P('fsdp'), may hold values from -0.1875 to 0.1875
- rate_weight: bfloat16 [1024, 16], P('fsdp'), may hold values from -0.1875 to 0.1875
- conv_weight: bfloat16 [4, 4096], P(None, 'fsdp'), may hold values from -3 to 3
- head_decay: bfloat16 [2, 8], P(None, 'fsdp'), may hold values from -8 to 1, as said below
- mixer_gain: bfloat16 [1024], P('fsdp'), may hold values from 0.099609375 to 1.8984375
- heads_gain: bfloat16 [256], P('fsdp'), may hold values from 0.099609375 to 1.8984375
- output_weight: bfloat16 [2048, 1024], P('fsdp'), may hold values from -0.25 to 0.25
- feed_gain: bfloat16 [1024], P('fsdp'), may hold values from 0.099609375 to 1.8984375
- up_weight: bfloat16 [1024, 5632], P('fsdp'), may hold values from -0.1875 to 0.1875
- down_weight: bfloat16 [2816, 1024], P('fsdp'), may hold values from -0.15625 to 0.15625
Outputs:
- block_out: bfloat16 [12288, 1024], P(('dp', 'fsdp', 'sp'))
- tokens_grad: bfloat16 [12288, 1024], P(('dp', 'fsdp', 'sp'))
- input_grad: float32 [1024, 6144], P('fsdp')
- rate_grad: float32 [1024, 16], P('fsdp')
- conv_grad: float32 [4, 4096], P(None, 'fsdp')
- decay_grad: float32 [2, 8], P(None, 'fsdp')
- mixer_grad: float32 [1024], P('fsdp')
- heads_grad: float32 [256], P('fsdp')
- output_grad: float32 [2048, 1024], P('fsdp')
- feed_grad: float32 [1024], P('fsdp')
- up_grad: float32 [1024, 5632], P('fsdp')
- down_grad: float32 [2816, 1024], P('fsdp')
Inputs may be any that keep to these rules, and one draw needn't show every extreme that they name: `head_decay`: row 0 holds the logarithms of the heads' decay rates, row 1 the offsets of their decay inputs.
All inputs are finite; a program needn't handle non-finite values.
Results may differ from a plain program's by a relative error of at most 0.019.
Values may be sent and summed in bfloat16 or wider, within the bound.
No kernel may reach another device: no remote copies, remote signals or barrier semaphores. Data moves between devices by JAX's collectives and lax.ppermute only.
A program may use at most 256 MiB of HBM per device.

v0:
```python
import jax
import jax.numpy as jnp
from jax import lax
from jax.sharding import PartitionSpec as P

H = 8
DK = 128
DV = 256
CONV = 4
BLOCK = 64


EPSILON = 1e-06


def rms_norm(values, scales):
    return values * lax.rsqrt(jnp.mean(values * values, axis=-1, keepdims=True) + EPSILON) * scales


def round_trip(values):
    return lax.optimization_barrier(values.astype(jnp.bfloat16)).astype(jnp.float32)


def short_conv(values, kernel, doc_ids):
    length = values.shape[0]
    result = values * kernel[0]
    for offset in range(1, kernel.shape[0]):
        shifted = jnp.concatenate(
            [jnp.zeros((offset,) + values.shape[1:], jnp.float32), values[: length - offset]],
            axis=0,
        )
        earlier = jnp.concatenate([jnp.full((offset,), -1, jnp.int32), doc_ids[: length - offset]])
        inside = (earlier == doc_ids).astype(jnp.float32)
        result = result + shifted * kernel[offset] * inside[:, None, None]
    return result


def block_step(carried_state, inputs):
    query_rows, key_rows, v, strength, log_decay, doc_ids, before = inputs
    block_len = query_rows.shape[1]
    query_rows = query_rows * query_rows.shape[2] ** (-0.5)
    cumulative = jnp.cumsum(log_decay, axis=-1)
    row_idx = lax.broadcasted_iota(jnp.int32, (block_len, block_len), 0)
    col_idx = lax.broadcasted_iota(jnp.int32, (block_len, block_len), 1)
    same_doc = doc_ids[:, None] == doc_ids[None, :]
    strictly = jnp.logical_and(same_doc, row_idx > col_idx)
    through = jnp.logical_and(same_doc, row_idx >= col_idx)
    spread = cumulative[:, :, None] - cumulative[:, None, :]
    strict = jnp.exp(jnp.where(strictly[None], spread, -1e30))
    within = jnp.exp(jnp.where(through[None], spread, -1e30))
    incoming_state = jnp.exp(cumulative) * (doc_ids == before).astype(jnp.float32)
    final_sum = cumulative[:, -1:]
    decay_to_last = jnp.exp(final_sum - cumulative) * (doc_ids == doc_ids[-1]).astype(jnp.float32)
    keep_factors = jnp.exp(final_sum[:, 0]) * (doc_ids[-1] == before).astype(jnp.float32)
    key_gram = jnp.einsum("nid,njd->nij", key_rows, key_rows, precision=lax.Precision.HIGHEST)
    system = jnp.eye(block_len, dtype=jnp.float32) + strength[:, :, None] * key_gram * strict
    targets = jnp.concatenate(
        [(strength * incoming_state)[:, :, None] * key_rows, strength[:, :, None] * v], axis=-1
    )
    triangular_result = jax.scipy.linalg.solve_triangular(
        system, targets, lower=True, unit_diagonal=True
    )
    key_portion = triangular_result[:, :, : key_rows.shape[2]]
    corrected_values = triangular_result[:, :, key_rows.shape[2] :] - jnp.einsum(
        "vfu,vub->vfb", key_portion, carried_state, precision=lax.Precision.HIGHEST
    )
    attention_scores = (
        jnp.einsum("nid,njd->nij", query_rows, key_rows, precision=lax.Precision.HIGHEST) * within
    )
    block_output = jnp.einsum(
        "vfu,vub->vfb",
        incoming_state[:, :, None] * query_rows,
        carried_state,
        precision=lax.Precision.HIGHEST,
    )
    block_output = block_output + jnp.einsum(
        "faq,fqp->fap", attention_scores, corrected_values, precision=lax.Precision.HIGHEST
    )
    next_state = keep_factors[:, None, None] * carried_state + jnp.einsum(
        "trz,trb->tzb",
        decay_to_last[:, :, None] * key_rows,
        corrected_values,
        precision=lax.Precision.HIGHEST,
    )
    return (next_state, block_output)


def prepare_heads(
    query_rows, key_rows, v, rate_inputs, kernel_q, kernel_k, kernel_v, decay_params, doc_ids
):
    query_rows = jax.nn.silu(short_conv(query_rows, kernel_q, doc_ids))
    key_rows = jax.nn.silu(short_conv(key_rows, kernel_k, doc_ids))
    v = jax.nn.silu(short_conv(v, kernel_v, doc_ids))
    query_rows = query_rows * lax.rsqrt(
        jnp.sum(query_rows * query_rows, axis=-1, keepdims=True) + EPSILON
    )
    key_rows = key_rows * lax.rsqrt(jnp.sum(key_rows * key_rows, axis=-1, keepdims=True) + EPSILON)
    strength = jax.nn.sigmoid(rate_inputs[:, :, 1])
    log_decay = -jnp.exp(decay_params[0]) * jax.nn.softplus(rate_inputs[:, :, 0] + decay_params[1])
    return (query_rows, key_rows, v, strength, log_decay)


def recurrence(query_rows, key_rows, v, strength, log_decay, doc_ids, block_size):
    length, head_count = (query_rows.shape[0], query_rows.shape[1])
    block_count = length // block_size

    def to_blocks(values):
        return jnp.swapaxes(values.reshape((block_count, block_size) + values.shape[1:]), 1, 2)

    doc_blocks = doc_ids.reshape(block_count, block_size)
    before = jnp.concatenate([jnp.full((1,), -1, jnp.int32), doc_blocks[:-1, -1]])
    initial = jnp.zeros((head_count, query_rows.shape[2], v.shape[2]), jnp.float32)
    inputs = (
        to_blocks(query_rows),
        to_blocks(key_rows),
        to_blocks(v),
        to_blocks(strength),
        to_blocks(log_decay),
        doc_blocks,
        before,
    )
    _, outputs = lax.scan(jax.checkpoint(block_step), initial, inputs)
    return jnp.swapaxes(outputs, 1, 2).reshape(length, head_count, v.shape[2])


def output_gate(mixed, gate_raw, scales):
    normed = rms_norm(mixed, scales) * jax.nn.silu(gate_raw).reshape(mixed.shape)
    return normed.reshape(mixed.shape[0], -1)


def residual_norm(values, attended, scales):
    hidden = values + attended
    return (hidden, rms_norm(hidden, scales))


def feed_act(gate_up):
    half_width = gate_up.shape[1] // 2
    return jax.nn.silu(gate_up[:, :half_width]) * gate_up[:, half_width:]


def head_starts(member, group):
    return (
        member * group * DK,
        H * DK + member * group * DK,
        2 * H * DK + member * group * DV,
        H * (2 * DK + DV) + member * group * DV,
    )


def take_heads(matrix, member, group, sections):
    widths = (group * DK, group * DK, group * DV, group * DV)
    starts = head_starts(member, group)
    return [
        lax.dynamic_slice_in_dim(matrix, s, w, 1)
        for s, w in zip(starts[:sections], widths[:sections])
    ]


def place_heads(target, sections_list, member, group):
    for section, offset in zip(sections_list, head_starts(member, group)):
        target = lax.dynamic_update_slice_in_dim(target, section, offset, 1)
    return target


def body(
    tokens,
    cotangent,
    doc_lengths,
    input_weight,
    rate_weight,
    conv_weight,
    head_decay,
    mixer_gain,
    heads_gain,
    output_weight,
    feed_gain,
    up_weight,
    down_weight,
):
    row_count = tokens.shape[0]
    sp_size = lax.axis_size("sp")
    seq_len = row_count * sp_size
    group = H // sp_size
    member = lax.axis_index("sp")
    qkv_cols = H * (2 * DK + DV)
    gathered = (
        lax.all_gather(input_weight, "fsdp", axis=0, tiled=True),
        lax.all_gather(rate_weight, "fsdp", axis=0, tiled=True),
        lax.all_gather(conv_weight, "fsdp", axis=1, tiled=True),
        lax.all_gather(head_decay, "fsdp", axis=1, tiled=True),
        lax.all_gather(mixer_gain, "fsdp", axis=0, tiled=True),
        lax.all_gather(heads_gain, "fsdp", axis=0, tiled=True),
        lax.all_gather(output_weight, "fsdp", axis=0, tiled=True),
        lax.all_gather(feed_gain, "fsdp", axis=0, tiled=True),
        lax.all_gather(up_weight, "fsdp", axis=0, tiled=True),
        lax.all_gather(down_weight, "fsdp", axis=0, tiled=True),
    )
    (
        in_full,
        rate_full,
        conv_full,
        decay_full,
        mixer_scale,
        heads_scale,
        out_full,
        feed_scale,
        up_full,
        down_full,
    ) = gathered
    ends = jnp.cumsum(doc_lengths[0])
    positions = lax.broadcasted_iota(jnp.int32, (seq_len, 1), 0)
    doc_ids = jnp.sum((positions >= ends[None, :]).astype(jnp.int32), axis=1)
    kernels = [
        kernel.reshape(CONV, group, -1)
        for kernel in take_heads(conv_full.astype(jnp.float32), member, group, 3)
    ]
    decay_group = lax.dynamic_slice_in_dim(decay_full.astype(jnp.float32), member * group, group, 1)

    def prep_local(
        query_rows, key_rows, v, rate_inputs, kernel_q, kernel_k, kernel_v, decay_params
    ):
        return prepare_heads(
            query_rows,
            key_rows,
            v,
            rate_inputs,
            kernel_q,
            kernel_k,
            kernel_v,
            decay_params,
            doc_ids,
        )

    def recur_local(query_rows, key_rows, v, strength, log_decay):
        return recurrence(query_rows, key_rows, v, strength, log_decay, doc_ids, BLOCK)

    def run_mixer(q_in, k_in, v_in, rate_in):
        prepared, pull_prep = jax.vjp(
            prep_local, q_in, k_in, v_in, rate_in, kernels[0], kernels[1], kernels[2], decay_group
        )
        rounded = (
            round_trip(prepared[0]),
            round_trip(prepared[1]),
            round_trip(prepared[2]),
            prepared[3],
            prepared[4],
        )
        mixed_out, pull_rec = jax.vjp(recur_local, *rounded)

        def pull_both(grad):
            return pull_prep(pull_rec(grad))

        return (mixed_out, pull_both)

    x_float = tokens.astype(jnp.float32)
    normed, pull_norm = jax.vjp(rms_norm, x_float, mixer_scale.astype(jnp.float32))
    normed_low = normed.astype(jnp.bfloat16)
    projected = jnp.dot(normed_low, in_full, preferred_element_type=jnp.float32)
    rate_raw = jnp.dot(normed_low, rate_full, preferred_element_type=jnp.float32)
    qkv_low = projected[:, :qkv_cols].astype(jnp.bfloat16)
    gate_raw = projected[:, qkv_cols:]
    q_tok = qkv_low[:, : H * DK].reshape(row_count, H, DK)
    k_tok = qkv_low[:, H * DK : 2 * H * DK].reshape(row_count, H, DK)
    v_tok = qkv_low[:, 2 * H * DK :].reshape(row_count, H, DV)
    rate_tok = rate_raw.astype(jnp.bfloat16).reshape(row_count, H, 2)
    q_grp, k_grp, v_grp, rate_grp = (
        lax.all_to_all(q_tok, "sp", split_axis=1, concat_axis=0, tiled=True),
        lax.all_to_all(k_tok, "sp", split_axis=1, concat_axis=0, tiled=True),
        lax.all_to_all(v_tok, "sp", split_axis=1, concat_axis=0, tiled=True),
        lax.all_to_all(rate_tok, "sp", split_axis=1, concat_axis=0, tiled=True),
    )
    mixed, pull_mix = run_mixer(
        q_grp.astype(jnp.float32),
        k_grp.astype(jnp.float32),
        v_grp.astype(jnp.float32),
        rate_grp.astype(jnp.float32),
    )
    mixed_tok = lax.all_to_all(
        mixed.astype(jnp.bfloat16), "sp", split_axis=0, concat_axis=1, tiled=True
    )
    gated, pull_gate = jax.vjp(
        output_gate, mixed_tok.astype(jnp.float32), gate_raw, heads_scale.astype(jnp.float32)
    )
    gated_low = gated.astype(jnp.bfloat16)
    attended = jnp.dot(gated_low, out_full, preferred_element_type=jnp.float32)
    (hidden, normed_two), pull_resid = jax.vjp(
        residual_norm, x_float, attended, feed_scale.astype(jnp.float32)
    )
    two_low = normed_two.astype(jnp.bfloat16)
    gate_up = jnp.dot(two_low, up_full, preferred_element_type=jnp.float32)
    activated, pull_act = jax.vjp(feed_act, gate_up)
    act_low = activated.astype(jnp.bfloat16)
    block_out = (hidden + jnp.dot(act_low, down_full, preferred_element_type=jnp.float32)).astype(
        jnp.bfloat16
    )
    down_grad = jnp.einsum("tf,td->fd", act_low, cotangent, preferred_element_type=jnp.float32)
    d_act = jnp.einsum("td,fd->tf", cotangent, down_full, preferred_element_type=jnp.float32)
    d_gate_up = pull_act(d_act)[0]
    d_gu_low = d_gate_up.astype(jnp.bfloat16)
    up_grad = jnp.einsum("td,tf->df", two_low, d_gu_low, preferred_element_type=jnp.float32)
    d_two = jnp.einsum("tf,df->td", d_gu_low, up_full, preferred_element_type=jnp.float32)
    d_resid, d_attended, feed_grad = pull_resid((cotangent.astype(jnp.float32), d_two))
    d_att_low = d_attended.astype(jnp.bfloat16)
    output_grad = jnp.einsum("te,td->ed", gated_low, d_att_low, preferred_element_type=jnp.float32)
    d_gated = jnp.einsum("td,ed->te", d_att_low, out_full, preferred_element_type=jnp.float32)
    d_mixed, d_gate, heads_grad = pull_gate(d_gated)
    d_mixed_grp = lax.all_to_all(
        d_mixed.astype(jnp.bfloat16), "sp", split_axis=1, concat_axis=0, tiled=True
    )
    mix_grads = pull_mix(d_mixed_grp.astype(jnp.float32))
    back_q, back_k, back_v, back_rate = (
        lax.all_to_all(
            mix_grads[0].astype(jnp.bfloat16), "sp", split_axis=0, concat_axis=1, tiled=True
        ),
        lax.all_to_all(
            mix_grads[1].astype(jnp.bfloat16), "sp", split_axis=0, concat_axis=1, tiled=True
        ),
        lax.all_to_all(
            mix_grads[2].astype(jnp.bfloat16), "sp", split_axis=0, concat_axis=1, tiled=True
        ),
        lax.all_to_all(
            mix_grads[3].astype(jnp.bfloat16), "sp", split_axis=0, concat_axis=1, tiled=True
        ),
    )
    d_project = jnp.concatenate(
        [
            back_q.reshape(row_count, -1),
            back_k.reshape(row_count, -1),
            back_v.reshape(row_count, -1),
            d_gate.astype(jnp.bfloat16),
        ],
        axis=1,
    )
    d_rate_low = back_rate.reshape(row_count, 2 * H)
    input_grad = jnp.einsum("td,tf->df", normed_low, d_project, preferred_element_type=jnp.float32)
    rate_grad = jnp.einsum("td,tf->df", normed_low, d_rate_low, preferred_element_type=jnp.float32)
    d_normed = jnp.einsum("tf,df->td", d_project, in_full, preferred_element_type=jnp.float32)
    d_normed = d_normed + jnp.einsum(
        "tf,df->td", d_rate_low, rate_full, preferred_element_type=jnp.float32
    )
    conv_sections = [
        mix_grads[4].reshape(CONV, -1),
        mix_grads[5].reshape(CONV, -1),
        mix_grads[6].reshape(CONV, -1),
    ]
    conv_grad = place_heads(jnp.zeros(conv_full.shape, jnp.float32), conv_sections, member, group)
    decay_grad = lax.dynamic_update_slice_in_dim(
        jnp.zeros(decay_full.shape, jnp.float32), mix_grads[7], member * group, 1
    )
    d_front, mixer_grad = pull_norm(d_normed)
    tokens_grad = (d_resid + d_front).astype(jnp.bfloat16)
    shards = (
        lax.psum_scatter(
            input_grad.astype(jnp.bfloat16), "fsdp", scatter_dimension=0, tiled=True
        ).astype(jnp.float32),
        lax.psum_scatter(
            rate_grad.astype(jnp.bfloat16), "fsdp", scatter_dimension=0, tiled=True
        ).astype(jnp.float32),
        lax.psum_scatter(
            conv_grad.astype(jnp.bfloat16), "fsdp", scatter_dimension=1, tiled=True
        ).astype(jnp.float32),
        lax.psum_scatter(
            decay_grad.astype(jnp.bfloat16), "fsdp", scatter_dimension=1, tiled=True
        ).astype(jnp.float32),
        lax.psum_scatter(
            mixer_grad.astype(jnp.bfloat16), "fsdp", scatter_dimension=0, tiled=True
        ).astype(jnp.float32),
        lax.psum_scatter(
            heads_grad.astype(jnp.bfloat16), "fsdp", scatter_dimension=0, tiled=True
        ).astype(jnp.float32),
        lax.psum_scatter(
            output_grad.astype(jnp.bfloat16), "fsdp", scatter_dimension=0, tiled=True
        ).astype(jnp.float32),
        lax.psum_scatter(
            feed_grad.astype(jnp.bfloat16), "fsdp", scatter_dimension=0, tiled=True
        ).astype(jnp.float32),
        lax.psum_scatter(
            up_grad.astype(jnp.bfloat16), "fsdp", scatter_dimension=0, tiled=True
        ).astype(jnp.float32),
        lax.psum_scatter(
            down_grad.astype(jnp.bfloat16), "fsdp", scatter_dimension=0, tiled=True
        ).astype(jnp.float32),
    )
    totals = lax.psum(
        (
            shards[0],
            shards[1],
            shards[2],
            shards[3],
            shards[4],
            shards[5],
            shards[6],
            shards[7],
            shards[8],
            shards[9],
        ),
        ("dp", "sp"),
    )
    return (
        block_out,
        tokens_grad,
        totals[0],
        totals[1],
        totals[2],
        totals[3],
        totals[4],
        totals[5],
        totals[6],
        totals[7],
        totals[8],
        totals[9],
    )


def solution(mesh):
    return jax.shard_map(
        body,
        mesh=mesh,
        in_specs=(
            P(("dp", "fsdp", "sp"), None),
            P(("dp", "fsdp", "sp"), None),
            P(("dp", "fsdp"), None),
            P("fsdp", None),
            P("fsdp", None),
            P(None, "fsdp"),
            P(None, "fsdp"),
            P("fsdp"),
            P("fsdp"),
            P("fsdp", None),
            P("fsdp"),
            P("fsdp", None),
            P("fsdp", None),
        ),
        out_specs=(
            P(("dp", "fsdp", "sp"), None),
            P(("dp", "fsdp", "sp"), None),
            P("fsdp", None),
            P("fsdp", None),
            P(None, "fsdp"),
            P(None, "fsdp"),
            P("fsdp"),
            P("fsdp"),
            P("fsdp", None),
            P("fsdp"),
            P("fsdp", None),
            P("fsdp", None),
        ),
        check_vma=False,
    )
```

profile of v0, /device:TPU:0, one launch (start us, length us, event | category | flops | bytes accessed | tf_op | source)
XLA Modules:
  0.0 2757.3 jit_solution(14248056916708624807)
XLA Ops:
  9.4 12.6 all-gather.1
  22.1 22.6 all_gather.32
  51.9 10.8 all-gather
  63.6 17.6 all_gather.34
  82.2 149.1 %all-gather.8.cloned.1.call-done = bf16[1024,6144]{1,0:T(8,128)(2,1)} async-done(((bf16[256,6144]{1,0:T(8,128)(2,1)}), bf16[1024,6144]{1,0:T(8,128)(2,1)}) %all-gather.8.cloned.1.call-update) | async-done | bytes 12582928 | tf_op jit(solution)/shard_map/all_gather | solution.py:187
  231.3 12.1 fusion.214
  252.1 9.5 all-to-all-done.3
  269.4 7.2 all-to-all-done.1
  276.6 5.1 all-to-all-start.2
  291.6 8.2 all-to-all-done.2
  308.5 424.8 %while.42 = (s32[]{:T(128)}, f32[4,128,256]{2,1,0:T(8,128)S(1)}, bf16[12,4,64,256]{3,2,0,1:T(8,128)(2,1)}, f32[12,4,128,256]{3,2,1,0:T(8,128)}, f32[12,4,64]{2,1...) while((s32[]{:T(128)}, f32[4,128,256]{2,1,0:T(8,128)S(1)}, ...), condition=%wide.region_7.9_spmd.clone, body=%wide.region_5.8_spmd.clone.sunk | while | flops 479585600 | bytes 7765844 | solution.py:122
  317.9 19.7 custom-call.25
  353.3 19.7 custom-call.25
  388.7 19.7 custom-call.25
  424.1 19.7 custom-call.25
  459.6 19.7 custom-call.25
  494.9 19.7 custom-call.25
  530.4 19.7 custom-call.25
  565.8 19.7 custom-call.25
  601.2 19.7 custom-call.25
  636.6 19.7 custom-call.25
  672.0 19.7 custom-call.25
  707.4 19.7 custom-call.25
  737.1 4.8 all-to-all-start.4
  743.5 8.6 all-reduce.41
  752.1 9.3 all-gather.2
  768.9 5.4 reshape.1011
  782.9 5.6 multiply_reduce_fusion.23
  788.5 12.8 fusion.201
  801.3 13.3 fusion.174
  814.6 13.5 multiply_reduce_fusion.13
  830.8 9.2 fusion.178
  840.0 5.2 mul.1624
  857.0 13.9 all-to-all-done.5
  878.1 520.6 %while.43 = (s32[]{:T(128)}, f32[4,128,256]{2,1,0:T(8,128)S(1)}, f32[12,4,64,128]{3,2,0,1:T(8,128)}, f32[12,4,64,128]{3,2,0,1:T(8,128)}, f32[12,4,64,256]{3,2,0,...) while((s32[]{:T(128)}, f32[4,128,256]{2,1,0:T(8,128)S(1)}, ...), condition=%wide.region_24.26_spmd.clone, body=%wide.region_12.25_spmd.clone.sunk | while | flops 1198436864 | bytes 24068516 | solution.py:122
  890.9 19.7 custom-call.26
  934.3 19.7 custom-call.26
  977.6 19.7 custom-call.26
  1020.9 19.7 custom-call.26
  1064.3 19.7 custom-call.26
  1107.6 19.7 custom-call.26
  1151.0 19.7 custom-call.26
  1194.3 19.7 custom-call.26
  1237.7 19.7 custom-call.26
  1281.0 19.7 custom-call.26
  1324.3 19.7 custom-call.26
  1367.7 19.7 custom-call.26
  1398.7 5.5 multiply_reduce_fusion.10
  1417.6 5.5 multiply_reduce_fusion.21
  1438.7 7.1 multiply_reduce_fusion.7
  1454.7 5.8 convolution_convert_fusion.3
  1461.6 6.8 convolution_convert_fusion.2
  1469.9 12.6 convolution_convert_fusion
  1490.3 5.4 all-to-all-done.7
  1502.4 7.5 all-to-all-done.6
  1519.2 6.6 all-to-all-done.8
  1530.0 11.9 convolution_convert_fusion.1
  1544.0 7.2 add_convert_fusion.4
  1552.7 11.5 fusion.172
  1566.4 10.4 all-reduce.47
  1579.8 101.7 %reduce-scatter.18.cloned.1.call-done = bf16[704,1024]{1,0:T(8,128)(2,1)} async-done(((bf16[2816,1024]{1,0:T(8,128)(2,1)}), bf16[704,1024]{1,0:T(8,128)(2,1)}) %reduce-scatter.18.cloned.1.call-update) | async-done | bytes 1441808 | tf_op jit(solution)/shard_map/reduce_scatter | solution.py:380
  1681.5 198.0 %reduce-scatter.16.cloned.1.call-done = bf16[256,5632]{1,0:T(8,128)(2,1)} async-done(((bf16[1024,5632]{1,0:T(8,128)(2,1)}), bf16[256,5632]{1,0:T(8,128)(2,1)}) %reduce-scatter.16.cloned.1.call-update) | async-done | bytes 2883600 | tf_op jit(solution)/shard_map/reduce_scatter | solution.py:377
  1879.5 215.3 %reduce-scatter.10.cloned.1.call-done = bf16[256,6144]{1,0:T(8,128)(2,1)} async-done(((bf16[1024,6144]{1,0:T(8,128)(2,1)}), bf16[256,6144]{1,0:T(8,128)(2,1)}) %reduce-scatter.10.cloned.1.call-update) | async-done | bytes 3145744 | tf_op jit(solution)/shard_map/reduce_scatter | solution.py:353
  2094.7 655.6 %all-reduce.49 = (f32[256,6144]{1,0:T(8,128)}, f32[256,16]{0,1:T(8,128)}, f32[4,1024]{1,0:T(4,128)}, f32[2,2]{1,0:T(2,128)}, f32[256]{0:T(256)}, /*index=5*/f32[...) all-reduce(bf16[256,6144]{1,0:T(8,128)(2,1)} %reduce-scatter.10.clo, ...), channel_id=1, replica_groups=mesh['dp'=4,'fsdp'=4,'sp'=2] {'dp','sp'}, use_global_device_ids=true, to_apply=%region_29.31 | all-reduce | flops 4268612 | bytes 25612832 | tf_op jit(solution)/shard_map/psum | solution.py:384
  (1342 shorter events, 600.2 us)
Async XLA Ops:
  7.2 224.2 %all-gather.8.cloned.1.call-start = ((), (), s32[]{:S(2)}) async-start(), calls=%async_computation.16 | async-start | bytes 15728640 | tf_op jit(solution)/shard_map/all_gather | solution.py:187
  7.9 775.0 %all-gather.10.cloned.1.call-start = ((), (), s32[]{:S(2)}) async-start(), calls=%async_computation.17 | async-start | bytes 5242880 | tf_op jit(solution)/shard_map/all_gather | solution.py:193
  8.7 13.4 copy-start.93
  8.7 36.1 %copy-start.22 = (bf16[384,1024]{1,0:T(8,128)(2,1)S(1)}, bf16[384,1024]{1,0:T(8,128)(2,1)}, u32[]{:S(2)}) copy-start(bf16[384,1024]{1,0:T(8,128)(2,1)} %param.19) | copy-start | bytes 2359300
  8.7 779.8 %all-gather.12.cloned.1.call-start = ((), (), s32[]{:S(2)}) async-start(), calls=%async_computation.18 | async-start | bytes 14417920 | tf_op jit(solution)/shard_map/all_gather | solution.py:195
  22.1 209.3 %copy-start.51 = (f32[4,1,256]{2,1,0:T(1,128)}, f32[4,1,256]{2,1,0:T(1,128)S(1)}, u32[]{:S(2)}) copy-start(f32[4,1,256]{2,1,0:T(1,128)S(1)} %convert_element_type.423) | copy-start | bytes 12292
  45.6 185.8 %copy-start.53 = (f32[384]{0:T(512)}, f32[384]{0:T(512)S(1)}, u32[]{:S(2)}) copy-start(f32[384]{0:T(512)S(1)} %fusion.193) | copy-start | bytes 4612
  46.0 17.1 copy-start.102
  46.0 17.7 copy-start.94
  46.6 200.2 %all-to-all-start = ((bf16[384,8,2]{0,2,1:T(2,128)(2,1)}), bf16[384,8,2]{0,2,1:T(2,128)(2,1)S(1)}, u32[]{:S(2)}, u32[]{:S(2)}) async-start(bf16[384,8,2]{0,2,1:T(2,128)(2,1)} %reshape.968), calls=%async_computation | async-start | bytes 24576 | tf_op jit(solution)/shard_map/all_to_all | solution.py:270
  49.8 751.5 %all-gather.14.cloned.1.call-start = ((), (), s32[]{:S(2)}) async-start(), calls=%async_computation.19 | async-start | bytes 7208960 | tf_op jit(solution)/shard_map/all_gather | solution.py:196
  63.1 18.1 copy-start.95
  63.1 202.9 %copy-start.79 = (f32[4]{0:T(128)}, f32[4]{0:T(128)S(1)}, u32[]{:S(2)}) copy-start(f32[4]{0:T(128)S(1)} %get-tuple-element.951) | copy-start | bytes 52
  63.1 202.9 %copy-start.82 = (f32[4]{0:T(128)}, f32[4]{0:T(128)S(1)}, u32[]{:S(2)}) copy-start(f32[4]{0:T(128)S(1)} %get-tuple-element.952) | copy-start | bytes 52
  82.1 201.0 %copy-start.57 = (f32[1,512]{1,0:T(1,128)}, f32[1,512]{1,0:T(1,128)S(1)}, u32[]{:S(2)}) copy-start(f32[1,512]{1,0:T(1,128)S(1)} %get-tuple-element.964) | copy-start | bytes 6148
  82.1 201.0 %copy-start.59 = (f32[1,512]{1,0:T(1,128)}, f32[1,512]{1,0:T(1,128)S(1)}, u32[]{:S(2)}) copy-start(f32[1,512]{1,0:T(1,128)S(1)} %get-tuple-element.965) | copy-start | bytes 6148
  82.1 201.0 %copy-start.61 = (f32[1,512]{1,0:T(1,128)}, f32[1,512]{1,0:T(1,128)S(1)}, u32[]{:S(2)}) copy-start(f32[1,512]{1,0:T(1,128)S(1)} %get-tuple-element.966) | copy-start | bytes 6148
  82.1 201.0 %copy-start.63 = (f32[1,512]{1,0:T(1,128)}, f32[1,512]{1,0:T(1,128)S(1)}, u32[]{:S(2)}) copy-start(f32[1,512]{1,0:T(1,128)S(1)} %get-tuple-element.961) | copy-start | bytes 6148
  82.1 201.0 %copy-start.65 = (f32[1,512]{1,0:T(1,128)}, f32[1,512]{1,0:T(1,128)S(1)}, u32[]{:S(2)}) copy-start(f32[1,512]{1,0:T(1,128)S(1)} %get-tuple-element.962) | copy-start | bytes 6148
  82.1 201.0 %copy-start.67 = (f32[1,512]{1,0:T(1,128)}, f32[1,512]{1,0:T(1,128)S(1)}, u32[]{:S(2)}) copy-start(f32[1,512]{1,0:T(1,128)S(1)} %get-tuple-element.963) | copy-start | bytes 6148
  82.1 201.0 %copy-start.69 = (f32[1,512]{1,0:T(1,128)}, f32[1,512]{1,0:T(1,128)S(1)}, u32[]{:S(2)}) copy-start(f32[1,512]{1,0:T(1,128)S(1)} %get-tuple-element.928) | copy-start | bytes 6148
  82.1 201.0 %copy-start.71 = (f32[1,512]{1,0:T(1,128)}, f32[1,512]{1,0:T(1,128)S(1)}, u32[]{:S(2)}) copy-start(f32[1,512]{1,0:T(1,128)S(1)} %get-tuple-element.927) | copy-start | bytes 6148
  246.8 14.8 all-to-all-start.3
  251.0 15.1 copy-start.49
  251.1 14.8 copy-start.41
  261.6 14.9 all-to-all-start.1
  269.4 13.8 copy-start.5
  276.6 23.2 all-to-all-start.2
  737.1 15.0 copy-start.104
  737.1 24.3 all-to-all-start.4
  761.4 66.8 %copy-start.76 = (f32[4,1,256]{2,1,0:T(1,128)}, f32[4,1,256]{2,1,0:T(1,128)S(1)}, u32[]{:S(2)}) copy-start(f32[4,1,256]{2,1,0:T(1,128)S(1)} %convert_element_type.424) | copy-start | bytes 12292
  788.5 39.7 %copy-start.85 = (f32[384]{0:T(512)}, f32[384]{0:T(512)S(1)}, u32[]{:S(2)}) copy-start(f32[384]{0:T(512)S(1)} %fusion.194) | copy-start | bytes 4612
  801.3 13.3 copy-start.37
  830.8 9.2 copy-start.24
  853.3 17.6 all-to-all-start.5
  1398.6 34.9 %copy-start.43 = (f32[12,4,64]{2,0,1:T(8,128)}, f32[12,4,64]{2,0,1:T(8,128)S(1)}, u32[]{:S(2)}) copy-start(f32[12,4,64]{2,0,1:T(8,128)S(1)} %get-tuple-element.500) | copy-start | bytes 36868
  1435.3 16.4 all-to-all-start.9
  1438.6 7.2 copy-start.73
  1438.6 7.2 copy-start.74
  1438.6 7.2 copy-start.75
  1438.6 7.2 copy-start.72
  1438.6 113.0 %reduce-scatter.20.cloned.1.call-start = ((), (), s32[]{:S(2)}) async-start(), calls=%async_computation.25 | async-start | bytes 1310720
  1438.7 7.2 copy-start.7
  1438.7 7.2 copy-start.17
  1438.7 7.2 copy-start.29
  1438.7 7.2 copy-start.30
  1451.7 101.0 %reduce-scatter.12.cloned.1.call-start = ((), (), s32[]{:S(2)}) async-start(), calls=%async_computation.21 | async-start | bytes 40960 | tf_op jit(solution)/shard_map/reduce_scatter | solution.py:356
  1454.6 125.2 %reduce-scatter.14.cloned.1.call-start = ((), (), s32[]{:S(2)}) async-start(), calls=%async_computation.22 | async-start | bytes 5242880 | tf_op jit(solution)/shard_map/reduce_scatter | solution.py:371
  1460.5 221.0 %reduce-scatter.18.cloned.1.call-start = ((), (), s32[]{:S(2)}) async-start(), calls=%async_computation.24 | async-start | bytes 7208960 | tf_op jit(solution)/shard_map/reduce_scatter | solution.py:380
  1468.5 411.0 %reduce-scatter.16.cloned.1.call-start = ((), (), s32[]{:S(2)}) async-start(), calls=%async_computation.23 | async-start | bytes 14417920 | tf_op jit(solution)/shard_map/reduce_scatter | solution.py:377
  1484.0 11.7 all-to-all-start.7
  1487.6 12.5 copy-start.32
  1495.7 14.2 all-to-all-start.6
  1509.9 15.9 all-to-all-start.8
  1513.6 581.1 %reduce-scatter.10.cloned.1.call-start = ((), (), s32[]{:S(2)}) async-start(), calls=%async_computation.20 | async-start | bytes 15728640 | tf_op jit(solution)/shard_map/reduce_scatter | solution.py:353
  1543.9 7.2 copy-start.42
  1543.9 7.2 copy-start.44
  1543.9 7.2 copy-start.81
  1543.9 7.2 copy-start.84
  1543.9 7.4 copy-start.96
  1543.9 8.8 copy-start.36
  1552.7 11.6 copy-start.48
  1564.2 12.8 copy-start.56
  1577.1 517.6 %copy-start.78 = (bf16[256,16]{0,1:T(8,128)(2,1)S(1)}, bf16[256,16]{0,1:T(8,128)(2,1)}, u32[]{:S(2)}) copy-start(bf16[256,16]{0,1:T(8,128)(2,1)} %reduce-scatter.12.cloned.1.call-done) | copy-start | bytes 24580
  (72 other events, 184.1 us)
Sparse Core Ops, SparseCore 0:
  9.6 221.7 all-gather.7
  232.9 79.0 all-gather.9
  313.5 200.1 all-gather.11
  515.1 104.3 all-gather.13
  1451.8 25.7 reduce-scatter.19
  1479.8 17.5 reduce-scatter.11
  1500.3 75.3 reduce-scatter.13
  1578.6 102.8 reduce-scatter.17
  1684.0 195.4 reduce-scatter.15
  1881.8 212.8 reduce-scatter.9
where the time goes:
time: 2770 us; the launch traced here: 2760 us
  blocking collectives  748 us (27%)
  waiting for transfers between devices  725 us (26%)
  other arithmetic  653 us (24%)
  matrix products  359 us (13%)
  local copies, waits for them, and re-layouts  178 us (6%)
  starting transfers between devices  39.8 us (1%)
  loops' own time  35.9 us (1%)
    psum x1, blocking collectives, body(): lax.psum((shards[0], shards[1], shards[2], shards[3], shards[4], shards[5...  656 us
    another operation x96, other arithmetic, block_step(): jax.scipy.linalg.solve_triangular(system, targets, lower=True, unit_diago...  475 us
    reduce_scatter x1, waiting for transfers between devices, body(): lax.psum_scatter(input_grad.astype(jnp.bfloat16), 'fsdp', scatter_dimensi...  215 us
    reduce_scatter x1, waiting for transfers between devices, body(): lax.psum_scatter(up_grad.astype(jnp.bfloat16), 'fsdp', scatter_dimension=...  198 us
    all_gather x1, waiting for transfers between devices, body(): lax.all_gather(input_weight, 'fsdp', axis=0, tiled=True)  149 us
    reduce_scatter x1, waiting for transfers between devices, body(): lax.psum_scatter(down_grad.astype(jnp.bfloat16), 'fsdp', scatter_dimensio...  102 us
  transfers between devices with their start and end apart: 20, of which 11 were waited for; matrix products, arithmetic and copies ran while one was open for 21% of the time, Pallas kernels for 0%

commit v1 on v0

v1 whole, which is shorter than its diff:
```python
import jax
import jax.numpy as jnp
from jax import lax
from jax.experimental import pallas as pl
from jax.experimental.pallas import tpu as pltpu
from jax.sharding import PartitionSpec as P

H = 8
DK = 128
DV = 256
CONV = 4
BLOCK = 64
EPSILON = 1e-06
HALO = 16
STACK = 4
ROWS = STACK * BLOCK
SCALE = DK ** (-0.5)
VMEM_BYTES = 56 * 1024 * 1024
F32 = jnp.float32
BF16 = jnp.bfloat16


def mm(a, b, dims=((1,), (0,))):
    return lax.dot_general(
        a.astype(BF16), b.astype(BF16), (dims, ((), ())), preferred_element_type=F32
    )


def halves(a):
    high = a.astype(BF16)
    return high, (a - high.astype(F32)).astype(BF16)


def mm_fine(a, b):
    (ah, al), (bh, bl) = a, b
    return mm(ah, bh) + (mm(ah, bl) + mm(al, bh))


def stack_heads(ref, block, group, base, width):
    rows = pl.ds(pl.multiple_of(block * BLOCK, BLOCK), BLOCK)
    return jnp.concatenate(
        [
            ref[rows, base + (group * STACK + h) * width : base + (group * STACK + h + 1) * width]
            for h in range(STACK)
        ],
        axis=0,
    )


def store_heads(ref, block, group, base, width, value):
    rows = pl.ds(pl.multiple_of(block * BLOCK, BLOCK), BLOCK)
    for h in range(STACK):
        start = base + (group * STACK + h) * width
        ref[rows, start : start + width] = value[h * BLOCK : (h + 1) * BLOCK].astype(ref.dtype)


def head(value, h):
    return value[h * BLOCK : (h + 1) * BLOCK]


def columns(col_ref, block, group):
    packed = col_ref[block, group]
    return [packed[:, i : i + 1] for i in range(6)]


def decay_matrix(cum, doc, row_ref, block, group):
    rows = row_ref[block, group]
    i = lax.broadcasted_iota(jnp.int32, (ROWS, ROWS), 0)
    j = lax.broadcasted_iota(jnp.int32, (ROWS, ROWS), 1)
    inside = ((i // BLOCK) == (j // BLOCK)) & (i >= j) & (doc == rows[1:2])
    decay = jnp.exp(jnp.where(inside, cum - rows[0:1], -1e30))
    return decay, jnp.where(i > j, decay, 0.0)


def unit_inverse(lower):
    i = lax.broadcasted_iota(jnp.int32, (ROWS, ROWS), 0)
    j = lax.broadcasted_iota(jnp.int32, (ROWS, ROWS), 1)
    apart = jnp.bitwise_xor(i, j)
    inverse = jnp.where(i == j, 1.0, 0.0) - jnp.where(apart == 1, lower, 0.0)
    size = 2
    while size < BLOCK:
        cross = jnp.where((apart >= size) & (apart < 2 * size), lower, 0.0)
        parts = halves(inverse)
        inverse = inverse - mm_fine(parts, halves(mm_fine(halves(cross), parts)))
        size *= 2
    return inverse


def conv_taps(x, masks, weights):
    taps = [x[HALO:]]
    for s in range(1, CONV):
        taps.append(pltpu.roll(x, s, 0)[HALO:] * masks[s - 1])
    z = taps[0] * weights[0:1]
    for s in range(1, CONV):
        z = z + taps[s] * weights[s : s + 1]
    return taps, z


def conv_masks(mask_ref, length):
    return [
        jnp.broadcast_to(mask_ref[:, s : s + 1], (length, 128)) for s in range(CONV - 1)
    ]


def prepare_kernel(x_ref, cw_ref, mask_ref, col_ref, row_ref, n_ref, inv_ref, state_ref):
    length = n_ref.shape[0]
    blocks = length // BLOCK
    qk_cols = 2 * H * DK

    def chunk(c, normalise):
        lanes = pl.ds(pl.multiple_of(c * 128, 128), 128)
        masks = conv_masks(mask_ref, length)
        _, z = conv_taps(x_ref[:, lanes].astype(F32), masks, cw_ref[:, lanes])
        y = z * jax.nn.sigmoid(z)
        if normalise:
            y = y * lax.rsqrt(jnp.sum(y * y, axis=1, keepdims=True) + EPSILON)
        n_ref[:, lanes] = y.astype(BF16)

    @pl.loop(0, qk_cols // 128)
    def _(c):
        chunk(c, True)

    @pl.loop(qk_cols // 128, x_ref.shape[1] // 128)
    def _(c):
        chunk(c, False)

    @pl.loop(0, blocks)
    def _(block):
        for group in range(H // STACK):
            cum, beta, _, _, _, doc = columns(col_ref, block, group)
            keys = stack_heads(n_ref, block, group, H * DK, DK)
            _, strict = decay_matrix(cum, doc, row_ref, block, group)
            gram = mm(keys, keys, ((1,), (1,)))
            inv_ref[block, group] = unit_inverse(beta * gram * strict)

    state_ref[...] = jnp.zeros_like(state_ref)
    state_steps(n_ref, inv_ref, col_ref, state_ref)


def state_steps(n_ref, inv_ref, col_ref, state_ref):
    @pl.loop(0, n_ref.shape[0] // BLOCK)
    def _(block):
        for group in range(H // STACK):
            _, beta, a, d, kappa, _ = columns(col_ref, block, group)
            keys = stack_heads(n_ref, block, group, H * DK, DK)
            values = stack_heads(n_ref, block, group, 2 * H * DK, DV).astype(F32)
            seen = jnp.concatenate(
                [mm(head(keys, h), state_ref[group * STACK + h]) for h in range(STACK)], axis=0
            )
            corrected = mm(inv_ref[block, group], beta * (values - a * seen))
            update = d * corrected
            for h in range(STACK):
                n = group * STACK + h
                state_ref[n] = kappa[h * BLOCK : h * BLOCK + 1] * state_ref[n] + mm(
                    head(keys, h), head(update, h), ((0,), (0,))
                )


def state_kernel(n_ref, inv_ref, col_ref, start_ref, state_ref):
    state_ref[...] = start_ref[...].astype(F32)
    state_steps(n_ref, inv_ref, col_ref, state_ref)


def scan_kernel(n_ref, inv_ref, col_ref, row_ref, start_ref, out_ref, cor_ref, states_ref, state):
    state[...] = start_ref[...].astype(F32)

    @pl.loop(0, n_ref.shape[0] // BLOCK)
    def _(block):
        for group in range(H // STACK):
            cum, beta, a, d, kappa, doc = columns(col_ref, block, group)
            queries = stack_heads(n_ref, block, group, 0, DK)
            keys = stack_heads(n_ref, block, group, H * DK, DK)
            values = stack_heads(n_ref, block, group, 2 * H * DK, DV).astype(F32)
            within, _ = decay_matrix(cum, doc, row_ref, block, group)
            scores = SCALE * mm(queries, keys, ((1,), (1,))) * within
            both = []
            for h in range(STACK):
                low = state[group * STACK + h].astype(BF16)
                states_ref[block, group * STACK + h] = low
                both.append(mm(jnp.concatenate([head(keys, h), head(queries, h)], axis=0), low))
            seen = jnp.concatenate([b[:BLOCK] for b in both], axis=0)
            asked = jnp.concatenate([b[BLOCK:] for b in both], axis=0)
            corrected = mm(inv_ref[block, group], beta * (values - a * seen))
            cor_ref[block, group] = corrected.astype(BF16)
            out = (SCALE * a) * asked + mm(scores, corrected)
            store_heads(out_ref, block, group, 0, DV, out)
            update = d * corrected
            for h in range(STACK):
                n = group * STACK + h
                state[n] = kappa[h * BLOCK : h * BLOCK + 1] * state[n] + mm(
                    head(keys, h), head(update, h), ((0,), (0,))
                )


def back_state_kernel(n_ref, inv_ref, col_ref, row_ref, dout_ref, start_ref, dstate_ref):
    blocks = n_ref.shape[0] // BLOCK
    dstate_ref[...] = start_ref[...].astype(F32)

    @pl.loop(0, blocks)
    def _(step):
        block = blocks - 1 - step
        for group in range(H // STACK):
            cum, beta, a, d, kappa, doc = columns(col_ref, block, group)
            queries = stack_heads(n_ref, block, group, 0, DK)
            keys = stack_heads(n_ref, block, group, H * DK, DK)
            within, _ = decay_matrix(cum, doc, row_ref, block, group)
            scores = SCALE * mm(queries, keys, ((1,), (1,))) * within
            dout = stack_heads(dout_ref, block, group, 0, DV)
            wide = (SCALE * a) * dout.astype(F32)
            pulled = jnp.concatenate(
                [mm(head(keys, h), dstate_ref[group * STACK + h]) for h in range(STACK)], axis=0
            )
            d_cor = mm(scores, dout, ((0,), (0,))) + d * pulled
            d_right = mm(inv_ref[block, group], d_cor, ((0,), (0,)))
            d_seen = (-a * beta) * d_right
            for h in range(STACK):
                n = group * STACK + h
                left = jnp.concatenate([head(keys, h), head(queries, h)], axis=0)
                right = jnp.concatenate([head(d_seen, h), head(wide, h)], axis=0)
                dstate_ref[n] = kappa[h * BLOCK : h * BLOCK + 1] * dstate_ref[n] + mm(
                    left, right, ((0,), (0,))
                )


def back_kernel(
    x_ref,
    cw_ref,
    mask_ref,
    n_ref,
    inv_ref,
    col_ref,
    row_ref,
    dout_ref,
    cor_ref,
    states_ref,
    start_ref,
    dx_ref,
    dcw_ref,
    gcol_ref,
    grow_ref,
    dstate,
    dn_ref,
):
    length = n_ref.shape[0]
    blocks = length // BLOCK
    dstate[...] = start_ref[...].astype(F32)

    @pl.loop(0, blocks)
    def _(step):
        block = blocks - 1 - step
        for group in range(H // STACK):
            cum, beta, a, d, kappa, doc = columns(col_ref, block, group)
            queries = stack_heads(n_ref, block, group, 0, DK)
            keys = stack_heads(n_ref, block, group, H * DK, DK)
            values = stack_heads(n_ref, block, group, 2 * H * DK, DV).astype(F32)
            within, strict = decay_matrix(cum, doc, row_ref, block, group)
            scores = SCALE * mm(queries, keys, ((1,), (1,))) * within
            weighted = mm(keys, keys, ((1,), (1,))) * strict
            dout = stack_heads(dout_ref, block, group, 0, DV)
            dout_wide = dout.astype(F32)
            corrected = cor_ref[block, group]
            cor_wide = corrected.astype(F32)
            wide = (SCALE * a) * dout_wide
            pulled, seen, asked, dk_state, d_kappa = [], [], [], [], []
            update = (d * cor_wide).astype(BF16)
            for h in range(STACK):
                n = group * STACK + h
                state = states_ref[block, n]
                after = dstate[n]
                after_low = after.astype(BF16)
                both = mm(jnp.concatenate([head(keys, h), head(queries, h)], axis=0), state)
                seen.append(both[:BLOCK])
                asked.append(both[BLOCK:])
                pulled.append(mm(head(keys, h), after_low))
                dk_state.append(mm(head(update, h), after_low, ((1,), (1,))))
                total = jnp.sum(
                    jnp.sum(state.astype(F32) * after, axis=0, keepdims=True),
                    axis=1,
                    keepdims=True,
                )
                d_kappa.append(jnp.broadcast_to(total * (1.0 / BLOCK), (BLOCK, 1)))
            pulled, seen, asked, d_kappa = (
                jnp.concatenate(p, axis=0) for p in (pulled, seen, asked, d_kappa)
            )
            d_cor = mm(scores, dout, ((0,), (0,))) + d * pulled
            d_right = mm(inv_ref[block, group], d_cor, ((0,), (0,)))
            scaled = beta * d_right
            d_seen = -a * scaled
            dk_left, dq_left = [], []
            for h in range(STACK):
                n = group * STACK + h
                left = jnp.concatenate([head(keys, h), head(queries, h)], axis=0)
                right = jnp.concatenate([head(d_seen, h), head(wide, h)], axis=0).astype(BF16)
                both = mm(right, states_ref[block, n], ((1,), (1,)))
                dk_left.append(both[:BLOCK])
                dq_left.append(both[BLOCK:])
                dstate[n] = kappa[h * BLOCK : h * BLOCK + 1] * dstate[n] + mm(
                    left, right, ((0,), (0,))
                )
            d_scores = mm(dout, corrected, ((1,), (1,)))
            d_system = -mm(d_right, corrected, ((1,), (1,)))
            to_rows = (SCALE * d_scores * within).astype(BF16)
            by_gram = d_system * weighted
            to_keys = (beta * d_system * strict).astype(BF16)
            dq = jnp.concatenate(dq_left, axis=0) + mm(to_rows, keys)
            dk = (
                jnp.concatenate(dk_left, axis=0)
                + jnp.concatenate(dk_state, axis=0)
                + mm(to_rows, queries, ((0,), (0,)))
                + mm(to_keys, keys)
                + mm(to_keys, keys, ((0,), (0,)))
            )
            store_heads(dn_ref, block, group, 0, DK, dq)
            store_heads(dn_ref, block, group, H * DK, DK, dk)
            store_heads(dn_ref, block, group, 2 * H * DK, DV, scaled)
            spread = d_scores * scores + beta * by_gram
            d_cum = jnp.sum(spread, axis=1, keepdims=True)
            d_beta = jnp.sum(by_gram, axis=1, keepdims=True) + jnp.sum(
                d_right * (values - a * seen), axis=1, keepdims=True
            )
            d_a = jnp.sum(SCALE * dout_wide * asked - scaled * seen, axis=1, keepdims=True)
            d_d = jnp.sum(cor_wide * pulled, axis=1, keepdims=True)
            lane = lax.broadcasted_iota(jnp.int32, (ROWS, 8), 1)
            packed = jnp.zeros((ROWS, 8), F32)
            for i, part in enumerate((d_cum, d_beta, d_a, d_d, d_kappa)):
                packed = jnp.where(lane == i, part, packed)
            gcol_ref[block, group] = packed
            grow_ref[block, group] = jnp.broadcast_to(
                -jnp.sum(spread, axis=0, keepdims=True), (8, ROWS)
            )

    def chunk(c, normalise):
        lanes = pl.ds(pl.multiple_of(c * 128, 128), 128)
        masks = conv_masks(mask_ref, length)
        weights = cw_ref[:, lanes]
        taps, z = conv_taps(x_ref[:, lanes].astype(F32), masks, weights)
        gate = jax.nn.sigmoid(z)
        dn = dn_ref[:, lanes]
        if normalise:
            y = z * gate
            r = lax.rsqrt(jnp.sum(y * y, axis=1, keepdims=True) + EPSILON)
            dn = r * dn - y * (r * r * r * jnp.sum(y * dn, axis=1, keepdims=True))
        dz = dn * gate * (1.0 + z * (1.0 - gate))
        edge = jnp.zeros((HALO, 128), F32)
        dx = jnp.concatenate([edge, dz * weights[0:1]], axis=0)
        sums = [jnp.sum(dz * taps[0], axis=0, keepdims=True)]
        for s in range(1, CONV):
            sums.append(jnp.sum(dz * taps[s], axis=0, keepdims=True))
            moved = jnp.concatenate([edge, dz * masks[s - 1] * weights[s : s + 1]], axis=0)
            dx = dx + pltpu.roll(moved, length + HALO - s, 0)
        dx_ref[:, lanes] = dx.astype(BF16)
        dcw_ref[:, lanes] = jnp.concatenate(sums, axis=0)

    qk_cols = 2 * H * DK

    @pl.loop(0, qk_cols // 128)
    def _(c):
        chunk(c, True)

    @pl.loop(qk_cols // 128, x_ref.shape[1] // 128)
    def _(c):
        chunk(c, False)


def call(kernel, outs, scratch, *args, flops=0):
    return pl.pallas_call(
        kernel,
        out_shape=[jax.ShapeDtypeStruct(s, t) for s, t in outs],
        in_specs=[pl.BlockSpec(memory_space=pltpu.VMEM)] * len(args),
        out_specs=[pl.BlockSpec(memory_space=pltpu.VMEM)] * len(outs),
        scratch_shapes=scratch,
        compiler_params=pltpu.CompilerParams(vmem_limit_bytes=VMEM_BYTES),
        cost_estimate=pl.CostEstimate(
            flops=flops, bytes_accessed=sum(a.nbytes for a in args), transcendentals=0
        ),
    )(*args)


def mixer(x, weights, rates, decay, doc_all, member, sp_size):
    length = x.shape[0] - HALO
    blocks = length // BLOCK
    groups = H // STACK
    channels = x.shape[1]
    padded = jnp.concatenate([jnp.full((HALO,), -1, jnp.int32), doc_all])
    near = lax.dynamic_slice_in_dim(padded, member * length, length + HALO, 0)
    docs = near[HALO:]
    masks = jnp.stack(
        [(near[HALO - s : HALO - s + length] == docs).astype(F32) for s in range(1, CONV)]
        + [jnp.zeros((length,), F32)] * (8 - CONV + 1),
        axis=1,
    )
    doc_blocks = docs.reshape(blocks, 1, BLOCK)
    before = jnp.concatenate([near[HALO - 1 : HALO], doc_blocks[:-1, 0, -1]]).reshape(
        blocks, 1, 1
    )
    last = doc_blocks[:, :, -1:]
    from_before = (doc_blocks == before).astype(F32)
    to_last = (doc_blocks == last).astype(F32)
    kept = (last == before).astype(F32)

    def small(rates, decay):
        by_block = jnp.transpose(rates.reshape(blocks, BLOCK, H, 2), (3, 0, 2, 1))
        beta = jax.nn.sigmoid(by_block[1])
        offset = decay[1].reshape(1, H, 1)
        log_decay = -jnp.exp(decay[0]).reshape(1, H, 1) * jax.nn.softplus(by_block[0] + offset)
        i = lax.broadcasted_iota(jnp.int32, (BLOCK, BLOCK), 0)
        j = lax.broadcasted_iota(jnp.int32, (BLOCK, BLOCK), 1)
        upper = (i <= j).astype(F32)
        cum = jnp.einsum("bhi,ij->bhj", log_decay, upper, precision=lax.Precision.HIGHEST)
        final = cum[:, :, -1:]
        a = jnp.exp(cum) * from_before
        d = jnp.exp(final - cum) * to_last
        kappa = jnp.broadcast_to(jnp.exp(final) * kept, cum.shape)
        return jnp.stack([cum, beta, a, d, kappa], axis=0)

    five, pull_small = jax.vjp(small, rates, decay)
    doc_row = jnp.broadcast_to(doc_blocks.astype(F32), (blocks, H, BLOCK))
    packed = jnp.concatenate([five, doc_row[None], jnp.zeros((2,) + doc_row.shape, F32)], axis=0)
    packed = packed.reshape(8, blocks, groups, ROWS)
    col = jnp.transpose(packed, (1, 2, 3, 0))
    row = jnp.transpose(jnp.stack([packed[0], packed[5]] + [packed[6]] * 6), (1, 2, 0, 3))

    n_shape = ((length, channels), BF16)
    inv_shape = ((blocks, groups, ROWS, ROWS), F32)
    state_shape = ((H, DK, DV), F32)
    cor_shape = ((blocks, groups, ROWS, ROWS), BF16)
    n, inv, state = call(
        prepare_kernel, [n_shape, inv_shape, state_shape], [], x, weights, masks, col, row
    )
    ahead = [(i, i + 1) for i in range(sp_size - 1)]
    behind = [(i + 1, i) for i in range(sp_size - 1)]
    start = lax.ppermute(state.astype(BF16), "sp", ahead)
    for _ in range(sp_size - 2):
        (state,) = call(state_kernel, [state_shape], [], n, inv, col, start)
        start = lax.ppermute(state.astype(BF16), "sp", ahead)
    mixed, cor, states = call(
        scan_kernel,
        [((length, H * DV), BF16), cor_shape, ((blocks, H, DK, DV), BF16)],
        [pltpu.VMEM((H, DK, DV), F32)],
        n,
        inv,
        col,
        row,
        start,
    )

    def pull(dout):
        dstart = jnp.zeros((H, DK, DV), BF16)
        for _ in range(sp_size - 1):
            (dstate,) = call(
                back_state_kernel, [state_shape], [], n, inv, col, row, dout, dstart
            )
            dstart = lax.ppermute(dstate.astype(BF16), "sp", behind)
        dx, dcw, gcol, grow = call(
            back_kernel,
            [
                ((length + HALO, channels), BF16),
                ((CONV, channels), F32),
                ((blocks, groups, ROWS, 8), F32),
                ((blocks, groups, 8, ROWS), F32),
            ],
            [pltpu.VMEM((H, DK, DV), F32), pltpu.VMEM((length, channels), F32)],
            x,
            weights,
            masks,
            n,
            inv,
            col,
            row,
            dout,
            cor,
            states,
            dstart,
        )
        grads = jnp.transpose(gcol[..., :5], (3, 0, 1, 2))
        grads = grads.at[0].add(grow[:, :, 0])
        d_rates, d_decay = pull_small(grads.reshape(5, blocks, H, BLOCK))
        from_next = lax.ppermute(dx[:HALO], "sp", behind)
        return dx, from_next, dcw, d_rates, d_decay

    return mixed, pull


def rms_norm(values, scales):
    return values * lax.rsqrt(jnp.mean(values * values, axis=-1, keepdims=True) + EPSILON) * scales


def output_gate(mixed, gate_raw, scales):
    length = mixed.shape[0]
    normed = rms_norm(mixed.reshape(length, H, DV), scales)
    return (normed * jax.nn.silu(gate_raw).reshape(length, H, DV)).reshape(length, H * DV)


def residual_norm(values, attended, scales):
    hidden = values + attended
    return (hidden, rms_norm(hidden, scales))


def feed_act(gate_up):
    half_width = gate_up.shape[1] // 2
    return jax.nn.silu(gate_up[:, :half_width]) * gate_up[:, half_width:]


WEIGHT_AXES = ("fsdp", "dp", "sp")
COPY_AXES = ("dp", "sp")


def copies():
    count = lax.axis_size("dp") * lax.axis_size("sp")
    return count, lax.axis_index("dp") * lax.axis_size("sp") + lax.axis_index("sp")


def gather_rows(shard):
    count, own = copies()
    rows = shard.shape[0] // count
    piece = lax.dynamic_slice_in_dim(shard, own * rows, rows, 0)
    return lax.all_gather(piece, WEIGHT_AXES, axis=0, tiled=True)


def sum_rows(grad):
    piece = lax.psum_scatter(
        grad.astype(BF16), WEIGHT_AXES, scatter_dimension=0, tiled=True
    )
    return lax.all_gather(piece, COPY_AXES, axis=0, tiled=True).astype(F32)


def gather_small(parts):
    flat = jnp.concatenate([p.reshape(-1) for p in parts])
    size = flat.shape[0]
    flat = jnp.pad(flat, (0, -size % 1024)).reshape(-1, 128)
    every = lax.all_gather(flat, "fsdp", axis=0).reshape(lax.axis_size("fsdp"), -1)
    out, start = [], 0
    for p in parts:
        out.append(every[:, start : start + p.size].reshape((-1,) + p.shape))
        start += p.size
    return out


def sum_small(parts):
    flat = jnp.concatenate([p.reshape(-1) for p in parts])
    size = flat.shape[0]
    flat = jnp.pad(flat, (0, -size % 1024)).reshape(-1, 128)
    total = lax.psum(flat, ("dp", "fsdp", "sp")).reshape(-1)
    out, start = [], 0
    for p in parts:
        out.append(total[start : start + p.size].reshape(p.shape))
        start += p.size
    return out


def own_part(value, axis):
    size = value.shape[axis] // lax.axis_size("fsdp")
    return lax.dynamic_slice_in_dim(value, lax.axis_index("fsdp") * size, size, axis)


def body(
    tokens,
    cotangent,
    doc_lengths,
    input_weight,
    rate_weight,
    conv_weight,
    head_decay,
    mixer_gain,
    heads_gain,
    output_weight,
    feed_gain,
    up_weight,
    down_weight,
):
    length = tokens.shape[0]
    sp_size = lax.axis_size("sp")
    member = lax.axis_index("sp")
    qkv_cols = H * (2 * DK + DV)
    rate_all, conv_all, decay_all, mixer_all, heads_all, feed_all = gather_small(
        (rate_weight, conv_weight, head_decay, mixer_gain, heads_gain, feed_gain)
    )
    rate_full = rate_all.reshape(-1, 2 * H)
    conv_full = jnp.swapaxes(conv_all, 0, 1).reshape(CONV, -1).astype(F32)
    decay_full = jnp.swapaxes(decay_all, 0, 1).reshape(2, H).astype(F32)
    mixer_scale = mixer_all.reshape(-1).astype(F32)
    heads_scale = heads_all.reshape(-1).astype(F32)
    feed_scale = feed_all.reshape(-1).astype(F32)
    in_full = gather_rows(input_weight)
    out_full = gather_rows(output_weight)
    up_full = gather_rows(up_weight)
    down_full = gather_rows(down_weight)

    ends = jnp.cumsum(doc_lengths[0])
    positions = lax.broadcasted_iota(jnp.int32, (length * sp_size, 1), 0)
    doc_ids = jnp.sum((positions >= ends[None, :]).astype(jnp.int32), axis=1)

    ahead = [(i, i + 1) for i in range(sp_size - 1)]
    halo = lax.ppermute(tokens[-HALO:], "sp", ahead)
    x_float = tokens.astype(F32)
    normed, pull_norm = jax.vjp(rms_norm, x_float, mixer_scale)
    normed_low = normed.astype(BF16)
    halo_low = rms_norm(halo.astype(F32), mixer_scale).astype(BF16)
    normed_more = jnp.concatenate([halo_low, normed_low], axis=0)
    qkv = jnp.dot(normed_more, in_full[:, :qkv_cols], preferred_element_type=F32).astype(BF16)
    gate_raw = jnp.dot(normed_low, in_full[:, qkv_cols:], preferred_element_type=F32)
    rate_raw = jnp.dot(normed_low, rate_full, preferred_element_type=F32)
    rates = rate_raw.astype(BF16).astype(F32).reshape(length, H, 2)
    mixed, pull_mix = mixer(qkv, conv_full, rates, decay_full, doc_ids, member, sp_size)
    gated, pull_gate = jax.vjp(output_gate, mixed.astype(F32), gate_raw, heads_scale)
    gated_low = gated.astype(BF16)
    attended = jnp.dot(gated_low, out_full, preferred_element_type=F32)
    (hidden, normed_two), pull_resid = jax.vjp(residual_norm, x_float, attended, feed_scale)
    two_low = normed_two.astype(BF16)
    gate_up = jnp.dot(two_low, up_full, preferred_element_type=F32)
    activated, pull_act = jax.vjp(feed_act, gate_up)
    act_low = activated.astype(BF16)
    block_out = (hidden + jnp.dot(act_low, down_full, preferred_element_type=F32)).astype(BF16)
    down_grad = jnp.einsum("tf,td->fd", act_low, cotangent, preferred_element_type=F32)
    down_shard = sum_rows(down_grad)
    d_act = jnp.einsum("td,fd->tf", cotangent, down_full, preferred_element_type=F32)
    d_gu_low = pull_act(d_act)[0].astype(BF16)
    up_grad = jnp.einsum("td,tf->df", two_low, d_gu_low, preferred_element_type=F32)
    up_shard = sum_rows(up_grad)
    d_two = jnp.einsum("tf,df->td", d_gu_low, up_full, preferred_element_type=F32)
    d_resid, d_attended, feed_grad = pull_resid((cotangent.astype(F32), d_two))
    d_att_low = d_attended.astype(BF16)
    output_grad = jnp.einsum("te,td->ed", gated_low, d_att_low, preferred_element_type=F32)
    output_shard = sum_rows(output_grad)
    d_gated = jnp.einsum("td,ed->te", d_att_low, out_full, preferred_element_type=F32)
    d_mixed, d_gate, heads_grad = pull_gate(d_gated)
    d_gate_low = d_gate.astype(BF16)
    gate_shard = sum_rows(
        jnp.einsum("td,tf->df", normed_low, d_gate_low, preferred_element_type=F32)
    )
    d_more, from_next, conv_grad, d_rates, decay_grad = pull_mix(d_mixed.astype(BF16))
    edge = jnp.pad(from_next.astype(F32), ((length - HALO, 0), (0, 0)))
    d_qkv = (d_more[HALO:].astype(F32) + edge).astype(BF16)
    d_rate_low = d_rates.reshape(length, 2 * H).astype(BF16)
    qkv_shard = sum_rows(
        jnp.einsum("td,tf->df", normed_low, d_qkv, preferred_element_type=F32)
    )
    rate_grad = jnp.einsum("td,tf->df", normed_low, d_rate_low, preferred_element_type=F32)
    d_project = jnp.concatenate([d_qkv, d_gate_low], axis=1)
    d_normed = jnp.einsum("tf,df->td", d_project, in_full, preferred_element_type=F32)
    d_normed = d_normed + jnp.einsum(
        "tf,df->td", d_rate_low, rate_full, preferred_element_type=F32
    )
    d_front, mixer_grad = pull_norm(d_normed)
    tokens_grad = (d_resid + d_front).astype(BF16)
    rate_sum, conv_sum, decay_sum, mixer_sum, heads_sum, feed_sum = sum_small(
        (rate_grad, conv_grad, decay_grad, mixer_grad, heads_grad, feed_grad)
    )
    return (
        block_out,
        tokens_grad,
        jnp.concatenate([qkv_shard, gate_shard], axis=1),
        own_part(rate_sum, 0),
        own_part(conv_sum, 1),
        own_part(decay_sum, 1),
        own_part(mixer_sum, 0),
        own_part(heads_sum, 0),
        output_shard,
        own_part(feed_sum, 0),
        up_shard,
        down_shard,
    )


def solution(mesh):
    rows = P(("dp", "fsdp", "sp"), None)
    split = P("fsdp", None)
    return jax.shard_map(
        body,
        mesh=mesh,
        in_specs=(
            rows,
            rows,
            P(("dp", "fsdp"), None),
            split,
            split,
            P(None, "fsdp"),
            P(None, "fsdp"),
            P("fsdp"),
            P("fsdp"),
            split,
            P("fsdp"),
            split,
            split,
        ),
        out_specs=(
            rows,
            rows,
            split,
            split,
            P(None, "fsdp"),
            P(None, "fsdp"),
            P("fsdp"),
            P("fsdp"),
            split,
            P("fsdp"),
            split,
            split,
        ),
        check_vma=False,
    )
```

time: 2770 us -> 1530 us (0.55)
  blocking collectives: 748 us -> 13.8 us
  other arithmetic: 653 us -> 38 us
  waiting for transfers between devices: 725 us -> 1100 us
  matrix products: 359 us -> 129 us
  Pallas kernels: 0 us -> 130 us
  local copies, waits for them, and re-layouts: 178 us -> 83.6 us
  loops' own time: 35.9 us -> 0 us
    psum x1 -> x0, blocking collectives: 656 us -> none  [body(): lax.psum((shards[0], shards[1], shards[2], shards[3], shards[4], shards[5...]
    another operation x157 -> x2, other arithmetic: 488 us -> 0.25 us  [the longest x96 475 us: block_step(): jax.scipy.linalg.solve_triangular(system, targets, lower=True, unit_diago...]
    dot_general x279 -> x19, matrix products: 335 us -> 129 us  [the longest x1 13.7 us: body(): jnp.einsum('tf,df->td', d_gu_low, up_full, preferred_element_type=F32)]
    reduce_scatter x5, waiting for transfers between devices: 515 us -> 679 us  [sum_rows(): lax.psum_scatter(grad.astype(BF16), WEIGHT_AXES, scatter_dimension=0, til...]
    pallas_call x0 -> x4, Pallas kernels: none -> 130 us  [call(): pl.pallas_call(kernel, out_shape=[jax.ShapeDtypeStruct(s, t) for s, t in...]
    psum x0 -> x1, waiting for transfers between devices: none -> 119 us  [sum_small(): total = lax.psum(flat, ('dp', 'fsdp', 'sp')).reshape(-1)]
    all_gather x4 -> x9, waiting for transfers between devices: 149 us -> 254 us  [the longest x4 131 us: gather_rows(): return lax.all_gather(piece, WEIGHT_AXES, axis=0, tiled=True)]
    all_gather x5 -> x1, blocking collectives: 72.9 us -> 13.8 us  [gather_small(): lax.all_gather(flat, 'fsdp', axis=0).reshape(lax.axis_size('fsdp'), -1)]
  transfers between devices with their start and end apart: 20 -> 19, of which waited for: 11 -> 16; matrix products, arithmetic and copies ran while one was open for 21% -> 13% of each run, Pallas kernels for 0% -> 9%
where the time goes in v1:
time: 1530 us; the launch traced here: 1520 us
  waiting for transfers between devices  1100 us (72%)
  Pallas kernels  130 us (8%)
  matrix products  129 us (8%)
  local copies, waits for them, and re-layouts  83.6 us (5%)
  other arithmetic  38 us (2%)
    reduce_scatter x5, waiting for transfers between devices, sum_rows(): lax.psum_scatter(grad.astype(BF16), WEIGHT_AXES, scatter_dimension=0, til...  679 us
    all_gather x4, waiting for transfers between devices, gather_rows(): return lax.all_gather(piece, WEIGHT_AXES, axis=0, tiled=True)  131 us
    pallas_call x4, Pallas kernels, call(): pl.pallas_call(kernel, out_shape=[jax.ShapeDtypeStruct(s, t) for s, t in...  130 us
    all_gather x5, waiting for transfers between devices, sum_rows(): return lax.all_gather(piece, COPY_AXES, axis=0, tiled=True).astype(F32)  122 us
    psum x1, waiting for transfers between devices, sum_small(): total = lax.psum(flat, ('dp', 'fsdp', 'sp')).reshape(-1)  119 us
  transfers between devices with their start and end apart: 19, of which 16 were waited for; matrix products, arithmetic and copies ran while one was open for 13% of the time, Pallas kernels for 9%

profile of v1, /device:TPU:0, one launch (start us, length us, event | category | flops | bytes accessed | tf_op | source)
XLA Modules:
  0.0 1521.7 jit_solution(6201016876133870920)
XLA Ops:
  7.3 1.8 copy-done
  9.9 1.6 constant_dynamic-slice_fusion.5
  11.6 1.8 constant_dynamic-slice_fusion.4
  13.5 1.6 constant_dynamic-slice_fusion.3
  16.5 5.5 collective-permute-start
  23.6 13.8 all_gather.30
  46.3 2.7 concatenate.51
  49.0 2.7 concatenate.52
  51.7 2.7 concatenate.53
  54.4 2.7 broadcast_in_dim.51
  57.2 1.7 copy.160
  61.0 7.4 concatenate.46
  70.1 41.0 %all-gather.10.cloned.1.call-done = bf16[1024,6144]{1,0:T(8,128)(2,1)} async-done(((bf16[32,6144]{1,0:T(8,128)(2,1)}), bf16[1024,6144]{1,0:T(8,128)(2,1)}) %all-gather.10.cloned.1.call-update) | async-done | bytes 12582928 | tf_op jit(solution)/shard_map/all_gather | solution.py:517
  111.1 8.4 fusion.2.x_ref
  119.5 59.6 %shard_map.220 = (bf16[384,4096]{1,0:T(8,128)(2,1)}, f32[6,2,256,256]{3,2,1,0:T(8,128)}, f32[8,128,256]{2,1,0:T(8,128)}) custom-call(bf16[400,4096]{1,0:T(8,128)(2,1)} %fusion.2.x_ref, f32[4,4096]{1,0:T(4,128)} %bitcast.134, f32[384,8]{1,0:T(8,128)} %copy.161.mask_ref, f32[6,2,256,8]{3,2,1,0:T(8,128)} %bitcast.116, f32[6,2,8,256]{3,2,1,0:T(8,128)} %bitcast.130), custom_call_target="tpu_custom_call" | custom-call | bytes 3551232 | tf_op jit(solution)/shard_map/pallas_call | solution.py:366
  180.4 3.4 collective-permute-start.1
  184.0 13.9 collective-permute-done.1.start_ref
  198.7 13.7 shard_map.221
  212.4 1.8 copy.180
  220.0 1.6 copy-done.2
  221.7 6.6 multiply_convert_fusion.1
  228.3 6.3 multiply_reduce_fusion.5
  234.6 34.7 %all-gather.14.cloned.1.call-done = bf16[1024,5632]{1,0:T(8,128)(2,1)} async-done(((bf16[32,5632]{1,0:T(8,128)(2,1)}), bf16[1024,5632]{1,0:T(8,128)(2,1)}) %all-gather.14.cloned.1.call-update) | async-done | bytes 11534352 | tf_op jit(solution)/shard_map/all_gather | solution.py:517
  269.3 12.8 fusion.85
  282.1 55.6 %all-gather.16.cloned.1.call-done = bf16[2816,1024]{1,0:T(8,128)(2,1)} async-done(((bf16[88,1024]{1,0:T(8,128)(2,1)}), bf16[2816,1024]{1,0:T(8,128)(2,1)}) %all-gather.16.cloned.1.call-update) | async-done | bytes 5767184 | tf_op jit(solution)/shard_map/all_gather | solution.py:517
  337.7 13.4 fusion.36
  351.1 13.7 multiply_reduce_fusion.3
  364.8 2.7 add_add_fusion.2
  368.7 4.3 convolution_convert_fusion.3
  373.1 7.5 convolution_convert_fusion.2
  380.7 9.9 multiply_reduce_fusion
  391.8 4.4 convolution_convert_fusion.4
  396.7 3.3 copy.184
  403.4 1.5 broadcast_in_dim.46
  407.8 2.4 fusion.14.dout_ref
  411.0 13.6 shard_map.222
  427.2 25.1 %collective-permute-done.2.start_ref = bf16[8,128,256]{2,1,0:T(8,128)(2,1)S(1)} collective-permute-done((bf16[8,128,256]{2,1,0:T(8,128)(2,1)S(1)}, bf16[8,128,256]{2,1,0:T(8,128)(2,1)S(1)}, u32[]{:S(2)}, u32[]{:S(2)}) %collective-permute-start.2) | collective-permute-done | bytes 524320 | tf_op jit(solution)/shard_map/ppermute | solution.py:453
  453.1 43.0 %shard_map.223 = (bf16[400,4096]{1,0:T(8,128)(2,1)}, f32[4,4096]{1,0:T(4,128)}, f32[6,2,256,8]{3,2,1,0:T(8,128)}, f32[6,2,8,256]{3,2,1,0:T(8,128)}) custom-call(bf16[400,4096]{1,0:T(8,128)(2,1)} %fusion.2.x_ref, f32[4,4096]{1,0:T(4,128)} %bitcast.135, f32[384,8]{1,0:T(8,128)} %copy.161.mask_ref, bf16[384,4096]{1,0:T(8,128)(2,1)} %get-tuple-element.34.n_ref, ...), custom_call_target="tpu_custom_call" | custom-call | bytes 16658432 | tf_op jit(solution)/shard_map/pallas_call | solution.py:366
  497.1 1.6 collective-permute-start.3
  498.7 8.8 collective-permute-done.3
  507.5 2.3 add_convert_fusion.1
  509.8 1.7 copy-done.15
  511.6 6.7 convolution_convert_fusion.1
  519.7 12.6 convolution_convert_fusion
  534.3 1.5 slice_bitcast_fusion
  535.8 3.4 slice_reduce_fusion.2
  540.9 1.9 slice_reduce_fusion.4
  547.1 12.6 fusion.22
  561.2 103.7 %reduce-scatter.14.cloned.1.call-done = bf16[88,1024]{1,0:T(8,128)(2,1)} async-done(((bf16[2816,1024]{1,0:T(8,128)(2,1)}), bf16[88,1024]{1,0:T(8,128)(2,1)}) %reduce-scatter.14.cloned.1.call-update) | async-done | bytes 180240 | tf_op jit(solution)/shard_map/reduce_scatter | solution.py:521
  665.0 141.5 %reduce-scatter.8.cloned.1.call-done = bf16[32,2048]{1,0:T(8,128)(2,1)} async-done(((bf16[1024,2048]{1,0:T(8,128)(2,1)}), bf16[32,2048]{1,0:T(8,128)(2,1)}) %reduce-scatter.8.cloned.1.call-update) | async-done | bytes 131088 | tf_op jit(solution)/shard_map/reduce_scatter | solution.py:521
  806.6 182.4 %reduce-scatter.6.cloned.1.call-done = bf16[32,4096]{1,0:T(8,128)(2,1)} async-done(((bf16[1024,4096]{1,0:T(8,128)(2,1)}), bf16[32,4096]{1,0:T(8,128)(2,1)}) %reduce-scatter.6.cloned.1.call-update) | async-done | bytes 262160 | tf_op jit(solution)/shard_map/reduce_scatter | solution.py:521
  989.3 250.9 %reduce-scatter.12.cloned.1.call-done = bf16[32,5632]{1,0:T(8,128)(2,1)} async-done(((bf16[1024,5632]{1,0:T(8,128)(2,1)}), bf16[32,5632]{1,0:T(8,128)(2,1)}) %reduce-scatter.12.cloned.1.call-update) | async-done | bytes 360464 | tf_op jit(solution)/shard_map/reduce_scatter | solution.py:521
  1240.2 7.1 add_convert_fusion.2
  1248.8 118.7 %all-reduce.13.cloned.1.call-done = f32[280,128]{1,0:T(8,128)} async-done(((f32[280,128]{1,0:T(8,128)}), f32[280,128]{1,0:T(8,128)}) %all-reduce.13.cloned.1.call-update) | async-done | bytes 143376 | tf_op jit(solution)/shard_map/psum | solution.py:543
  1369.3 2.2 slice.179
  1376.2 18.8 %all-gather.22.cloned.1.call-done = bf16[512,1024]{1,0:T(8,128)(2,1)} async-done(((bf16[64,1024]{1,0:T(8,128)(2,1)}), bf16[512,1024]{1,0:T(8,128)(2,1)}) %all-gather.22.cloned.1.call-update) | async-done | bytes 1048592 | tf_op jit(solution)/shard_map/all_gather | solution.py:524
  1394.9 2.8 convert_element_type.232
  1397.7 24.1 %all-gather.26.cloned.1.call-done = bf16[704,1024]{1,0:T(8,128)(2,1)} async-done(((bf16[88,1024]{1,0:T(8,128)(2,1)}), bf16[704,1024]{1,0:T(8,128)(2,1)}) %all-gather.26.cloned.1.call-update) | async-done | bytes 1441808 | tf_op jit(solution)/shard_map/all_gather | solution.py:524
  1421.9 3.3 convert_element_type.236
  1425.2 22.1 %all-gather.20.cloned.1.call-done = bf16[256,2048]{1,0:T(8,128)(2,1)} async-done(((bf16[32,2048]{1,0:T(8,128)(2,1)}), bf16[256,2048]{1,0:T(8,128)(2,1)}) %all-gather.20.cloned.1.call-update) | async-done | bytes 1048592 | tf_op jit(solution)/shard_map/all_gather | solution.py:524
  1447.3 29.7 %all-gather.18.cloned.1.call-done = bf16[256,4096]{1,0:T(8,128)(2,1)} async-done(((bf16[32,4096]{1,0:T(8,128)(2,1)}), bf16[256,4096]{1,0:T(8,128)(2,1)}) %all-gather.18.cloned.1.call-update) | async-done | bytes 2097168 | tf_op jit(solution)/shard_map/all_gather | solution.py:524
  1476.9 5.5 maximum_convert_fusion
  1482.4 27.5 %all-gather.24.cloned.1.call-done = bf16[256,5632]{1,0:T(8,128)(2,1)} async-done(((bf16[32,5632]{1,0:T(8,128)(2,1)}), bf16[256,5632]{1,0:T(8,128)(2,1)}) %all-gather.24.cloned.1.call-update) | async-done | bytes 2883600 | tf_op jit(solution)/shard_map/all_gather | solution.py:524
  1509.9 5.0 convert_element_type.234
  (265 shorter events, 57.9 us)
Async XLA Ops:
  7.2 1.9 copy-start
  7.2 14.8 copy-start.46
  7.2 16.0 %copy-start.34 = (bf16[256,16]{0,1:T(8,128)(2,1)S(1)}, bf16[256,16]{0,1:T(8,128)(2,1)}, u32[]{:S(2)}) copy-start(bf16[256,16]{0,1:T(8,128)(2,1)} %param.19) | copy-start | bytes 24580
  7.2 16.2 %copy-start.35 = (bf16[4,1024]{1,0:T(4,128)(2,1)S(1)}, bf16[4,1024]{1,0:T(4,128)(2,1)}, u32[]{:S(2)}) copy-start(bf16[4,1024]{1,0:T(4,128)(2,1)} %param.20) | copy-start | bytes 24580
  7.2 16.2 %copy-start.47 = (bf16[2,2]{1,0:T(2,128)(2,1)S(1)}, bf16[2,2]{1,0:T(2,128)(2,1)}, u32[]{:S(2)}) copy-start(bf16[2,2]{1,0:T(2,128)(2,1)} %param.21) | copy-start | bytes 28
  7.2 16.3 %copy-start.40 = (bf16[256]{0:T(256)(128)(2,1)S(1)}, bf16[256]{0:T(256)(128)(2,1)}, u32[]{:S(2)}) copy-start(bf16[256]{0:T(256)(128)(2,1)} %param.22) | copy-start | bytes 1540
  7.2 16.3 %copy-start.41 = (bf16[64]{0:T(256)(128)(2,1)S(1)}, bf16[64]{0:T(256)(128)(2,1)}, u32[]{:S(2)}) copy-start(bf16[64]{0:T(256)(128)(2,1)} %param.23) | copy-start | bytes 388
  7.3 16.3 %copy-start.42 = (bf16[256]{0:T(256)(128)(2,1)S(1)}, bf16[256]{0:T(256)(128)(2,1)}, u32[]{:S(2)}) copy-start(bf16[256]{0:T(256)(128)(2,1)} %param.25) | copy-start | bytes 1540
  7.3 103.9 %all-gather.10.cloned.1.call-start = ((), (), s32[]{:S(2)}) async-start(), calls=%async_computation.5 | async-start | bytes 12976128 | tf_op jit(solution)/shard_map/all_gather | solution.py:517
  9.8 29.4 %copy-start.5 = (bf16[384,1024]{1,0:T(8,128)(2,1)S(1)}, bf16[384,1024]{1,0:T(8,128)(2,1)}, u32[]{:S(2)}) copy-start(bf16[384,1024]{1,0:T(8,128)(2,1)} %param.15) | copy-start | bytes 2359300
  9.9 218.4 %all-gather.12.cloned.1.call-start = ((), (), s32[]{:S(2)}) async-start(), calls=%async_computation.6 | async-start | bytes 4325376 | tf_op jit(solution)/shard_map/all_gather | solution.py:517
  11.6 257.7 %all-gather.14.cloned.1.call-start = ((), (), s32[]{:S(2)}) async-start(), calls=%async_computation.7 | async-start | bytes 11894784 | tf_op jit(solution)/shard_map/all_gather | solution.py:517
  13.4 324.3 %all-gather.16.cloned.1.call-start = ((), (), s32[]{:S(2)}) async-start(), calls=%async_computation.8 | async-start | bytes 5947392 | tf_op jit(solution)/shard_map/all_gather | solution.py:517
  15.1 545.4 %reduce-scatter.10.cloned.1.call-start = ((), (), s32[]{:S(2)}) async-start(), calls=%async_computation.14 | async-start | bytes 4325376 | tf_op jit(solution)/shard_map/reduce_scatter | solution.py:521
  16.5 51.8 %collective-permute-start = (bf16[16,1024]{1,0:T(8,128)(2,1)}, bf16[16,1024]{1,0:T(8,128)(2,1)}, u32[]{:S(2)}, u32[]{:S(2)}) collective-permute-start(bf16[16,1024]{1,0:T(8,128)(2,1)} %slice.148), channel_id=1, source_target_pairs={{0,1},{2,3},{4,5},{6,7},{8,9},{10,11},{12,13},{14,15},{16,17},{18,... | collective-permute-start | bytes 98312 | tf_op jit(solution)/shard_map/ppermute | solution.py:594
  38.1 1.4 copy-start.20
  39.0 6.0 copy-start.43
  40.4 70.8 %copy-start.7 = (bf16[384,1024]{1,0:T(8,128)(2,1)}, bf16[384,1024]{1,0:T(8,128)(2,1)S(1)}, u32[]{:S(2)}) copy-start(bf16[384,1024]{1,0:T(8,128)(2,1)S(1)} %fusion.21) | copy-start | bytes 2359300
  41.0 2.1 copy-start.44
  43.6 1.4 copy-start.24
  61.0 8.3 copy-start.21
  119.5 64.4 %copy-start.32 = (f32[1,2,4,128]{3,2,1,0:T(4,128)S(1)}, f32[1,2,4,128]{3,2,1,0:T(4,128)}, u32[]{:S(2)}) copy-start(f32[1,2,4,128]{3,2,1,0:T(4,128)} %get-tuple-element.139) | copy-start | bytes 12292
  180.4 17.5 %collective-permute-start.1 = (bf16[8,128,256]{2,1,0:T(8,128)(2,1)S(1)}, bf16[8,128,256]{2,1,0:T(8,128)(2,1)S(1)}, u32[]{:S(2)}, u32[]{:S(2)}) collective-permute-start(bf16[8,128,256]{2,1,0:T(8,128)(2,1)S(1)} %convert_element_type.207), channel_id=1, source_target_pairs={{0,1},{2,3},{4,5},{6,7},{8,9},{10,11},{12,13},{14,15},{16,17},{18,... | collective-permute-start | bytes 1572872 | tf_op jit(solution)/shard_map/ppermute | solution.py:432
  197.9 0.8 copy-start.19
  218.5 3.1 copy-start.8
  218.6 3.1 copy-start.13
  220.0 1.6 copy-start.2
  364.8 3.9 copy-start.48
  367.5 1.2 copy-start.11
  373.1 291.9 %reduce-scatter.14.cloned.1.call-start = ((), (), s32[]{:S(2)}) async-start(), calls=%async_computation.18 | async-start | bytes 5947392 | tf_op jit(solution)/shard_map/reduce_scatter | solution.py:521
  380.6 425.8 %reduce-scatter.8.cloned.1.call-start = ((), (), s32[]{:S(2)}) async-start(), calls=%async_computation.11 | async-start | bytes 4325376 | tf_op jit(solution)/shard_map/reduce_scatter | solution.py:521
  380.7 11.1 copy-start.9
  390.6 1.2 copy-start.49
  396.3 592.7 %reduce-scatter.6.cloned.1.call-start = ((), (), s32[]{:S(2)}) async-start(), calls=%async_computation.9 | async-start | bytes 8650752 | tf_op jit(solution)/shard_map/reduce_scatter | solution.py:521
  403.3 3.0 copy-start.14
  404.9 1.9 copy-start.3
  404.9 2.9 copy-start.4
  425.9 26.4 %collective-permute-start.2 = (bf16[8,128,256]{2,1,0:T(8,128)(2,1)S(1)}, bf16[8,128,256]{2,1,0:T(8,128)(2,1)S(1)}, u32[]{:S(2)}, u32[]{:S(2)}) collective-permute-start(bf16[8,128,256]{2,1,0:T(8,128)(2,1)S(1)} %convert_element_type.221), channel_id=1, source_target_pairs={{1,0},{3,2},{5,4},{7,6},{9,8},{11,10},{13,12},{15,14},{17,16},{19,... | collective-permute-start | bytes 1572872 | tf_op jit(solution)/shard_map/ppermute | solution.py:453
  452.4 0.8 copy-start.18
  497.1 14.5 copy-start.10
  497.1 10.4 collective-permute-start.3
  509.8 1.7 copy-start.15
  518.3 1.4 copy-start.16
  518.3 721.8 %reduce-scatter.12.cloned.1.call-start = ((), (), s32[]{:S(2)}) async-start(), calls=%async_computation.16 | async-start | bytes 11894784 | tf_op jit(solution)/shard_map/reduce_scatter | solution.py:521
  532.3 0.7 copy-start.39
  532.4 835.1 %all-reduce.13.cloned.1.call-start = ((), (), s32[]{:S(2)}) async-start(), calls=%async_computation.13 | async-start | bytes 286720 | tf_op jit(solution)/shard_map/psum | solution.py:543
  535.8 3.6 copy-start.25
  535.8 3.6 copy-start.27
  539.2 7.2 copy-start.23
  539.3 7.3 copy-start.45
  539.9 7.2 copy-start.6
  539.9 7.2 copy-start.22
  539.9 7.2 copy-start.29
  547.1 12.6 copy-start.37
  547.1 12.6 copy-start.38
  560.5 834.5 %all-gather.22.cloned.1.call-start = ((), (), s32[]{:S(2)}) async-start(), calls=%async_computation.15 | async-start | bytes 1179648 | tf_op jit(solution)/shard_map/all_gather | solution.py:524
  561.2 860.7 %all-gather.26.cloned.1.call-start = ((), (), s32[]{:S(2)}) async-start(), calls=%async_computation.19 | async-start | bytes 1622016 | tf_op jit(solution)/shard_map/all_gather | solution.py:524
  665.0 782.3 %all-gather.20.cloned.1.call-start = ((), (), s32[]{:S(2)}) async-start(), calls=%async_computation.12 | async-start | bytes 1179648 | tf_op jit(solution)/shard_map/all_gather | solution.py:524
  806.5 670.4 %all-gather.18.cloned.1.call-start = ((), (), s32[]{:S(2)}) async-start(), calls=%async_computation.10 | async-start | bytes 2359296 | tf_op jit(solution)/shard_map/all_gather | solution.py:524
  989.0 520.9 %all-gather.24.cloned.1.call-start = ((), (), s32[]{:S(2)}) async-start(), calls=%async_computation.17 | async-start | bytes 3244032 | tf_op jit(solution)/shard_map/all_gather | solution.py:524
  1240.2 7.2 copy-start.31
  1240.2 7.2 copy-start.12
  1240.2 7.2 copy-start.17
  1476.9 38.0 %copy-start.1 = (bf16[256,6144]{1,0:T(8,128)(2,1)S(1)}, bf16[256,6144]{1,0:T(8,128)(2,1)}, u32[]{:S(2)}) copy-start(bf16[256,6144]{1,0:T(8,128)(2,1)} %param.18) | copy-start | bytes 9437188
  (5 other events, 2.9 us)
Sparse Core Ops, SparseCore 0:
  11.6 99.5 all-gather.9
  114.0 60.4 all-gather.11
  177.4 91.8 all-gather.13
  272.1 65.6 all-gather.15
  373.2 145.8 reduce-scatter.9
  521.8 143.1 reduce-scatter.13
  667.2 139.2 reduce-scatter.7
  808.8 180.1 reduce-scatter.5
  991.3 248.8 reduce-scatter.11
  1246.2 121.2 all-reduce.12
  1369.4 25.5 all-gather.21
  1396.7 25.1 all-gather.25
  1423.7 23.4 all-gather.19
  1449.0 27.8 all-gather.17
  1478.7 31.1 all-gather.23

commit v2 on v1

--- a/solution.py
+++ b/solution.py
@@ -72,18 +72,26 @@
     return decay, jnp.where(i > j, decay, 0.0)
 
 
-def unit_inverse(lower):
+def unit_inverses(lowers):
     i = lax.broadcasted_iota(jnp.int32, (ROWS, ROWS), 0)
     j = lax.broadcasted_iota(jnp.int32, (ROWS, ROWS), 1)
     apart = jnp.bitwise_xor(i, j)
-    inverse = jnp.where(i == j, 1.0, 0.0) - jnp.where(apart == 1, lower, 0.0)
+    inverses = [
+        jnp.where(i == j, 1.0, 0.0) - jnp.where(apart == 1, lower, 0.0) for lower in lowers
+    ]
     size = 2
     while size < BLOCK:
-        cross = jnp.where((apart >= size) & (apart < 2 * size), lower, 0.0)
-        parts = halves(inverse)
-        inverse = inverse - mm_fine(parts, halves(mm_fine(halves(cross), parts)))
+        cross = (apart >= size) & (apart < 2 * size)
+        parts = [halves(inverse) for inverse in inverses]
+        right = [
+            halves(mm_fine(halves(jnp.where(cross, lower, 0.0)), part))
+            for lower, part in zip(lowers, parts)
+        ]
+        inverses = [
+            inverse - mm_fine(part, r) for inverse, part, r in zip(inverses, parts, right)
+        ]
         size *= 2
-    return inverse
+    return inverses
 
 
 def conv_taps(x, masks, weights):
@@ -102,9 +110,8 @@
     ]
 
 
-def prepare_kernel(x_ref, cw_ref, mask_ref, col_ref, row_ref, n_ref, inv_ref, state_ref):
+def conv_kernel(x_ref, cw_ref, mask_ref, n_ref):
     length = n_ref.shape[0]
-    blocks = length // BLOCK
     qk_cols = 2 * H * DK
 
     def chunk(c, normalise):
@@ -124,17 +131,18 @@
     def _(c):
         chunk(c, False)
 
-    @pl.loop(0, blocks)
+
+def inverse_kernel(n_ref, col_ref, row_ref, inv_ref):
+    @pl.loop(0, n_ref.shape[0] // BLOCK)
     def _(block):
+        lowers = []
         for group in range(H // STACK):
             cum, beta, _, _, _, doc = columns(col_ref, block, group)
             keys = stack_heads(n_ref, block, group, H * DK, DK)
             _, strict = decay_matrix(cum, doc, row_ref, block, group)
-            gram = mm(keys, keys, ((1,), (1,)))
-            inv_ref[block, group] = unit_inverse(beta * gram * strict)
-
-    state_ref[...] = jnp.zeros_like(state_ref)
-    state_steps(n_ref, inv_ref, col_ref, state_ref)
+            lowers.append(beta * mm(keys, keys, ((1,), (1,))) * strict)
+        for group, inverse in enumerate(unit_inverses(lowers)):
+            inv_ref[block, group] = inverse
 
 
 def state_steps(n_ref, inv_ref, col_ref, state_ref):
@@ -223,9 +231,6 @@
 
 
 def back_kernel(
-    x_ref,
-    cw_ref,
-    mask_ref,
     n_ref,
     inv_ref,
     col_ref,
@@ -234,12 +239,10 @@
     cor_ref,
     states_ref,
     start_ref,
-    dx_ref,
-    dcw_ref,
+    dn_ref,
     gcol_ref,
     grow_ref,
     dstate,
-    dn_ref,
 ):
     length = n_ref.shape[0]
     blocks = length // BLOCK
@@ -329,6 +332,10 @@
                 -jnp.sum(spread, axis=0, keepdims=True), (8, ROWS)
             )
 
+
+def conv_back_kernel(x_ref, cw_ref, mask_ref, dn_ref, dx_ref, dcw_ref):
+    length = dn_ref.shape[0]
+
     def chunk(c, normalise):
         lanes = pl.ds(pl.multiple_of(c * 128, 128), 128)
         masks = conv_masks(mask_ref, length)
@@ -362,7 +369,7 @@
         chunk(c, False)
 
 
-def call(kernel, outs, scratch, *args, flops=0):
+def call(kernel, outs, scratch, *args, micros):
     return pl.pallas_call(
         kernel,
         out_shape=[jax.ShapeDtypeStruct(s, t) for s, t in outs],
@@ -371,12 +378,12 @@
         scratch_shapes=scratch,
         compiler_params=pltpu.CompilerParams(vmem_limit_bytes=VMEM_BYTES),
         cost_estimate=pl.CostEstimate(
-            flops=flops, bytes_accessed=sum(a.nbytes for a in args), transcendentals=0
+            flops=int(micros * 1e9), bytes_accessed=4 * 2**20, transcendentals=0
         ),
     )(*args)
 
 
-def mixer(x, weights, rates, decay, doc_all, member, sp_size):
+def mixer(x, weights, rates, decay, doc_all, member, sp_size, points):
     length = x.shape[0] - HALO
     blocks = length // BLOCK
     groups = H // STACK
@@ -424,14 +431,15 @@
     inv_shape = ((blocks, groups, ROWS, ROWS), F32)
     state_shape = ((H, DK, DV), F32)
     cor_shape = ((blocks, groups, ROWS, ROWS), BF16)
-    n, inv, state = call(
-        prepare_kernel, [n_shape, inv_shape, state_shape], [], x, weights, masks, col, row
-    )
+    (n,) = call(conv_kernel, [n_shape], [], x, weights, masks, micros=5)
+    n = points("inverse", n)
+    (inv,) = call(inverse_kernel, [inv_shape], [], n, col, row, micros=10)
+    inv = points("state", inv)
+    start = jnp.zeros((H, DK, DV), BF16)
     ahead = [(i, i + 1) for i in range(sp_size - 1)]
     behind = [(i + 1, i) for i in range(sp_size - 1)]
-    start = lax.ppermute(state.astype(BF16), "sp", ahead)
-    for _ in range(sp_size - 2):
-        (state,) = call(state_kernel, [state_shape], [], n, inv, col, start)
+    for _ in range(sp_size - 1):
+        (state,) = call(state_kernel, [state_shape], [], n, inv, col, start, micros=4)
         start = lax.ppermute(state.astype(BF16), "sp", ahead)
     mixed, cor, states = call(
         scan_kernel,
@@ -442,27 +450,25 @@
         col,
         row,
         start,
+        micros=4,
     )
 
     def pull(dout):
         dstart = jnp.zeros((H, DK, DV), BF16)
         for _ in range(sp_size - 1):
             (dstate,) = call(
-                back_state_kernel, [state_shape], [], n, inv, col, row, dout, dstart
+                back_state_kernel, [state_shape], [], n, inv, col, row, dout, dstart, micros=4
             )
             dstart = lax.ppermute(dstate.astype(BF16), "sp", behind)
-        dx, dcw, gcol, grow = call(
+        dstart = points("back", dstart)
+        dn, gcol, grow = call(
             back_kernel,
             [
-                ((length + HALO, channels), BF16),
-                ((CONV, channels), F32),
+                ((length, channels), F32),
                 ((blocks, groups, ROWS, 8), F32),
                 ((blocks, groups, 8, ROWS), F32),
             ],
-            [pltpu.VMEM((H, DK, DV), F32), pltpu.VMEM((length, channels), F32)],
-            x,
-            weights,
-            masks,
+            [pltpu.VMEM((H, DK, DV), F32)],
             n,
             inv,
             col,
@@ -471,6 +477,18 @@
             cor,
             states,
             dstart,
+            micros=10,
+        )
+        dn = points("conv_back", dn)
+        dx, dcw = call(
+            conv_back_kernel,
+            [((length + HALO, channels), BF16), ((CONV, channels), F32)],
+            [],
+            x,
+            weights,
+            masks,
+            dn,
+            micros=4,
         )
         grads = jnp.transpose(gcol[..., :5], (3, 0, 1, 2))
         grads = grads.at[0].add(grow[:, :, 0])
@@ -496,39 +514,234 @@
     return (hidden, rms_norm(hidden, scales))
 
 
-def feed_act(gate_up):
-    half_width = gate_up.shape[1] // 2
-    return jax.nn.silu(gate_up[:, :half_width]) * gate_up[:, half_width:]
-
-
-WEIGHT_AXES = ("fsdp", "dp", "sp")
-COPY_AXES = ("dp", "sp")
-
-
-def copies():
-    count = lax.axis_size("dp") * lax.axis_size("sp")
-    return count, lax.axis_index("dp") * lax.axis_size("sp") + lax.axis_index("sp")
-
-
-def gather_rows(shard):
-    count, own = copies()
-    rows = shard.shape[0] // count
-    piece = lax.dynamic_slice_in_dim(shard, own * rows, rows, 0)
-    return lax.all_gather(piece, WEIGHT_AXES, axis=0, tiled=True)
-
-
-def sum_rows(grad):
-    piece = lax.psum_scatter(
-        grad.astype(BF16), WEIGHT_AXES, scatter_dimension=0, tiled=True
-    )
-    return lax.all_gather(piece, COPY_AXES, axis=0, tiled=True).astype(F32)
+def after(value, *earlier):
+    return lax.optimization_barrier((value,) + earlier)[0]
+
+
+def swap(value, axis):
+    return lax.ppermute(value, axis, [(0, 1), (1, 0)])
+
+
+def other(first):
+    return "sp" if first == "x" else "x"
+
+
+def pair(axis, mine, theirs, dim):
+    first = lax.axis_index(axis) == 0
+    return jnp.where(
+        first,
+        jnp.concatenate([mine, theirs], axis=dim),
+        jnp.concatenate([theirs, mine], axis=dim),
+    )
+
+
+def relative_axes(first):
+    return ("core", first, other(first))
+
+
+def place(first, k):
+    total = 0
+    for shift, axis in zip((2, 1, 0), relative_axes(first)):
+        bit = lax.axis_index(axis)
+        total = total + (1 << shift) * (1 - bit if (k >> shift) & 1 else bit)
+    return total
+
+
+def reorder(value, first):
+    width = value.shape[1] // 8
+    return jnp.concatenate(
+        [lax.dynamic_slice_in_dim(value, place(first, i) * width, width, 1) for i in range(8)],
+        axis=1,
+    )
+
+
+def shifted(value, step):
+    count = lax.axis_size("fsdp")
+    return lax.ppermute(value, "fsdp", [(i, (i + step) % count) for i in range(count)])
+
+
+def gather_blocks(piece):
+    count, rows = lax.axis_size("fsdp"), piece.shape[0]
+    parts = [piece] + [shifted(piece, s) for s in range(1, count)]
+    line = jnp.concatenate([parts[(count - 1 - i) % count] for i in range(2 * count - 1)], axis=0)
+    start = (count - 1 - lax.axis_index("fsdp")) * rows
+    return lax.dynamic_slice_in_dim(line, start, count * rows, 0)
+
+
+def sum_blocks(value):
+    count = lax.axis_size("fsdp")
+    rows = value.shape[0] // count
+    index = lax.axis_index("fsdp")
+
+    def block(s):
+        return lax.dynamic_slice_in_dim(value, lax.rem(index + s, count) * rows, rows, 0)
+
+    total = block(0)
+    for s in range(1, count):
+        total = total + shifted(block(s).astype(BF16), s).astype(F32)
+    if lax.axis_size("hi") > 1:
+        total = lax.psum(total, "hi")
+    return total
+
+
+class ColumnGather:
+    def __init__(self, shard, first):
+        width = shard.shape[1] // 8
+        self.first = first
+        self.piece = lax.dynamic_slice_in_dim(shard, place(first, 0) * width, width, 1)
+
+    def blocks(self, *earlier):
+        self.held = gather_blocks(after(self.piece, *earlier) if earlier else self.piece)
+        return self.held
+
+    def second(self, *earlier):
+        held = after(self.held, *earlier) if earlier else self.held
+        self.held = jnp.concatenate([held, swap(held, other(self.first))], axis=1)
+        return self.held
+
+    def third(self, *earlier):
+        held = after(self.held, *earlier) if earlier else self.held
+        self.held = jnp.concatenate([held, swap(held, self.first)], axis=1)
+        return self.held
+
+    def full(self):
+        return self.held, swap(self.held, "core")
+
+
+class HalfGather(ColumnGather):
+    def __init__(self, shard):
+        rows, width = shard.shape[0] // 2, shard.shape[1] // 4
+        column = (2 * lax.axis_index("core") + lax.axis_index("x")) * width
+        self.first = "x"
+        self.piece = lax.dynamic_slice(
+            shard, (lax.axis_index("sp") * rows, column), (rows, width)
+        )
+
+    def second(self, *earlier):
+        held = after(self.held, *earlier) if earlier else self.held
+        self.held = jnp.concatenate([held, swap(held, "sp")], axis=0)
+        return self.held
+
+
+def dot_columns(values, halves_of):
+    parts = [jnp.dot(values, w, preferred_element_type=F32) for w in halves_of]
+    return jnp.concatenate(parts, axis=1)
+
+
+def dot_back(grads, halves_of):
+    half = grads.shape[1] // 2
+    return jnp.einsum(
+        "tf,df->td", grads[:, :half], halves_of[0], preferred_element_type=F32
+    ) + jnp.einsum("tf,df->td", grads[:, half:], halves_of[1], preferred_element_type=F32)
+
+
+def grad_dot(left, right):
+    return jnp.einsum("td,tf->df", left, right, preferred_element_type=F32)
+
+
+class ColumnSum:
+    def __init__(self, left, right, first):
+        self.left, self.right, self.first = left, right, first
+        self.width = right.shape[1] // 8
+        self.from_core = swap(grad_dot(left, right[:, 4 * self.width :]).astype(BF16), "core")
+
+    def second(self):
+        width = self.width
+        outgoing = grad_dot(self.left, self.right[:, 2 * width : 4 * width])
+        self.outgoing = (outgoing + self.from_core[:, 2 * width :].astype(F32)).astype(BF16)
+        self.from_first = swap(self.outgoing, self.first)
+        return self.outgoing
+
+    def third(self):
+        width = self.width
+        self.outgoing = (
+            grad_dot(self.left, self.right[:, width : 2 * width])
+            + self.from_core[:, width : 2 * width].astype(F32)
+            + self.from_first[:, width:].astype(F32)
+        ).astype(BF16)
+        self.from_second = swap(self.outgoing, other(self.first))
+        return self.outgoing
+
+    def own(self):
+        width = self.width
+        return (
+            grad_dot(self.left, self.right[:, :width])
+            + self.from_core[:, :width].astype(F32)
+            + self.from_first[:, :width].astype(F32)
+            + self.from_second.astype(F32)
+        )
+
+    def finish(self):
+        total = sum_blocks(self.own()).astype(BF16)
+        for axis in (other(self.first), self.first, "core"):
+            total = pair(axis, total, swap(total, axis), 1)
+        return total.astype(F32)
+
+
+def by_half(values):
+    blocks = values.reshape(values.shape[0], lax.axis_size("fsdp"), 2, -1)
+    low = blocks[:, :, 0].reshape(values.shape[0], -1)
+    high = blocks[:, :, 1].reshape(values.shape[0], -1)
+    first = lax.axis_index("sp") == 0
+    return jnp.concatenate(
+        [jnp.where(first, low, high), jnp.where(first, high, low)], axis=1
+    )
+
+
+def from_half(values):
+    half = values.shape[1] // 2
+    first = lax.axis_index("sp") == 0
+    low = jnp.where(first, values[:, :half], values[:, half:])
+    high = jnp.where(first, values[:, half:], values[:, :half])
+    shape = (values.shape[0], lax.axis_size("fsdp"), 1, half // lax.axis_size("fsdp"))
+    return jnp.concatenate([low.reshape(shape), high.reshape(shape)], axis=2).reshape(
+        values.shape
+    )
+
+
+class HalfSum:
+    def __init__(self, left, near_core, far_core):
+        self.left, self.near = left, near_core
+        self.width = near_core.shape[1] // 2
+        self.rows = left.shape[1] // 2
+        self.from_core = swap(grad_dot(left, far_core).astype(BF16), "core")
+
+    def second(self):
+        width = self.width
+        outgoing = grad_dot(self.left, self.near[:, width:])
+        self.outgoing = (outgoing + self.from_core[:, width:].astype(F32)).astype(BF16)
+        self.from_x = swap(self.outgoing, "x")
+        return self.outgoing
+
+    def third(self):
+        rows, width = self.rows, self.width
+        self.outgoing = (
+            grad_dot(self.left[:, rows:], self.near[:, :width])
+            + self.from_core[rows:, :width].astype(F32)
+            + self.from_x[rows:].astype(F32)
+        ).astype(BF16)
+        self.from_y = swap(self.outgoing, "sp")
+        return self.outgoing
+
+    def finish(self):
+        rows, width = self.rows, self.width
+        own = (
+            grad_dot(self.left[:, :rows], self.near[:, :width])
+            + self.from_core[:rows, :width].astype(F32)
+            + self.from_x[:rows].astype(F32)
+            + self.from_y.astype(F32)
+        )
+        total = sum_blocks(own).astype(BF16)
+        for axis, dim in (("sp", 0), ("x", 1), ("core", 1)):
+            total = pair(axis, total, swap(total, axis), dim)
+        return total.astype(F32)
 
 
 def gather_small(parts):
     flat = jnp.concatenate([p.reshape(-1) for p in parts])
     size = flat.shape[0]
     flat = jnp.pad(flat, (0, -size % 1024)).reshape(-1, 128)
-    every = lax.all_gather(flat, "fsdp", axis=0).reshape(lax.axis_size("fsdp"), -1)
+    every = gather_blocks(flat).reshape(lax.axis_size("fsdp"), -1)
     out, start = [], 0
     for p in parts:
         out.append(every[:, start : start + p.size].reshape((-1,) + p.shape))
@@ -540,7 +753,14 @@
     flat = jnp.concatenate([p.reshape(-1) for p in parts])
     size = flat.shape[0]
     flat = jnp.pad(flat, (0, -size % 1024)).reshape(-1, 128)
-    total = lax.psum(flat, ("dp", "fsdp", "sp")).reshape(-1)
+    for axis in ("core", "x", "sp"):
+        flat = flat + swap(flat, axis)
+    members = lax.axis_size("fsdp")
+    for bit in range(members.bit_length() - 1):
+        flat = flat + lax.ppermute(flat, "fsdp", [(i, i ^ (1 << bit)) for i in range(members)])
+    if lax.axis_size("hi") > 1:
+        flat = lax.psum(flat, "hi")
+    total = flat.reshape(-1)
     out, start = [], 0
     for p in parts:
         out.append(total[start : start + p.size].reshape(p.shape))
@@ -581,10 +801,37 @@
     mixer_scale = mixer_all.reshape(-1).astype(F32)
     heads_scale = heads_all.reshape(-1).astype(F32)
     feed_scale = feed_all.reshape(-1).astype(F32)
-    in_full = gather_rows(input_weight)
-    out_full = gather_rows(output_weight)
-    up_full = gather_rows(up_weight)
-    down_full = gather_rows(down_weight)
+    qk_cols = 2 * H * DK
+    qk_way = ColumnGather(input_weight[:, :qk_cols], "x")
+    v_way = ColumnGather(input_weight[:, qk_cols:qkv_cols], "sp")
+    gate_way = ColumnGather(input_weight[:, qkv_cols:], "sp")
+    out_way = ColumnGather(output_weight, "sp")
+    up_way = HalfGather(up_weight)
+    down_way = ColumnGather(down_weight, "sp")
+    qkv_blocks = (qk_way.blocks(), v_way.blocks())
+    qkv_second = (qk_way.second(), v_way.second())
+    gate_way.blocks(*qkv_blocks)
+    out_way.blocks(*qkv_blocks)
+    qkv_third = (qk_way.third(), v_way.third())
+    up_way.blocks(*qkv_second)
+    down_way.blocks(*qkv_second)
+    early = (gate_way.second(*qkv_third), out_way.second(*qkv_third))
+    qk_full, v_full = qk_way.full(), v_way.full()
+
+    def points(name, value):
+        if name == "inverse":
+            return after(value, up_way.second(*early), down_way.second(*early))
+        if name == "state":
+            late = (gate_way.third(*early), out_way.third(*early))
+            up_way.third(*late)
+            down_way.third(*late)
+            return after(value, *late)
+        if name == "back":
+            return after(value, sums["down"].third())
+        if name == "conv_back":
+            return after(value, *(sums[key].third() for key in ("up", "out", "gate")))
+
+    sums = {}
 
     ends = jnp.cumsum(doc_lengths[0])
     positions = lax.broadcasted_iota(jnp.int32, (length * sp_size, 1), 0)
@@ -597,47 +844,74 @@
     normed_low = normed.astype(BF16)
     halo_low = rms_norm(halo.astype(F32), mixer_scale).astype(BF16)
     normed_more = jnp.concatenate([halo_low, normed_low], axis=0)
-    qkv = jnp.dot(normed_more, in_full[:, :qkv_cols], preferred_element_type=F32).astype(BF16)
-    gate_raw = jnp.dot(normed_low, in_full[:, qkv_cols:], preferred_element_type=F32)
+    qkv = jnp.concatenate(
+        [
+            reorder(dot_columns(normed_more, qk_full).astype(BF16), "x"),
+            reorder(dot_columns(normed_more, v_full).astype(BF16), "sp"),
+        ],
+        axis=1,
+    )
     rate_raw = jnp.dot(normed_low, rate_full, preferred_element_type=F32)
     rates = rate_raw.astype(BF16).astype(F32).reshape(length, H, 2)
-    mixed, pull_mix = mixer(qkv, conv_full, rates, decay_full, doc_ids, member, sp_size)
+    mixed, pull_mix = mixer(after(qkv, *early), conv_full, rates, decay_full, doc_ids, member, sp_size, points)
+    gate_full, out_full = gate_way.full(), out_way.full()
+    up_full, down_full = up_way.full(), down_way.full()
+    gate_raw = reorder(dot_columns(normed_low, gate_full), "sp")
     gated, pull_gate = jax.vjp(output_gate, mixed.astype(F32), gate_raw, heads_scale)
     gated_low = gated.astype(BF16)
-    attended = jnp.dot(gated_low, out_full, preferred_element_type=F32)
+    attended = reorder(dot_columns(gated_low, out_full), "sp")
     (hidden, normed_two), pull_resid = jax.vjp(residual_norm, x_float, attended, feed_scale)
-    two_low = normed_two.astype(BF16)
-    gate_up = jnp.dot(two_low, up_full, preferred_element_type=F32)
-    activated, pull_act = jax.vjp(feed_act, gate_up)
-    act_low = activated.astype(BF16)
-    block_out = (hidden + jnp.dot(act_low, down_full, preferred_element_type=F32)).astype(BF16)
-    down_grad = jnp.einsum("tf,td->fd", act_low, cotangent, preferred_element_type=F32)
-    down_shard = sum_rows(down_grad)
-    d_act = jnp.einsum("td,fd->tf", cotangent, down_full, preferred_element_type=F32)
-    d_gu_low = pull_act(d_act)[0].astype(BF16)
-    up_grad = jnp.einsum("td,tf->df", two_low, d_gu_low, preferred_element_type=F32)
-    up_shard = sum_rows(up_grad)
-    d_two = jnp.einsum("tf,df->td", d_gu_low, up_full, preferred_element_type=F32)
+    two_low = by_half(normed_two.astype(BF16))
+    core_first = lax.axis_index("core") == 0
+    own_side, far_side = (jnp.dot(two_low, w, preferred_element_type=F32) for w in up_full)
+
+    def feed_act(own_side, far_side):
+        gate = jnp.where(core_first, own_side, far_side)
+        return jax.nn.silu(gate) * jnp.where(core_first, far_side, own_side)
+
+    activated, pull_act = jax.vjp(feed_act, own_side, far_side)
+
+    def turn(values):
+        half = values.shape[1] // 2
+        return pair("x", values[:, :half], values[:, half:], 1)
+
+    act_low = turn(activated.astype(BF16))
+    block_out = (hidden + reorder(dot_columns(act_low, down_full), "sp")).astype(BF16)
+    cot_rel = reorder(cotangent, "sp")
+    sums["down"] = ColumnSum(act_low, cot_rel, "sp")
+    d_act = turn(dot_back(cot_rel, down_full))
+    d_own, d_far = (d.astype(BF16) for d in pull_act(d_act))
+    sums["up"] = HalfSum(two_low, d_own, d_far)
+    d_both = after(jnp.concatenate([d_own, d_far], axis=1), sums["down"].second())
+    d_two = from_half(dot_back(d_both, up_full))
     d_resid, d_attended, feed_grad = pull_resid((cotangent.astype(F32), d_two))
-    d_att_low = d_attended.astype(BF16)
-    output_grad = jnp.einsum("te,td->ed", gated_low, d_att_low, preferred_element_type=F32)
-    output_shard = sum_rows(output_grad)
-    d_gated = jnp.einsum("td,ed->te", d_att_low, out_full, preferred_element_type=F32)
+    d_att_rel = reorder(d_attended.astype(BF16), "sp")
+    sums["out"] = ColumnSum(gated_low, d_att_rel, "sp")
+    d_gated = dot_back(d_att_rel, out_full)
     d_mixed, d_gate, heads_grad = pull_gate(d_gated)
     d_gate_low = d_gate.astype(BF16)
-    gate_shard = sum_rows(
-        jnp.einsum("td,tf->df", normed_low, d_gate_low, preferred_element_type=F32)
-    )
-    d_more, from_next, conv_grad, d_rates, decay_grad = pull_mix(d_mixed.astype(BF16))
+    d_gate_rel = reorder(d_gate_low, "sp")
+    sums["gate"] = ColumnSum(normed_low, d_gate_rel, "sp")
+    d_mixed_low = after(
+        d_mixed.astype(BF16), *(sums[key].second() for key in ("up", "out", "gate"))
+    )
+    d_more, from_next, conv_grad, d_rates, decay_grad = pull_mix(d_mixed_low)
     edge = jnp.pad(from_next.astype(F32), ((length - HALO, 0), (0, 0)))
     d_qkv = (d_more[HALO:].astype(F32) + edge).astype(BF16)
     d_rate_low = d_rates.reshape(length, 2 * H).astype(BF16)
-    qkv_shard = sum_rows(
-        jnp.einsum("td,tf->df", normed_low, d_qkv, preferred_element_type=F32)
+    d_qk_rel = reorder(d_qkv[:, :qk_cols], "x")
+    d_v_rel = reorder(d_qkv[:, qk_cols:], "sp")
+    sums["qk"] = ColumnSum(normed_low, d_qk_rel, "x")
+    sums["v"] = ColumnSum(normed_low, d_v_rel, "sp")
+    for step in ("second", "third"):
+        for key in ("qk", "v"):
+            getattr(sums[key], step)()
+    down_shard, up_shard, output_shard, gate_shard, qk_shard, v_shard = (
+        sums[key].finish() for key in ("down", "up", "out", "gate", "qk", "v")
     )
     rate_grad = jnp.einsum("td,tf->df", normed_low, d_rate_low, preferred_element_type=F32)
-    d_project = jnp.concatenate([d_qkv, d_gate_low], axis=1)
-    d_normed = jnp.einsum("tf,df->td", d_project, in_full, preferred_element_type=F32)
+    d_normed = dot_back(d_qk_rel, qk_full) + dot_back(d_v_rel, v_full)
+    d_normed = d_normed + dot_back(d_gate_rel, gate_full)
     d_normed = d_normed + jnp.einsum(
         "tf,df->td", d_rate_low, rate_full, preferred_element_type=F32
     )
@@ -649,7 +923,7 @@
     return (
         block_out,
         tokens_grad,
-        jnp.concatenate([qkv_shard, gate_shard], axis=1),
+        jnp.concatenate([qk_shard, v_shard, gate_shard], axis=1),
         own_part(rate_sum, 0),
         own_part(conv_sum, 1),
         own_part(decay_sum, 1),
@@ -663,15 +937,20 @@
 
 
 def solution(mesh):
-    rows = P(("dp", "fsdp", "sp"), None)
+    dp, fsdp, sp = (mesh.shape[axis] for axis in ("dp", "fsdp", "sp"))
+    dp_axes = ("hi", "x", "core")
+    cut = jax.sharding.Mesh(
+        mesh.devices.reshape(dp // 4, 2, 2, fsdp, sp), dp_axes + ("fsdp", "sp")
+    )
+    rows = P(dp_axes + ("fsdp", "sp"), None)
     split = P("fsdp", None)
     return jax.shard_map(
         body,
-        mesh=mesh,
+        mesh=cut,
         in_specs=(
             rows,
             rows,
-            P(("dp", "fsdp"), None),
+            P(dp_axes + ("fsdp",), None),
             split,
             split,
             P(None, "fsdp"),

time: 1530 us -> 925 us (0.60)
  waiting for transfers between devices: 1100 us -> 303 us
  starting transfers between devices: 13 us -> 110 us
  local copies, waits for them, and re-layouts: 83.6 us -> 151 us
  other arithmetic: 38 us -> 83.8 us
    reduce_scatter x5 -> x0, waiting for transfers between devices: 679 us -> none  [sum_rows(): lax.psum_scatter(grad.astype(BF16), WEIGHT_AXES, scatter_dimension=0, til...]
    ppermute x0 -> x98, waiting for transfers between devices: none -> 296 us  [the longest x57 190 us: swap(): return lax.ppermute(value, axis, [(0, 1), (1, 0)])]
    all_gather x9 -> x0, waiting for transfers between devices: 254 us -> none  [the longest x4 131 us: gather_rows(): return lax.all_gather(piece, WEIGHT_AXES, axis=0, tiled=True)]
    psum x1 -> x0, waiting for transfers between devices: 119 us -> none  [sum_small(): total = lax.psum(flat, ('dp', 'fsdp', 'sp')).reshape(-1)]
    ppermute x0 -> x98, starting transfers between devices: none -> 99.2 us  [the longest x39 62 us: shifted(): lax.ppermute(value, 'fsdp', [(i, (i + step) % count) for i in range(count)])]
    unnamed x114 -> x424, local copies, waits for them, and re-layouts: 23.1 us -> 48.7 us
    ppermute x1, waiting for transfers between devices: 25.1 us -> 0.01 us  [pull(): dstart = lax.ppermute(dstate.astype(BF16), 'sp', behind)]
    pallas_call x4 -> x7, Pallas kernels: 130 us -> 127 us  [call(): pl.pallas_call(kernel, out_shape=[jax.ShapeDtypeStruct(s, t) for s, t in...]
  transfers between devices with their start and end apart: 19 -> 102, of which waited for: 16 -> 34; matrix products, arithmetic and copies ran while one was open for 13% -> 35% of each run, Pallas kernels for 9% -> 14%
where the time goes in v2:
time: 925 us; the launch traced here: 914 us
  waiting for transfers between devices  303 us (33%)
  local copies, waits for them, and re-layouts  151 us (16%)
  matrix products  134 us (14%)
  Pallas kernels  127 us (14%)
  starting transfers between devices  110 us (12%)
  other arithmetic  83.8 us (9%)
    ppermute x57, waiting for transfers between devices, swap(): return lax.ppermute(value, axis, [(0, 1), (1, 0)])  190 us
    pallas_call x7, Pallas kernels, call(): pl.pallas_call(kernel, out_shape=[jax.ShapeDtypeStruct(s, t) for s, t in...  127 us
    ppermute x39, waiting for transfers between devices, shifted(): lax.ppermute(value, 'fsdp', [(i, (i + step) % count) for i in range(count)])  106 us
    ppermute x39, starting transfers between devices, shifted(): lax.ppermute(value, 'fsdp', [(i, (i + step) % count) for i in range(count)])  62 us
    dot_general x24, matrix products, grad_dot(): return jnp.einsum('td,tf->df', left, right, preferred_element_type=F32)  57.9 us
    unnamed x424, local copies, waits for them, and re-layouts  48.7 us
    ppermute x57, starting transfers between devices, swap(): return lax.ppermute(value, axis, [(0, 1), (1, 0)])  33.7 us
    dot_general x10, matrix products, dot_columns(): parts = [jnp.dot(values, w, preferred_element_type=F32) for w in halves_of]  21.1 us
  transfers between devices with their start and end apart: 102, of which 34 were waited for; matrix products, arithmetic and copies ran while one was open for 35% of the time, Pallas kernels for 14%

profile of v2, /device:TPU:0, one launch (start us, length us, event | category | flops | bytes accessed | tf_op | source)
XLA Modules:
  0.0 913.6 jit_solution(4474975901028094024)
XLA Ops:
  5.2 5.1 collective-permute-start.1
  11.3 3.7 fusion.220
  36.4 4.0 collective-permute-start
  40.5 3.8 collective-permute-start.10
  70.6 7.2 concatenate.345
  98.2 9.1 collective-permute-done.17
  107.4 7.1 collective-permute-done.21
  125.2 8.8 collective-permute-done.29
  134.1 12.5 %collective-permute-start.26 = (bf16[128,1408]{1,0:T(8,128)(2,1)S(1)}, bf16[128,1408]{1,0:T(8,128)(2,1)S(1)}, u32[]{:S(2)}, u32[]{:S(2)}) collective-permute-start(bf16[128,1408]{1,0:T(8,128)(2,1)S(1)} %copy-done.64), channel_id=1, source_target_pairs={{0,2},{2,4},{4,6},{6,0},{1,3},{3,5},{5,7},{7,1},{8,10},{10,12},{12... | collective-permute-start | bytes 1081352 | tf_op jit(solution)/shard_map/ppermute | solution.py:560
  146.8 15.7 %collective-permute-done.25 = bf16[128,1408]{1,0:T(8,128)(2,1)S(1)} collective-permute-done((bf16[128,1408]{1,0:T(8,128)(2,1)S(1)}, bf16[128,1408]{1,0:T(8,128)(2,1)S(1)}, u32[]{:S(2)}, u32[]{:S(2)}) %collective-permute-start.25) | collective-permute-done | bytes 360480 | tf_op jit(solution)/shard_map/ppermute | solution.py:560
  168.0 10.5 %collective-permute-done.19 = bf16[1024,256]{1,0:T(8,128)(2,1)S(1)} collective-permute-done((bf16[1024,256]{1,0:T(8,128)(2,1)S(1)}, bf16[1024,256]{1,0:T(8,128)(2,1)S(1)}, u32[]{:S(2)}, u32[]{:S(2)}) %collective-permute-start.19) | collective-permute-done | bytes 524320 | tf_op jit(solution)/shard_map/ppermute | solution.py:522
  178.5 10.8 %collective-permute-done.23 = bf16[2048,128]{1,0:T(8,128)(2,1)S(1)} collective-permute-done((bf16[2048,128]{1,0:T(8,128)(2,1)S(1)}, bf16[2048,128]{1,0:T(8,128)(2,1)S(1)}, u32[]{:S(2)}, u32[]{:S(2)}) %collective-permute-start.23) | collective-permute-done | bytes 524320 | tf_op jit(solution)/shard_map/ppermute | solution.py:522
  197.2 11.1 %collective-permute-done.31 = bf16[2816,128]{1,0:T(8,128)(2,1)S(1)} collective-permute-done((bf16[2816,128]{1,0:T(8,128)(2,1)S(1)}, bf16[2816,128]{1,0:T(8,128)(2,1)S(1)}, u32[]{:S(2)}, u32[]{:S(2)}) %collective-permute-start.31) | collective-permute-done | bytes 720928 | tf_op jit(solution)/shard_map/ppermute | solution.py:522
  209.2 59.5 %collective-permute-done.33 = bf16[2048,256]{1,0:T(8,128)(2,1)S(1)} collective-permute-done((bf16[2048,256]{1,0:T(8,128)(2,1)S(1)}, bf16[2048,256]{1,0:T(8,128)(2,1)S(1)}, u32[]{:S(2)}, u32[]{:S(2)}) %collective-permute-start.33) | collective-permute-done | bytes 1048608 | tf_op jit(solution)/shard_map/ppermute | solution.py:522
  283.3 13.1 %shard_map.220.n_ref = bf16[384,4096]{1,0:T(8,128)(2,1)} custom-call(bf16[400,4096]{1,0:T(8,128)(2,1)} %copy-done.165, f32[4,4096]{1,0:T(4,128)} %bitcast.238, f32[384,8]{1,0:T(8,128)} %copy.222.mask_ref), custom_call_target="tpu_custom_call" | custom-call | flops 5000000000 | bytes 4194304 | tf_op jit(solution)/shard_map/pallas_call | solution.py:373
  296.3 27.0 %shard_map.221.inv_ref = f32[6,2,256,256]{3,2,1,0:T(8,128)} custom-call(bf16[384,4096]{1,0:T(8,128)(2,1)} %shard_map.220.n_ref, f32[6,2,256,8]{3,2,1,0:T(8,128)} %bitcast.206, f32[6,2,8,256]{3,2,1,0:T(8,128)} %bitcast.232), custom_call_target="tpu_custom_call" | custom-call | flops 10000000000 | bytes 4194304 | tf_op jit(solution)/shard_map/pallas_call | solution.py:373
  324.2 10.4 %shard_map.222 = f32[8,128,256]{2,1,0:T(8,128)} custom-call(bf16[384,4096]{1,0:T(8,128)(2,1)} %shard_map.220.n_ref, f32[6,2,256,256]{3,2,1,0:T(8,128)} %shard_map.221.inv_ref, f32[6,2,256,8]{3,2,1,0:T(8,128)} %bitcast.207, bf16[8,128,256]{2,1,0:T(8,128)(2,1)} %broadcast_18_start_ref.2.start_ref), custom_call_target="tpu_custom_call" | custom-call | flops 4000000000 | bytes 4194304 | tf_op jit(solution)/shard_map/pallas_call | solution.py:373
  335.9 3.7 collective-permute-start.34
  342.2 3.6 constant_dynamic-update-slice_fusion.86
  345.8 4.5 collective-permute-done.34.start_ref
  351.1 14.0 %shard_map.223 = (bf16[384,2048]{1,0:T(8,128)(2,1)}, bf16[6,2,256,256]{3,2,1,0:T(8,128)(2,1)}, bf16[6,8,128,256]{3,2,1,0:T(8,128)(2,1)}) custom-call(bf16[384,4096]{1,0:T(8,128)(2,1)} %shard_map.220.n_ref, f32[6,2,256,256]{3,2,1,0:T(8,128)} %shard_map.221.inv_ref, f32[6,2,256,8]{3,2,1,0:T(8,128)} %bitcast.208, f32[6,2,8,256]{3,2,1,0:T(8,128)} %bitcast.233, ...), custom_call_target="tpu_custom_call" | custom-call | flops 4000000000 | bytes 4194304 | tf_op jit(solution)/shard_map/pallas_call | solution.py:373
  371.5 3.7 constant_dynamic-update-slice_fusion.87
  380.5 4.8 constant_dynamic-update-slice_fusion.85
  386.9 3.1 fusion.228
  396.7 3.4 reshape.472
  400.1 4.0 fusion.222
  416.7 3.3 fusion.150
  420.0 3.2 convolution_add_fusion
  423.5 5.1 fusion.213
  428.6 8.4 add_convert_fusion.3
  440.5 5.6 convolution_convert_fusion
  462.7 5.1 fusion.11
  467.8 5.1 fusion.24
  495.5 5.5 multiply_reduce_fusion
  512.2 4.2 fusion.148
  516.4 9.7 %collective-permute-done.95 = bf16[2816,128]{1,0:T(8,128)(2,1)} collective-permute-done((bf16[2816,128]{1,0:T(8,128)(2,1)}, bf16[2816,128]{1,0:T(8,128)(2,1)}, u32[]{:S(2)}, u32[]{:S(2)}) %collective-permute-start.95) | collective-permute-done | bytes 720928 | tf_op jit(solution)/shard_map/ppermute | solution.py:522
  535.4 9.0 collective-permute-done.97
  552.0 5.1 add_convert_fusion.1
  557.7 13.5 %shard_map.224 = f32[8,128,256]{2,1,0:T(8,128)} custom-call(bf16[384,4096]{1,0:T(8,128)(2,1)} %shard_map.220.n_ref, f32[6,2,256,256]{3,2,1,0:T(8,128)} %shard_map.221.inv_ref, f32[6,2,256,8]{3,2,1,0:T(8,128)} %bitcast.209, f32[6,2,8,256]{3,2,1,0:T(8,128)} %bitcast.234, bf16[384,2048]{1,0:T(8,128)(2,1)} %get-tuple-element.68.dout_ref, ...), custom_call_target="tpu_custom_call" | custom-call | flops 4000000000 | bytes 4194304 | tf_op jit(solution)/shard_map/pallas_call | solution.py:373
  573.8 17.8 %collective-permute-done.100 = bf16[704,256]{1,0:T(8,128)(2,1)} collective-permute-done((bf16[704,256]{1,0:T(8,128)(2,1)}, bf16[704,256]{1,0:T(8,128)(2,1)}, u32[]{:S(2)}, u32[]{:S(2)}) %collective-permute-start.100) | collective-permute-done | bytes 360480 | tf_op jit(solution)/shard_map/ppermute | solution.py:522
  602.0 25.6 %shard_map.225 = (f32[384,4096]{1,0:T(8,128)}, f32[6,2,256,8]{3,2,1,0:T(8,128)}, f32[6,2,8,256]{3,2,1,0:T(8,128)}) custom-call(bf16[384,4096]{1,0:T(8,128)(2,1)} %shard_map.220.n_ref, f32[6,2,256,256]{3,2,1,0:T(8,128)} %shard_map.221.inv_ref, f32[6,2,256,8]{3,2,1,0:T(8,128)} %bitcast.210, f32[6,2,8,256]{3,2,1,0:T(8,128)} %bitcast.235, ...), custom_call_target="tpu_custom_call" | custom-call | flops 10000000000 | bytes 4194304 | tf_op jit(solution)/shard_map/pallas_call | solution.py:373
  630.0 4.0 slice_reduce_fusion.2
  649.9 4.4 collective-permute-start.72
  656.6 3.2 collective-permute-start.84
  661.0 4.8 collective-permute-done.71
  667.7 3.2 collective-permute-done.73
  674.4 5.5 collective-permute-done.74
  683.4 3.4 fusion.23
  686.8 5.1 collective-permute-done.86
  696.1 4.0 add_convert_fusion.4
  700.0 23.5 %shard_map.226 = (bf16[400,4096]{1,0:T(8,128)(2,1)}, f32[4,4096]{1,0:T(4,128)}) custom-call(bf16[400,4096]{1,0:T(8,128)(2,1)} %copy-done.165, f32[4,4096]{1,0:T(4,128)} %bitcast.239, f32[384,8]{1,0:T(8,128)} %copy.222.mask_ref, f32[384,4096]{1,0:T(8,128)} %get-tuple-element.73.dn_ref), custom_call_target="tpu_custom_call" | custom-call | flops 4000000000 | bytes 4194304 | tf_op jit(solution)/shard_map/pallas_call | solution.py:373
  742.2 4.4 fusion.18
  752.1 3.6 collective-permute-done.77
  755.8 10.5 %collective-permute-done.78 = f32[280,128]{1,0:T(8,128)S(1)} collective-permute-done((f32[280,128]{1,0:T(8,128)S(1)}, f32[280,128]{1,0:T(8,128)S(1)}, u32[]{:S(2)}, u32[]{:S(2)}) %collective-permute-start.78) | collective-permute-done | bytes 143392 | tf_op jit(solution)/shard_map/ppermute | solution.py:522
  772.1 3.4 collective-permute-start.91
  779.0 5.5 collective-permute-done.91
  785.5 24.2 %collective-permute-done.90 = bf16[128,1408]{1,0:T(8,128)(2,1)S(1)} collective-permute-done((bf16[128,1408]{1,0:T(8,128)(2,1)S(1)}, bf16[128,1408]{1,0:T(8,128)(2,1)S(1)}, u32[]{:S(2)}, u32[]{:S(2)}) %collective-permute-start.90) | collective-permute-done | bytes 360480 | tf_op jit(solution)/shard_map/ppermute | solution.py:560
  822.7 18.3 %collective-permute-done.61 = bf16[1024,512]{1,0:T(8,128)(2,1)} collective-permute-done((bf16[1024,512]{1,0:T(8,128)(2,1)}, bf16[1024,512]{1,0:T(8,128)(2,1)}, u32[]{:S(2)}, u32[]{:S(2)}) %collective-permute-start.61) | collective-permute-done | bytes 1048608 | tf_op jit(solution)/shard_map/ppermute | solution.py:522
  845.2 12.1 %collective-permute-done.93 = bf16[256,1408]{1,0:T(8,128)(2,1)S(1)} collective-permute-done((bf16[256,1408]{1,0:T(8,128)(2,1)S(1)}, bf16[256,1408]{1,0:T(8,128)(2,1)S(1)}, u32[]{:S(2)}, u32[]{:S(2)}) %collective-permute-start.93) | collective-permute-done | bytes 720928 | tf_op jit(solution)/shard_map/ppermute | solution.py:522
  857.8 7.4 collective-permute-done.62
  876.1 7.9 collective-permute-done.64
  884.7 3.6 collective-permute-done.55
  904.2 4.6 fusion.10
  910.0 3.4 maximum_convert_fusion
  (899 shorter events, 348.8 us)
Async XLA Ops:
  5.2 31.2 %collective-permute-start.1 = (bf16[72,128]{1,0:T(8,128)(2,1)S(1)}, bf16[72,128]{1,0:T(8,128)(2,1)S(1)}, u32[]{:S(2)}, u32[]{:S(2)}) collective-permute-start(bf16[72,128]{1,0:T(8,128)(2,1)S(1)} %pad_bitcast_fusion.1), channel_id=1, source_target_pairs={{0,6},{2,0},{4,2},{6,4},{1,7},{3,1},{5,3},{7,5},{8,14},{10,8},{12,... | collective-permute-start | bytes 55304 | tf_op jit(solution)/shard_map/ppermute | solution.py:560
  10.3 26.1 %collective-permute-start.2 = (bf16[72,128]{1,0:T(8,128)(2,1)S(1)}, bf16[72,128]{1,0:T(8,128)(2,1)S(1)}, u32[]{:S(2)}, u32[]{:S(2)}) collective-permute-start(bf16[72,128]{1,0:T(8,128)(2,1)S(1)} %pad_bitcast_fusion.1), channel_id=1, source_target_pairs={{0,4},{2,6},{4,0},{6,2},{1,5},{3,7},{5,1},{7,3},{8,12},{10,14},{12... | collective-permute-start | bytes 55304 | tf_op jit(solution)/shard_map/ppermute | solution.py:560
  10.3 30.1 %collective-permute-start.3 = (bf16[72,128]{1,0:T(8,128)(2,1)S(1)}, bf16[72,128]{1,0:T(8,128)(2,1)S(1)}, u32[]{:S(2)}, u32[]{:S(2)}) collective-permute-start(bf16[72,128]{1,0:T(8,128)(2,1)S(1)} %pad_bitcast_fusion.1), channel_id=1, source_target_pairs={{0,2},{2,4},{4,6},{6,0},{1,3},{3,5},{5,7},{7,1},{8,10},{10,12},{12... | collective-permute-start | bytes 55304 | tf_op jit(solution)/shard_map/ppermute | solution.py:560
  16.7 62.1 %collective-permute-start.4 = (bf16[256,256]{1,0:T(8,128)(2,1)}, bf16[256,256]{1,0:T(8,128)(2,1)S(1)}, u32[]{:S(2)}, u32[]{:S(2)}) collective-permute-start(bf16[256,256]{1,0:T(8,128)(2,1)} %constant_dynamic-slice_fusion.53), channel_id=1, source_target_pairs={{0,6},{2,0},{4,2},{6,4},{1,7},{3,1},{5,3},{7,5},{8,14},{10,8},{12,... | collective-permute-start | bytes 393224 | tf_op jit(solution)/shard_map/ppermute | solution.py:560
  19.5 59.9 %collective-permute-start.5 = (bf16[256,256]{1,0:T(8,128)(2,1)}, bf16[256,256]{1,0:T(8,128)(2,1)}, u32[]{:S(2)}, u32[]{:S(2)}) collective-permute-start(bf16[256,256]{1,0:T(8,128)(2,1)} %constant_dynamic-slice_fusion.53), channel_id=1, source_target_pairs={{0,4},{2,6},{4,0},{6,2},{1,5},{3,7},{5,1},{7,3},{8,12},{10,14},{12... | collective-permute-start | bytes 393224 | tf_op jit(solution)/shard_map/ppermute | solution.py:560
  36.4 44.0 %collective-permute-start.6 = (bf16[256,256]{1,0:T(8,128)(2,1)}, bf16[256,256]{1,0:T(8,128)(2,1)}, u32[]{:S(2)}, u32[]{:S(2)}) collective-permute-start(bf16[256,256]{1,0:T(8,128)(2,1)} %constant_dynamic-slice_fusion.53), channel_id=1, source_target_pairs={{0,2},{2,4},{4,6},{6,0},{1,3},{3,5},{5,7},{7,1},{8,10},{10,12},{12... | collective-permute-start | bytes 393224 | tf_op jit(solution)/shard_map/ppermute | solution.py:560
  36.4 41.4 %collective-permute-start = (bf16[16,1024]{1,0:T(8,128)(2,1)}, bf16[16,1024]{1,0:T(8,128)(2,1)}, u32[]{:S(2)}, u32[]{:S(2)}) collective-permute-start(bf16[16,1024]{1,0:T(8,128)(2,1)} %slice.317), channel_id=1, source_target_pairs={{0,1},{2,3},{4,5},{6,7},{8,9},{10,11},{12,13},{14,15},{16,17},{18,... | collective-permute-start | bytes 98312 | tf_op jit(solution)/shard_map/ppermute | solution.py:841
  40.5 41.8 %collective-permute-start.10 = (bf16[256,256]{1,0:T(8,128)(2,1)}, bf16[256,256]{1,0:T(8,128)(2,1)}, u32[]{:S(2)}, u32[]{:S(2)}) collective-permute-start(bf16[256,256]{1,0:T(8,128)(2,1)} %constant_dynamic-slice_fusion.51), channel_id=1, source_target_pairs={{0,6},{2,0},{4,2},{6,4},{1,7},{3,1},{5,3},{7,5},{8,14},{10,8},{12,... | collective-permute-start | bytes 393224 | tf_op jit(solution)/shard_map/ppermute | solution.py:560
  91.3 16.0 %collective-permute-start.17 = (bf16[256,256]{1,0:T(8,128)(2,1)S(1)}, bf16[256,256]{1,0:T(8,128)(2,1)S(1)}, u32[]{:S(2)}, u32[]{:S(2)}) collective-permute-start(bf16[256,256]{1,0:T(8,128)(2,1)S(1)} %copy-done.84), channel_id=1, source_target_pairs={{0,4},{2,6},{4,0},{6,2},{1,5},{3,7},{5,1},{7,3},{8,12},{10,14},{12... | collective-permute-start | bytes 393224 | tf_op jit(solution)/shard_map/ppermute | solution.py:560
  92.6 22.2 %collective-permute-start.7 = (bf16[1024,256]{1,0:T(8,128)(2,1)S(1)}, bf16[1024,256]{1,0:T(8,128)(2,1)S(1)}, u32[]{:S(2)}, u32[]{:S(2)}) collective-permute-start(bf16[1024,256]{1,0:T(8,128)(2,1)S(1)} %constant_dynamic-slice_fusion.52), channel_id=1, source_target_pairs={{0,1},{1,0},{2,3},{3,2},{4,5},{5,4},{6,7},{7,6},{8,9},{9,8},{10,11... | collective-permute-start | bytes 1572872 | tf_op jit(solution)/shard_map/ppermute | solution.py:522
  92.6 22.3 %collective-permute-start.13 = (bf16[1024,256]{1,0:T(8,128)(2,1)S(1)}, bf16[1024,256]{1,0:T(8,128)(2,1)S(1)}, u32[]{:S(2)}, u32[]{:S(2)}) collective-permute-start(bf16[1024,256]{1,0:T(8,128)(2,1)S(1)} %constant_dynamic-slice_fusion.50), channel_id=1, source_target_pairs={{0,16},{16,0},{1,17},{17,1},{2,18},{18,2},{3,19},{19,3},{4,20},{20... | collective-permute-start | bytes 1572872 | tf_op jit(solution)/shard_map/ppermute | solution.py:522
  116.5 17.5 %collective-permute-start.29 = (bf16[704,128]{1,0:T(8,128)(2,1)S(1)}, bf16[704,128]{1,0:T(8,128)(2,1)S(1)}, u32[]{:S(2)}, u32[]{:S(2)}) collective-permute-start(bf16[704,128]{1,0:T(8,128)(2,1)S(1)} %copy-done.80), channel_id=1, source_target_pairs={{0,4},{2,6},{4,0},{6,2},{1,5},{3,7},{5,1},{7,3},{8,12},{10,14},{12... | collective-permute-start | bytes 540680 | tf_op jit(solution)/shard_map/ppermute | solution.py:560
  117.1 45.8 %collective-permute-start.8 = (bf16[1024,512]{1,0:T(8,128)(2,1)S(1)}, bf16[1024,512]{1,0:T(8,128)(2,1)S(1)}, u32[]{:S(2)}, u32[]{:S(2)}) collective-permute-start(bf16[1024,512]{1,0:T(8,128)(2,1)S(1)} %pad_maximum_fusion.4), channel_id=1, source_target_pairs={{0,16},{16,0},{1,17},{17,1},{2,18},{18,2},{3,19},{19,3},{4,20},{20... | collective-permute-start | bytes 3145736 | tf_op jit(solution)/shard_map/ppermute | solution.py:522
  118.7 44.7 %collective-permute-start.14 = (bf16[1024,512]{1,0:T(8,128)(2,1)S(1)}, bf16[1024,512]{1,0:T(8,128)(2,1)S(1)}, u32[]{:S(2)}, u32[]{:S(2)}) collective-permute-start(bf16[1024,512]{1,0:T(8,128)(2,1)S(1)} %pad_maximum_fusion.5), channel_id=1, source_target_pairs={{0,1},{1,0},{2,3},{3,2},{4,5},{5,4},{6,7},{7,6},{8,9},{9,8},{10,11... | collective-permute-start | bytes 3145736 | tf_op jit(solution)/shard_map/ppermute | solution.py:522
  118.7 15.4 %collective-permute-start.30 = (bf16[704,128]{1,0:T(8,128)(2,1)S(1)}, bf16[704,128]{1,0:T(8,128)(2,1)S(1)}, u32[]{:S(2)}, u32[]{:S(2)}) collective-permute-start(bf16[704,128]{1,0:T(8,128)(2,1)S(1)} %copy-done.80), channel_id=1, source_target_pairs={{0,2},{2,4},{4,6},{6,0},{1,3},{3,5},{5,7},{7,1},{8,10},{10,12},{12... | collective-permute-start | bytes 540680 | tf_op jit(solution)/shard_map/ppermute | solution.py:560
  123.6 23.2 %collective-permute-start.24 = (bf16[128,1408]{1,0:T(8,128)(2,1)S(1)}, bf16[128,1408]{1,0:T(8,128)(2,1)S(1)}, u32[]{:S(2)}, u32[]{:S(2)}) collective-permute-start(bf16[128,1408]{1,0:T(8,128)(2,1)S(1)} %copy-done.64), channel_id=1, source_target_pairs={{0,6},{2,0},{4,2},{6,4},{1,7},{3,1},{5,3},{7,5},{8,14},{10,8},{12,... | collective-permute-start | bytes 1081352 | tf_op jit(solution)/shard_map/ppermute | solution.py:560
  134.0 28.5 %collective-permute-start.25 = (bf16[128,1408]{1,0:T(8,128)(2,1)S(1)}, bf16[128,1408]{1,0:T(8,128)(2,1)S(1)}, u32[]{:S(2)}, u32[]{:S(2)}) collective-permute-start(bf16[128,1408]{1,0:T(8,128)(2,1)S(1)} %copy-done.64), channel_id=1, source_target_pairs={{0,4},{2,6},{4,0},{6,2},{1,5},{3,7},{5,1},{7,3},{8,12},{10,14},{12... | collective-permute-start | bytes 1081352 | tf_op jit(solution)/shard_map/ppermute | solution.py:560
  134.1 28.5 %collective-permute-start.26 = (bf16[128,1408]{1,0:T(8,128)(2,1)S(1)}, bf16[128,1408]{1,0:T(8,128)(2,1)S(1)}, u32[]{:S(2)}, u32[]{:S(2)}) collective-permute-start(bf16[128,1408]{1,0:T(8,128)(2,1)S(1)} %copy-done.64), channel_id=1, source_target_pairs={{0,2},{2,4},{4,6},{6,0},{1,3},{3,5},{5,7},{7,1},{8,10},{10,12},{12... | collective-permute-start | bytes 1081352 | tf_op jit(solution)/shard_map/ppermute | solution.py:560
  163.3 112.2 %collective-permute-start.9 = (bf16[1024,1024]{1,0:T(8,128)(2,1)S(1)}, bf16[1024,1024]{1,0:T(8,128)(2,1)S(1)}, u32[]{:S(2)}, u32[]{:S(2)}) collective-permute-start(bf16[1024,1024]{1,0:T(8,128)(2,1)S(1)} %pad_maximum_fusion.1), channel_id=1, source_target_pairs={{0,8},{8,0},{1,9},{9,1},{2,10},{10,2},{3,11},{11,3},{4,12},{12,4},... | collective-permute-start | bytes 6291464 | tf_op jit(solution)/shard_map/ppermute | solution.py:522
  163.7 14.8 %collective-permute-start.19 = (bf16[1024,256]{1,0:T(8,128)(2,1)S(1)}, bf16[1024,256]{1,0:T(8,128)(2,1)S(1)}, u32[]{:S(2)}, u32[]{:S(2)}) collective-permute-start(bf16[1024,256]{1,0:T(8,128)(2,1)S(1)} %constant_dynamic-slice_fusion.48), channel_id=1, source_target_pairs={{0,16},{16,0},{1,17},{17,1},{2,18},{18,2},{3,19},{19,3},{4,20},{20... | collective-permute-start | bytes 1572872 | tf_op jit(solution)/shard_map/ppermute | solution.py:522
  165.2 24.0 %collective-permute-start.23 = (bf16[2048,128]{1,0:T(8,128)(2,1)S(1)}, bf16[2048,128]{1,0:T(8,128)(2,1)S(1)}, u32[]{:S(2)}, u32[]{:S(2)}) collective-permute-start(bf16[2048,128]{1,0:T(8,128)(2,1)S(1)} %constant_dynamic-slice_fusion.46), channel_id=1, source_target_pairs={{0,16},{16,0},{1,17},{17,1},{2,18},{18,2},{3,19},{19,3},{4,20},{20... | collective-permute-start | bytes 1572872 | tf_op jit(solution)/shard_map/ppermute | solution.py:522
  190.6 83.4 %collective-permute-start.27 = (bf16[512,1408]{1,0:T(8,128)(2,1)S(1)}, bf16[512,1408]{1,0:T(8,128)(2,1)S(1)}, u32[]{:S(2)}, u32[]{:S(2)}) collective-permute-start(bf16[512,1408]{1,0:T(8,128)(2,1)S(1)} %constant_dynamic-slice_fusion.45), channel_id=1, source_target_pairs={{0,1},{1,0},{2,3},{3,2},{4,5},{5,4},{6,7},{7,6},{8,9},{9,8},{10,11... | collective-permute-start | bytes 4325384 | tf_op jit(solution)/shard_map/ppermute | solution.py:522
  190.6 17.7 %collective-permute-start.31 = (bf16[2816,128]{1,0:T(8,128)(2,1)S(1)}, bf16[2816,128]{1,0:T(8,128)(2,1)S(1)}, u32[]{:S(2)}, u32[]{:S(2)}) collective-permute-start(bf16[2816,128]{1,0:T(8,128)(2,1)S(1)} %constant_dynamic-slice_fusion.43), channel_id=1, source_target_pairs={{0,16},{16,0},{1,17},{17,1},{2,18},{18,2},{3,19},{19,3},{4,20},{20... | collective-permute-start | bytes 2162696 | tf_op jit(solution)/shard_map/ppermute | solution.py:522
  192.1 77.7 %collective-permute-start.32 = (bf16[1024,512]{1,0:T(8,128)(2,1)S(1)}, bf16[1024,512]{1,0:T(8,128)(2,1)S(1)}, u32[]{:S(2)}, u32[]{:S(2)}) collective-permute-start(bf16[1024,512]{1,0:T(8,128)(2,1)S(1)} %constant_dynamic-update-slice_fusion.44), channel_id=1, source_target_pairs={{0,1},{1,0},{2,3},{3,2},{4,5},{5,4},{6,7},{7,6},{8,9},{9,8},{10,11... | collective-permute-start | bytes 3145736 | tf_op jit(solution)/shard_map/ppermute | solution.py:522
  194.1 74.6 %collective-permute-start.33 = (bf16[2048,256]{1,0:T(8,128)(2,1)S(1)}, bf16[2048,256]{1,0:T(8,128)(2,1)S(1)}, u32[]{:S(2)}, u32[]{:S(2)}) collective-permute-start(bf16[2048,256]{1,0:T(8,128)(2,1)S(1)} %constant_dynamic-update-slice_fusion.53), channel_id=1, source_target_pairs={{0,1},{1,0},{2,3},{3,2},{4,5},{5,4},{6,7},{7,6},{8,9},{9,8},{10,11... | collective-permute-start | bytes 3145736 | tf_op jit(solution)/shard_map/ppermute | solution.py:522
  208.3 70.8 %collective-permute-start.15 = (bf16[1024,1024]{1,0:T(8,128)(2,1)S(1)}, bf16[1024,1024]{1,0:T(8,128)(2,1)S(1)}, u32[]{:S(2)}, u32[]{:S(2)}) collective-permute-start(bf16[1024,1024]{1,0:T(8,128)(2,1)S(1)} %pad_maximum_fusion.2), channel_id=1, source_target_pairs={{0,8},{8,0},{1,9},{9,1},{2,10},{10,2},{3,11},{11,3},{4,12},{12,4},... | collective-permute-start | bytes 6291464 | tf_op jit(solution)/shard_map/ppermute | solution.py:522
  269.8 120.3 %collective-permute-start.36 = (bf16[2048,512]{1,0:T(8,128)(2,1)}, bf16[2048,512]{1,0:T(8,128)(2,1)}, u32[]{:S(2)}, u32[]{:S(2)}) collective-permute-start(bf16[2048,512]{1,0:T(8,128)(2,1)} %constant_dynamic-update-slice_fusion.75), channel_id=1, source_target_pairs={{0,8},{8,0},{1,9},{9,1},{2,10},{10,2},{3,11},{11,3},{4,12},{12,4},... | collective-permute-start | bytes 6291464 | tf_op jit(solution)/shard_map/ppermute | solution.py:522
  270.8 104.4 %collective-permute-start.35 = (bf16[1024,1024]{1,0:T(8,128)(2,1)}, bf16[1024,1024]{1,0:T(8,128)(2,1)}, u32[]{:S(2)}, u32[]{:S(2)}) collective-permute-start(bf16[1024,1024]{1,0:T(8,128)(2,1)} %constant_dynamic-update-slice_fusion.73), channel_id=1, source_target_pairs={{0,8},{8,0},{1,9},{9,1},{2,10},{10,2},{3,11},{11,3},{4,12},{12,4},... | collective-permute-start | bytes 6291464 | tf_op jit(solution)/shard_map/ppermute | solution.py:522
  274.0 97.6 %collective-permute-start.39 = (bf16[2816,256]{1,0:T(8,128)(2,1)}, bf16[2816,256]{1,0:T(8,128)(2,1)}, u32[]{:S(2)}, u32[]{:S(2)}) collective-permute-start(bf16[2816,256]{1,0:T(8,128)(2,1)} %constant_dynamic-update-slice_fusion.71), channel_id=1, source_target_pairs={{0,1},{1,0},{2,3},{3,2},{4,5},{5,4},{6,7},{7,6},{8,9},{9,8},{10,11... | collective-permute-start | bytes 4325384 | tf_op jit(solution)/shard_map/ppermute | solution.py:522
  275.5 105.0 %collective-permute-start.37 = (bf16[1024,1408]{1,0:T(8,128)(2,1)}, bf16[1024,1408]{1,0:T(8,128)(2,1)}, u32[]{:S(2)}, u32[]{:S(2)}) collective-permute-start(bf16[1024,1408]{1,0:T(8,128)(2,1)} %constant_dynamic-update-slice_fusion.62), channel_id=1, source_target_pairs={{0,16},{16,0},{1,17},{17,1},{2,18},{18,2},{3,19},{19,3},{4,20},{20... | collective-permute-start | bytes 8650760 | tf_op jit(solution)/shard_map/ppermute | solution.py:522
  335.9 14.4 %collective-permute-start.34 = (bf16[8,128,256]{2,1,0:T(8,128)(2,1)S(1)}, bf16[8,128,256]{2,1,0:T(8,128)(2,1)S(1)}, u32[]{:S(2)}, u32[]{:S(2)}) collective-permute-start(bf16[8,128,256]{2,1,0:T(8,128)(2,1)S(1)} %convert_element_type.482), channel_id=1, source_target_pairs={{0,1},{2,3},{4,5},{6,7},{8,9},{10,11},{12,13},{14,15},{16,17},{18,... | collective-permute-start | bytes 1572872 | tf_op jit(solution)/shard_map/ppermute | solution.py:443
  375.3 41.2 %collective-permute-start.40 = (bf16[2816,512]{1,0:T(8,128)(2,1)}, bf16[2816,512]{1,0:T(8,128)(2,1)}, u32[]{:S(2)}, u32[]{:S(2)}) collective-permute-start(bf16[2816,512]{1,0:T(8,128)(2,1)} %constant_dynamic-update-slice_fusion.87), channel_id=1, source_target_pairs={{0,8},{8,0},{1,9},{9,1},{2,10},{10,2},{3,11},{11,3},{4,12},{12,4},... | collective-permute-start | bytes 8650760 | tf_op jit(solution)/shard_map/ppermute | solution.py:522
  385.2 38.2 %collective-permute-start.38 = (bf16[1024,2816]{1,0:T(8,128)(2,1)}, bf16[1024,2816]{1,0:T(8,128)(2,1)}, u32[]{:S(2)}, u32[]{:S(2)}) collective-permute-start(bf16[1024,2816]{1,0:T(8,128)(2,1)} %constant_dynamic-update-slice_fusion.85), channel_id=1, source_target_pairs={{0,8},{8,0},{1,9},{9,1},{2,10},{10,2},{3,11},{11,3},{4,12},{12,4},... | collective-permute-start | bytes 17301512 | tf_op jit(solution)/shard_map/ppermute | solution.py:522
  440.5 17.7 %collective-permute-start.41 = (bf16[2816,512]{1,0:T(8,128)(2,1)S(1)}, bf16[2816,512]{1,0:T(8,128)(2,1)S(1)}, u32[]{:S(2)}, u32[]{:S(2)}) collective-permute-start(bf16[2816,512]{1,0:T(8,128)(2,1)S(1)} %convolution_convert_fusion.1), channel_id=1, source_target_pairs={{0,8},{8,0},{1,9},{9,1},{2,10},{10,2},{3,11},{11,3},{4,12},{12,4},... | collective-permute-start | bytes 8650760 | tf_op jit(solution)/shard_map/ppermute | solution.py:522
  449.2 102.8 %collective-permute-start.42 = (bf16[1024,2816]{1,0:T(8,128)(2,1)}, bf16[1024,2816]{1,0:T(8,128)(2,1)}, u32[]{:S(2)}, u32[]{:S(2)}) collective-permute-start(bf16[1024,2816]{1,0:T(8,128)(2,1)} %convolution_convert_fusion), channel_id=1, source_target_pairs={{0,8},{8,0},{1,9},{9,1},{2,10},{10,2},{3,11},{11,3},{4,12},{12,4},... | collective-permute-start | bytes 17301512 | tf_op jit(solution)/shard_map/ppermute | solution.py:522
  460.2 44.8 %collective-permute-start.46 = (bf16[2816,256]{1,0:T(8,128)(2,1)}, bf16[2816,256]{1,0:T(8,128)(2,1)}, u32[]{:S(2)}, u32[]{:S(2)}) collective-permute-start(bf16[2816,256]{1,0:T(8,128)(2,1)} %add_convert_fusion.5), channel_id=1, source_target_pairs={{0,1},{1,0},{2,3},{3,2},{4,5},{5,4},{6,7},{7,6},{8,9},{9,8},{10,11... | collective-permute-start | bytes 4325384 | tf_op jit(solution)/shard_map/ppermute | solution.py:522
  494.1 36.0 %collective-permute-start.43 = (bf16[2048,512]{1,0:T(8,128)(2,1)}, bf16[2048,512]{1,0:T(8,128)(2,1)}, u32[]{:S(2)}, u32[]{:S(2)}) collective-permute-start(bf16[2048,512]{1,0:T(8,128)(2,1)} %convolution_convert_fusion.2), channel_id=1, source_target_pairs={{0,8},{8,0},{1,9},{9,1},{2,10},{10,2},{3,11},{11,3},{4,12},{12,4},... | collective-permute-start | bytes 6291464 | tf_op jit(solution)/shard_map/ppermute | solution.py:522
  508.0 18.1 %collective-permute-start.95 = (bf16[2816,128]{1,0:T(8,128)(2,1)}, bf16[2816,128]{1,0:T(8,128)(2,1)}, u32[]{:S(2)}, u32[]{:S(2)}) collective-permute-start(bf16[2816,128]{1,0:T(8,128)(2,1)} %add_convert_fusion.11), channel_id=1, source_target_pairs={{0,16},{16,0},{1,17},{17,1},{2,18},{18,2},{3,19},{19,3},{4,20},{20... | collective-permute-start | bytes 2162696 | tf_op jit(solution)/shard_map/ppermute | solution.py:522
  510.2 34.9 %collective-permute-start.44 = (bf16[1024,1024]{1,0:T(8,128)(2,1)}, bf16[1024,1024]{1,0:T(8,128)(2,1)}, u32[]{:S(2)}, u32[]{:S(2)}) collective-permute-start(bf16[1024,1024]{1,0:T(8,128)(2,1)} %convolution_convert_fusion.5), channel_id=1, source_target_pairs={{0,8},{8,0},{1,9},{9,1},{2,10},{10,2},{3,11},{11,3},{4,12},{12,4},... | collective-permute-start | bytes 6291464 | tf_op jit(solution)/shard_map/ppermute | solution.py:522
  530.0 14.3 %collective-permute-start.97 = (bf16[704,128]{1,0:T(8,128)(2,1)S(1)}, bf16[704,128]{1,0:T(8,128)(2,1)S(1)}, u32[]{:S(2)}, u32[]{:S(2)}) collective-permute-start(bf16[704,128]{1,0:T(8,128)(2,1)S(1)} %get-tuple-element.212), channel_id=1, source_target_pairs={{0,4},{2,6},{4,0},{6,2},{1,5},{3,7},{5,1},{7,3},{8,12},{10,14},{12... | collective-permute-start | bytes 540680 | tf_op jit(solution)/shard_map/ppermute | solution.py:560
  530.0 14.3 %collective-permute-start.96 = (bf16[704,128]{1,0:T(8,128)(2,1)S(1)}, bf16[704,128]{1,0:T(8,128)(2,1)S(1)}, u32[]{:S(2)}, u32[]{:S(2)}) collective-permute-start(bf16[704,128]{1,0:T(8,128)(2,1)S(1)} %get-tuple-element.210), channel_id=1, source_target_pairs={{0,2},{2,4},{4,6},{6,0},{1,3},{3,5},{5,7},{7,1},{8,10},{10,12},{12... | collective-permute-start | bytes 540680 | tf_op jit(solution)/shard_map/ppermute | solution.py:560
  535.1 62.0 %collective-permute-start.48 = (bf16[2048,256]{1,0:T(8,128)(2,1)}, bf16[2048,256]{1,0:T(8,128)(2,1)}, u32[]{:S(2)}, u32[]{:S(2)}) collective-permute-start(bf16[2048,256]{1,0:T(8,128)(2,1)} %add_convert_fusion.9), channel_id=1, source_target_pairs={{0,1},{1,0},{2,3},{3,2},{4,5},{5,4},{6,7},{7,6},{8,9},{9,8},{10,11... | collective-permute-start | bytes 3145736 | tf_op jit(solution)/shard_map/ppermute | solution.py:522
  548.2 45.8 %collective-permute-start.49 = (bf16[1024,512]{1,0:T(8,128)(2,1)}, bf16[1024,512]{1,0:T(8,128)(2,1)}, u32[]{:S(2)}, u32[]{:S(2)}) collective-permute-start(bf16[1024,512]{1,0:T(8,128)(2,1)} %add_convert_fusion.8), channel_id=1, source_target_pairs={{0,1},{1,0},{2,3},{3,2},{4,5},{5,4},{6,7},{7,6},{8,9},{9,8},{10,11... | collective-permute-start | bytes 3145736 | tf_op jit(solution)/shard_map/ppermute | solution.py:522
  551.3 40.4 %collective-permute-start.100 = (bf16[704,256]{1,0:T(8,128)(2,1)}, bf16[704,256]{1,0:T(8,128)(2,1)}, u32[]{:S(2)}, u32[]{:S(2)}) collective-permute-start(bf16[704,256]{1,0:T(8,128)(2,1)} %maximum_select_fusion.15), channel_id=1, source_target_pairs={{0,1},{1,0},{2,3},{3,2},{4,5},{5,4},{6,7},{7,6},{8,9},{9,8},{10,11... | collective-permute-start | bytes 1081352 | tf_op jit(solution)/shard_map/ppermute | solution.py:522
  557.1 139.0 %collective-permute-start.47 = (bf16[1024,1408]{1,0:T(8,128)(2,1)}, bf16[1024,1408]{1,0:T(8,128)(2,1)}, u32[]{:S(2)}, u32[]{:S(2)}) collective-permute-start(bf16[1024,1408]{1,0:T(8,128)(2,1)} %add_convert_fusion.1), channel_id=1, source_target_pairs={{0,16},{16,0},{1,17},{17,1},{2,18},{18,2},{3,19},{19,3},{4,20},{20... | collective-permute-start | bytes 8650760 | tf_op jit(solution)/shard_map/ppermute | solution.py:522
  572.5 28.7 %collective-permute-start.45 = (bf16[8,128,256]{2,1,0:T(8,128)(2,1)S(1)}, bf16[8,128,256]{2,1,0:T(8,128)(2,1)S(1)}, u32[]{:S(2)}, u32[]{:S(2)}) collective-permute-start(bf16[8,128,256]{2,1,0:T(8,128)(2,1)S(1)} %convert_element_type.510), channel_id=1, source_target_pairs={{1,0},{3,2},{5,4},{7,6},{9,8},{11,10},{13,12},{15,14},{17,16},{19,... | collective-permute-start | bytes 1572872 | tf_op jit(solution)/shard_map/ppermute | solution.py:462
  596.5 51.7 %collective-permute-start.69 = (bf16[1024,256]{1,0:T(8,128)(2,1)}, bf16[1024,256]{1,0:T(8,128)(2,1)}, u32[]{:S(2)}, u32[]{:S(2)}) collective-permute-start(bf16[1024,256]{1,0:T(8,128)(2,1)} %add_convert_fusion.14), channel_id=1, source_target_pairs={{0,16},{16,0},{1,17},{17,1},{2,18},{18,2},{3,19},{19,3},{4,20},{20... | collective-permute-start | bytes 1572872 | tf_op jit(solution)/shard_map/ppermute | solution.py:522
  599.7 55.2 %collective-permute-start.81 = (bf16[2048,128]{1,0:T(8,128)(2,1)}, bf16[2048,128]{1,0:T(8,128)(2,1)}, u32[]{:S(2)}, u32[]{:S(2)}) collective-permute-start(bf16[2048,128]{1,0:T(8,128)(2,1)} %add_convert_fusion.15), channel_id=1, source_target_pairs={{0,16},{16,0},{1,17},{17,1},{2,18},{18,2},{3,19},{19,3},{4,20},{20... | collective-permute-start | bytes 1572872 | tf_op jit(solution)/shard_map/ppermute | solution.py:522
  656.6 14.4 %collective-permute-start.84 = (bf16[512,128]{1,0:T(8,128)(2,1)S(1)}, bf16[512,128]{1,0:T(8,128)(2,1)S(1)}, u32[]{:S(2)}, u32[]{:S(2)}) collective-permute-start(bf16[512,128]{1,0:T(8,128)(2,1)S(1)} %get-tuple-element.214), channel_id=1, source_target_pairs={{0,6},{2,0},{4,2},{6,4},{1,7},{3,1},{5,3},{7,5},{8,14},{10,8},{12,... | collective-permute-start | bytes 393224 | tf_op jit(solution)/shard_map/ppermute | solution.py:560
  693.0 32.9 %collective-permute-start.87 = (bf16[512,512]{1,0:T(8,128)(2,1)S(1)}, bf16[512,512]{1,0:T(8,128)(2,1)S(1)}, u32[]{:S(2)}, u32[]{:S(2)}) collective-permute-start(bf16[512,512]{1,0:T(8,128)(2,1)S(1)} %maximum_select_fusion.14), channel_id=1, source_target_pairs={{0,8},{8,0},{1,9},{9,1},{2,10},{10,2},{3,11},{11,3},{4,12},{12,4},... | collective-permute-start | bytes 1572872 | tf_op jit(solution)/shard_map/ppermute | solution.py:522
  727.5 41.4 %collective-permute-start.88 = (bf16[512,1408]{1,0:T(8,128)(2,1)}, bf16[512,1408]{1,0:T(8,128)(2,1)}, u32[]{:S(2)}, u32[]{:S(2)}) collective-permute-start(bf16[512,1408]{1,0:T(8,128)(2,1)} %add_convert_fusion.4), channel_id=1, source_target_pairs={{0,1},{1,0},{2,3},{3,2},{4,5},{5,4},{6,7},{7,6},{8,9},{9,8},{10,11... | collective-permute-start | bytes 4325384 | tf_op jit(solution)/shard_map/ppermute | solution.py:522
  751.5 59.2 %collective-permute-start.60 = (bf16[1024,1024]{1,0:T(8,128)(2,1)S(1)}, bf16[1024,1024]{1,0:T(8,128)(2,1)S(1)}, u32[]{:S(2)}, u32[]{:S(2)}) collective-permute-start(bf16[1024,1024]{1,0:T(8,128)(2,1)S(1)} %convolution_convert_fusion.3), channel_id=1, source_target_pairs={{0,8},{8,0},{1,9},{9,1},{2,10},{10,2},{3,11},{11,3},{4,12},{12,4},... | collective-permute-start | bytes 6291464 | tf_op jit(solution)/shard_map/ppermute | solution.py:522
  751.7 62.1 %collective-permute-start.51 = (bf16[1024,1024]{1,0:T(8,128)(2,1)S(1)}, bf16[1024,1024]{1,0:T(8,128)(2,1)S(1)}, u32[]{:S(2)}, u32[]{:S(2)}) collective-permute-start(bf16[1024,1024]{1,0:T(8,128)(2,1)S(1)} %convolution_convert_fusion.4), channel_id=1, source_target_pairs={{0,8},{8,0},{1,9},{9,1},{2,10},{10,2},{3,11},{11,3},{4,12},{12,4},... | collective-permute-start | bytes 6291464 | tf_op jit(solution)/shard_map/ppermute | solution.py:522
  775.6 34.1 %collective-permute-start.90 = (bf16[128,1408]{1,0:T(8,128)(2,1)S(1)}, bf16[128,1408]{1,0:T(8,128)(2,1)S(1)}, u32[]{:S(2)}, u32[]{:S(2)}) collective-permute-start(bf16[128,1408]{1,0:T(8,128)(2,1)S(1)} %get-tuple-element.179), channel_id=1, source_target_pairs={{0,4},{2,6},{4,0},{6,2},{1,5},{3,7},{5,1},{7,3},{8,12},{10,14},{12... | collective-permute-start | bytes 1081352 | tf_op jit(solution)/shard_map/ppermute | solution.py:560
  775.6 34.1 %collective-permute-start.89 = (bf16[128,1408]{1,0:T(8,128)(2,1)S(1)}, bf16[128,1408]{1,0:T(8,128)(2,1)S(1)}, u32[]{:S(2)}, u32[]{:S(2)}) collective-permute-start(bf16[128,1408]{1,0:T(8,128)(2,1)S(1)} %get-tuple-element.177), channel_id=1, source_target_pairs={{0,2},{2,4},{4,6},{6,0},{1,3},{3,5},{5,7},{7,1},{8,10},{10,12},{12... | collective-permute-start | bytes 1081352 | tf_op jit(solution)/shard_map/ppermute | solution.py:560
  784.5 33.1 %collective-permute-start.80 = (f32[280,128]{1,0:T(8,128)S(1)}, f32[280,128]{1,0:T(8,128)S(1)}, u32[]{:S(2)}, u32[]{:S(2)}) collective-permute-start(f32[280,128]{1,0:T(8,128)S(1)} %add.925), channel_id=1, source_target_pairs={{0,4},{2,6},{4,0},{6,2},{1,5},{3,7},{5,1},{7,3},{8,12},{10,14},{12... | collective-permute-start | bytes 430088 | tf_op jit(solution)/shard_map/ppermute | solution.py:760
  812.6 28.4 %collective-permute-start.61 = (bf16[1024,512]{1,0:T(8,128)(2,1)}, bf16[1024,512]{1,0:T(8,128)(2,1)}, u32[]{:S(2)}, u32[]{:S(2)}) collective-permute-start(bf16[1024,512]{1,0:T(8,128)(2,1)} %add_convert_fusion.6), channel_id=1, source_target_pairs={{0,1},{1,0},{2,3},{3,2},{4,5},{5,4},{6,7},{7,6},{8,9},{9,8},{10,11... | collective-permute-start | bytes 3145736 | tf_op jit(solution)/shard_map/ppermute | solution.py:522
  815.6 27.7 %collective-permute-start.52 = (bf16[1024,512]{1,0:T(8,128)(2,1)}, bf16[1024,512]{1,0:T(8,128)(2,1)}, u32[]{:S(2)}, u32[]{:S(2)}) collective-permute-start(bf16[1024,512]{1,0:T(8,128)(2,1)} %add_convert_fusion.7), channel_id=1, source_target_pairs={{0,16},{16,0},{1,17},{17,1},{2,18},{18,2},{3,19},{19,3},{4,20},{20... | collective-permute-start | bytes 3145736 | tf_op jit(solution)/shard_map/ppermute | solution.py:522
  821.4 35.9 %collective-permute-start.93 = (bf16[256,1408]{1,0:T(8,128)(2,1)S(1)}, bf16[256,1408]{1,0:T(8,128)(2,1)S(1)}, u32[]{:S(2)}, u32[]{:S(2)}) collective-permute-start(bf16[256,1408]{1,0:T(8,128)(2,1)S(1)} %maximum_select_fusion.9), channel_id=1, source_target_pairs={{0,16},{16,0},{1,17},{17,1},{2,18},{18,2},{3,19},{19,3},{4,20},{20... | collective-permute-start | bytes 2162696 | tf_op jit(solution)/shard_map/ppermute | solution.py:522
  842.7 22.4 %collective-permute-start.62 = (bf16[1024,256]{1,0:T(8,128)(2,1)S(1)}, bf16[1024,256]{1,0:T(8,128)(2,1)S(1)}, u32[]{:S(2)}, u32[]{:S(2)}) collective-permute-start(bf16[1024,256]{1,0:T(8,128)(2,1)S(1)} %add_convert_fusion.12), channel_id=1, source_target_pairs={{0,16},{16,0},{1,17},{17,1},{2,18},{18,2},{3,19},{19,3},{4,20},{20... | collective-permute-start | bytes 1572872 | tf_op jit(solution)/shard_map/ppermute | solution.py:522
  844.8 26.9 %collective-permute-start.53 = (bf16[1024,256]{1,0:T(8,128)(2,1)S(1)}, bf16[1024,256]{1,0:T(8,128)(2,1)S(1)}, u32[]{:S(2)}, u32[]{:S(2)}) collective-permute-start(bf16[1024,256]{1,0:T(8,128)(2,1)S(1)} %add_convert_fusion.13), channel_id=1, source_target_pairs={{0,1},{1,0},{2,3},{3,2},{4,5},{5,4},{6,7},{7,6},{8,9},{9,8},{10,11... | collective-permute-start | bytes 1572872 | tf_op jit(solution)/shard_map/ppermute | solution.py:522
  857.7 46.5 %collective-permute-start.94 = (bf16[256,2816]{1,0:T(8,128)(2,1)S(1)}, bf16[256,2816]{1,0:T(8,128)(2,1)}, u32[]{:S(2)}, u32[]{:S(2)}) collective-permute-start(bf16[256,2816]{1,0:T(8,128)(2,1)S(1)} %maximum_select_fusion.3), channel_id=1, source_target_pairs={{0,8},{8,0},{1,9},{9,1},{2,10},{10,2},{3,11},{11,3},{4,12},{12,4},... | collective-permute-start | bytes 4325384 | tf_op jit(solution)/shard_map/ppermute | solution.py:522
  866.7 17.3 %collective-permute-start.64 = (bf16[256,256]{1,0:T(8,128)(2,1)S(1)}, bf16[256,256]{1,0:T(8,128)(2,1)S(1)}, u32[]{:S(2)}, u32[]{:S(2)}) collective-permute-start(bf16[256,256]{1,0:T(8,128)(2,1)S(1)} %get-tuple-element.221), channel_id=1, source_target_pairs={{0,4},{2,6},{4,0},{6,2},{1,5},{3,7},{5,1},{7,3},{8,12},{10,14},{12... | collective-permute-start | bytes 393224 | tf_op jit(solution)/shard_map/ppermute | solution.py:560
  869.8 14.3 %collective-permute-start.63 = (bf16[256,256]{1,0:T(8,128)(2,1)S(1)}, bf16[256,256]{1,0:T(8,128)(2,1)S(1)}, u32[]{:S(2)}, u32[]{:S(2)}) collective-permute-start(bf16[256,256]{1,0:T(8,128)(2,1)S(1)} %get-tuple-element.219), channel_id=1, source_target_pairs={{0,2},{2,4},{4,6},{6,0},{1,3},{3,5},{5,7},{7,1},{8,10},{10,12},{12... | collective-permute-start | bytes 393224 | tf_op jit(solution)/shard_map/ppermute | solution.py:560
  (218 other events, 2257.2 us)

commit v3 on v2

--- a/solution.py
+++ b/solution.py
@@ -434,13 +434,13 @@
     (n,) = call(conv_kernel, [n_shape], [], x, weights, masks, micros=5)
     n = points("inverse", n)
     (inv,) = call(inverse_kernel, [inv_shape], [], n, col, row, micros=10)
-    inv = points("state", inv)
     start = jnp.zeros((H, DK, DV), BF16)
     ahead = [(i, i + 1) for i in range(sp_size - 1)]
     behind = [(i + 1, i) for i in range(sp_size - 1)]
     for _ in range(sp_size - 1):
         (state,) = call(state_kernel, [state_shape], [], n, inv, col, start, micros=4)
         start = lax.ppermute(state.astype(BF16), "sp", ahead)
+    start = points("scan", start)
     mixed, cor, states = call(
         scan_kernel,
         [((length, H * DV), BF16), cor_shape, ((blocks, H, DK, DV), BF16)],
@@ -569,19 +569,23 @@
 
 
 def sum_blocks(value):
-    count = lax.axis_size("fsdp")
-    rows = value.shape[0] // count
-    index = lax.axis_index("fsdp")
-
-    def block(s):
-        return lax.dynamic_slice_in_dim(value, lax.rem(index + s, count) * rows, rows, 0)
-
-    total = block(0)
-    for s in range(1, count):
-        total = total + shifted(block(s).astype(BF16), s).astype(F32)
+    total = lax.psum_scatter(value.astype(BF16), "fsdp", scatter_dimension=0, tiled=True)
     if lax.axis_size("hi") > 1:
         total = lax.psum(total, "hi")
     return total
+
+
+WEIGHT_AXES = ("fsdp", "hi", "x", "core", "sp")
+
+
+def gather_rows(shard):
+    count, own = 1, 0
+    for axis in WEIGHT_AXES[1:]:
+        count = count * lax.axis_size(axis)
+        own = own * lax.axis_size(axis) + lax.axis_index(axis)
+    rows = shard.shape[0] // count
+    piece = lax.dynamic_slice_in_dim(shard, own * rows, rows, 0)
+    return lax.all_gather(piece, WEIGHT_AXES, axis=0, tiled=True)
 
 
 class ColumnGather:
@@ -606,21 +610,6 @@
 
     def full(self):
         return self.held, swap(self.held, "core")
-
-
-class HalfGather(ColumnGather):
-    def __init__(self, shard):
-        rows, width = shard.shape[0] // 2, shard.shape[1] // 4
-        column = (2 * lax.axis_index("core") + lax.axis_index("x")) * width
-        self.first = "x"
-        self.piece = lax.dynamic_slice(
-            shard, (lax.axis_index("sp") * rows, column), (rows, width)
-        )
-
-    def second(self, *earlier):
-        held = after(self.held, *earlier) if earlier else self.held
-        self.held = jnp.concatenate([held, swap(held, "sp")], axis=0)
-        return self.held
 
 
 def dot_columns(values, halves_of):
@@ -671,11 +660,28 @@
             + self.from_second.astype(F32)
         )
 
-    def finish(self):
-        total = sum_blocks(self.own()).astype(BF16)
-        for axis in (other(self.first), self.first, "core"):
-            total = pair(axis, total, swap(total, axis), 1)
-        return total.astype(F32)
+    def block(self):
+        return sum_blocks(self.own())
+
+    def spread(self, every):
+        ways = {"core": 0, "x": 1, "sp": 2}
+        order = tuple(ways[axis] for axis in relative_axes(self.first))
+        pieces = widen(jnp.transpose(every, order + (3, 4)), self.width)
+        pieces = pieces.reshape((8,) + pieces.shape[3:])
+        return jnp.swapaxes(pieces, 0, 1).reshape(pieces.shape[1], -1).astype(F32)
+
+
+def finish(sums):
+    blocks = [narrow(s.block()) for s in sums]
+    held = jnp.concatenate(blocks, axis=0)[None]
+    for axis in ("sp", "x", "core"):
+        held = pair(axis, held, swap(held, axis), 0)
+    held = held.reshape((2, 2, 2) + held.shape[1:])
+    out, start = [], 0
+    for s, block in zip(sums, blocks):
+        out.append(s.spread(held[:, :, :, start : start + block.shape[0]]))
+        start += block.shape[0]
+    return out
 
 
 def by_half(values):
@@ -688,21 +694,22 @@
     )
 
 
-def from_half(values):
-    half = values.shape[1] // 2
-    first = lax.axis_index("sp") == 0
-    low = jnp.where(first, values[:, :half], values[:, half:])
-    high = jnp.where(first, values[:, half:], values[:, :half])
-    shape = (values.shape[0], lax.axis_size("fsdp"), 1, half // lax.axis_size("fsdp"))
-    return jnp.concatenate([low.reshape(shape), high.reshape(shape)], axis=2).reshape(
-        values.shape
-    )
-
-
 class HalfSum:
-    def __init__(self, left, near_core, far_core):
-        self.left, self.near = left, near_core
-        self.width = near_core.shape[1] // 2
+    def __init__(self, left, right):
+        self.left, self.first = left, "x"
+        self.width = width = right.shape[1] // 4
+        core, x = lax.axis_index("core"), lax.axis_index("x")
+
+        def half(c):
+            return jnp.concatenate(
+                [
+                    lax.dynamic_slice_in_dim(right, (2 * c + d) * width, width, 1)
+                    for d in (x, 1 - x)
+                ],
+                axis=1,
+            )
+
+        self.near, far_core = half(core), half(1 - core)
         self.rows = left.shape[1] // 2
         self.from_core = swap(grad_dot(left, far_core).astype(BF16), "core")
 
@@ -723,7 +730,7 @@
         self.from_y = swap(self.outgoing, "sp")
         return self.outgoing
 
-    def finish(self):
+    def block(self):
         rows, width = self.rows, self.width
         own = (
             grad_dot(self.left[:, :rows], self.near[:, :width])
@@ -731,17 +738,35 @@
             + self.from_x[:rows].astype(F32)
             + self.from_y.astype(F32)
         )
-        total = sum_blocks(own).astype(BF16)
-        for axis, dim in (("sp", 0), ("x", 1), ("core", 1)):
-            total = pair(axis, total, swap(total, axis), dim)
-        return total.astype(F32)
-
-
-def gather_small(parts):
+        return sum_blocks(own)
+
+    def spread(self, every):
+        pieces = widen(every, self.width)
+        return (
+            jnp.transpose(pieces, (2, 3, 0, 1, 4))
+            .reshape(2 * pieces.shape[3], 4 * self.width)
+            .astype(F32)
+        )
+
+
+def narrow(value):
+    return jnp.concatenate(
+        [value[:, i : i + 128] for i in range(0, value.shape[1], 128)], axis=0
+    )
+
+
+def widen(value, width):
+    blocks = width // 128
+    split = value.reshape(value.shape[:-2] + (blocks, value.shape[-2] // blocks, 128))
+    return jnp.swapaxes(split, -3, -2).reshape(value.shape[:-2] + (-1, width))
+
+
+def pack_small(parts, width):
     flat = jnp.concatenate([p.reshape(-1) for p in parts])
-    size = flat.shape[0]
-    flat = jnp.pad(flat, (0, -size % 1024)).reshape(-1, 128)
-    every = gather_blocks(flat).reshape(lax.axis_size("fsdp"), -1)
+    return jnp.pad(flat, (0, -flat.shape[0] % (16 * width))).reshape(-1, width)
+
+
+def unpack_small(every, parts):
     out, start = [], 0
     for p in parts:
         out.append(every[:, start : start + p.size].reshape((-1,) + p.shape))
@@ -792,44 +817,63 @@
     sp_size = lax.axis_size("sp")
     member = lax.axis_index("sp")
     qkv_cols = H * (2 * DK + DV)
-    rate_all, conv_all, decay_all, mixer_all, heads_all, feed_all = gather_small(
-        (rate_weight, conv_weight, head_decay, mixer_gain, heads_gain, feed_gain)
-    )
+    qk_cols = 2 * H * DK
+    members = lax.axis_size("fsdp")
+    qk_way = ColumnGather(input_weight[:, :qk_cols], "x")
+    v_way = ColumnGather(input_weight[:, qk_cols:qkv_cols], "sp")
+    gate_way = ColumnGather(input_weight[:, qkv_cols:], "x")
+    down_way = ColumnGather(down_weight, "sp")
+    pair_rows, pair_cols = qk_way.piece.shape[0], 2 * qk_way.piece.shape[1]
+    smalls = (rate_weight, conv_weight, head_decay, mixer_gain, heads_gain, feed_gain)
+    first_load = jnp.concatenate(
+        [
+            jnp.concatenate([qk_way.piece, v_way.piece], axis=1),
+            pack_small(smalls, pair_cols),
+        ],
+        axis=0,
+    )
+    first_all = gather_blocks(first_load).reshape(members, -1, pair_cols)
+    both = first_all[:, :pair_rows].reshape(-1, pair_cols)
+    qk_way.held, v_way.held = both[:, : pair_cols // 2], both[:, pair_cols // 2 :]
+    rate_all, conv_all, decay_all, mixer_all, heads_all, feed_all = unpack_small(
+        first_all[:, pair_rows:].reshape(members, -1), smalls
+    )
+    qkv_second = (qk_way.second(), v_way.second())
+    gate_rows = narrow(gate_way.piece).shape[0]
+    second_load = after(
+        jnp.concatenate([narrow(gate_way.piece), narrow(down_way.piece)], axis=0), both
+    )
+    second_all = gather_blocks(second_load).reshape(members, -1, 128)
+    gate_way.held = widen(second_all[:, :gate_rows], gate_way.piece.shape[1]).reshape(
+        -1, gate_way.piece.shape[1]
+    )
+    down_way.held = widen(second_all[:, gate_rows:], down_way.piece.shape[1]).reshape(
+        -1, down_way.piece.shape[1]
+    )
+    qkv_third = (qk_way.third(), v_way.third())
+    early = (gate_way.second(*qkv_third), down_way.second(*qkv_third))
+    qk_full, v_full = qk_way.full(), v_way.full()
+    out_full = gather_rows(output_weight)
+    up_full = gather_rows(up_weight)
     rate_full = rate_all.reshape(-1, 2 * H)
     conv_full = jnp.swapaxes(conv_all, 0, 1).reshape(CONV, -1).astype(F32)
     decay_full = jnp.swapaxes(decay_all, 0, 1).reshape(2, H).astype(F32)
     mixer_scale = mixer_all.reshape(-1).astype(F32)
     heads_scale = heads_all.reshape(-1).astype(F32)
     feed_scale = feed_all.reshape(-1).astype(F32)
-    qk_cols = 2 * H * DK
-    qk_way = ColumnGather(input_weight[:, :qk_cols], "x")
-    v_way = ColumnGather(input_weight[:, qk_cols:qkv_cols], "sp")
-    gate_way = ColumnGather(input_weight[:, qkv_cols:], "sp")
-    out_way = ColumnGather(output_weight, "sp")
-    up_way = HalfGather(up_weight)
-    down_way = ColumnGather(down_weight, "sp")
-    qkv_blocks = (qk_way.blocks(), v_way.blocks())
-    qkv_second = (qk_way.second(), v_way.second())
-    gate_way.blocks(*qkv_blocks)
-    out_way.blocks(*qkv_blocks)
-    qkv_third = (qk_way.third(), v_way.third())
-    up_way.blocks(*qkv_second)
-    down_way.blocks(*qkv_second)
-    early = (gate_way.second(*qkv_third), out_way.second(*qkv_third))
-    qk_full, v_full = qk_way.full(), v_way.full()
 
     def points(name, value):
         if name == "inverse":
-            return after(value, up_way.second(*early), down_way.second(*early))
-        if name == "state":
-            late = (gate_way.third(*early), out_way.third(*early))
-            up_way.third(*late)
-            down_way.third(*late)
-            return after(value, *late)
+            for way in (gate_way, down_way):
+                way.third(value)
+            return after(value, *early)
+        if name == "scan":
+            return after(value, gate_way.held, down_way.held)
         if name == "back":
             return after(value, sums["down"].third())
         if name == "conv_back":
             return after(value, *(sums[key].third() for key in ("up", "out", "gate")))
+        return value
 
     sums = {}
 
@@ -853,45 +897,39 @@
     )
     rate_raw = jnp.dot(normed_low, rate_full, preferred_element_type=F32)
     rates = rate_raw.astype(BF16).astype(F32).reshape(length, H, 2)
-    mixed, pull_mix = mixer(after(qkv, *early), conv_full, rates, decay_full, doc_ids, member, sp_size, points)
-    gate_full, out_full = gate_way.full(), out_way.full()
-    up_full, down_full = up_way.full(), down_way.full()
-    gate_raw = reorder(dot_columns(normed_low, gate_full), "sp")
+    mixed, pull_mix = mixer(qkv, conv_full, rates, decay_full, doc_ids, member, sp_size, points)
+    gate_full, down_full = gate_way.full(), down_way.full()
+    gate_raw = reorder(dot_columns(normed_low, gate_full), "x")
     gated, pull_gate = jax.vjp(output_gate, mixed.astype(F32), gate_raw, heads_scale)
     gated_low = gated.astype(BF16)
-    attended = reorder(dot_columns(gated_low, out_full), "sp")
+    attended = jnp.dot(gated_low, out_full, preferred_element_type=F32)
     (hidden, normed_two), pull_resid = jax.vjp(residual_norm, x_float, attended, feed_scale)
-    two_low = by_half(normed_two.astype(BF16))
-    core_first = lax.axis_index("core") == 0
-    own_side, far_side = (jnp.dot(two_low, w, preferred_element_type=F32) for w in up_full)
-
-    def feed_act(own_side, far_side):
-        gate = jnp.where(core_first, own_side, far_side)
-        return jax.nn.silu(gate) * jnp.where(core_first, far_side, own_side)
-
-    activated, pull_act = jax.vjp(feed_act, own_side, far_side)
-
-    def turn(values):
-        half = values.shape[1] // 2
-        return pair("x", values[:, :half], values[:, half:], 1)
-
-    act_low = turn(activated.astype(BF16))
+    two_low = normed_two.astype(BF16)
+    gate_up = jnp.dot(two_low, up_full, preferred_element_type=F32)
+
+    def feed_act(gate_up):
+        half = gate_up.shape[1] // 2
+        return jax.nn.silu(gate_up[:, :half]) * gate_up[:, half:]
+
+    activated, pull_act = jax.vjp(feed_act, gate_up)
+    act_low = activated.astype(BF16)
     block_out = (hidden + reorder(dot_columns(act_low, down_full), "sp")).astype(BF16)
     cot_rel = reorder(cotangent, "sp")
     sums["down"] = ColumnSum(act_low, cot_rel, "sp")
-    d_act = turn(dot_back(cot_rel, down_full))
-    d_own, d_far = (d.astype(BF16) for d in pull_act(d_act))
-    sums["up"] = HalfSum(two_low, d_own, d_far)
-    d_both = after(jnp.concatenate([d_own, d_far], axis=1), sums["down"].second())
-    d_two = from_half(dot_back(d_both, up_full))
+    d_act = dot_back(cot_rel, down_full)
+    d_gu_low = pull_act(d_act)[0].astype(BF16)
+    sums["up"] = HalfSum(by_half(two_low), d_gu_low)
+    d_gu_low = after(d_gu_low, sums["down"].second())
+    d_two = jnp.einsum("tf,df->td", d_gu_low, up_full, preferred_element_type=F32)
     d_resid, d_attended, feed_grad = pull_resid((cotangent.astype(F32), d_two))
-    d_att_rel = reorder(d_attended.astype(BF16), "sp")
+    d_att_low = d_attended.astype(BF16)
+    d_att_rel = reorder(d_att_low, "sp")
     sums["out"] = ColumnSum(gated_low, d_att_rel, "sp")
-    d_gated = dot_back(d_att_rel, out_full)
+    d_gated = jnp.einsum("td,ed->te", d_att_low, out_full, preferred_element_type=F32)
     d_mixed, d_gate, heads_grad = pull_gate(d_gated)
     d_gate_low = d_gate.astype(BF16)
-    d_gate_rel = reorder(d_gate_low, "sp")
-    sums["gate"] = ColumnSum(normed_low, d_gate_rel, "sp")
+    d_gate_rel = reorder(d_gate_low, "x")
+    sums["gate"] = ColumnSum(normed_low, d_gate_rel, "x")
     d_mixed_low = after(
         d_mixed.astype(BF16), *(sums[key].second() for key in ("up", "out", "gate"))
     )
@@ -906,9 +944,9 @@
     for step in ("second", "third"):
         for key in ("qk", "v"):
             getattr(sums[key], step)()
-    down_shard, up_shard, output_shard, gate_shard, qk_shard, v_shard = (
-        sums[key].finish() for key in ("down", "up", "out", "gate", "qk", "v")
-    )
+    down_shard, output_shard, gate_shard = finish([sums[k] for k in ("down", "out", "gate")])
+    (up_shard,) = finish([sums["up"]])
+    qk_shard, v_shard = finish([sums["qk"], sums["v"]])
     rate_grad = jnp.einsum("td,tf->df", normed_low, d_rate_low, preferred_element_type=F32)
     d_normed = dot_back(d_qk_rel, qk_full) + dot_back(d_v_rel, v_full)
     d_normed = d_normed + dot_back(d_gate_rel, gate_full)

time: 925 us -> 841 us (0.909)
  waiting for transfers between devices: 303 us -> 223 us
  starting transfers between devices: 110 us -> 60.2 us
  local copies, waits for them, and re-layouts: 151 us -> 165 us
  other arithmetic: 83.8 us -> 97.1 us
  between operations: 4.4 us -> 17.4 us
    ppermute x39 -> x6, waiting for transfers between devices: 106 us -> 15.1 us  [shifted(): lax.ppermute(value, 'fsdp', [(i, (i + step) % count) for i in range(count)])]
    ppermute x39 -> x6, starting transfers between devices: 62 us -> 12.6 us  [shifted(): lax.ppermute(value, 'fsdp', [(i, (i + step) % count) for i in range(count)])]
    reduce_scatter x0 -> x6, waiting for transfers between devices: none -> 37.6 us  [sum_blocks(): lax.psum_scatter(value.astype(BF16), 'fsdp', scatter_dimension=0, tiled=T...]
    convert_element_type x6 -> x11, local copies, waits for them, and re-layouts: 0.42 us -> 35.2 us  [the longest x3 21.5 us: spread(): return jnp.transpose(pieces, (2, 3, 0, 1, 4)).reshape(2 * pieces.shape[3]...]
    ppermute x57 -> x42, waiting for transfers between devices: 190 us -> 155 us  [swap(): return lax.ppermute(value, axis, [(0, 1), (1, 0)])]
    convert_element_type x11, other arithmetic: 11.6 us -> 24.8 us  [the longest x6 17.5 us: sum_blocks(): value.astype(BF16)]
    add x6 -> x0, other arithmetic: 11 us -> none  [the longest x5 7.92 us: own(): grad_dot(self.left, self.right[:, :width])]
    dot_general x24, matrix products: 57.9 us -> 68 us  [grad_dot(): return jnp.einsum('td,tf->df', left, right, preferred_element_type=F32)]
  transfers between devices with their start and end apart: 102 -> 62, of which waited for: 34 -> 25; matrix products, arithmetic and copies ran while one was open for 35% -> 41% of each run, Pallas kernels for 14% -> 15%
where the time goes in v3:
time: 841 us; the launch traced here: 831 us
  waiting for transfers between devices  223 us (27%)
  local copies, waits for them, and re-layouts  165 us (20%)
  matrix products  141 us (17%)
  Pallas kernels  127 us (15%)
  other arithmetic  97.1 us (12%)
  starting transfers between devices  60.2 us (7%)
  between operations  17.4 us (2%)
    ppermute x42, waiting for transfers between devices, swap(): return lax.ppermute(value, axis, [(0, 1), (1, 0)])  155 us
    pallas_call x7, Pallas kernels, call(): pl.pallas_call(kernel, out_shape=[jax.ShapeDtypeStruct(s, t) for s, t in...  127 us
    dot_general x24, matrix products, grad_dot(): return jnp.einsum('td,tf->df', left, right, preferred_element_type=F32)  68 us
    unnamed x355, local copies, waits for them, and re-layouts  50.2 us
    reduce_scatter x6, waiting for transfers between devices, sum_blocks(): lax.psum_scatter(value.astype(BF16), 'fsdp', scatter_dimension=0, tiled=T...  37.6 us
    ppermute x42, starting transfers between devices, swap(): return lax.ppermute(value, axis, [(0, 1), (1, 0)])  35.3 us
    convert_element_type x3, local copies, waits for them, and re-layouts, spread(): return jnp.transpose(pieces, (2, 3, 0, 1, 4)).reshape(2 * pieces.shape[3]...  21.5 us
    dot_general x8, matrix products, dot_columns(): parts = [jnp.dot(values, w, preferred_element_type=F32) for w in halves_of]  18.6 us
  transfers between devices with their start and end apart: 62, of which 25 were waited for; matrix products, arithmetic and copies ran while one was open for 41% of the time, Pallas kernels for 15%

profile of v3, /device:TPU:0, one launch (start us, length us, event | category | flops | bytes accessed | tf_op | source)
XLA Modules:
  0.0 830.9 jit_solution(6975890475659622103)
XLA Ops:
  13.6 3.2 fusion.238
  17.6 5.0 collective-permute-start.1
  25.1 3.4 collective-permute-start
  40.7 10.1 %collective-permute-done.2 = bf16[288,512]{1,0:T(8,128)(2,1)S(1)} collective-permute-done((bf16[288,512]{1,0:T(8,128)(2,1)}, bf16[288,512]{1,0:T(8,128)(2,1)S(1)}, u32[]{:S(2)}, u32[]{:S(2)}) %collective-permute-start.2) | collective-permute-done | bytes 294944 | tf_op jit(solution)/shard_map/ppermute | solution.py:560
  54.0 4.5 collective-permute-start.11
  85.3 7.4 concatenate.259
  93.7 5.0 collective-permute-done.11
  109.6 14.4 %collective-permute-done.5 = bf16[1024,512]{1,0:T(8,128)(2,1)S(1)} collective-permute-done((bf16[1024,512]{1,0:T(8,128)(2,1)S(1)}, bf16[1024,512]{1,0:T(8,128)(2,1)S(1)}, u32[]{:S(2)}, u32[]{:S(2)}) %collective-permute-start.5) | collective-permute-done | bytes 1048608 | tf_op jit(solution)/shard_map/ppermute | solution.py:522
  136.5 13.2 %collective-permute-done.13 = bf16[1024,256]{1,0:T(8,128)(2,1)S(1)} collective-permute-done((bf16[1024,256]{1,0:T(8,128)(2,1)S(1)}, bf16[1024,256]{1,0:T(8,128)(2,1)S(1)}, u32[]{:S(2)}, u32[]{:S(2)}) %collective-permute-start.13) | collective-permute-done | bytes 524320 | tf_op jit(solution)/shard_map/ppermute | solution.py:522
  149.7 9.3 %collective-permute-done.14 = bf16[2816,128]{1,0:T(8,128)(2,1)S(1)} collective-permute-done((bf16[2816,128]{1,0:T(8,128)(2,1)S(1)}, bf16[2816,128]{1,0:T(8,128)(2,1)S(1)}, u32[]{:S(2)}, u32[]{:S(2)}) %collective-permute-start.14) | collective-permute-done | bytes 720928 | tf_op jit(solution)/shard_map/ppermute | solution.py:522
  165.9 13.8 %shard_map.220.n_ref = bf16[384,4096]{1,0:T(8,128)(2,1)} custom-call(bf16[400,4096]{1,0:T(8,128)(2,1)} %copy-done.134, f32[4,4096]{1,0:T(4,128)} %bitcast.326, f32[384,8]{1,0:T(8,128)} %copy.239.mask_ref), custom_call_target="tpu_custom_call" | custom-call | flops 5000000000 | bytes 4194304 | tf_op jit(solution)/shard_map/pallas_call | solution.py:373
  181.0 27.2 %shard_map.221.inv_ref = f32[6,2,256,256]{3,2,1,0:T(8,128)} custom-call(bf16[384,4096]{1,0:T(8,128)(2,1)} %shard_map.220.n_ref, f32[6,2,256,8]{3,2,1,0:T(8,128)} %bitcast.290, f32[6,2,8,256]{3,2,1,0:T(8,128)} %bitcast.316), custom_call_target="tpu_custom_call" | custom-call | flops 10000000000 | bytes 4194304 | tf_op jit(solution)/shard_map/pallas_call | solution.py:373
  209.2 2.9 collective-permute-done.16
  214.0 10.6 %shard_map.222 = f32[8,128,256]{2,1,0:T(8,128)} custom-call(bf16[384,4096]{1,0:T(8,128)(2,1)} %shard_map.220.n_ref, f32[6,2,256,256]{3,2,1,0:T(8,128)} %shard_map.221.inv_ref, f32[6,2,256,8]{3,2,1,0:T(8,128)} %bitcast.291, bf16[8,128,256]{2,1,0:T(8,128)(2,1)} %broadcast_18_start_ref.2.start_ref), custom_call_target="tpu_custom_call" | custom-call | flops 4000000000 | bytes 4194304 | tf_op jit(solution)/shard_map/pallas_call | solution.py:373
  225.9 3.4 collective-permute-start.15
  234.5 6.6 collective-permute-done.15.start_ref
  241.9 13.7 %shard_map.223 = (bf16[384,2048]{1,0:T(8,128)(2,1)}, bf16[6,2,256,256]{3,2,1,0:T(8,128)(2,1)}, bf16[6,8,128,256]{3,2,1,0:T(8,128)(2,1)}) custom-call(bf16[384,4096]{1,0:T(8,128)(2,1)} %shard_map.220.n_ref, f32[6,2,256,256]{3,2,1,0:T(8,128)} %shard_map.221.inv_ref, f32[6,2,256,8]{3,2,1,0:T(8,128)} %bitcast.292, f32[6,2,8,256]{3,2,1,0:T(8,128)} %bitcast.317, ...), custom_call_target="tpu_custom_call" | custom-call | flops 4000000000 | bytes 4194304 | tf_op jit(solution)/shard_map/pallas_call | solution.py:373
  262.0 3.7 fusion.249
  274.8 4.7 multiply_reduce_fusion.4
  281.9 5.2 fusion.165
  287.1 8.3 fusion.250
  295.4 7.3 fusion.55
  302.7 3.3 convolution_convert_fusion.1
  314.5 4.1 add_convert_fusion
  318.9 5.7 convolution_convert_fusion
  325.2 3.1 fusion.251
  328.3 3.5 add_convert_fusion.5
  331.9 8.4 %multiply_reduce_fusion.2 = (f32[1024]{0:T(1024)}, f32[384]{0:T(512)S(1)}, f32[384,1024]{1,0:T(8,128)S(1)}) fusion(f32[384,1024]{1,0:T(8,128)S(1)} %copy-done.14, f32[384]{0:T(512)S(1)} %copy-done.123, f32[1024]{0:T(1024)S(1)} %bitcast.323, bf16[384,5632]{1,0:T(8,128)(2,1)S(1)} %add_convert_fusion, bf16[1024,5632]{1,0:T(8,128)(2,1)} %all-gather.5.cloned.1.call-done), kind=kOutput, calls=%fused_computation.131 | convolution fusion | flops 4431542784 | bytes 19016704 | tf_op jit(solution)/shard_map/tf,df->td/dot_general | solution.py:923
  351.6 6.1 multiply_reduce_fusion
  360.7 3.1 fusion.252
  377.7 3.8 fusion.26
  386.0 3.1 fusion.159
  389.1 3.9 fusion.158
  393.1 13.3 %collective-permute-done.25 = bf16[2816,256]{1,0:T(8,128)(2,1)} collective-permute-done((bf16[2816,256]{1,0:T(8,128)(2,1)}, bf16[2816,256]{1,0:T(8,128)(2,1)}, u32[]{:S(2)}, u32[]{:S(2)}) %collective-permute-start.25) | collective-permute-done | bytes 1441824 | tf_op jit(solution)/shard_map/ppermute | solution.py:522
  406.4 3.0 add_convert_fusion.12
  413.3 3.0 add_convert_fusion.9
  416.6 5.9 add_convert_fusion.2
  422.5 3.9 collective-permute-done.41
  428.7 13.6 %shard_map.224 = f32[8,128,256]{2,1,0:T(8,128)} custom-call(bf16[384,4096]{1,0:T(8,128)(2,1)} %shard_map.220.n_ref, f32[6,2,256,256]{3,2,1,0:T(8,128)} %shard_map.221.inv_ref, f32[6,2,256,8]{3,2,1,0:T(8,128)} %bitcast.293, f32[6,2,8,256]{3,2,1,0:T(8,128)} %bitcast.318, bf16[384,2048]{1,0:T(8,128)(2,1)} %get-tuple-element.52.dout_ref, ...), custom_call_target="tpu_custom_call" | custom-call | flops 4000000000 | bytes 4194304 | tf_op jit(solution)/shard_map/pallas_call | solution.py:373
  450.1 3.1 add_convert_fusion.20
  453.8 4.8 collective-permute-done.24.start_ref
  458.6 25.4 %shard_map.225 = (f32[384,4096]{1,0:T(8,128)}, f32[6,2,256,8]{3,2,1,0:T(8,128)}, f32[6,2,8,256]{3,2,1,0:T(8,128)}) custom-call(bf16[384,4096]{1,0:T(8,128)(2,1)} %shard_map.220.n_ref, f32[6,2,256,256]{3,2,1,0:T(8,128)} %shard_map.221.inv_ref, f32[6,2,256,8]{3,2,1,0:T(8,128)} %bitcast.294, f32[6,2,8,256]{3,2,1,0:T(8,128)} %bitcast.319, ...), custom_call_target="tpu_custom_call" | custom-call | flops 10000000000 | bytes 4194304 | tf_op jit(solution)/shard_map/pallas_call | solution.py:373
  486.5 3.4 slice_reduce_fusion.2
  493.0 28.4 %collective-permute-done.40 = bf16[2048,128]{1,0:T(8,128)(2,1)S(1)} collective-permute-done((bf16[2048,128]{1,0:T(8,128)(2,1)}, bf16[2048,128]{1,0:T(8,128)(2,1)S(1)}, u32[]{:S(2)}, u32[]{:S(2)}) %collective-permute-start.40) | collective-permute-done | bytes 524320 | tf_op jit(solution)/shard_map/ppermute | solution.py:522
  529.9 18.2 %reduce-scatter.13.cloned.1.call-done = bf16[512,128]{1,0:T(8,128)(2,1)} async-done(((bf16[2048,128]{1,0:T(8,128)(2,1)}), bf16[512,128]{1,0:T(8,128)(2,1)}) %reduce-scatter.13.cloned.1.call-update) | async-done | bytes 131088 | tf_op jit(solution)/shard_map/reduce_scatter | solution.py:572
  550.6 4.3 add_convert_fusion.4
  554.8 23.1 %shard_map.226 = (bf16[400,4096]{1,0:T(8,128)(2,1)}, f32[4,4096]{1,0:T(4,128)}) custom-call(bf16[400,4096]{1,0:T(8,128)(2,1)} %copy-done.134, f32[4,4096]{1,0:T(4,128)} %bitcast.327, f32[384,8]{1,0:T(8,128)} %copy.239.mask_ref, f32[384,4096]{1,0:T(8,128)} %get-tuple-element.57.dn_ref), custom_call_target="tpu_custom_call" | custom-call | flops 4000000000 | bytes 4194304 | tf_op jit(solution)/shard_map/pallas_call | solution.py:373
  602.8 5.1 fusion.16
  616.2 4.8 add_convert_fusion.3
  624.1 3.5 fusion.18
  631.8 18.2 %collective-permute-done.47 = f32[280,128]{1,0:T(8,128)S(1)} collective-permute-done((f32[280,128]{1,0:T(8,128)S(1)}, f32[280,128]{1,0:T(8,128)S(1)}, u32[]{:S(2)}, u32[]{:S(2)}) %collective-permute-start.47) | collective-permute-done | bytes 143392 | tf_op jit(solution)/shard_map/ppermute | solution.py:522
  650.1 3.0 add_convert_fusion.7
  663.7 3.2 collective-permute-done.49
  669.8 17.3 %collective-permute-done.35 = bf16[1024,256]{1,0:T(8,128)(2,1)} collective-permute-done((bf16[1024,256]{1,0:T(8,128)(2,1)}, bf16[1024,256]{1,0:T(8,128)(2,1)}, u32[]{:S(2)}, u32[]{:S(2)}) %collective-permute-start.35) | collective-permute-done | bytes 524320 | tf_op jit(solution)/shard_map/ppermute | solution.py:522
  696.5 6.2 collective-permute-done.32
  713.1 19.3 %reduce-scatter.7.cloned.1.call-done = bf16[256,256]{1,0:T(8,128)(2,1)} async-done(((bf16[1024,256]{1,0:T(8,128)(2,1)}), bf16[256,256]{1,0:T(8,128)(2,1)}) %reduce-scatter.7.cloned.1.call-update) | async-done | bytes 131088 | tf_op jit(solution)/shard_map/reduce_scatter | solution.py:572
  737.0 5.6 collective-permute-done.36
  749.1 7.6 collective-permute-done.37
  758.2 9.2 %collective-permute-done.52 = bf16[2,1408,128]{2,1,0:T(8,128)(2,1)S(1)} collective-permute-done((bf16[2,1408,128]{2,1,0:T(8,128)(2,1)S(1)}, bf16[2,1408,128]{2,1,0:T(8,128)(2,1)S(1)}, u32[]{:S(2)}, u32[]{:S(2)}) %collective-permute-start.52) | collective-permute-done | bytes 720928 | tf_op jit(solution)/shard_map/ppermute | solution.py:522
  795.8 3.4 maximum_convert_fusion
  799.2 2.9 maximum_select_fusion.1
  802.1 3.4 copy.271
  805.5 9.7 %copy.272 = f32[2,128,2,2,1408]{4,3,2,1,0:T(2,128)} copy(f32[2,128,2,2,1408]{1,4,0,3,2:T(8,128)} %bitcast.252) | data formatting | bytes 11534336 | tf_op jit(solution)/shard_map/convert_element_type | solution.py:748
  815.2 8.4 %reshape.558 = f32[256,5632]{1,0:T(8,128)} reshape(f32[2,128,2,2,1408]{4,3,2,1,0:T(2,128)} %copy.272) | data formatting | bytes 11534336 | tf_op jit(solution)/shard_map/convert_element_type | solution.py:748
  (732 shorter events, 298.2 us)
Async XLA Ops:
  7.2 267.6 %all-gather.3.cloned.1.call-start = ((), (), s32[]{:S(2)}) async-start(), calls=%async_computation.6 | async-start | bytes 4325376 | tf_op jit(solution)/shard_map/all_gather | solution.py:588
  9.0 278.1 %all-gather.5.cloned.1.call-start = ((), (), s32[]{:S(2)}) async-start(), calls=%async_computation.7 | async-start | bytes 11894784 | tf_op jit(solution)/shard_map/all_gather | solution.py:588
  17.6 23.0 %collective-permute-start.1 = (bf16[288,512]{1,0:T(8,128)(2,1)}, bf16[288,512]{1,0:T(8,128)(2,1)S(1)}, u32[]{:S(2)}, u32[]{:S(2)}) collective-permute-start(bf16[288,512]{1,0:T(8,128)(2,1)} %pad_maximum_fusion.13), channel_id=1, source_target_pairs={{0,6},{2,0},{4,2},{6,4},{1,7},{3,1},{5,3},{7,5},{8,14},{10,8},{12,... | collective-permute-start | bytes 884744 | tf_op jit(solution)/shard_map/ppermute | solution.py:560
  22.7 28.1 %collective-permute-start.2 = (bf16[288,512]{1,0:T(8,128)(2,1)}, bf16[288,512]{1,0:T(8,128)(2,1)S(1)}, u32[]{:S(2)}, u32[]{:S(2)}) collective-permute-start(bf16[288,512]{1,0:T(8,128)(2,1)} %pad_maximum_fusion.13), channel_id=1, source_target_pairs={{0,4},{2,6},{4,0},{6,2},{1,5},{3,7},{5,1},{7,3},{8,12},{10,14},{12... | collective-permute-start | bytes 884744 | tf_op jit(solution)/shard_map/ppermute | solution.py:560
  22.7 28.1 %collective-permute-start.3 = (bf16[288,512]{1,0:T(8,128)(2,1)}, bf16[288,512]{1,0:T(8,128)(2,1)}, u32[]{:S(2)}, u32[]{:S(2)}) collective-permute-start(bf16[288,512]{1,0:T(8,128)(2,1)} %pad_maximum_fusion.13), channel_id=1, source_target_pairs={{0,2},{2,4},{4,6},{6,0},{1,3},{3,5},{5,7},{7,1},{8,10},{10,12},{12... | collective-permute-start | bytes 884744 | tf_op jit(solution)/shard_map/ppermute | solution.py:560
  25.1 15.4 %collective-permute-start = (bf16[16,1024]{1,0:T(8,128)(2,1)}, bf16[16,1024]{1,0:T(8,128)(2,1)S(1)}, u32[]{:S(2)}, u32[]{:S(2)}) collective-permute-start(bf16[16,1024]{1,0:T(8,128)(2,1)} %slice.375), channel_id=1, source_target_pairs={{0,1},{2,3},{4,5},{6,7},{8,9},{10,11},{12,13},{14,15},{16,17},{18,... | collective-permute-start | bytes 98312 | tf_op jit(solution)/shard_map/ppermute | solution.py:885
  29.3 499.7 %reduce-scatter.15.cloned.1.call-start = ((), (), s32[]{:S(2)}) async-start(), calls=%async_computation.12 | async-start | bytes 655360 | tf_op jit(solution)/shard_map/reduce_scatter | solution.py:572
  54.0 38.6 %collective-permute-start.10 = (bf16[1216,128]{1,0:T(8,128)(2,1)}, bf16[1216,128]{1,0:T(8,128)(2,1)}, u32[]{:S(2)}, u32[]{:S(2)}) collective-permute-start(bf16[1216,128]{1,0:T(8,128)(2,1)} %pad_maximum_fusion.12), channel_id=1, source_target_pairs={{0,6},{2,0},{4,2},{6,4},{1,7},{3,1},{5,3},{7,5},{8,14},{10,8},{12,... | collective-permute-start | bytes 933896 | tf_op jit(solution)/shard_map/ppermute | solution.py:560
  54.0 44.6 %collective-permute-start.11 = (bf16[1216,128]{1,0:T(8,128)(2,1)}, bf16[1216,128]{1,0:T(8,128)(2,1)}, u32[]{:S(2)}, u32[]{:S(2)}) collective-permute-start(bf16[1216,128]{1,0:T(8,128)(2,1)} %pad_maximum_fusion.12), channel_id=1, source_target_pairs={{0,4},{2,6},{4,0},{6,2},{1,5},{3,7},{5,1},{7,3},{8,12},{10,14},{12... | collective-permute-start | bytes 933896 | tf_op jit(solution)/shard_map/ppermute | solution.py:560
  58.6 41.1 %collective-permute-start.12 = (bf16[1216,128]{1,0:T(8,128)(2,1)}, bf16[1216,128]{1,0:T(8,128)(2,1)}, u32[]{:S(2)}, u32[]{:S(2)}) collective-permute-start(bf16[1216,128]{1,0:T(8,128)(2,1)} %pad_maximum_fusion.12), channel_id=1, source_target_pairs={{0,2},{2,4},{4,6},{6,0},{1,3},{3,5},{5,7},{7,1},{8,10},{10,12},{12... | collective-permute-start | bytes 933896 | tf_op jit(solution)/shard_map/ppermute | solution.py:560
  66.2 34.5 %collective-permute-start.4 = (bf16[1024,256]{1,0:T(8,128)(2,1)S(1)}, bf16[1024,256]{1,0:T(8,128)(2,1)}, u32[]{:S(2)}, u32[]{:S(2)}) collective-permute-start(bf16[1024,256]{1,0:T(8,128)(2,1)S(1)} %get-tuple-element.192), channel_id=1, source_target_pairs={{0,1},{1,0},{2,3},{3,2},{4,5},{5,4},{6,7},{7,6},{8,9},{9,8},{10,11... | collective-permute-start | bytes 1572872 | tf_op jit(solution)/shard_map/ppermute | solution.py:522
  67.6 37.6 %collective-permute-start.7 = (bf16[1024,256]{1,0:T(8,128)(2,1)S(1)}, bf16[1024,256]{1,0:T(8,128)(2,1)}, u32[]{:S(2)}, u32[]{:S(2)}) collective-permute-start(bf16[1024,256]{1,0:T(8,128)(2,1)S(1)} %get-tuple-element.191), channel_id=1, source_target_pairs={{0,16},{16,0},{1,17},{17,1},{2,18},{18,2},{3,19},{19,3},{4,20},{20... | collective-permute-start | bytes 1572872 | tf_op jit(solution)/shard_map/ppermute | solution.py:522
  83.1 188.9 %copy-start.113 = (f32[1,2,8,128]{3,1,2,0:T(2,128)}, f32[1,2,8,128]{3,1,2,0:T(2,128)S(1)}, u32[]{:S(2)}) copy-start(f32[1,2,8,128]{3,1,2,0:T(2,128)S(1)} %copy.293) | copy-start | bytes 24580
  83.2 257.1 %copy-start.115 = (f32[1,2,4,128]{3,1,2,0:T(2,128)}, f32[1,2,4,128]{3,1,2,0:T(2,128)S(1)}, u32[]{:S(2)}) copy-start(f32[1,2,4,128]{3,1,2,0:T(2,128)S(1)} %copy.294) | copy-start | bytes 12292
  101.8 22.2 %collective-permute-start.5 = (bf16[1024,512]{1,0:T(8,128)(2,1)S(1)}, bf16[1024,512]{1,0:T(8,128)(2,1)S(1)}, u32[]{:S(2)}, u32[]{:S(2)}) collective-permute-start(bf16[1024,512]{1,0:T(8,128)(2,1)S(1)} %pad_maximum_fusion.2), channel_id=1, source_target_pairs={{0,16},{16,0},{1,17},{17,1},{2,18},{18,2},{3,19},{19,3},{4,20},{20... | collective-permute-start | bytes 3145736 | tf_op jit(solution)/shard_map/ppermute | solution.py:522
  106.3 22.4 %collective-permute-start.8 = (bf16[1024,512]{1,0:T(8,128)(2,1)S(1)}, bf16[1024,512]{1,0:T(8,128)(2,1)S(1)}, u32[]{:S(2)}, u32[]{:S(2)}) collective-permute-start(bf16[1024,512]{1,0:T(8,128)(2,1)S(1)} %pad_maximum_fusion.3), channel_id=1, source_target_pairs={{0,1},{1,0},{2,3},{3,2},{4,5},{5,4},{6,7},{7,6},{8,9},{9,8},{10,11... | collective-permute-start | bytes 3145736 | tf_op jit(solution)/shard_map/ppermute | solution.py:522
  125.7 33.5 %collective-permute-start.6 = (bf16[1024,1024]{1,0:T(8,128)(2,1)S(1)}, bf16[1024,1024]{1,0:T(8,128)(2,1)S(1)}, u32[]{:S(2)}, u32[]{:S(2)}) collective-permute-start(bf16[1024,1024]{1,0:T(8,128)(2,1)S(1)} %pad_maximum_fusion), channel_id=1, source_target_pairs={{0,8},{8,0},{1,9},{9,1},{2,10},{10,2},{3,11},{11,3},{4,12},{12,4},... | collective-permute-start | bytes 6291464 | tf_op jit(solution)/shard_map/ppermute | solution.py:522
  130.4 31.3 %collective-permute-start.9 = (bf16[1024,1024]{1,0:T(8,128)(2,1)S(1)}, bf16[1024,1024]{1,0:T(8,128)(2,1)S(1)}, u32[]{:S(2)}, u32[]{:S(2)}) collective-permute-start(bf16[1024,1024]{1,0:T(8,128)(2,1)S(1)} %pad_maximum_fusion.1), channel_id=1, source_target_pairs={{0,8},{8,0},{1,9},{9,1},{2,10},{10,2},{3,11},{11,3},{4,12},{12,4},... | collective-permute-start | bytes 6291464 | tf_op jit(solution)/shard_map/ppermute | solution.py:522
  130.5 19.2 %collective-permute-start.13 = (bf16[1024,256]{1,0:T(8,128)(2,1)S(1)}, bf16[1024,256]{1,0:T(8,128)(2,1)S(1)}, u32[]{:S(2)}, u32[]{:S(2)}) collective-permute-start(bf16[1024,256]{1,0:T(8,128)(2,1)S(1)} %bitcast.286), channel_id=1, source_target_pairs={{0,1},{1,0},{2,3},{3,2},{4,5},{5,4},{6,7},{7,6},{8,9},{9,8},{10,11... | collective-permute-start | bytes 1572872 | tf_op jit(solution)/shard_map/ppermute | solution.py:522
  131.9 27.2 %collective-permute-start.14 = (bf16[2816,128]{1,0:T(8,128)(2,1)S(1)}, bf16[2816,128]{1,0:T(8,128)(2,1)S(1)}, u32[]{:S(2)}, u32[]{:S(2)}) collective-permute-start(bf16[2816,128]{1,0:T(8,128)(2,1)S(1)} %bitcast.281), channel_id=1, source_target_pairs={{0,16},{16,0},{1,17},{17,1},{2,18},{18,2},{3,19},{19,3},{4,20},{20... | collective-permute-start | bytes 2162696 | tf_op jit(solution)/shard_map/ppermute | solution.py:522
  179.8 32.3 %collective-permute-start.16 = (bf16[1024,512]{1,0:T(8,128)(2,1)S(1)}, bf16[1024,512]{1,0:T(8,128)(2,1)S(1)}, u32[]{:S(2)}, u32[]{:S(2)}) collective-permute-start(bf16[1024,512]{1,0:T(8,128)(2,1)S(1)} %constant_dynamic-update-slice_fusion.14), channel_id=1, source_target_pairs={{0,16},{16,0},{1,17},{17,1},{2,18},{18,2},{3,19},{19,3},{4,20},{20... | collective-permute-start | bytes 3145736 | tf_op jit(solution)/shard_map/ppermute | solution.py:522
  179.8 53.3 %collective-permute-start.17 = (bf16[2816,256]{1,0:T(8,128)(2,1)S(1)}, bf16[2816,256]{1,0:T(8,128)(2,1)S(1)}, u32[]{:S(2)}, u32[]{:S(2)}) collective-permute-start(bf16[2816,256]{1,0:T(8,128)(2,1)S(1)} %constant_dynamic-update-slice_fusion.16), channel_id=1, source_target_pairs={{0,1},{1,0},{2,3},{3,2},{4,5},{5,4},{6,7},{7,6},{8,9},{9,8},{10,11... | collective-permute-start | bytes 4325384 | tf_op jit(solution)/shard_map/ppermute | solution.py:522
  213.1 48.8 %collective-permute-start.18 = (bf16[1024,1024]{1,0:T(8,128)(2,1)}, bf16[1024,1024]{1,0:T(8,128)(2,1)}, u32[]{:S(2)}, u32[]{:S(2)}) collective-permute-start(bf16[1024,1024]{1,0:T(8,128)(2,1)} %constant_dynamic-update-slice_fusion.18), channel_id=1, source_target_pairs={{0,8},{8,0},{1,9},{9,1},{2,10},{10,2},{3,11},{11,3},{4,12},{12,4},... | collective-permute-start | bytes 6291464 | tf_op jit(solution)/shard_map/ppermute | solution.py:522
  225.9 15.2 %collective-permute-start.15 = (bf16[8,128,256]{2,1,0:T(8,128)(2,1)S(1)}, bf16[8,128,256]{2,1,0:T(8,128)(2,1)S(1)}, u32[]{:S(2)}, u32[]{:S(2)}) collective-permute-start(bf16[8,128,256]{2,1,0:T(8,128)(2,1)S(1)} %convert_element_type.443), channel_id=1, source_target_pairs={{0,1},{2,3},{4,5},{6,7},{8,9},{10,11},{12,13},{14,15},{16,17},{18,... | collective-permute-start | bytes 1572872 | tf_op jit(solution)/shard_map/ppermute | solution.py:442
  234.3 47.6 %collective-permute-start.19 = (bf16[2816,512]{1,0:T(8,128)(2,1)}, bf16[2816,512]{1,0:T(8,128)(2,1)}, u32[]{:S(2)}, u32[]{:S(2)}) collective-permute-start(bf16[2816,512]{1,0:T(8,128)(2,1)} %constant_dynamic-update-slice_fusion.20), channel_id=1, source_target_pairs={{0,8},{8,0},{1,9},{9,1},{2,10},{10,2},{3,11},{11,3},{4,12},{12,4},... | collective-permute-start | bytes 8650760 | tf_op jit(solution)/shard_map/ppermute | solution.py:522
  306.1 22.2 %collective-permute-start.20 = (bf16[2816,512]{1,0:T(8,128)(2,1)}, bf16[2816,512]{1,0:T(8,128)(2,1)}, u32[]{:S(2)}, u32[]{:S(2)}) collective-permute-start(bf16[2816,512]{1,0:T(8,128)(2,1)} %convolution_convert_fusion.1), channel_id=1, source_target_pairs={{0,8},{8,0},{1,9},{9,1},{2,10},{10,2},{3,11},{11,3},{4,12},{12,4},... | collective-permute-start | bytes 8650760 | tf_op jit(solution)/shard_map/ppermute | solution.py:522
  324.6 92.1 %collective-permute-start.21 = (bf16[1024,2816]{1,0:T(8,128)(2,1)}, bf16[1024,2816]{1,0:T(8,128)(2,1)}, u32[]{:S(2)}, u32[]{:S(2)}) collective-permute-start(bf16[1024,2816]{1,0:T(8,128)(2,1)} %convolution_convert_fusion), channel_id=1, source_target_pairs={{0,8},{8,0},{1,9},{9,1},{2,10},{10,2},{3,11},{11,3},{4,12},{12,4},... | collective-permute-start | bytes 17301512 | tf_op jit(solution)/shard_map/ppermute | solution.py:522
  360.2 21.3 %collective-permute-start.23 = (bf16[1024,1024]{1,0:T(8,128)(2,1)S(1)}, bf16[1024,1024]{1,0:T(8,128)(2,1)S(1)}, u32[]{:S(2)}, u32[]{:S(2)}) collective-permute-start(bf16[1024,1024]{1,0:T(8,128)(2,1)S(1)} %convolution_convert_fusion.5), channel_id=1, source_target_pairs={{0,8},{8,0},{1,9},{9,1},{2,10},{10,2},{3,11},{11,3},{4,12},{12,4},... | collective-permute-start | bytes 6291464 | tf_op jit(solution)/shard_map/ppermute | solution.py:522
  371.8 34.6 %collective-permute-start.25 = (bf16[2816,256]{1,0:T(8,128)(2,1)}, bf16[2816,256]{1,0:T(8,128)(2,1)}, u32[]{:S(2)}, u32[]{:S(2)}) collective-permute-start(bf16[2816,256]{1,0:T(8,128)(2,1)} %add_convert_fusion.5), channel_id=1, source_target_pairs={{0,1},{1,0},{2,3},{3,2},{4,5},{5,4},{6,7},{7,6},{8,9},{9,8},{10,11... | collective-permute-start | bytes 4325384 | tf_op jit(solution)/shard_map/ppermute | solution.py:522
  377.7 35.6 %collective-permute-start.22 = (bf16[2048,512]{1,0:T(8,128)(2,1)}, bf16[2048,512]{1,0:T(8,128)(2,1)}, u32[]{:S(2)}, u32[]{:S(2)}) collective-permute-start(bf16[2048,512]{1,0:T(8,128)(2,1)} %convolution_convert_fusion.2), channel_id=1, source_target_pairs={{0,8},{8,0},{1,9},{9,1},{2,10},{10,2},{3,11},{11,3},{4,12},{12,4},... | collective-permute-start | bytes 6291464 | tf_op jit(solution)/shard_map/ppermute | solution.py:522
  383.3 26.6 %collective-permute-start.28 = (bf16[1024,512]{1,0:T(8,128)(2,1)}, bf16[1024,512]{1,0:T(8,128)(2,1)}, u32[]{:S(2)}, u32[]{:S(2)}) collective-permute-start(bf16[1024,512]{1,0:T(8,128)(2,1)} %add_convert_fusion.8), channel_id=1, source_target_pairs={{0,16},{16,0},{1,17},{17,1},{2,18},{18,2},{3,19},{19,3},{4,20},{20... | collective-permute-start | bytes 3145736 | tf_op jit(solution)/shard_map/ppermute | solution.py:522
  409.4 36.3 %collective-permute-start.39 = (bf16[2816,128]{1,0:T(8,128)(2,1)}, bf16[2816,128]{1,0:T(8,128)(2,1)}, u32[]{:S(2)}, u32[]{:S(2)}) collective-permute-start(bf16[2816,128]{1,0:T(8,128)(2,1)} %add_convert_fusion.12), channel_id=1, source_target_pairs={{0,16},{16,0},{1,17},{17,1},{2,18},{18,2},{3,19},{19,3},{4,20},{20... | collective-permute-start | bytes 2162696 | tf_op jit(solution)/shard_map/ppermute | solution.py:522
  411.5 14.9 %collective-permute-start.41 = (bf16[1024,256]{1,0:T(8,128)(2,1)S(1)}, bf16[1024,256]{1,0:T(8,128)(2,1)S(1)}, u32[]{:S(2)}, u32[]{:S(2)}) collective-permute-start(bf16[1024,256]{1,0:T(8,128)(2,1)S(1)} %add_convert_fusion.19), channel_id=1, source_target_pairs={{0,1},{1,0},{2,3},{3,2},{4,5},{5,4},{6,7},{7,6},{8,9},{9,8},{10,11... | collective-permute-start | bytes 1572872 | tf_op jit(solution)/shard_map/ppermute | solution.py:522
  416.4 33.8 %collective-permute-start.27 = (bf16[2048,256]{1,0:T(8,128)(2,1)}, bf16[2048,256]{1,0:T(8,128)(2,1)}, u32[]{:S(2)}, u32[]{:S(2)}) collective-permute-start(bf16[2048,256]{1,0:T(8,128)(2,1)} %add_convert_fusion.9), channel_id=1, source_target_pairs={{0,1},{1,0},{2,3},{3,2},{4,5},{5,4},{6,7},{7,6},{8,9},{9,8},{10,11... | collective-permute-start | bytes 3145736 | tf_op jit(solution)/shard_map/ppermute | solution.py:522
  428.6 101.3 %reduce-scatter.11.cloned.1.call-start = ((), (), s32[]{:S(2)}) async-start(), calls=%async_computation.10 | async-start | bytes 901120 | tf_op jit(solution)/shard_map/reduce_scatter | solution.py:572
  444.4 14.2 %collective-permute-start.24 = (bf16[8,128,256]{2,1,0:T(8,128)(2,1)}, bf16[8,128,256]{2,1,0:T(8,128)(2,1)}, u32[]{:S(2)}, u32[]{:S(2)}) collective-permute-start(bf16[8,128,256]{2,1,0:T(8,128)(2,1)} %convert_element_type.470), channel_id=1, source_target_pairs={{1,0},{3,2},{5,4},{7,6},{9,8},{11,10},{13,12},{15,14},{17,16},{19,... | collective-permute-start | bytes 1572872 | tf_op jit(solution)/shard_map/ppermute | solution.py:462
  448.5 99.6 %reduce-scatter.13.cloned.1.call-start = ((), (), s32[]{:S(2)}) async-start(), calls=%async_computation.11 | async-start | bytes 655360 | tf_op jit(solution)/shard_map/reduce_scatter | solution.py:572
  448.6 102.0 %collective-permute-start.26 = (bf16[1024,1408]{1,0:T(8,128)(2,1)}, bf16[1024,1408]{1,0:T(8,128)(2,1)}, u32[]{:S(2)}, u32[]{:S(2)}) collective-permute-start(bf16[1024,1408]{1,0:T(8,128)(2,1)} %add_convert_fusion.2), channel_id=1, source_target_pairs={{0,16},{16,0},{1,17},{17,1},{2,18},{18,2},{3,19},{19,3},{4,20},{20... | collective-permute-start | bytes 8650760 | tf_op jit(solution)/shard_map/ppermute | solution.py:522
  453.3 68.2 %collective-permute-start.40 = (bf16[2048,128]{1,0:T(8,128)(2,1)}, bf16[2048,128]{1,0:T(8,128)(2,1)S(1)}, u32[]{:S(2)}, u32[]{:S(2)}) collective-permute-start(bf16[2048,128]{1,0:T(8,128)(2,1)} %add_convert_fusion.20), channel_id=1, source_target_pairs={{0,16},{16,0},{1,17},{17,1},{2,18},{18,2},{3,19},{19,3},{4,20},{20... | collective-permute-start | bytes 1572872 | tf_op jit(solution)/shard_map/ppermute | solution.py:522
  524.0 181.3 %reduce-scatter.17.cloned.1.call-start = ((), (), s32[]{:S(2)}) async-start(), calls=%async_computation.13 | async-start | bytes 1802240 | tf_op jit(solution)/shard_map/reduce_scatter | solution.py:572
  549.1 31.1 %collective-permute-start.42 = (bf16[1,1728,128]{2,1,0:T(8,128)(2,1)S(1)}, bf16[1,1728,128]{2,1,0:T(8,128)(2,1)S(1)}, u32[]{:S(2)}, u32[]{:S(2)}) collective-permute-start(bf16[1,1728,128]{2,1,0:T(8,128)(2,1)S(1)} %maximum_bitcast_fusion), channel_id=1, source_target_pairs={{0,1},{1,0},{2,3},{3,2},{4,5},{5,4},{6,7},{7,6},{8,9},{9,8},{10,11... | collective-permute-start | bytes 1327112 | tf_op jit(solution)/shard_map/ppermute | solution.py:522
  578.9 8.2 collective-permute-start.29
  581.2 80.1 %collective-permute-start.43 = (bf16[2,1728,128]{2,1,0:T(8,128)(2,1)}, bf16[2,1728,128]{2,1,0:T(8,128)(2,1)}, u32[]{:S(2)}, u32[]{:S(2)}) collective-permute-start(bf16[2,1728,128]{2,1,0:T(8,128)(2,1)} %maximum_select_fusion.6), channel_id=1, source_target_pairs={{0,16},{16,0},{1,17},{17,1},{2,18},{18,2},{3,19},{19,3},{4,20},{20... | collective-permute-start | bytes 2654216 | tf_op jit(solution)/shard_map/ppermute | solution.py:522
  582.7 33.5 %collective-permute-start.50 = (bf16[512,1408]{1,0:T(8,128)(2,1)}, bf16[512,1408]{1,0:T(8,128)(2,1)}, u32[]{:S(2)}, u32[]{:S(2)}) collective-permute-start(bf16[512,1408]{1,0:T(8,128)(2,1)} %add_convert_fusion.4), channel_id=1, source_target_pairs={{0,1},{1,0},{2,3},{3,2},{4,5},{5,4},{6,7},{7,6},{8,9},{9,8},{10,11... | collective-permute-start | bytes 4325384 | tf_op jit(solution)/shard_map/ppermute | solution.py:522
  592.6 28.8 %collective-permute-start.33 = (bf16[1024,1024]{1,0:T(8,128)(2,1)}, bf16[1024,1024]{1,0:T(8,128)(2,1)}, u32[]{:S(2)}, u32[]{:S(2)}) collective-permute-start(bf16[1024,1024]{1,0:T(8,128)(2,1)} %convolution_convert_fusion.3), channel_id=1, source_target_pairs={{0,8},{8,0},{1,9},{9,1},{2,10},{10,2},{3,11},{11,3},{4,12},{12,4},... | collective-permute-start | bytes 6291464 | tf_op jit(solution)/shard_map/ppermute | solution.py:522
  595.2 54.9 %collective-permute-start.30 = (bf16[1024,1024]{1,0:T(8,128)(2,1)}, bf16[1024,1024]{1,0:T(8,128)(2,1)}, u32[]{:S(2)}, u32[]{:S(2)}) collective-permute-start(bf16[1024,1024]{1,0:T(8,128)(2,1)} %convolution_convert_fusion.4), channel_id=1, source_target_pairs={{0,8},{8,0},{1,9},{9,1},{2,10},{10,2},{3,11},{11,3},{4,12},{12,4},... | collective-permute-start | bytes 6291464 | tf_op jit(solution)/shard_map/ppermute | solution.py:522
  608.8 1.6 collective-permute-start.45
  611.8 15.9 %collective-permute-start.46 = (f32[280,128]{1,0:T(8,128)}, f32[280,128]{1,0:T(8,128)}, u32[]{:S(2)}, u32[]{:S(2)}) collective-permute-start(f32[280,128]{1,0:T(8,128)} %fusion.232), channel_id=1, source_target_pairs={{0,16},{16,0},{1,17},{17,1},{2,18},{18,2},{3,19},{19,3},{4,20},{20... | collective-permute-start | bytes 430088 | tf_op jit(solution)/shard_map/ppermute | solution.py:522
  621.0 91.2 %reduce-scatter.9.cloned.1.call-start = ((), (), s32[]{:S(2)}) async-start(), calls=%async_computation.9 | async-start | bytes 655360 | tf_op jit(solution)/shard_map/reduce_scatter | solution.py:572
  623.7 29.5 %collective-permute-start.34 = (bf16[1024,512]{1,0:T(8,128)(2,1)S(1)}, bf16[1024,512]{1,0:T(8,128)(2,1)S(1)}, u32[]{:S(2)}, u32[]{:S(2)}) collective-permute-start(bf16[1024,512]{1,0:T(8,128)(2,1)S(1)} %add_convert_fusion.6), channel_id=1, source_target_pairs={{0,1},{1,0},{2,3},{3,2},{4,5},{5,4},{6,7},{7,6},{8,9},{9,8},{10,11... | collective-permute-start | bytes 3145736 | tf_op jit(solution)/shard_map/ppermute | solution.py:522
  628.6 21.4 %collective-permute-start.47 = (f32[280,128]{1,0:T(8,128)S(1)}, f32[280,128]{1,0:T(8,128)S(1)}, u32[]{:S(2)}, u32[]{:S(2)}) collective-permute-start(f32[280,128]{1,0:T(8,128)S(1)} %fusion.320), channel_id=1, source_target_pairs={{0,1},{1,0},{2,3},{3,2},{4,5},{5,4},{6,7},{7,6},{8,9},{9,8},{10,11... | collective-permute-start | bytes 430088 | tf_op jit(solution)/shard_map/ppermute | solution.py:522
  650.0 9.3 %collective-permute-start.48 = (f32[280,128]{1,0:T(8,128)S(1)}, f32[280,128]{1,0:T(8,128)S(1)}, u32[]{:S(2)}, u32[]{:S(2)}) collective-permute-start(f32[280,128]{1,0:T(8,128)S(1)} %add.787), channel_id=1, source_target_pairs={{0,2},{2,0},{4,6},{6,4},{1,3},{3,1},{5,7},{7,5},{8,10},{10,8},{12,... | collective-permute-start | bytes 430088 | tf_op jit(solution)/shard_map/ppermute | solution.py:785
  653.1 36.7 %collective-permute-start.31 = (bf16[1024,512]{1,0:T(8,128)(2,1)}, bf16[1024,512]{1,0:T(8,128)(2,1)}, u32[]{:S(2)}, u32[]{:S(2)}) collective-permute-start(bf16[1024,512]{1,0:T(8,128)(2,1)} %add_convert_fusion.7), channel_id=1, source_target_pairs={{0,16},{16,0},{1,17},{17,1},{2,18},{18,2},{3,19},{19,3},{4,20},{20... | collective-permute-start | bytes 3145736 | tf_op jit(solution)/shard_map/ppermute | solution.py:522
  655.8 31.2 %collective-permute-start.35 = (bf16[1024,256]{1,0:T(8,128)(2,1)}, bf16[1024,256]{1,0:T(8,128)(2,1)}, u32[]{:S(2)}, u32[]{:S(2)}) collective-permute-start(bf16[1024,256]{1,0:T(8,128)(2,1)} %add_convert_fusion.16), channel_id=1, source_target_pairs={{0,16},{16,0},{1,17},{17,1},{2,18},{18,2},{3,19},{19,3},{4,20},{20... | collective-permute-start | bytes 1572872 | tf_op jit(solution)/shard_map/ppermute | solution.py:522
  659.3 7.6 collective-permute-start.49
  663.6 80.6 %collective-permute-start.44 = (bf16[4,1728,128]{2,1,0:T(8,128)(2,1)S(1)}, bf16[4,1728,128]{2,1,0:T(8,128)(2,1)}, u32[]{:S(2)}, u32[]{:S(2)}) collective-permute-start(bf16[4,1728,128]{2,1,0:T(8,128)(2,1)S(1)} %maximum_select_fusion.3), channel_id=1, source_target_pairs={{0,8},{8,0},{1,9},{9,1},{2,10},{10,2},{3,11},{11,3},{4,12},{12,4},... | collective-permute-start | bytes 5308424 | tf_op jit(solution)/shard_map/ppermute | solution.py:522
  689.8 42.7 %reduce-scatter.7.cloned.1.call-start = ((), (), s32[]{:S(2)}) async-start(), calls=%async_computation.8 | async-start | bytes 655360 | tf_op jit(solution)/shard_map/reduce_scatter | solution.py:572
  692.3 10.4 %collective-permute-start.32 = (bf16[1024,256]{1,0:T(8,128)(2,1)}, bf16[1024,256]{1,0:T(8,128)(2,1)S(1)}, u32[]{:S(2)}, u32[]{:S(2)}) collective-permute-start(bf16[1024,256]{1,0:T(8,128)(2,1)} %add_convert_fusion.18), channel_id=1, source_target_pairs={{0,1},{1,0},{2,3},{3,2},{4,5},{5,4},{6,7},{7,6},{8,9},{9,8},{10,11... | collective-permute-start | bytes 1572872 | tf_op jit(solution)/shard_map/ppermute | solution.py:522
  733.4 9.2 %collective-permute-start.36 = (bf16[1,1024,128]{2,1,0:T(8,128)(2,1)S(1)}, bf16[1,1024,128]{2,1,0:T(8,128)(2,1)S(1)}, u32[]{:S(2)}, u32[]{:S(2)}) collective-permute-start(bf16[1,1024,128]{2,1,0:T(8,128)(2,1)S(1)} %maximum_bitcast_fusion.1), channel_id=1, source_target_pairs={{0,1},{1,0},{2,3},{3,2},{4,5},{5,4},{6,7},{7,6},{8,9},{9,8},{10,11... | collective-permute-start | bytes 786440 | tf_op jit(solution)/shard_map/ppermute | solution.py:522
  736.4 10.9 %collective-permute-start.51 = (bf16[1,1408,128]{2,1,0:T(8,128)(2,1)S(1)}, bf16[1,1408,128]{2,1,0:T(8,128)(2,1)S(1)}, u32[]{:S(2)}, u32[]{:S(2)}) collective-permute-start(bf16[1,1408,128]{2,1,0:T(8,128)(2,1)S(1)} %bitcast.297), channel_id=1, source_target_pairs={{0,1},{1,0},{2,3},{3,2},{4,5},{5,4},{6,7},{7,6},{8,9},{9,8},{10,11... | collective-permute-start | bytes 1081352 | tf_op jit(solution)/shard_map/ppermute | solution.py:522
  742.7 14.0 %collective-permute-start.37 = (bf16[2,1024,128]{2,1,0:T(8,128)(2,1)S(1)}, bf16[2,1024,128]{2,1,0:T(8,128)(2,1)S(1)}, u32[]{:S(2)}, u32[]{:S(2)}) collective-permute-start(bf16[2,1024,128]{2,1,0:T(8,128)(2,1)S(1)} %maximum_select_fusion.8), channel_id=1, source_target_pairs={{0,16},{16,0},{1,17},{17,1},{2,18},{18,2},{3,19},{19,3},{4,20},{20... | collective-permute-start | bytes 1572872 | tf_op jit(solution)/shard_map/ppermute | solution.py:522
  747.4 19.9 %collective-permute-start.52 = (bf16[2,1408,128]{2,1,0:T(8,128)(2,1)S(1)}, bf16[2,1408,128]{2,1,0:T(8,128)(2,1)S(1)}, u32[]{:S(2)}, u32[]{:S(2)}) collective-permute-start(bf16[2,1408,128]{2,1,0:T(8,128)(2,1)S(1)} %maximum_select_fusion.7), channel_id=1, source_target_pairs={{0,16},{16,0},{1,17},{17,1},{2,18},{18,2},{3,19},{19,3},{4,20},{20... | collective-permute-start | bytes 2162696 | tf_op jit(solution)/shard_map/ppermute | solution.py:522
  757.8 27.2 %collective-permute-start.38 = (bf16[4,1024,128]{2,1,0:T(8,128)(2,1)}, bf16[4,1024,128]{2,1,0:T(8,128)(2,1)}, u32[]{:S(2)}, u32[]{:S(2)}) collective-permute-start(bf16[4,1024,128]{2,1,0:T(8,128)(2,1)} %maximum_select_fusion.5), channel_id=1, source_target_pairs={{0,8},{8,0},{1,9},{9,1},{2,10},{10,2},{3,11},{11,3},{4,12},{12,4},... | collective-permute-start | bytes 3145736 | tf_op jit(solution)/shard_map/ppermute | solution.py:522
  768.7 30.5 %collective-permute-start.53 = (bf16[4,1408,128]{2,1,0:T(8,128)(2,1)}, bf16[4,1408,128]{2,1,0:T(8,128)(2,1)}, u32[]{:S(2)}, u32[]{:S(2)}) collective-permute-start(bf16[4,1408,128]{2,1,0:T(8,128)(2,1)} %maximum_select_fusion.4), channel_id=1, source_target_pairs={{0,8},{8,0},{1,9},{9,1},{2,10},{10,2},{3,11},{11,3},{4,12},{12,4},... | collective-permute-start | bytes 4325384 | tf_op jit(solution)/shard_map/ppermute | solution.py:522
  (153 other events, 1283.6 us)
Sparse Core Ops, SparseCore 0:
  10.9 89.1 all-gather.2
  102.9 110.3 all-gather.4
  428.7 22.8 reduce-scatter.14
  454.3 20.9 reduce-scatter.10
  524.1 23.9 reduce-scatter.12
  621.1 30.4 reduce-scatter.16
  689.9 19.7 reduce-scatter.8
  712.5 19.9 reduce-scatter.6

commit v4 on v3

--- a/solution.py
+++ b/solution.py
@@ -1,3 +1,4 @@
+import functools
 import jax
 import jax.numpy as jnp
 from jax import lax
@@ -369,7 +370,7 @@
         chunk(c, False)
 
 
-def call(kernel, outs, scratch, *args, micros):
+def call(kernel, outs, scratch, *args):
     return pl.pallas_call(
         kernel,
         out_shape=[jax.ShapeDtypeStruct(s, t) for s, t in outs],
@@ -377,9 +378,7 @@
         out_specs=[pl.BlockSpec(memory_space=pltpu.VMEM)] * len(outs),
         scratch_shapes=scratch,
         compiler_params=pltpu.CompilerParams(vmem_limit_bytes=VMEM_BYTES),
-        cost_estimate=pl.CostEstimate(
-            flops=int(micros * 1e9), bytes_accessed=4 * 2**20, transcendentals=0
-        ),
+        cost_estimate=pl.CostEstimate(flops=1, bytes_accessed=1, transcendentals=0),
     )(*args)
 
 
@@ -431,16 +430,17 @@
     inv_shape = ((blocks, groups, ROWS, ROWS), F32)
     state_shape = ((H, DK, DV), F32)
     cor_shape = ((blocks, groups, ROWS, ROWS), BF16)
-    (n,) = call(conv_kernel, [n_shape], [], x, weights, masks, micros=5)
+    x = points("conv", x)
+    (n,) = call(conv_kernel, [n_shape], [], x, weights, masks)
     n = points("inverse", n)
-    (inv,) = call(inverse_kernel, [inv_shape], [], n, col, row, micros=10)
+    (inv,) = call(inverse_kernel, [inv_shape], [], n, col, row)
+    inv = points("state", inv)
     start = jnp.zeros((H, DK, DV), BF16)
     ahead = [(i, i + 1) for i in range(sp_size - 1)]
     behind = [(i + 1, i) for i in range(sp_size - 1)]
     for _ in range(sp_size - 1):
-        (state,) = call(state_kernel, [state_shape], [], n, inv, col, start, micros=4)
+        (state,) = call(state_kernel, [state_shape], [], n, inv, col, start)
         start = lax.ppermute(state.astype(BF16), "sp", ahead)
-    start = points("scan", start)
     mixed, cor, states = call(
         scan_kernel,
         [((length, H * DV), BF16), cor_shape, ((blocks, H, DK, DV), BF16)],
@@ -450,14 +450,13 @@
         col,
         row,
         start,
-        micros=4,
     )
 
     def pull(dout):
         dstart = jnp.zeros((H, DK, DV), BF16)
         for _ in range(sp_size - 1):
             (dstate,) = call(
-                back_state_kernel, [state_shape], [], n, inv, col, row, dout, dstart, micros=4
+                back_state_kernel, [state_shape], [], n, inv, col, row, dout, dstart
             )
             dstart = lax.ppermute(dstate.astype(BF16), "sp", behind)
         dstart = points("back", dstart)
@@ -477,7 +476,6 @@
             cor,
             states,
             dstart,
-            micros=10,
         )
         dn = points("conv_back", dn)
         dx, dcw = call(
@@ -488,7 +486,6 @@
             weights,
             masks,
             dn,
-            micros=4,
         )
         grads = jnp.transpose(gcol[..., :5], (3, 0, 1, 2))
         grads = grads.at[0].add(grow[:, :, 0])
@@ -660,28 +657,49 @@
             + self.from_second.astype(F32)
         )
 
-    def block(self):
-        return sum_blocks(self.own())
-
-    def spread(self, every):
-        ways = {"core": 0, "x": 1, "sp": 2}
-        order = tuple(ways[axis] for axis in relative_axes(self.first))
-        pieces = widen(jnp.transpose(every, order + (3, 4)), self.width)
-        pieces = pieces.reshape((8,) + pieces.shape[3:])
-        return jnp.swapaxes(pieces, 0, 1).reshape(pieces.shape[1], -1).astype(F32)
-
-
-def finish(sums):
-    blocks = [narrow(s.block()) for s in sums]
+
+def spread(blocks):
     held = jnp.concatenate(blocks, axis=0)[None]
-    for axis in ("sp", "x", "core"):
-        held = pair(axis, held, swap(held, axis), 0)
-    held = held.reshape((2, 2, 2) + held.shape[1:])
-    out, start = [], 0
-    for s, block in zip(sums, blocks):
-        out.append(s.spread(held[:, :, :, start : start + block.shape[0]]))
-        start += block.shape[0]
-    return out
+    for axis in ("sp", "x"):
+        held = jnp.concatenate([held, swap(held, axis)], axis=0)
+    return held, swap(held, "core")
+
+
+def unpack_kernel(segments, count, places_ref, *refs):
+    sources, outs = refs[:count], refs[count:]
+    for source, row, out, column, rows, blocks, way in segments:
+        for k in range(8):
+            piece = sources[2 * source + k // 4]
+            at = pl.multiple_of(column + places_ref[2 * way, k] * (128 * blocks), 128)
+            down = pl.multiple_of(places_ref[2 * way + 1, k] * rows, 16)
+            for j in range(blocks):
+                outs[out][pl.ds(down, rows), pl.ds(at + 128 * j, 128)] = piece[
+                    k % 4, row + j * rows : row + (j + 1) * rows
+                ].astype(F32)
+
+
+def unpack(places, segments, sources, shapes):
+    count = len(sources)
+    return pl.pallas_call(
+        functools.partial(unpack_kernel, segments, count),
+        out_shape=[jax.ShapeDtypeStruct(s, F32) for s in shapes],
+        in_specs=[pl.BlockSpec(memory_space=pltpu.SMEM)]
+        + [pl.BlockSpec(memory_space=pltpu.VMEM)] * count,
+        out_specs=[pl.BlockSpec(memory_space=pltpu.VMEM)] * len(shapes),
+        compiler_params=pltpu.CompilerParams(vmem_limit_bytes=VMEM_BYTES),
+    )(places, *sources)
+
+
+def spread_places():
+    core, x, y = lax.axis_index("core"), lax.axis_index("x"), lax.axis_index("sp")
+    table = [[] for _ in range(6)]
+    for k in range(8):
+        c, d, e = (
+            1 - bit if (k >> shift) & 1 else bit for shift, bit in ((2, core), (1, x), (0, y))
+        )
+        for line, value in enumerate((4 * c + 2 * d + e, 0, 4 * c + 2 * e + d, 0, 2 * c + d, e)):
+            table[line].append(jnp.asarray(value, jnp.int32))
+    return jnp.stack([jnp.stack(line) for line in table])
 
 
 def by_half(values):
@@ -730,35 +748,20 @@
         self.from_y = swap(self.outgoing, "sp")
         return self.outgoing
 
-    def block(self):
+    def own(self):
         rows, width = self.rows, self.width
-        own = (
+        return (
             grad_dot(self.left[:, :rows], self.near[:, :width])
             + self.from_core[:rows, :width].astype(F32)
             + self.from_x[:rows].astype(F32)
             + self.from_y.astype(F32)
         )
-        return sum_blocks(own)
-
-    def spread(self, every):
-        pieces = widen(every, self.width)
-        return (
-            jnp.transpose(pieces, (2, 3, 0, 1, 4))
-            .reshape(2 * pieces.shape[3], 4 * self.width)
-            .astype(F32)
-        )
 
 
 def narrow(value):
     return jnp.concatenate(
         [value[:, i : i + 128] for i in range(0, value.shape[1], 128)], axis=0
     )
-
-
-def widen(value, width):
-    blocks = width // 128
-    split = value.reshape(value.shape[:-2] + (blocks, value.shape[-2] // blocks, 128))
-    return jnp.swapaxes(split, -3, -2).reshape(value.shape[:-2] + (-1, width))
 
 
 def pack_small(parts, width):
@@ -774,10 +777,10 @@
     return out
 
 
-def sum_small(parts):
+def sum_small(parts, *earlier):
     flat = jnp.concatenate([p.reshape(-1) for p in parts])
     size = flat.shape[0]
-    flat = jnp.pad(flat, (0, -size % 1024)).reshape(-1, 128)
+    flat = after(jnp.pad(flat, (0, -size % 1024)).reshape(-1, 128), *earlier)
     for axis in ("core", "x", "sp"):
         flat = flat + swap(flat, axis)
     members = lax.axis_size("fsdp")
@@ -839,19 +842,9 @@
         first_all[:, pair_rows:].reshape(members, -1), smalls
     )
     qkv_second = (qk_way.second(), v_way.second())
-    gate_rows = narrow(gate_way.piece).shape[0]
-    second_load = after(
-        jnp.concatenate([narrow(gate_way.piece), narrow(down_way.piece)], axis=0), both
-    )
-    second_all = gather_blocks(second_load).reshape(members, -1, 128)
-    gate_way.held = widen(second_all[:, :gate_rows], gate_way.piece.shape[1]).reshape(
-        -1, gate_way.piece.shape[1]
-    )
-    down_way.held = widen(second_all[:, gate_rows:], down_way.piece.shape[1]).reshape(
-        -1, down_way.piece.shape[1]
-    )
+    gate_way.blocks(*qkv_second)
     qkv_third = (qk_way.third(), v_way.third())
-    early = (gate_way.second(*qkv_third), down_way.second(*qkv_third))
+    gate_way.second(*qkv_third)
     qk_full, v_full = qk_way.full(), v_way.full()
     out_full = gather_rows(output_weight)
     up_full = gather_rows(up_weight)
@@ -863,16 +856,22 @@
     feed_scale = feed_all.reshape(-1).astype(F32)
 
     def points(name, value):
+        if name == "conv":
+            down_way.blocks(value)
+            return value
         if name == "inverse":
-            for way in (gate_way, down_way):
-                way.third(value)
-            return after(value, *early)
-        if name == "scan":
-            return after(value, gate_way.held, down_way.held)
+            value = after(value, gate_way.held, down_way.held)
+            gate_way.third(value)
+            down_way.second(value)
+            return value
+        if name == "state":
+            value = after(value, gate_way.held, down_way.held)
+            down_way.third(value)
+            return value
         if name == "back":
             return after(value, sums["down"].third())
         if name == "conv_back":
-            return after(value, *(sums[key].third() for key in ("up", "out", "gate")))
+            return after(value, *(sums[key].third() for key in ("out", "gate")))
         return value
 
     sums = {}
@@ -944,9 +943,37 @@
     for step in ("second", "third"):
         for key in ("qk", "v"):
             getattr(sums[key], step)()
-    down_shard, output_shard, gate_shard = finish([sums[k] for k in ("down", "out", "gate")])
-    (up_shard,) = finish([sums["up"]])
-    qk_shard, v_shard = finish([sums["qk"], sums["v"]])
+    sums["up"].third()
+    places = spread_places()
+    blocks = [sum_blocks(sums[k].own()) for k in ("down", "out", "gate")]
+    down_rows, out_rows = blocks[0].shape[0], blocks[1].shape[0]
+    early_sums = spread([narrow(block) for block in blocks])
+    down_shard, output_shard = unpack(
+        places,
+        [(0, 0, 0, 0, down_rows, 1, 1), (0, down_rows, 1, 0, out_rows, 1, 1)],
+        early_sums,
+        [down_weight.shape, output_weight.shape],
+    )
+    up_block = sum_blocks(sums["up"].own())
+    (up_shard,) = unpack(
+        places,
+        [(0, 0, 0, 0, up_block.shape[0], up_block.shape[1] // 128, 2)],
+        spread([narrow(up_block)]),
+        [up_weight.shape],
+    )
+    late_block = sum_blocks(jnp.concatenate([sums["qk"].own(), sums["v"].own()], axis=1))
+    rows, wide = late_block.shape[0], late_block.shape[1] // 256
+    gate_wide = blocks[2].shape[1] // 128
+    (input_shard,) = unpack(
+        places,
+        [
+            (0, 0, 0, 0, rows, wide, 0),
+            (0, wide * rows, 0, qk_cols, rows, wide, 1),
+            (1, down_rows + out_rows, 0, qkv_cols, rows, gate_wide, 0),
+        ],
+        spread([narrow(late_block)]) + early_sums,
+        [input_weight.shape],
+    )
     rate_grad = jnp.einsum("td,tf->df", normed_low, d_rate_low, preferred_element_type=F32)
     d_normed = dot_back(d_qk_rel, qk_full) + dot_back(d_v_rel, v_full)
     d_normed = d_normed + dot_back(d_gate_rel, gate_full)
@@ -956,12 +983,14 @@
     d_front, mixer_grad = pull_norm(d_normed)
     tokens_grad = (d_resid + d_front).astype(BF16)
     rate_sum, conv_sum, decay_sum, mixer_sum, heads_sum, feed_sum = sum_small(
-        (rate_grad, conv_grad, decay_grad, mixer_grad, heads_grad, feed_grad)
+        (rate_grad, conv_grad, decay_grad, mixer_grad, heads_grad, feed_grad),
+        sums["qk"].outgoing,
+        sums["v"].outgoing,
     )
     return (
         block_out,
         tokens_grad,
-        jnp.concatenate([qk_shard, v_shard, gate_shard], axis=1),
+        input_shard,
         own_part(rate_sum, 0),
         own_part(conv_sum, 1),
         own_part(decay_sum, 1),

time: 841 us -> 792 us (0.942)
  local copies, waits for them, and re-layouts: 165 us -> 121 us
  waiting for transfers between devices: 223 us -> 185 us
  Pallas kernels: 127 us -> 143 us
  starting transfers between devices: 60.2 us -> 74.6 us
    convert_element_type x11 -> x0, local copies, waits for them, and re-layouts: 35.2 us -> none  [the longest x3 21.5 us: spread(): return jnp.transpose(pieces, (2, 3, 0, 1, 4)).reshape(2 * pieces.shape[3]...]
    ppermute x42, waiting for transfers between devices: 155 us -> 121 us  [swap(): return lax.ppermute(value, axis, [(0, 1), (1, 0)])]
    reduce_scatter x6 -> x5, waiting for transfers between devices: 37.6 us -> 12 us  [sum_blocks(): lax.psum_scatter(value.astype(BF16), 'fsdp', scatter_dimension=0, tiled=T...]
    pallas_call x0 -> x3, Pallas kernels: none -> 16.1 us  [unpack(): pl.pallas_call(functools.partial(unpack_kernel, segments, count), out_sha...]
    select_n x9 -> x0, other arithmetic: 14 us -> none  [pair(): jnp.where(first, jnp.concatenate([mine, theirs], axis=dim), jnp.concatena...]
    ppermute x1, waiting for transfers between devices: 6.6 us -> 20 us  [mixer(): start = lax.ppermute(state.astype(BF16), 'sp', ahead)]
    unnamed x355 -> x350, local copies, waits for them, and re-layouts: 50.2 us -> 36.9 us
    ppermute x6 -> x9, starting transfers between devices: 12.6 us -> 25.2 us  [shifted(): lax.ppermute(value, 'fsdp', [(i, (i + step) % count) for i in range(count)])]
  transfers between devices with their start and end apart: 62 -> 64, of which waited for: 25 -> 23; matrix products, arithmetic and copies ran while one was open for 41% -> 42% of each run, Pallas kernels for 15% -> 18%
where the time goes in v4:
time: 792 us; the launch traced here: 781 us
  waiting for transfers between devices  185 us (23%)
  matrix products  149 us (19%)
  Pallas kernels  143 us (18%)
  local copies, waits for them, and re-layouts  121 us (15%)
  other arithmetic  90 us (11%)
  starting transfers between devices  74.6 us (9%)
  between operations  17.1 us (2%)
    pallas_call x7, Pallas kernels, call(): pl.pallas_call(kernel, out_shape=[jax.ShapeDtypeStruct(s, t) for s, t in...  127 us
    ppermute x42, waiting for transfers between devices, swap(): return lax.ppermute(value, axis, [(0, 1), (1, 0)])  121 us
    dot_general x24, matrix products, grad_dot(): return jnp.einsum('td,tf->df', left, right, preferred_element_type=F32)  66.2 us
    ppermute x42, starting transfers between devices, swap(): return lax.ppermute(value, axis, [(0, 1), (1, 0)])  37.2 us
    unnamed x350, local copies, waits for them, and re-layouts  36.9 us
    ppermute x9, starting transfers between devices, shifted(): lax.ppermute(value, 'fsdp', [(i, (i + step) % count) for i in range(count)])  25.2 us
    dot_general x4, matrix products, dot_back(): jnp.einsum('tf,df->td', grads[:, :half], halves_of[0], preferred_element_...  22 us
    ppermute x1, waiting for transfers between devices, mixer(): start = lax.ppermute(state.astype(BF16), 'sp', ahead)  20 us
  transfers between devices with their start and end apart: 64, of which 23 were waited for; matrix products, arithmetic and copies ran while one was open for 42% of the time, Pallas kernels for 18%

profile of v4, /device:TPU:0, one launch (start us, length us, event | category | flops | bytes accessed | tf_op | source)
XLA Modules:
  0.0 780.5 jit_solution(7943548385108309802)
XLA Ops:
  17.6 3.0 collective-permute-start.3
  25.2 4.0 collective-permute-start
  50.4 13.2 %collective-permute-done.4 = bf16[1024,256]{1,0:T(8,128)(2,1)S(1)} collective-permute-done((bf16[1024,256]{1,0:T(8,128)(2,1)S(1)}, bf16[1024,256]{1,0:T(8,128)(2,1)S(1)}, u32[]{:S(2)}, u32[]{:S(2)}) %collective-permute-start.4) | collective-permute-done | bytes 524320 | tf_op jit(solution)/shard_map/ppermute | solution.py:519
  71.7 24.8 %collective-permute-done.5 = bf16[1024,512]{1,0:T(8,128)(2,1)} collective-permute-done((bf16[1024,512]{1,0:T(8,128)(2,1)}, bf16[1024,512]{1,0:T(8,128)(2,1)}, u32[]{:S(2)}, u32[]{:S(2)}) %collective-permute-start.5) | collective-permute-done | bytes 1048608 | tf_op jit(solution)/shard_map/ppermute | solution.py:519
  96.5 2.8 pad_maximum_fusion
  99.8 5.2 collective-permute-start.11
  108.1 7.4 collective-permute-done.10
  115.5 5.9 collective-permute-done.12
  135.4 4.1 collective-permute-start.14
  143.0 5.0 collective-permute-start.16
  148.0 13.0 %shard_map.220.n_ref = bf16[384,4096]{1,0:T(8,128)(2,1)} custom-call(bf16[400,4096]{1,0:T(8,128)(2,1)} %copy-done.20, f32[4,4096]{1,0:T(4,128)} %bitcast.240, f32[384,8]{1,0:T(8,128)} %copy.198.mask_ref), custom_call_target="tpu_custom_call" | custom-call | flops 1 | bytes 1 | tf_op jit(solution)/shard_map/pallas_call | solution.py:374
  161.1 5.6 collective-permute-done.15
  177.4 2.7 broadcast_in_dim.59
  184.1 7.2 concatenate.223
  191.3 27.2 %shard_map.221.inv_ref = f32[6,2,256,256]{3,2,1,0:T(8,128)} custom-call(bf16[384,4096]{1,0:T(8,128)(2,1)} %shard_map.220.n_ref, f32[6,2,256,8]{3,2,1,0:T(8,128)} %bitcast.208, f32[6,2,8,256]{3,2,1,0:T(8,128)} %bitcast.228), custom_call_target="tpu_custom_call" | custom-call | flops 1 | bytes 1 | tf_op jit(solution)/shard_map/pallas_call | solution.py:374
  224.1 4.1 collective-permute-done.18
  233.2 10.4 %shard_map.222 = f32[8,128,256]{2,1,0:T(8,128)} custom-call(bf16[384,4096]{1,0:T(8,128)(2,1)} %shard_map.220.n_ref, f32[6,2,256,256]{3,2,1,0:T(8,128)} %shard_map.221.inv_ref, f32[6,2,256,8]{3,2,1,0:T(8,128)} %bitcast.209, bf16[8,128,256]{2,1,0:T(8,128)(2,1)} %broadcast_20_start_ref.2.start_ref), custom_call_target="tpu_custom_call" | custom-call | flops 1 | bytes 1 | tf_op jit(solution)/shard_map/pallas_call | solution.py:374
  244.9 3.1 collective-permute-start.19
  253.2 20.0 %collective-permute-done.19.start_ref = bf16[8,128,256]{2,1,0:T(8,128)(2,1)S(1)} collective-permute-done((bf16[8,128,256]{2,1,0:T(8,128)(2,1)S(1)}, bf16[8,128,256]{2,1,0:T(8,128)(2,1)S(1)}, u32[]{:S(2)}, u32[]{:S(2)}) %collective-permute-start.19) | collective-permute-done | bytes 524320 | tf_op jit(solution)/shard_map/ppermute | solution.py:443
  273.9 13.6 %shard_map.223 = (bf16[384,2048]{1,0:T(8,128)(2,1)}, bf16[6,2,256,256]{3,2,1,0:T(8,128)(2,1)}, bf16[6,8,128,256]{3,2,1,0:T(8,128)(2,1)}) custom-call(bf16[384,4096]{1,0:T(8,128)(2,1)} %shard_map.220.n_ref, f32[6,2,256,256]{3,2,1,0:T(8,128)} %shard_map.221.inv_ref, f32[6,2,256,8]{3,2,1,0:T(8,128)} %bitcast.210, f32[6,2,8,256]{3,2,1,0:T(8,128)} %bitcast.229, ...), custom_call_target="tpu_custom_call" | custom-call | flops 1 | bytes 1 | tf_op jit(solution)/shard_map/pallas_call | solution.py:374
  293.9 3.7 constant_dynamic-update-slice_fusion.27
  306.6 4.8 multiply_reduce_fusion.4
  313.7 5.2 fusion.165
  319.0 8.0 %fusion.246 = f32[384,5632]{1,0:T(8,128)S(1)} fusion(bf16[384,1024]{1,0:T(8,128)(2,1)} %multiply_convert_fusion.2, bf16[1024,5632]{1,0:T(8,128)(2,1)} %all-gather.5.cloned.1.call-done), kind=kOutput, calls=%fused_computation.535 | convolution fusion | flops 4429185024 | bytes 20971520 | tf_op jit(solution)/shard_map/dot_general | solution.py:907
  327.0 7.3 fusion.55
  334.3 3.3 convolution_convert_fusion.1
  350.1 4.1 add_convert_fusion
  354.4 5.7 convolution_convert_fusion
  360.3 3.5 add_convert_fusion.5
  363.9 8.4 %multiply_reduce_fusion.2 = (f32[1024]{0:T(1024)}, f32[384]{0:T(512)S(1)}, f32[384,1024]{1,0:T(8,128)S(1)}) fusion(f32[384,1024]{1,0:T(8,128)S(1)} %copy-done.16, f32[384]{0:T(512)S(1)} %copy-done.128, f32[1024]{0:T(1024)S(1)} %bitcast.262, bf16[384,5632]{1,0:T(8,128)(2,1)S(1)} %add_convert_fusion, bf16[1024,5632]{1,0:T(8,128)(2,1)} %all-gather.5.cloned.1.call-done), kind=kOutput, calls=%fused_computation.126 | convolution fusion | flops 4431542784 | bytes 19016704 | tf_op jit(solution)/shard_map/tf,df->td/dot_general | solution.py:922
  385.9 5.7 multiply_reduce_fusion
  394.7 3.1 fusion.247
  397.7 3.1 fusion.248
  402.3 3.8 fusion.28
  425.5 4.0 fusion.158
  429.5 12.9 %collective-permute-done.30 = bf16[1024,512]{1,0:T(8,128)(2,1)} collective-permute-done((bf16[1024,512]{1,0:T(8,128)(2,1)}, bf16[1024,512]{1,0:T(8,128)(2,1)}, u32[]{:S(2)}, u32[]{:S(2)}) %collective-permute-start.30) | collective-permute-done | bytes 1048608 | tf_op jit(solution)/shard_map/ppermute | solution.py:519
  444.3 3.5 collective-permute-done.28
  447.9 3.0 add_convert_fusion.12
  452.9 3.0 add_convert_fusion.9
  461.5 5.5 add_convert_fusion.2
  466.9 13.6 %shard_map.224 = f32[8,128,256]{2,1,0:T(8,128)} custom-call(bf16[384,4096]{1,0:T(8,128)(2,1)} %shard_map.220.n_ref, f32[6,2,256,256]{3,2,1,0:T(8,128)} %shard_map.221.inv_ref, f32[6,2,256,8]{3,2,1,0:T(8,128)} %bitcast.211, f32[6,2,8,256]{3,2,1,0:T(8,128)} %bitcast.230, bf16[384,2048]{1,0:T(8,128)(2,1)} %get-tuple-element.57.dout_ref, ...), custom_call_target="tpu_custom_call" | custom-call | flops 1 | bytes 1 | tf_op jit(solution)/shard_map/pallas_call | solution.py:374
  484.2 2.8 add_convert_fusion.11
  491.9 6.3 collective-permute-done.27.start_ref
  498.2 25.5 %shard_map.225 = (f32[384,4096]{1,0:T(8,128)}, f32[6,2,256,8]{3,2,1,0:T(8,128)}, f32[6,2,8,256]{3,2,1,0:T(8,128)}) custom-call(bf16[384,4096]{1,0:T(8,128)(2,1)} %shard_map.220.n_ref, f32[6,2,256,256]{3,2,1,0:T(8,128)} %shard_map.221.inv_ref, f32[6,2,256,8]{3,2,1,0:T(8,128)} %bitcast.212, f32[6,2,8,256]{3,2,1,0:T(8,128)} %bitcast.231, ...), custom_call_target="tpu_custom_call" | custom-call | flops 1 | bytes 1 | tf_op jit(solution)/shard_map/pallas_call | solution.py:374
  525.9 23.1 %shard_map.226 = (bf16[400,4096]{1,0:T(8,128)(2,1)}, f32[4,4096]{1,0:T(4,128)}) custom-call(bf16[400,4096]{1,0:T(8,128)(2,1)} %copy-done.20, f32[4,4096]{1,0:T(4,128)} %bitcast.241, f32[384,8]{1,0:T(8,128)} %copy.198.mask_ref, f32[384,4096]{1,0:T(8,128)} %get-tuple-element.62.dn_ref), custom_call_target="tpu_custom_call" | custom-call | flops 1 | bytes 1 | tf_op jit(solution)/shard_map/pallas_call | solution.py:374
  552.1 3.4 slice_reduce_fusion.2
  576.3 3.9 fusion.157
  582.5 3.5 fusion.32
  585.9 4.4 add_convert_fusion.4
  590.4 3.5 fusion.40
  596.6 7.7 fusion.16
  605.9 18.2 %collective-permute-done.53 = bf16[512,1408]{1,0:T(8,128)(2,1)} collective-permute-done((bf16[512,1408]{1,0:T(8,128)(2,1)}, bf16[512,1408]{1,0:T(8,128)(2,1)}, u32[]{:S(2)}, u32[]{:S(2)}) %collective-permute-start.53) | collective-permute-done | bytes 1441824 | tf_op jit(solution)/shard_map/ppermute | solution.py:519
  624.2 4.8 add_convert_fusion.3
  629.3 3.0 add_convert_fusion.6
  632.6 3.0 add_convert_fusion.7
  641.5 15.5 %collective-permute-done.36 = bf16[1024,512]{1,0:T(8,128)(2,1)} collective-permute-done((bf16[1024,512]{1,0:T(8,128)(2,1)}, bf16[1024,512]{1,0:T(8,128)(2,1)}, u32[]{:S(2)}, u32[]{:S(2)}) %collective-permute-start.36) | collective-permute-done | bytes 1048608 | tf_op jit(solution)/shard_map/ppermute | solution.py:519
  667.0 5.1 collective-permute-done.37
  674.0 5.1 collective-permute-done.34
  695.0 12.0 %reduce-scatter.6.cloned.1.call-done = bf16[256,512]{1,0:T(8,128)(2,1)} async-done(((bf16[1024,512]{1,0:T(8,128)(2,1)}), bf16[256,512]{1,0:T(8,128)(2,1)}) %reduce-scatter.6.cloned.1.call-update) | async-done | bytes 262160 | tf_op jit(solution)/shard_map/reduce_scatter | solution.py:569
  715.9 15.2 %collective-permute-done.48 = f32[280,128]{1,0:T(8,128)S(1)} collective-permute-done((f32[280,128]{1,0:T(8,128)S(1)}, f32[280,128]{1,0:T(8,128)S(1)}, u32[]{:S(2)}, u32[]{:S(2)}) %collective-permute-start.48) | collective-permute-done | bytes 143392 | tf_op jit(solution)/shard_map/ppermute | solution.py:519
  745.1 3.4 fusion.18
  757.1 4.9 shard_map.228
  762.0 6.1 shard_map.227
  768.2 5.1 shard_map.229
  (717 shorter events, 280.3 us)
Async XLA Ops:
  7.2 299.5 %all-gather.3.cloned.1.call-start = ((), (), s32[]{:S(2)}) async-start(), calls=%async_computation.5 | async-start | bytes 4325376 | tf_op jit(solution)/shard_map/all_gather | solution.py:585
  9.0 309.9 %all-gather.5.cloned.1.call-start = ((), (), s32[]{:S(2)}) async-start(), calls=%async_computation.6 | async-start | bytes 11894784 | tf_op jit(solution)/shard_map/all_gather | solution.py:585
  9.9 630.7 %reduce-scatter.12.cloned.1.call-start = ((), (), s32[]{:S(2)}) async-start(), calls=%async_computation.10 | async-start | bytes 655360 | tf_op jit(solution)/shard_map/reduce_scatter | solution.py:569
  17.6 27.8 %collective-permute-start.3 = (bf16[288,512]{1,0:T(8,128)(2,1)}, bf16[288,512]{1,0:T(8,128)(2,1)S(1)}, u32[]{:S(2)}, u32[]{:S(2)}) collective-permute-start(bf16[288,512]{1,0:T(8,128)(2,1)} %pad_maximum_fusion.19), channel_id=1, source_target_pairs={{0,2},{2,4},{4,6},{6,0},{1,3},{3,5},{5,7},{7,1},{8,10},{10,12},{12... | collective-permute-start | bytes 884744 | tf_op jit(solution)/shard_map/ppermute | solution.py:557
  20.6 24.8 %collective-permute-start.2 = (bf16[288,512]{1,0:T(8,128)(2,1)}, bf16[288,512]{1,0:T(8,128)(2,1)S(1)}, u32[]{:S(2)}, u32[]{:S(2)}) collective-permute-start(bf16[288,512]{1,0:T(8,128)(2,1)} %pad_maximum_fusion.19), channel_id=1, source_target_pairs={{0,4},{2,6},{4,0},{6,2},{1,5},{3,7},{5,1},{7,3},{8,12},{10,14},{12... | collective-permute-start | bytes 884744 | tf_op jit(solution)/shard_map/ppermute | solution.py:557
  23.2 21.5 %collective-permute-start.1 = (bf16[288,512]{1,0:T(8,128)(2,1)}, bf16[288,512]{1,0:T(8,128)(2,1)S(1)}, u32[]{:S(2)}, u32[]{:S(2)}) collective-permute-start(bf16[288,512]{1,0:T(8,128)(2,1)} %pad_maximum_fusion.19), channel_id=1, source_target_pairs={{0,6},{2,0},{4,2},{6,4},{1,7},{3,1},{5,3},{7,5},{8,14},{10,8},{12,... | collective-permute-start | bytes 884744 | tf_op jit(solution)/shard_map/ppermute | solution.py:557
  25.2 18.7 %collective-permute-start = (bf16[16,1024]{1,0:T(8,128)(2,1)}, bf16[16,1024]{1,0:T(8,128)(2,1)}, u32[]{:S(2)}, u32[]{:S(2)}) collective-permute-start(bf16[16,1024]{1,0:T(8,128)(2,1)} %slice.348), channel_id=1, source_target_pairs={{0,1},{2,3},{4,5},{6,7},{8,9},{10,11},{12,13},{14,15},{16,17},{18,... | collective-permute-start | bytes 98312 | tf_op jit(solution)/shard_map/ppermute | solution.py:884
  46.6 22.3 %collective-permute-start.7 = (bf16[1024,256]{1,0:T(8,128)(2,1)S(1)}, bf16[1024,256]{1,0:T(8,128)(2,1)S(1)}, u32[]{:S(2)}, u32[]{:S(2)}) collective-permute-start(bf16[1024,256]{1,0:T(8,128)(2,1)S(1)} %get-tuple-element.193), channel_id=1, source_target_pairs={{0,16},{16,0},{1,17},{17,1},{2,18},{18,2},{3,19},{19,3},{4,20},{20... | collective-permute-start | bytes 1572872 | tf_op jit(solution)/shard_map/ppermute | solution.py:519
  48.2 15.4 %collective-permute-start.4 = (bf16[1024,256]{1,0:T(8,128)(2,1)S(1)}, bf16[1024,256]{1,0:T(8,128)(2,1)S(1)}, u32[]{:S(2)}, u32[]{:S(2)}) collective-permute-start(bf16[1024,256]{1,0:T(8,128)(2,1)S(1)} %get-tuple-element.194), channel_id=1, source_target_pairs={{0,1},{1,0},{2,3},{3,2},{4,5},{5,4},{6,7},{7,6},{8,9},{9,8},{10,11... | collective-permute-start | bytes 1572872 | tf_op jit(solution)/shard_map/ppermute | solution.py:519
  64.7 31.8 %collective-permute-start.5 = (bf16[1024,512]{1,0:T(8,128)(2,1)}, bf16[1024,512]{1,0:T(8,128)(2,1)}, u32[]{:S(2)}, u32[]{:S(2)}) collective-permute-start(bf16[1024,512]{1,0:T(8,128)(2,1)} %pad_maximum_fusion.4), channel_id=1, source_target_pairs={{0,16},{16,0},{1,17},{17,1},{2,18},{18,2},{3,19},{19,3},{4,20},{20... | collective-permute-start | bytes 3145736 | tf_op jit(solution)/shard_map/ppermute | solution.py:519
  70.1 51.5 %collective-permute-start.8 = (bf16[1024,512]{1,0:T(8,128)(2,1)}, bf16[1024,512]{1,0:T(8,128)(2,1)}, u32[]{:S(2)}, u32[]{:S(2)}) collective-permute-start(bf16[1024,512]{1,0:T(8,128)(2,1)} %pad_maximum_fusion.5), channel_id=1, source_target_pairs={{0,1},{1,0},{2,3},{3,2},{4,5},{5,4},{6,7},{7,6},{8,9},{9,8},{10,11... | collective-permute-start | bytes 3145736 | tf_op jit(solution)/shard_map/ppermute | solution.py:519
  99.3 29.3 %collective-permute-start.6 = (bf16[1024,1024]{1,0:T(8,128)(2,1)}, bf16[1024,1024]{1,0:T(8,128)(2,1)}, u32[]{:S(2)}, u32[]{:S(2)}) collective-permute-start(bf16[1024,1024]{1,0:T(8,128)(2,1)} %pad_maximum_fusion), channel_id=1, source_target_pairs={{0,8},{8,0},{1,9},{9,1},{2,10},{10,2},{3,11},{11,3},{4,12},{12,4},... | collective-permute-start | bytes 6291464 | tf_op jit(solution)/shard_map/ppermute | solution.py:519
  99.8 15.7 %collective-permute-start.11 = (bf16[256,256]{1,0:T(8,128)(2,1)S(1)}, bf16[256,256]{1,0:T(8,128)(2,1)S(1)}, u32[]{:S(2)}, u32[]{:S(2)}) collective-permute-start(bf16[256,256]{1,0:T(8,128)(2,1)S(1)} %copy-done.74), channel_id=1, source_target_pairs={{0,4},{2,6},{4,0},{6,2},{1,5},{3,7},{5,1},{7,3},{8,12},{10,14},{12... | collective-permute-start | bytes 393224 | tf_op jit(solution)/shard_map/ppermute | solution.py:557
  105.0 10.5 %collective-permute-start.10 = (bf16[256,256]{1,0:T(8,128)(2,1)S(1)}, bf16[256,256]{1,0:T(8,128)(2,1)S(1)}, u32[]{:S(2)}, u32[]{:S(2)}) collective-permute-start(bf16[256,256]{1,0:T(8,128)(2,1)S(1)} %copy-done.74), channel_id=1, source_target_pairs={{0,6},{2,0},{4,2},{6,4},{1,7},{3,1},{5,3},{7,5},{8,14},{10,8},{12,... | collective-permute-start | bytes 393224 | tf_op jit(solution)/shard_map/ppermute | solution.py:557
  108.1 13.4 %collective-permute-start.12 = (bf16[256,256]{1,0:T(8,128)(2,1)S(1)}, bf16[256,256]{1,0:T(8,128)(2,1)S(1)}, u32[]{:S(2)}, u32[]{:S(2)}) collective-permute-start(bf16[256,256]{1,0:T(8,128)(2,1)S(1)} %copy-done.74), channel_id=1, source_target_pairs={{0,2},{2,4},{4,6},{6,0},{1,3},{3,5},{5,7},{7,1},{8,10},{10,12},{12... | collective-permute-start | bytes 393224 | tf_op jit(solution)/shard_map/ppermute | solution.py:557
  123.1 9.3 %collective-permute-start.9 = (bf16[1024,1024]{1,0:T(8,128)(2,1)S(1)}, bf16[1024,1024]{1,0:T(8,128)(2,1)S(1)}, u32[]{:S(2)}, u32[]{:S(2)}) collective-permute-start(bf16[1024,1024]{1,0:T(8,128)(2,1)S(1)} %pad_maximum_fusion.1), channel_id=1, source_target_pairs={{0,8},{8,0},{1,9},{9,1},{2,10},{10,2},{3,11},{11,3},{4,12},{12,4},... | collective-permute-start | bytes 6291464 | tf_op jit(solution)/shard_map/ppermute | solution.py:519
  123.3 18.9 %collective-permute-start.13 = (bf16[1024,256]{1,0:T(8,128)(2,1)S(1)}, bf16[1024,256]{1,0:T(8,128)(2,1)S(1)}, u32[]{:S(2)}, u32[]{:S(2)}) collective-permute-start(bf16[1024,256]{1,0:T(8,128)(2,1)S(1)} %constant_dynamic-slice_fusion.47), channel_id=1, source_target_pairs={{0,1},{1,0},{2,3},{3,2},{4,5},{5,4},{6,7},{7,6},{8,9},{9,8},{10,11... | collective-permute-start | bytes 1572872 | tf_op jit(solution)/shard_map/ppermute | solution.py:519
  135.4 25.6 %collective-permute-start.14 = (bf16[704,128]{1,0:T(8,128)(2,1)S(1)}, bf16[704,128]{1,0:T(8,128)(2,1)S(1)}, u32[]{:S(2)}, u32[]{:S(2)}) collective-permute-start(bf16[704,128]{1,0:T(8,128)(2,1)S(1)} %copy-done.69), channel_id=1, source_target_pairs={{0,6},{2,0},{4,2},{6,4},{1,7},{3,1},{5,3},{7,5},{8,14},{10,8},{12,... | collective-permute-start | bytes 540680 | tf_op jit(solution)/shard_map/ppermute | solution.py:557
  140.4 26.3 %collective-permute-start.15 = (bf16[704,128]{1,0:T(8,128)(2,1)S(1)}, bf16[704,128]{1,0:T(8,128)(2,1)S(1)}, u32[]{:S(2)}, u32[]{:S(2)}) collective-permute-start(bf16[704,128]{1,0:T(8,128)(2,1)S(1)} %copy-done.69), channel_id=1, source_target_pairs={{0,4},{2,6},{4,0},{6,2},{1,5},{3,7},{5,1},{7,3},{8,12},{10,14},{12... | collective-permute-start | bytes 540680 | tf_op jit(solution)/shard_map/ppermute | solution.py:557
  143.0 23.7 %collective-permute-start.16 = (bf16[704,128]{1,0:T(8,128)(2,1)S(1)}, bf16[704,128]{1,0:T(8,128)(2,1)S(1)}, u32[]{:S(2)}, u32[]{:S(2)}) collective-permute-start(bf16[704,128]{1,0:T(8,128)(2,1)S(1)} %copy-done.69), channel_id=1, source_target_pairs={{0,2},{2,4},{4,6},{6,0},{1,3},{3,5},{5,7},{7,1},{8,10},{10,12},{12... | collective-permute-start | bytes 540680 | tf_op jit(solution)/shard_map/ppermute | solution.py:557
  166.9 54.8 %collective-permute-start.17 = (bf16[1024,512]{1,0:T(8,128)(2,1)}, bf16[1024,512]{1,0:T(8,128)(2,1)}, u32[]{:S(2)}, u32[]{:S(2)}) collective-permute-start(bf16[1024,512]{1,0:T(8,128)(2,1)} %constant_dynamic-update-slice_fusion.14), channel_id=1, source_target_pairs={{0,16},{16,0},{1,17},{17,1},{2,18},{18,2},{3,19},{19,3},{4,20},{20... | collective-permute-start | bytes 3145736 | tf_op jit(solution)/shard_map/ppermute | solution.py:519
  168.9 59.3 %collective-permute-start.18 = (bf16[2816,128]{1,0:T(8,128)(2,1)S(1)}, bf16[2816,128]{1,0:T(8,128)(2,1)}, u32[]{:S(2)}, u32[]{:S(2)}) collective-permute-start(bf16[2816,128]{1,0:T(8,128)(2,1)S(1)} %constant_dynamic-slice_fusion.45), channel_id=1, source_target_pairs={{0,16},{16,0},{1,17},{17,1},{2,18},{18,2},{3,19},{19,3},{4,20},{20... | collective-permute-start | bytes 2162696 | tf_op jit(solution)/shard_map/ppermute | solution.py:519
  224.1 73.5 %collective-permute-start.20 = (bf16[1024,1024]{1,0:T(8,128)(2,1)}, bf16[1024,1024]{1,0:T(8,128)(2,1)}, u32[]{:S(2)}, u32[]{:S(2)}) collective-permute-start(bf16[1024,1024]{1,0:T(8,128)(2,1)} %constant_dynamic-update-slice_fusion.23), channel_id=1, source_target_pairs={{0,8},{8,0},{1,9},{9,1},{2,10},{10,2},{3,11},{11,3},{4,12},{12,4},... | collective-permute-start | bytes 6291464 | tf_op jit(solution)/shard_map/ppermute | solution.py:519
  230.2 63.6 %collective-permute-start.21 = (bf16[2816,256]{1,0:T(8,128)(2,1)}, bf16[2816,256]{1,0:T(8,128)(2,1)}, u32[]{:S(2)}, u32[]{:S(2)}) collective-permute-start(bf16[2816,256]{1,0:T(8,128)(2,1)} %constant_dynamic-update-slice_fusion.25), channel_id=1, source_target_pairs={{0,1},{1,0},{2,3},{3,2},{4,5},{5,4},{6,7},{7,6},{8,9},{9,8},{10,11... | collective-permute-start | bytes 4325384 | tf_op jit(solution)/shard_map/ppermute | solution.py:519
  244.9 28.2 %collective-permute-start.19 = (bf16[8,128,256]{2,1,0:T(8,128)(2,1)S(1)}, bf16[8,128,256]{2,1,0:T(8,128)(2,1)S(1)}, u32[]{:S(2)}, u32[]{:S(2)}) collective-permute-start(bf16[8,128,256]{2,1,0:T(8,128)(2,1)S(1)} %convert_element_type.354), channel_id=1, source_target_pairs={{0,1},{2,3},{4,5},{6,7},{8,9},{10,11},{12,13},{14,15},{16,17},{18,... | collective-permute-start | bytes 1572872 | tf_op jit(solution)/shard_map/ppermute | solution.py:443
  297.6 16.1 %collective-permute-start.22 = (bf16[2816,512]{1,0:T(8,128)(2,1)}, bf16[2816,512]{1,0:T(8,128)(2,1)}, u32[]{:S(2)}, u32[]{:S(2)}) collective-permute-start(bf16[2816,512]{1,0:T(8,128)(2,1)} %constant_dynamic-update-slice_fusion.27), channel_id=1, source_target_pairs={{0,8},{8,0},{1,9},{9,1},{2,10},{10,2},{3,11},{11,3},{4,12},{12,4},... | collective-permute-start | bytes 8650760 | tf_op jit(solution)/shard_map/ppermute | solution.py:519
  337.6 22.7 %collective-permute-start.23 = (bf16[2816,512]{1,0:T(8,128)(2,1)}, bf16[2816,512]{1,0:T(8,128)(2,1)}, u32[]{:S(2)}, u32[]{:S(2)}) collective-permute-start(bf16[2816,512]{1,0:T(8,128)(2,1)} %convolution_convert_fusion.1), channel_id=1, source_target_pairs={{0,8},{8,0},{1,9},{9,1},{2,10},{10,2},{3,11},{11,3},{4,12},{12,4},... | collective-permute-start | bytes 8650760 | tf_op jit(solution)/shard_map/ppermute | solution.py:519
  360.2 101.2 %collective-permute-start.24 = (bf16[1024,2816]{1,0:T(8,128)(2,1)}, bf16[1024,2816]{1,0:T(8,128)(2,1)}, u32[]{:S(2)}, u32[]{:S(2)}) collective-permute-start(bf16[1024,2816]{1,0:T(8,128)(2,1)} %convolution_convert_fusion), channel_id=1, source_target_pairs={{0,8},{8,0},{1,9},{9,1},{2,10},{10,2},{3,11},{11,3},{4,12},{12,4},... | collective-permute-start | bytes 17301512 | tf_op jit(solution)/shard_map/ppermute | solution.py:519
  394.1 21.1 %collective-permute-start.26 = (bf16[1024,1024]{1,0:T(8,128)(2,1)S(1)}, bf16[1024,1024]{1,0:T(8,128)(2,1)S(1)}, u32[]{:S(2)}, u32[]{:S(2)}) collective-permute-start(bf16[1024,1024]{1,0:T(8,128)(2,1)S(1)} %convolution_convert_fusion.5), channel_id=1, source_target_pairs={{0,8},{8,0},{1,9},{9,1},{2,10},{10,2},{3,11},{11,3},{4,12},{12,4},... | collective-permute-start | bytes 6291464 | tf_op jit(solution)/shard_map/ppermute | solution.py:519
  411.6 41.3 %collective-permute-start.25 = (bf16[2048,512]{1,0:T(8,128)(2,1)}, bf16[2048,512]{1,0:T(8,128)(2,1)}, u32[]{:S(2)}, u32[]{:S(2)}) collective-permute-start(bf16[2048,512]{1,0:T(8,128)(2,1)} %convolution_convert_fusion.2), channel_id=1, source_target_pairs={{0,8},{8,0},{1,9},{9,1},{2,10},{10,2},{3,11},{11,3},{4,12},{12,4},... | collective-permute-start | bytes 6291464 | tf_op jit(solution)/shard_map/ppermute | solution.py:519
  412.7 35.2 %collective-permute-start.28 = (bf16[2816,256]{1,0:T(8,128)(2,1)}, bf16[2816,256]{1,0:T(8,128)(2,1)}, u32[]{:S(2)}, u32[]{:S(2)}) collective-permute-start(bf16[2816,256]{1,0:T(8,128)(2,1)} %add_convert_fusion.5), channel_id=1, source_target_pairs={{0,1},{1,0},{2,3},{3,2},{4,5},{5,4},{6,7},{7,6},{8,9},{9,8},{10,11... | collective-permute-start | bytes 4325384 | tf_op jit(solution)/shard_map/ppermute | solution.py:519
  416.9 25.5 %collective-permute-start.30 = (bf16[1024,512]{1,0:T(8,128)(2,1)}, bf16[1024,512]{1,0:T(8,128)(2,1)}, u32[]{:S(2)}, u32[]{:S(2)}) collective-permute-start(bf16[1024,512]{1,0:T(8,128)(2,1)} %add_convert_fusion.8), channel_id=1, source_target_pairs={{0,16},{16,0},{1,17},{17,1},{2,18},{18,2},{3,19},{19,3},{4,20},{20... | collective-permute-start | bytes 3145736 | tf_op jit(solution)/shard_map/ppermute | solution.py:519
  443.9 15.0 %collective-permute-start.43 = (bf16[1024,256]{1,0:T(8,128)(2,1)S(1)}, bf16[1024,256]{1,0:T(8,128)(2,1)S(1)}, u32[]{:S(2)}, u32[]{:S(2)}) collective-permute-start(bf16[1024,256]{1,0:T(8,128)(2,1)S(1)} %add_convert_fusion.19), channel_id=1, source_target_pairs={{0,1},{1,0},{2,3},{3,2},{4,5},{5,4},{6,7},{7,6},{8,9},{9,8},{10,11... | collective-permute-start | bytes 1572872 | tf_op jit(solution)/shard_map/ppermute | solution.py:519
  450.9 33.4 %collective-permute-start.41 = (bf16[2816,128]{1,0:T(8,128)(2,1)}, bf16[2816,128]{1,0:T(8,128)(2,1)}, u32[]{:S(2)}, u32[]{:S(2)}) collective-permute-start(bf16[2816,128]{1,0:T(8,128)(2,1)} %add_convert_fusion.12), channel_id=1, source_target_pairs={{0,16},{16,0},{1,17},{17,1},{2,18},{18,2},{3,19},{19,3},{4,20},{20... | collective-permute-start | bytes 2162696 | tf_op jit(solution)/shard_map/ppermute | solution.py:519
  455.8 33.4 %collective-permute-start.29 = (bf16[2048,256]{1,0:T(8,128)(2,1)}, bf16[2048,256]{1,0:T(8,128)(2,1)}, u32[]{:S(2)}, u32[]{:S(2)}) collective-permute-start(bf16[2048,256]{1,0:T(8,128)(2,1)} %add_convert_fusion.9), channel_id=1, source_target_pairs={{0,1},{1,0},{2,3},{3,2},{4,5},{5,4},{6,7},{7,6},{8,9},{9,8},{10,11... | collective-permute-start | bytes 3145736 | tf_op jit(solution)/shard_map/ppermute | solution.py:519
  461.2 203.4 %reduce-scatter.8.cloned.1.call-start = ((), (), s32[]{:S(2)}) async-start(), calls=%async_computation.8 | async-start | bytes 901120 | tf_op jit(solution)/shard_map/reduce_scatter | solution.py:569
  482.8 15.4 %collective-permute-start.27 = (bf16[8,128,256]{2,1,0:T(8,128)(2,1)}, bf16[8,128,256]{2,1,0:T(8,128)(2,1)}, u32[]{:S(2)}, u32[]{:S(2)}) collective-permute-start(bf16[8,128,256]{2,1,0:T(8,128)(2,1)} %convert_element_type.381), channel_id=1, source_target_pairs={{1,0},{3,2},{5,4},{7,6},{9,8},{11,10},{13,12},{15,14},{17,16},{19,... | collective-permute-start | bytes 1572872 | tf_op jit(solution)/shard_map/ppermute | solution.py:461
  487.1 177.5 %reduce-scatter.10.cloned.1.call-start = ((), (), s32[]{:S(2)}) async-start(), calls=%async_computation.9 | async-start | bytes 655360 | tf_op jit(solution)/shard_map/reduce_scatter | solution.py:569
  487.1 98.8 %collective-permute-start.52 = (bf16[1024,1408]{1,0:T(8,128)(2,1)}, bf16[1024,1408]{1,0:T(8,128)(2,1)}, u32[]{:S(2)}, u32[]{:S(2)}) collective-permute-start(bf16[1024,1408]{1,0:T(8,128)(2,1)} %add_convert_fusion.2), channel_id=1, source_target_pairs={{0,16},{16,0},{1,17},{17,1},{2,18},{18,2},{3,19},{19,3},{4,20},{20... | collective-permute-start | bytes 8650760 | tf_op jit(solution)/shard_map/ppermute | solution.py:519
  491.9 102.0 %collective-permute-start.42 = (bf16[2048,128]{1,0:T(8,128)(2,1)}, bf16[2048,128]{1,0:T(8,128)(2,1)}, u32[]{:S(2)}, u32[]{:S(2)}) collective-permute-start(bf16[2048,128]{1,0:T(8,128)(2,1)} %add_convert_fusion.20), channel_id=1, source_target_pairs={{0,16},{16,0},{1,17},{17,1},{2,18},{18,2},{3,19},{19,3},{4,20},{20... | collective-permute-start | bytes 1572872 | tf_op jit(solution)/shard_map/ppermute | solution.py:519
  560.6 7.1 collective-permute-start.31
  572.9 56.4 %collective-permute-start.35 = (bf16[1024,1024]{1,0:T(8,128)(2,1)}, bf16[1024,1024]{1,0:T(8,128)(2,1)}, u32[]{:S(2)}, u32[]{:S(2)}) collective-permute-start(bf16[1024,1024]{1,0:T(8,128)(2,1)} %convolution_convert_fusion.3), channel_id=1, source_target_pairs={{0,8},{8,0},{1,9},{9,1},{2,10},{10,2},{3,11},{11,3},{4,12},{12,4},... | collective-permute-start | bytes 6291464 | tf_op jit(solution)/shard_map/ppermute | solution.py:519
  575.8 56.8 %collective-permute-start.32 = (bf16[1024,1024]{1,0:T(8,128)(2,1)}, bf16[1024,1024]{1,0:T(8,128)(2,1)}, u32[]{:S(2)}, u32[]{:S(2)}) collective-permute-start(bf16[1024,1024]{1,0:T(8,128)(2,1)} %convolution_convert_fusion.4), channel_id=1, source_target_pairs={{0,8},{8,0},{1,9},{9,1},{2,10},{10,2},{3,11},{11,3},{4,12},{12,4},... | collective-permute-start | bytes 6291464 | tf_op jit(solution)/shard_map/ppermute | solution.py:519
  590.3 33.8 %collective-permute-start.53 = (bf16[512,1408]{1,0:T(8,128)(2,1)}, bf16[512,1408]{1,0:T(8,128)(2,1)}, u32[]{:S(2)}, u32[]{:S(2)}) collective-permute-start(bf16[512,1408]{1,0:T(8,128)(2,1)} %add_convert_fusion.4), channel_id=1, source_target_pairs={{0,1},{1,0},{2,3},{3,2},{4,5},{5,4},{6,7},{7,6},{8,9},{9,8},{10,11... | collective-permute-start | bytes 4325384 | tf_op jit(solution)/shard_map/ppermute | solution.py:519
  596.5 85.6 %reduce-scatter.14.cloned.1.call-start = ((), (), s32[]{:S(2)}) async-start(), calls=%async_computation.11 | async-start | bytes 1802240 | tf_op jit(solution)/shard_map/reduce_scatter | solution.py:569
  629.0 78.0 %reduce-scatter.6.cloned.1.call-start = ((), (), s32[]{:S(2)}) async-start(), calls=%async_computation.7 | async-start | bytes 1310720 | tf_op jit(solution)/shard_map/reduce_scatter | solution.py:569
  632.4 24.6 %collective-permute-start.36 = (bf16[1024,512]{1,0:T(8,128)(2,1)}, bf16[1024,512]{1,0:T(8,128)(2,1)}, u32[]{:S(2)}, u32[]{:S(2)}) collective-permute-start(bf16[1024,512]{1,0:T(8,128)(2,1)} %add_convert_fusion.6), channel_id=1, source_target_pairs={{0,1},{1,0},{2,3},{3,2},{4,5},{5,4},{6,7},{7,6},{8,9},{9,8},{10,11... | collective-permute-start | bytes 3145736 | tf_op jit(solution)/shard_map/ppermute | solution.py:519
  635.6 25.8 %collective-permute-start.33 = (bf16[1024,512]{1,0:T(8,128)(2,1)}, bf16[1024,512]{1,0:T(8,128)(2,1)}, u32[]{:S(2)}, u32[]{:S(2)}) collective-permute-start(bf16[1024,512]{1,0:T(8,128)(2,1)} %add_convert_fusion.7), channel_id=1, source_target_pairs={{0,16},{16,0},{1,17},{17,1},{2,18},{18,2},{3,19},{19,3},{4,20},{20... | collective-permute-start | bytes 3145736 | tf_op jit(solution)/shard_map/ppermute | solution.py:519
  659.4 12.7 %collective-permute-start.37 = (bf16[1024,256]{1,0:T(8,128)(2,1)}, bf16[1024,256]{1,0:T(8,128)(2,1)}, u32[]{:S(2)}, u32[]{:S(2)}) collective-permute-start(bf16[1024,256]{1,0:T(8,128)(2,1)} %add_convert_fusion.16), channel_id=1, source_target_pairs={{0,16},{16,0},{1,17},{17,1},{2,18},{18,2},{3,19},{19,3},{4,20},{20... | collective-permute-start | bytes 1572872 | tf_op jit(solution)/shard_map/ppermute | solution.py:519
  663.9 15.2 %collective-permute-start.34 = (bf16[1024,256]{1,0:T(8,128)(2,1)}, bf16[1024,256]{1,0:T(8,128)(2,1)}, u32[]{:S(2)}, u32[]{:S(2)}) collective-permute-start(bf16[1024,256]{1,0:T(8,128)(2,1)} %add_convert_fusion.18), channel_id=1, source_target_pairs={{0,1},{1,0},{2,3},{3,2},{4,5},{5,4},{6,7},{7,6},{8,9},{9,8},{10,11... | collective-permute-start | bytes 1572872 | tf_op jit(solution)/shard_map/ppermute | solution.py:519
  665.6 25.6 %collective-permute-start.44 = (bf16[1,1728,128]{2,1,0:T(8,128)(2,1)S(1)}, bf16[1,1728,128]{2,1,0:T(8,128)(2,1)}, u32[]{:S(2)}, u32[]{:S(2)}) collective-permute-start(bf16[1,1728,128]{2,1,0:T(8,128)(2,1)S(1)} %maximum_bitcast_fusion), channel_id=1, source_target_pairs={{0,1},{1,0},{2,3},{3,2},{4,5},{5,4},{6,7},{7,6},{8,9},{9,8},{10,11... | collective-permute-start | bytes 1327112 | tf_op jit(solution)/shard_map/ppermute | solution.py:519
  690.6 19.0 %collective-permute-start.54 = (bf16[1,1408,128]{2,1,0:T(8,128)(2,1)S(1)}, bf16[1,1408,128]{2,1,0:T(8,128)(2,1)}, u32[]{:S(2)}, u32[]{:S(2)}) collective-permute-start(bf16[1,1408,128]{2,1,0:T(8,128)(2,1)S(1)} %bitcast.235), channel_id=1, source_target_pairs={{0,1},{1,0},{2,3},{3,2},{4,5},{5,4},{6,7},{7,6},{8,9},{9,8},{10,11... | collective-permute-start | bytes 1081352 | tf_op jit(solution)/shard_map/ppermute | solution.py:519
  693.3 40.1 %collective-permute-start.45 = (bf16[2,1728,128]{2,1,0:T(8,128)(2,1)}, bf16[2,1728,128]{2,1,0:T(8,128)(2,1)}, u32[]{:S(2)}, u32[]{:S(2)}) collective-permute-start(bf16[2,1728,128]{2,1,0:T(8,128)(2,1)} %pad_maximum_fusion.8), channel_id=1, source_target_pairs={{0,16},{16,0},{1,17},{17,1},{2,18},{18,2},{3,19},{19,3},{4,20},{20... | collective-permute-start | bytes 2654216 | tf_op jit(solution)/shard_map/ppermute | solution.py:519
  695.0 17.9 %collective-permute-start.47 = (f32[280,128]{1,0:T(8,128)S(1)}, f32[280,128]{1,0:T(8,128)}, u32[]{:S(2)}, u32[]{:S(2)}) collective-permute-start(f32[280,128]{1,0:T(8,128)S(1)} %copy-done.72), channel_id=1, source_target_pairs={{0,8},{8,0},{1,9},{9,1},{2,10},{10,2},{3,11},{11,3},{4,12},{12,4},... | collective-permute-start | bytes 430088 | tf_op jit(solution)/shard_map/ppermute | solution.py:519
  708.0 23.8 %collective-permute-start.38 = (bf16[1,1024,128]{2,1,0:T(8,128)(2,1)S(1)}, bf16[1,1024,128]{2,1,0:T(8,128)(2,1)S(1)}, u32[]{:S(2)}, u32[]{:S(2)}) collective-permute-start(bf16[1,1024,128]{2,1,0:T(8,128)(2,1)S(1)} %maximum_bitcast_fusion.1), channel_id=1, source_target_pairs={{0,1},{1,0},{2,3},{3,2},{4,5},{5,4},{6,7},{7,6},{8,9},{9,8},{10,11... | collective-permute-start | bytes 786440 | tf_op jit(solution)/shard_map/ppermute | solution.py:519
  710.6 25.9 %collective-permute-start.55 = (bf16[2,1408,128]{2,1,0:T(8,128)(2,1)S(1)}, bf16[2,1408,128]{2,1,0:T(8,128)(2,1)S(1)}, u32[]{:S(2)}, u32[]{:S(2)}) collective-permute-start(bf16[2,1408,128]{2,1,0:T(8,128)(2,1)S(1)} %pad_maximum_fusion.14), channel_id=1, source_target_pairs={{0,16},{16,0},{1,17},{17,1},{2,18},{18,2},{3,19},{19,3},{4,20},{20... | collective-permute-start | bytes 2162696 | tf_op jit(solution)/shard_map/ppermute | solution.py:519
  713.9 17.3 %collective-permute-start.48 = (f32[280,128]{1,0:T(8,128)S(1)}, f32[280,128]{1,0:T(8,128)S(1)}, u32[]{:S(2)}, u32[]{:S(2)}) collective-permute-start(f32[280,128]{1,0:T(8,128)S(1)} %add.824), channel_id=1, source_target_pairs={{0,16},{16,0},{1,17},{17,1},{2,18},{18,2},{3,19},{19,3},{4,20},{20... | collective-permute-start | bytes 430088 | tf_op jit(solution)/shard_map/ppermute | solution.py:519
  731.2 5.2 collective-permute-start.49
  731.9 12.1 %collective-permute-start.39 = (bf16[2,1024,128]{2,1,0:T(8,128)(2,1)S(1)}, bf16[2,1024,128]{2,1,0:T(8,128)(2,1)S(1)}, u32[]{:S(2)}, u32[]{:S(2)}) collective-permute-start(bf16[2,1024,128]{2,1,0:T(8,128)(2,1)S(1)} %pad_maximum_fusion.15), channel_id=1, source_target_pairs={{0,16},{16,0},{1,17},{17,1},{2,18},{18,2},{3,19},{19,3},{4,20},{20... | collective-permute-start | bytes 1572872 | tf_op jit(solution)/shard_map/ppermute | solution.py:519
  734.9 22.2 %collective-permute-start.46 = (bf16[4,1728,128]{2,1,0:T(8,128)(2,1)S(1)}, bf16[4,1728,128]{2,1,0:T(8,128)(2,1)}, u32[]{:S(2)}, u32[]{:S(2)}) collective-permute-start(bf16[4,1728,128]{2,1,0:T(8,128)(2,1)S(1)} %pad_maximum_fusion.2.refs_2_.refs_0_), channel_id=1, source_target_pairs={{0,8},{8,0},{1,9},{9,1},{2,10},{10,2},{3,11},{11,3},{4,12},{12,4},... | collective-permute-start | bytes 5308424 | tf_op jit(solution)/shard_map/ppermute | solution.py:519
  736.4 5.2 collective-permute-start.50
  738.9 29.2 %collective-permute-start.56 = (bf16[4,1408,128]{2,1,0:T(8,128)(2,1)}, bf16[4,1408,128]{2,1,0:T(8,128)(2,1)}, u32[]{:S(2)}, u32[]{:S(2)}) collective-permute-start(bf16[4,1408,128]{2,1,0:T(8,128)(2,1)} %pad_maximum_fusion.3.refs_0_), channel_id=1, source_target_pairs={{0,8},{8,0},{1,9},{9,1},{2,10},{10,2},{3,11},{11,3},{4,12},{12,4},... | collective-permute-start | bytes 4325384 | tf_op jit(solution)/shard_map/ppermute | solution.py:519
  741.6 8.0 %collective-permute-start.51 = (f32[280,128]{1,0:T(8,128)S(1)}, f32[280,128]{1,0:T(8,128)S(1)}, u32[]{:S(2)}, u32[]{:S(2)}) collective-permute-start(f32[280,128]{1,0:T(8,128)S(1)} %add.827), channel_id=1, source_target_pairs={{0,4},{2,6},{4,0},{6,2},{1,5},{3,7},{5,1},{7,3},{8,12},{10,14},{12... | collective-permute-start | bytes 430088 | tf_op jit(solution)/shard_map/ppermute | solution.py:788
  745.1 17.0 %collective-permute-start.40 = (bf16[4,1024,128]{2,1,0:T(8,128)(2,1)}, bf16[4,1024,128]{2,1,0:T(8,128)(2,1)}, u32[]{:S(2)}, u32[]{:S(2)}) collective-permute-start(bf16[4,1024,128]{2,1,0:T(8,128)(2,1)} %pad_maximum_fusion.7.refs_0_), channel_id=1, source_target_pairs={{0,8},{8,0},{1,9},{9,1},{2,10},{10,2},{3,11},{11,3},{4,12},{12,4},... | collective-permute-start | bytes 3145736 | tf_op jit(solution)/shard_map/ppermute | solution.py:519
  (151 other events, 1629.6 us)
Sparse Core Ops, SparseCore 0:
  10.9 85.6 all-gather.2
  99.5 130.2 all-gather.4
  461.3 20.7 reduce-scatter.11
  487.2 23.4 reduce-scatter.7
  596.6 20.7 reduce-scatter.9
  629.1 31.0 reduce-scatter.13
  682.2 24.7 reduce-scatter.5

commit v5 on v4

--- a/solution.py
+++ b/solution.py
@@ -59,17 +59,28 @@
     return value[h * BLOCK : (h + 1) * BLOCK]
 
 
-def columns(col_ref, block, group):
-    packed = col_ref[block, group]
-    return [packed[:, i : i + 1] for i in range(6)]
-
-
-def decay_matrix(cum, doc, row_ref, block, group):
-    rows = row_ref[block, group]
+def columns(feat_ref, block, group):
+    packed = feat_ref[pl.ds(pl.multiple_of(block * BLOCK, BLOCK), BLOCK), :]
+    return [
+        jnp.concatenate(
+            [
+                packed[:, f * H + group * STACK + h : f * H + group * STACK + h + 1]
+                for h in range(STACK)
+            ],
+            axis=0,
+        )
+        for f in range(6)
+    ]
+
+
+def decay_matrix(cum, doc):
     i = lax.broadcasted_iota(jnp.int32, (ROWS, ROWS), 0)
     j = lax.broadcasted_iota(jnp.int32, (ROWS, ROWS), 1)
-    inside = ((i // BLOCK) == (j // BLOCK)) & (i >= j) & (doc == rows[1:2])
-    decay = jnp.exp(jnp.where(inside, cum - rows[0:1], -1e30))
+    cum_row, doc_row = (
+        jnp.sum(jnp.where(i == j, c, 0.0), axis=0, keepdims=True) for c in (cum, doc)
+    )
+    inside = ((i // BLOCK) == (j // BLOCK)) & (i >= j) & (doc == doc_row)
+    decay = jnp.exp(jnp.where(inside, cum - cum_row, -1e30))
     return decay, jnp.where(i > j, decay, 0.0)
 
 
@@ -133,14 +144,14 @@
         chunk(c, False)
 
 
-def inverse_kernel(n_ref, col_ref, row_ref, inv_ref):
+def inverse_kernel(n_ref, col_ref, inv_ref):
     @pl.loop(0, n_ref.shape[0] // BLOCK)
     def _(block):
         lowers = []
         for group in range(H // STACK):
             cum, beta, _, _, _, doc = columns(col_ref, block, group)
             keys = stack_heads(n_ref, block, group, H * DK, DK)
-            _, strict = decay_matrix(cum, doc, row_ref, block, group)
+            _, strict = decay_matrix(cum, doc)
             lowers.append(beta * mm(keys, keys, ((1,), (1,))) * strict)
         for group, inverse in enumerate(unit_inverses(lowers)):
             inv_ref[block, group] = inverse
@@ -170,7 +181,7 @@
     state_steps(n_ref, inv_ref, col_ref, state_ref)
 
 
-def scan_kernel(n_ref, inv_ref, col_ref, row_ref, start_ref, out_ref, cor_ref, states_ref, state):
+def scan_kernel(n_ref, inv_ref, col_ref, start_ref, out_ref, cor_ref, states_ref, state):
     state[...] = start_ref[...].astype(F32)
 
     @pl.loop(0, n_ref.shape[0] // BLOCK)
@@ -180,7 +191,7 @@
             queries = stack_heads(n_ref, block, group, 0, DK)
             keys = stack_heads(n_ref, block, group, H * DK, DK)
             values = stack_heads(n_ref, block, group, 2 * H * DK, DV).astype(F32)
-            within, _ = decay_matrix(cum, doc, row_ref, block, group)
+            within, _ = decay_matrix(cum, doc)
             scores = SCALE * mm(queries, keys, ((1,), (1,))) * within
             both = []
             for h in range(STACK):
@@ -201,7 +212,7 @@
                 )
 
 
-def back_state_kernel(n_ref, inv_ref, col_ref, row_ref, dout_ref, start_ref, dstate_ref):
+def back_state_kernel(n_ref, inv_ref, col_ref, dout_ref, start_ref, dstate_ref):
     blocks = n_ref.shape[0] // BLOCK
     dstate_ref[...] = start_ref[...].astype(F32)
 
@@ -212,7 +223,7 @@
             cum, beta, a, d, kappa, doc = columns(col_ref, block, group)
             queries = stack_heads(n_ref, block, group, 0, DK)
             keys = stack_heads(n_ref, block, group, H * DK, DK)
-            within, _ = decay_matrix(cum, doc, row_ref, block, group)
+            within, _ = decay_matrix(cum, doc)
             scores = SCALE * mm(queries, keys, ((1,), (1,))) * within
             dout = stack_heads(dout_ref, block, group, 0, DV)
             wide = (SCALE * a) * dout.astype(F32)
@@ -235,14 +246,13 @@
     n_ref,
     inv_ref,
     col_ref,
-    row_ref,
+
     dout_ref,
     cor_ref,
     states_ref,
     start_ref,
     dn_ref,
-    gcol_ref,
-    grow_ref,
+    gfeat_ref,
     dstate,
 ):
     length = n_ref.shape[0]
@@ -252,12 +262,13 @@
     @pl.loop(0, blocks)
     def _(step):
         block = blocks - 1 - step
+        packed = jnp.zeros((BLOCK, 128), F32)
         for group in range(H // STACK):
             cum, beta, a, d, kappa, doc = columns(col_ref, block, group)
             queries = stack_heads(n_ref, block, group, 0, DK)
             keys = stack_heads(n_ref, block, group, H * DK, DK)
             values = stack_heads(n_ref, block, group, 2 * H * DK, DV).astype(F32)
-            within, strict = decay_matrix(cum, doc, row_ref, block, group)
+            within, strict = decay_matrix(cum, doc)
             scores = SCALE * mm(queries, keys, ((1,), (1,))) * within
             weighted = mm(keys, keys, ((1,), (1,))) * strict
             dout = stack_heads(dout_ref, block, group, 0, DV)
@@ -324,14 +335,15 @@
             )
             d_a = jnp.sum(SCALE * dout_wide * asked - scaled * seen, axis=1, keepdims=True)
             d_d = jnp.sum(cor_wide * pulled, axis=1, keepdims=True)
-            lane = lax.broadcasted_iota(jnp.int32, (ROWS, 8), 1)
-            packed = jnp.zeros((ROWS, 8), F32)
-            for i, part in enumerate((d_cum, d_beta, d_a, d_d, d_kappa)):
-                packed = jnp.where(lane == i, part, packed)
-            gcol_ref[block, group] = packed
-            grow_ref[block, group] = jnp.broadcast_to(
-                -jnp.sum(spread, axis=0, keepdims=True), (8, ROWS)
-            )
+            i = lax.broadcasted_iota(jnp.int32, (ROWS, ROWS), 0)
+            j = lax.broadcasted_iota(jnp.int32, (ROWS, ROWS), 1)
+            by_column = jnp.sum(spread, axis=0, keepdims=True)
+            d_cum = d_cum - jnp.sum(jnp.where(i == j, by_column, 0.0), axis=1, keepdims=True)
+            lane = lax.broadcasted_iota(jnp.int32, (BLOCK, 128), 1)
+            for f, part in enumerate((d_cum, d_beta, d_a, d_d, d_kappa)):
+                for h in range(STACK):
+                    packed = jnp.where(lane == f * H + group * STACK + h, head(part, h), packed)
+        gfeat_ref[pl.ds(pl.multiple_of(block * BLOCK, BLOCK), BLOCK), :] = packed
 
 
 def conv_back_kernel(x_ref, cw_ref, mask_ref, dn_ref, dx_ref, dcw_ref):
@@ -395,36 +407,33 @@
         + [jnp.zeros((length,), F32)] * (8 - CONV + 1),
         axis=1,
     )
-    doc_blocks = docs.reshape(blocks, 1, BLOCK)
-    before = jnp.concatenate([near[HALO - 1 : HALO], doc_blocks[:-1, 0, -1]]).reshape(
-        blocks, 1, 1
-    )
-    last = doc_blocks[:, :, -1:]
+    doc_blocks = docs.reshape(blocks, BLOCK, 1)
+    before = near[HALO - 1 : -1].reshape(blocks, BLOCK, 1)[:, :1]
+    last = doc_blocks[:, -1:]
     from_before = (doc_blocks == before).astype(F32)
     to_last = (doc_blocks == last).astype(F32)
     kept = (last == before).astype(F32)
 
     def small(rates, decay):
-        by_block = jnp.transpose(rates.reshape(blocks, BLOCK, H, 2), (3, 0, 2, 1))
-        beta = jax.nn.sigmoid(by_block[1])
-        offset = decay[1].reshape(1, H, 1)
-        log_decay = -jnp.exp(decay[0]).reshape(1, H, 1) * jax.nn.softplus(by_block[0] + offset)
+        beta = jax.nn.sigmoid(rates[:, H:]).reshape(blocks, BLOCK, H)
+        log_decay = -jnp.exp(decay[:1]) * jax.nn.softplus(rates[:, :H] + decay[1:])
         i = lax.broadcasted_iota(jnp.int32, (BLOCK, BLOCK), 0)
         j = lax.broadcasted_iota(jnp.int32, (BLOCK, BLOCK), 1)
-        upper = (i <= j).astype(F32)
-        cum = jnp.einsum("bhi,ij->bhj", log_decay, upper, precision=lax.Precision.HIGHEST)
-        final = cum[:, :, -1:]
+        cum = jnp.einsum(
+            "bih,ij->bjh",
+            log_decay.reshape(blocks, BLOCK, H),
+            (i <= j).astype(F32),
+            precision=lax.Precision.HIGHEST,
+        )
+        final = cum[:, -1:]
         a = jnp.exp(cum) * from_before
         d = jnp.exp(final - cum) * to_last
         kappa = jnp.broadcast_to(jnp.exp(final) * kept, cum.shape)
-        return jnp.stack([cum, beta, a, d, kappa], axis=0)
+        return jnp.concatenate([cum, beta, a, d, kappa], axis=2).reshape(length, 5 * H)
 
     five, pull_small = jax.vjp(small, rates, decay)
-    doc_row = jnp.broadcast_to(doc_blocks.astype(F32), (blocks, H, BLOCK))
-    packed = jnp.concatenate([five, doc_row[None], jnp.zeros((2,) + doc_row.shape, F32)], axis=0)
-    packed = packed.reshape(8, blocks, groups, ROWS)
-    col = jnp.transpose(packed, (1, 2, 3, 0))
-    row = jnp.transpose(jnp.stack([packed[0], packed[5]] + [packed[6]] * 6), (1, 2, 0, 3))
+    doc_lanes = jnp.broadcast_to(docs.astype(F32)[:, None], (length, H))
+    col = jnp.concatenate([five, doc_lanes, jnp.zeros((length, 128 - 6 * H), F32)], axis=1)
 
     n_shape = ((length, channels), BF16)
     inv_shape = ((blocks, groups, ROWS, ROWS), F32)
@@ -432,8 +441,9 @@
     cor_shape = ((blocks, groups, ROWS, ROWS), BF16)
     x = points("conv", x)
     (n,) = call(conv_kernel, [n_shape], [], x, weights, masks)
+    n = points("conv_done", n)
     n = points("inverse", n)
-    (inv,) = call(inverse_kernel, [inv_shape], [], n, col, row)
+    (inv,) = call(inverse_kernel, [inv_shape], [], n, col)
     inv = points("state", inv)
     start = jnp.zeros((H, DK, DV), BF16)
     ahead = [(i, i + 1) for i in range(sp_size - 1)]
@@ -448,7 +458,6 @@
         n,
         inv,
         col,
-        row,
         start,
     )
 
@@ -456,23 +465,21 @@
         dstart = jnp.zeros((H, DK, DV), BF16)
         for _ in range(sp_size - 1):
             (dstate,) = call(
-                back_state_kernel, [state_shape], [], n, inv, col, row, dout, dstart
+                back_state_kernel, [state_shape], [], n, inv, col, dout, dstart
             )
-            dstart = lax.ppermute(dstate.astype(BF16), "sp", behind)
+            dstart = lax.ppermute(points("sent", dstate.astype(BF16)), "sp", behind)
         dstart = points("back", dstart)
-        dn, gcol, grow = call(
+        dn, gfeat = call(
             back_kernel,
             [
                 ((length, channels), F32),
-                ((blocks, groups, ROWS, 8), F32),
-                ((blocks, groups, 8, ROWS), F32),
+                ((length, 128), F32),
             ],
             [pltpu.VMEM((H, DK, DV), F32)],
             n,
             inv,
             col,
-            row,
-            dout,
+                dout,
             cor,
             states,
             dstart,
@@ -487,9 +494,7 @@
             masks,
             dn,
         )
-        grads = jnp.transpose(gcol[..., :5], (3, 0, 1, 2))
-        grads = grads.at[0].add(grow[:, :, 0])
-        d_rates, d_decay = pull_small(grads.reshape(5, blocks, H, BLOCK))
+        d_rates, d_decay = pull_small(gfeat[:, : 5 * H])
         from_next = lax.ppermute(dx[:HALO], "sp", behind)
         return dx, from_next, dcw, d_rates, d_decay
 
@@ -512,7 +517,7 @@
 
 
 def after(value, *earlier):
-    return lax.optimization_barrier((value,) + earlier)[0]
+    return lax.optimization_barrier((value,) + earlier)[0] if earlier else value
 
 
 def swap(value, axis):
@@ -557,9 +562,9 @@
     return lax.ppermute(value, "fsdp", [(i, (i + step) % count) for i in range(count)])
 
 
-def gather_blocks(piece):
+def gather_blocks(piece, *late):
     count, rows = lax.axis_size("fsdp"), piece.shape[0]
-    parts = [piece] + [shifted(piece, s) for s in range(1, count)]
+    parts = [piece] + [after(shifted(piece, s), *late) for s in range(1, count)]
     line = jnp.concatenate([parts[(count - 1 - i) % count] for i in range(2 * count - 1)], axis=0)
     start = (count - 1 - lax.axis_index("fsdp")) * rows
     return lax.dynamic_slice_in_dim(line, start, count * rows, 0)
@@ -591,8 +596,8 @@
         self.first = first
         self.piece = lax.dynamic_slice_in_dim(shard, place(first, 0) * width, width, 1)
 
-    def blocks(self, *earlier):
-        self.held = gather_blocks(after(self.piece, *earlier) if earlier else self.piece)
+    def blocks(self, earlier, late):
+        self.held = gather_blocks(after(self.piece, *earlier), late)
         return self.held
 
     def second(self, *earlier):
@@ -638,8 +643,9 @@
         self.from_first = swap(self.outgoing, self.first)
         return self.outgoing
 
-    def third(self):
+    def third(self, *late):
         width = self.width
+        self.from_first = after(self.from_first, *late)
         self.outgoing = (
             grad_dot(self.left, self.right[:, width : 2 * width])
             + self.from_core[:, width : 2 * width].astype(F32)
@@ -663,6 +669,11 @@
     for axis in ("sp", "x"):
         held = jnp.concatenate([held, swap(held, axis)], axis=0)
     return held, swap(held, "core")
+
+
+def spread_aside(blocks):
+    every = lax.all_gather(jnp.concatenate(blocks, axis=0), ("x", "core", "sp"), axis=0)
+    return every[:4], every[4:]
 
 
 def unpack_kernel(segments, count, places_ref, *refs):
@@ -692,13 +703,16 @@
 
 def spread_places():
     core, x, y = lax.axis_index("core"), lax.axis_index("x"), lax.axis_index("sp")
-    table = [[] for _ in range(6)]
+    table = [[] for _ in range(12)]
     for k in range(8):
         c, d, e = (
             1 - bit if (k >> shift) & 1 else bit for shift, bit in ((2, core), (1, x), (0, y))
         )
         for line, value in enumerate((4 * c + 2 * d + e, 0, 4 * c + 2 * e + d, 0, 2 * c + d, e)):
             table[line].append(jnp.asarray(value, jnp.int32))
+        d, c, e = (k >> 2) & 1, (k >> 1) & 1, k & 1
+        for line, value in enumerate((4 * c + 2 * d + e, 0, 4 * c + 2 * e + d, 0, 2 * c + d, e)):
+            table[6 + line].append(jnp.asarray(value, jnp.int32))
     return jnp.stack([jnp.stack(line) for line in table])
 
 
@@ -825,7 +839,7 @@
     qk_way = ColumnGather(input_weight[:, :qk_cols], "x")
     v_way = ColumnGather(input_weight[:, qk_cols:qkv_cols], "sp")
     gate_way = ColumnGather(input_weight[:, qkv_cols:], "x")
-    down_way = ColumnGather(down_weight, "sp")
+    down_way = ColumnGather(down_weight, "x")
     pair_rows, pair_cols = qk_way.piece.shape[0], 2 * qk_way.piece.shape[1]
     smalls = (rate_weight, conv_weight, head_decay, mixer_gain, heads_gain, feed_gain)
     first_load = jnp.concatenate(
@@ -842,13 +856,11 @@
         first_all[:, pair_rows:].reshape(members, -1), smalls
     )
     qkv_second = (qk_way.second(), v_way.second())
-    gate_way.blocks(*qkv_second)
     qkv_third = (qk_way.third(), v_way.third())
-    gate_way.second(*qkv_third)
     qk_full, v_full = qk_way.full(), v_way.full()
     out_full = gather_rows(output_weight)
     up_full = gather_rows(up_weight)
-    rate_full = rate_all.reshape(-1, 2 * H)
+    rate_full = jnp.swapaxes(rate_all.reshape(-1, H, 2), 1, 2).reshape(-1, 2 * H)
     conv_full = jnp.swapaxes(conv_all, 0, 1).reshape(CONV, -1).astype(F32)
     decay_full = jnp.swapaxes(decay_all, 0, 1).reshape(2, H).astype(F32)
     mixer_scale = mixer_all.reshape(-1).astype(F32)
@@ -857,7 +869,12 @@
 
     def points(name, value):
         if name == "conv":
-            down_way.blocks(value)
+            gate_way.blocks(qkv_third, value)
+            gate_way.second()
+            x_ready.append(value)
+            return value
+        if name == "conv_done":
+            down_way.blocks((x_ready[0],), value)
             return value
         if name == "inverse":
             value = after(value, gate_way.held, down_way.held)
@@ -868,13 +885,20 @@
             value = after(value, gate_way.held, down_way.held)
             down_way.third(value)
             return value
+        if name == "sent":
+            for key in ("out", "gate"):
+                sums[key].third(value)
+            return value
         if name == "back":
             return after(value, sums["down"].third())
         if name == "conv_back":
-            return after(value, *(sums[key].third() for key in ("out", "gate")))
+            for key in ("out", "gate"):
+                sums[key].from_second = after(sums[key].from_second, value)
+            owns.extend(sums[key].own().astype(BF16) for key in ("down", "out", "gate"))
+            return after(value, *owns)
         return value
 
-    sums = {}
+    sums, x_ready, owns = {}, [], []
 
     ends = jnp.cumsum(doc_lengths[0])
     positions = lax.broadcasted_iota(jnp.int32, (length * sp_size, 1), 0)
@@ -895,7 +919,7 @@
         axis=1,
     )
     rate_raw = jnp.dot(normed_low, rate_full, preferred_element_type=F32)
-    rates = rate_raw.astype(BF16).astype(F32).reshape(length, H, 2)
+    rates = rate_raw.astype(BF16).astype(F32)
     mixed, pull_mix = mixer(qkv, conv_full, rates, decay_full, doc_ids, member, sp_size, points)
     gate_full, down_full = gate_way.full(), down_way.full()
     gate_raw = reorder(dot_columns(normed_low, gate_full), "x")
@@ -912,9 +936,9 @@
 
     activated, pull_act = jax.vjp(feed_act, gate_up)
     act_low = activated.astype(BF16)
-    block_out = (hidden + reorder(dot_columns(act_low, down_full), "sp")).astype(BF16)
-    cot_rel = reorder(cotangent, "sp")
-    sums["down"] = ColumnSum(act_low, cot_rel, "sp")
+    block_out = (hidden + reorder(dot_columns(act_low, down_full), "x")).astype(BF16)
+    cot_rel = reorder(cotangent, "x")
+    sums["down"] = ColumnSum(act_low, cot_rel, "x")
     d_act = dot_back(cot_rel, down_full)
     d_gu_low = pull_act(d_act)[0].astype(BF16)
     sums["up"] = HalfSum(by_half(two_low), d_gu_low)
@@ -935,30 +959,30 @@
     d_more, from_next, conv_grad, d_rates, decay_grad = pull_mix(d_mixed_low)
     edge = jnp.pad(from_next.astype(F32), ((length - HALO, 0), (0, 0)))
     d_qkv = (d_more[HALO:].astype(F32) + edge).astype(BF16)
-    d_rate_low = d_rates.reshape(length, 2 * H).astype(BF16)
+    d_rate_low = d_rates.astype(BF16)
     d_qk_rel = reorder(d_qkv[:, :qk_cols], "x")
     d_v_rel = reorder(d_qkv[:, qk_cols:], "sp")
     sums["qk"] = ColumnSum(normed_low, d_qk_rel, "x")
     sums["v"] = ColumnSum(normed_low, d_v_rel, "sp")
-    for step in ("second", "third"):
-        for key in ("qk", "v"):
-            getattr(sums[key], step)()
     sums["up"].third()
+    sums["up"].from_y = after(sums["up"].from_y, sums["qk"].second(), sums["v"].second())
+    for key in ("qk", "v"):
+        sums[key].third()
     places = spread_places()
-    blocks = [sum_blocks(sums[k].own()) for k in ("down", "out", "gate")]
+    blocks = [sum_blocks(own) for own in owns]
     down_rows, out_rows = blocks[0].shape[0], blocks[1].shape[0]
-    early_sums = spread([narrow(block) for block in blocks])
+    early_sums = spread_aside([narrow(block) for block in blocks])
     down_shard, output_shard = unpack(
         places,
-        [(0, 0, 0, 0, down_rows, 1, 1), (0, down_rows, 1, 0, out_rows, 1, 1)],
+        [(0, 0, 0, 0, down_rows, 1, 3), (0, down_rows, 1, 0, out_rows, 1, 4)],
         early_sums,
         [down_weight.shape, output_weight.shape],
     )
     up_block = sum_blocks(sums["up"].own())
     (up_shard,) = unpack(
         places,
-        [(0, 0, 0, 0, up_block.shape[0], up_block.shape[1] // 128, 2)],
-        spread([narrow(up_block)]),
+        [(0, 0, 0, 0, up_block.shape[0], up_block.shape[1] // 128, 5)],
+        spread_aside([narrow(up_block)]),
         [up_weight.shape],
     )
     late_block = sum_blocks(jnp.concatenate([sums["qk"].own(), sums["v"].own()], axis=1))
@@ -969,7 +993,7 @@
         [
             (0, 0, 0, 0, rows, wide, 0),
             (0, wide * rows, 0, qk_cols, rows, wide, 1),
-            (1, down_rows + out_rows, 0, qkv_cols, rows, gate_wide, 0),
+            (1, down_rows + out_rows, 0, qkv_cols, rows, gate_wide, 3),
         ],
         spread([narrow(late_block)]) + early_sums,
         [input_weight.shape],
@@ -991,7 +1015,7 @@
         block_out,
         tokens_grad,
         input_shard,
-        own_part(rate_sum, 0),
+        own_part(jnp.swapaxes(rate_sum.reshape(-1, 2, H), 1, 2).reshape(-1, 2 * H), 0),
         own_part(conv_sum, 1),
         own_part(decay_sum, 1),
         own_part(mixer_sum, 0),

time: 792 us -> 779 us (0.984)
  waiting for transfers between devices: 185 us -> 219 us
  local copies, waits for them, and re-layouts: 121 us -> 102 us
  other arithmetic: 90 us -> 78.2 us
  starting transfers between devices: 74.6 us -> 65.2 us
    ppermute x42 -> x36, waiting for transfers between devices: 121 us -> 167 us  [swap(): return lax.ppermute(value, axis, [(0, 1), (1, 0)])]
    concatenate x6 -> x1, local copies, waits for them, and re-layouts: 17 us -> 2.29 us  [mixer(): jnp.concatenate([five, doc_lanes, jnp.zeros((length, 128 - 6 * H), F32)],...]
    ppermute x1, waiting for transfers between devices: 20 us -> 5.98 us  [mixer(): start = lax.ppermute(state.astype(BF16), 'sp', ahead)]
    ppermute x9, waiting for transfers between devices: 19.5 us -> 31.7 us  [shifted(): lax.ppermute(value, 'fsdp', [(i, (i + step) % count) for i in range(count)])]
    reduce_scatter x5, waiting for transfers between devices: 12 us -> 0.06 us  [sum_blocks(): lax.psum_scatter(value.astype(BF16), 'fsdp', scatter_dimension=0, tiled=T...]
    ppermute x9, starting transfers between devices: 25.2 us -> 13.7 us  [shifted(): lax.ppermute(value, 'fsdp', [(i, (i + step) % count) for i in range(count)])]
    convert_element_type x4 -> x1, other arithmetic: 12.4 us -> 3.66 us  [sum_blocks(): value.astype(BF16)]
    unnamed x350 -> x401, local copies, waits for them, and re-layouts: 36.9 us -> 36.2 us
  transfers between devices with their start and end apart: 64 -> 60, of which waited for: 23 -> 21; matrix products, arithmetic and copies ran while one was open for 42% -> 37% of each run, Pallas kernels for 18% -> 15%
where the time goes in v5:
time: 779 us; the launch traced here: 770 us
  waiting for transfers between devices  219 us (28%)
  matrix products  147 us (19%)
  Pallas kernels  142 us (18%)
  local copies, waits for them, and re-layouts  102 us (13%)
  other arithmetic  78.2 us (10%)
  starting transfers between devices  65.2 us (8%)
  between operations  17.1 us (2%)
    ppermute x36, waiting for transfers between devices, swap(): return lax.ppermute(value, axis, [(0, 1), (1, 0)])  167 us
    pallas_call x7, Pallas kernels, call(): pl.pallas_call(kernel, out_shape=[jax.ShapeDtypeStruct(s, t) for s, t in...  126 us
    dot_general x24, matrix products, grad_dot(): return jnp.einsum('td,tf->df', left, right, preferred_element_type=F32)  65.8 us
    ppermute x36, starting transfers between devices, swap(): return lax.ppermute(value, axis, [(0, 1), (1, 0)])  37.6 us
    unnamed x401, local copies, waits for them, and re-layouts  36.2 us
    ppermute x9, waiting for transfers between devices, shifted(): lax.ppermute(value, 'fsdp', [(i, (i + step) % count) for i in range(count)])  31.7 us
    dot_general x4, matrix products, dot_back(): jnp.einsum('tf,df->td', grads[:, :half], halves_of[0], preferred_element_...  21 us
    dot_general x8, matrix products, dot_columns(): parts = [jnp.dot(values, w, preferred_element_type=F32) for w in halves_of]  19 us
  transfers between devices with their start and end apart: 60, of which 21 were waited for; matrix products, arithmetic and copies ran while one was open for 37% of the time, Pallas kernels for 15%

profile of v5, /device:TPU:0, one launch (start us, length us, event | category | flops | bytes accessed | tf_op | source)
XLA Modules:
  0.0 770.1 jit_solution(102340546018529229)
XLA Ops:
  17.6 5.0 collective-permute-start.1
  24.3 4.0 collective-permute-start
  36.2 14.5 %collective-permute-done.2 = bf16[288,512]{1,0:T(8,128)(2,1)S(1)} collective-permute-done((bf16[288,512]{1,0:T(8,128)(2,1)}, bf16[288,512]{1,0:T(8,128)(2,1)S(1)}, u32[]{:S(2)}, u32[]{:S(2)}) %collective-permute-start.2) | collective-permute-done | bytes 294944 | tf_op jit(solution)/shard_map/ppermute | solution.py:562
  55.4 9.4 %collective-permute-done.4 = bf16[1024,256]{1,0:T(8,128)(2,1)S(1)} collective-permute-done((bf16[1024,256]{1,0:T(8,128)(2,1)S(1)}, bf16[1024,256]{1,0:T(8,128)(2,1)S(1)}, u32[]{:S(2)}, u32[]{:S(2)}) %collective-permute-start.4) | collective-permute-done | bytes 524320 | tf_op jit(solution)/shard_map/ppermute | solution.py:524
  70.4 26.3 %collective-permute-done.5 = bf16[1024,512]{1,0:T(8,128)(2,1)S(1)} collective-permute-done((bf16[1024,512]{1,0:T(8,128)(2,1)S(1)}, bf16[1024,512]{1,0:T(8,128)(2,1)S(1)}, u32[]{:S(2)}, u32[]{:S(2)}) %collective-permute-start.5) | collective-permute-done | bytes 1048608 | tf_op jit(solution)/shard_map/ppermute | solution.py:524
  98.7 4.5 reshape_reshape.6
  127.2 3.4 collective-permute-done.11
  132.3 13.4 %shard_map.220.n_ref = bf16[384,4096]{1,0:T(8,128)(2,1)} custom-call(bf16[400,4096]{1,0:T(8,128)(2,1)} %copy-done.19, f32[4,4096]{1,0:T(4,128)} %bitcast.246, f32[384,8]{1,0:T(8,128)} %copy.205.mask_ref), custom_call_target="tpu_custom_call" | custom-call | flops 1 | bytes 1 | tf_op jit(solution)/shard_map/pallas_call | solution.py:386
  145.7 13.8 %collective-permute-done.15 = bf16[704,128]{1,0:T(8,128)(2,1)S(1)} collective-permute-done((bf16[704,128]{1,0:T(8,128)(2,1)S(1)}, bf16[704,128]{1,0:T(8,128)(2,1)S(1)}, u32[]{:S(2)}, u32[]{:S(2)}) %collective-permute-start.15) | collective-permute-done | bytes 180256 | tf_op jit(solution)/shard_map/ppermute | solution.py:562
  169.9 27.4 %shard_map.221.inv_ref = f32[6,2,256,256]{3,2,1,0:T(8,128)} custom-call(bf16[384,4096]{1,0:T(8,128)(2,1)} %shard_map.220.n_ref, f32[384,128]{1,0:T(8,128)} %concatenate.205.col_ref), custom_call_target="tpu_custom_call" | custom-call | flops 1 | bytes 1 | tf_op jit(solution)/shard_map/pallas_call | solution.py:386
  199.3 5.2 collective-permute-done.17
  213.0 10.3 %shard_map.222 = f32[8,128,256]{2,1,0:T(8,128)} custom-call(bf16[384,4096]{1,0:T(8,128)(2,1)} %shard_map.220.n_ref, f32[6,2,256,256]{3,2,1,0:T(8,128)} %shard_map.221.inv_ref, f32[384,128]{1,0:T(8,128)} %concatenate.205.col_ref, bf16[8,128,256]{2,1,0:T(8,128)(2,1)} %broadcast_20_start_ref.2.start_ref), custom_call_target="tpu_custom_call" | custom-call | flops 1 | bytes 1 | tf_op jit(solution)/shard_map/pallas_call | solution.py:386
  224.6 3.6 collective-permute-start.19
  233.3 6.0 collective-permute-done.19.start_ref
  240.1 13.5 %shard_map.223 = (bf16[384,2048]{1,0:T(8,128)(2,1)}, bf16[6,2,256,256]{3,2,1,0:T(8,128)(2,1)}, bf16[6,8,128,256]{3,2,1,0:T(8,128)(2,1)}) custom-call(bf16[384,4096]{1,0:T(8,128)(2,1)} %shard_map.220.n_ref, f32[6,2,256,256]{3,2,1,0:T(8,128)} %shard_map.221.inv_ref, f32[384,128]{1,0:T(8,128)} %concatenate.205.col_ref, bf16[8,128,256]{2,1,0:T(8,128)(2,1)} %copy-done.77), custom_call_target="tpu_custom_call" | custom-call | flops 1 | bytes 1 | tf_op jit(solution)/shard_map/pallas_call | solution.py:386
  260.0 3.7 constant_dynamic-update-slice_fusion.25
  272.9 4.7 multiply_reduce_fusion.4
  280.0 5.2 fusion.172
  285.2 8.0 %fusion.245 = f32[384,5632]{1,0:T(8,128)S(1)} fusion(bf16[384,1024]{1,0:T(8,128)(2,1)} %multiply_convert_fusion.2, bf16[1024,5632]{1,0:T(8,128)(2,1)} %all-gather.9.cloned.1.call-done), kind=kOutput, calls=%fused_computation.528 | convolution fusion | flops 4429185024 | bytes 20971520 | tf_op jit(solution)/shard_map/dot_general | solution.py:931
  293.3 7.3 fusion.54
  300.5 3.3 convolution_convert_fusion.1
  316.3 4.2 add_convert_fusion
  320.8 5.7 convolution_convert_fusion
  326.7 3.5 add_convert_fusion.5
  330.2 8.4 %multiply_reduce_fusion.2 = (f32[1024]{0:T(1024)}, f32[384]{0:T(512)S(1)}, f32[384,1024]{1,0:T(8,128)S(1)}) fusion(f32[384,1024]{1,0:T(8,128)S(1)} %copy-done.15, f32[384]{0:T(512)S(1)} %copy-done.147, f32[1024]{0:T(1024)S(1)} %bitcast.264, bf16[384,5632]{1,0:T(8,128)(2,1)S(1)} %add_convert_fusion, bf16[1024,5632]{1,0:T(8,128)(2,1)} %all-gather.9.cloned.1.call-done), kind=kOutput, calls=%fused_computation.121 | convolution fusion | flops 4431542784 | bytes 19016704 | tf_op jit(solution)/shard_map/tf,df->td/dot_general | solution.py:946
  348.7 2.7 convolution_convert_fusion.2
  352.3 5.7 multiply_reduce_fusion
  368.2 3.0 add_convert_fusion.9
  373.8 3.1 add_convert_fusion.8
  378.5 18.6 %collective-permute-done.28 = bf16[2816,256]{1,0:T(8,128)(2,1)S(1)} collective-permute-done((bf16[2816,256]{1,0:T(8,128)(2,1)}, bf16[2816,256]{1,0:T(8,128)(2,1)S(1)}, u32[]{:S(2)}, u32[]{:S(2)}) %collective-permute-start.28) | collective-permute-done | bytes 1441824 | tf_op jit(solution)/shard_map/ppermute | solution.py:524
  397.1 3.3 add_convert_fusion.12
  402.9 5.5 add_convert_fusion.2
  408.5 13.4 %shard_map.224 = f32[8,128,256]{2,1,0:T(8,128)} custom-call(bf16[384,4096]{1,0:T(8,128)(2,1)} %shard_map.220.n_ref, f32[6,2,256,256]{3,2,1,0:T(8,128)} %shard_map.221.inv_ref, f32[384,128]{1,0:T(8,128)} %concatenate.205.col_ref, bf16[384,2048]{1,0:T(8,128)(2,1)} %get-tuple-element.59.dout_ref, bf16[8,128,256]{2,1,0:T(8,128)(2,1)} %broadcast_20_start_ref.2.start_ref), custom_call_target="tpu_custom_call" | custom-call | flops 1 | bytes 1 | tf_op jit(solution)/shard_map/pallas_call | solution.py:386
  425.3 2.7 add_convert_fusion.20
  430.9 3.4 collective-permute-start.33
  436.7 4.4 collective-permute-done.27.start_ref
  441.1 24.9 %shard_map.225 = (f32[384,4096]{1,0:T(8,128)}, f32[384,128]{1,0:T(8,128)}) custom-call(bf16[384,4096]{1,0:T(8,128)(2,1)} %shard_map.220.n_ref, f32[6,2,256,256]{3,2,1,0:T(8,128)} %shard_map.221.inv_ref, f32[384,128]{1,0:T(8,128)} %concatenate.205.col_ref, bf16[384,2048]{1,0:T(8,128)(2,1)} %get-tuple-element.59.dout_ref, ...), custom_call_target="tpu_custom_call" | custom-call | flops 1 | bytes 1 | tf_op jit(solution)/shard_map/pallas_call | solution.py:386
  470.8 23.1 %shard_map.226 = (bf16[400,4096]{1,0:T(8,128)(2,1)}, f32[4,4096]{1,0:T(4,128)}) custom-call(bf16[400,4096]{1,0:T(8,128)(2,1)} %copy-done.19, f32[4,4096]{1,0:T(4,128)} %bitcast.247, f32[384,8]{1,0:T(8,128)} %copy.205.mask_ref, f32[384,4096]{1,0:T(8,128)} %get-tuple-element.68.dn_ref), custom_call_target="tpu_custom_call" | custom-call | flops 1 | bytes 1 | tf_op jit(solution)/shard_map/pallas_call | solution.py:386
  496.6 5.0 collective-permute-done.34
  511.3 44.1 %collective-permute-done.49 = bf16[1024,1408]{1,0:T(8,128)(2,1)} collective-permute-done((bf16[1024,1408]{1,0:T(8,128)(2,1)}, bf16[1024,1408]{1,0:T(8,128)(2,1)}, u32[]{:S(2)}, u32[]{:S(2)}) %collective-permute-start.49) | collective-permute-done | bytes 2883616 | tf_op jit(solution)/shard_map/ppermute | solution.py:524
  555.5 4.3 add_convert_fusion.4
  562.1 3.8 fusion.27
  566.0 3.0 add_convert_fusion.6
  569.0 3.1 add_convert_fusion.7
  572.1 15.7 %collective-permute-done.50 = bf16[512,1408]{1,0:T(8,128)(2,1)S(1)} collective-permute-done((bf16[512,1408]{1,0:T(8,128)(2,1)}, bf16[512,1408]{1,0:T(8,128)(2,1)S(1)}, u32[]{:S(2)}, u32[]{:S(2)}) %collective-permute-start.50) | collective-permute-done | bytes 1441824 | tf_op jit(solution)/shard_map/ppermute | solution.py:524
  587.8 3.7 add_convert_fusion.3
  594.6 17.2 %collective-permute-done.39 = bf16[1024,512]{1,0:T(8,128)(2,1)S(1)} collective-permute-done((bf16[1024,512]{1,0:T(8,128)(2,1)}, bf16[1024,512]{1,0:T(8,128)(2,1)S(1)}, u32[]{:S(2)}, u32[]{:S(2)}) %collective-permute-start.39) | collective-permute-done | bytes 1048608 | tf_op jit(solution)/shard_map/ppermute | solution.py:524
  617.5 5.1 collective-permute-done.40
  630.1 3.9 fusion.246
  634.1 3.1 fusion.247
  641.7 3.8 fusion.165
  652.9 4.0 fusion.39
  661.5 4.0 fusion.164
  674.9 7.6 fusion.16
  686.3 4.6 collective-permute-done.45
  697.3 4.5 collective-permute-done.47
  701.8 3.1 collective-permute-start.48
  707.3 4.4 fusion.18
  723.5 13.6 %collective-permute-done.42 = bf16[2,1024,128]{2,1,0:T(8,128)(2,1)S(1)} collective-permute-done((bf16[2,1024,128]{2,1,0:T(8,128)(2,1)S(1)}, bf16[2,1024,128]{2,1,0:T(8,128)(2,1)S(1)}, u32[]{:S(2)}, u32[]{:S(2)}) %collective-permute-start.42) | collective-permute-done | bytes 524320 | tf_op jit(solution)/shard_map/ppermute | solution.py:524
  738.2 4.3 fusion.230
  742.5 4.9 shard_map.228
  748.4 6.1 shard_map.227
  754.5 3.6 fusion.233
  758.1 5.1 shard_map.229
  (741 shorter events, 239.3 us)
Async XLA Ops:
  7.2 265.7 %all-gather.7.cloned.1.call-start = ((), (), s32[]{:S(2)}) async-start(), calls=%async_computation.5 | async-start | bytes 4325376 | tf_op jit(solution)/shard_map/all_gather | solution.py:590
  9.0 276.2 %all-gather.9.cloned.1.call-start = ((), (), s32[]{:S(2)}) async-start(), calls=%async_computation.6 | async-start | bytes 11894784 | tf_op jit(solution)/shard_map/all_gather | solution.py:590
  9.9 627.3 %reduce-scatter.12.cloned.1.call-start = ((), (), s32[]{:S(2)}) async-start(), calls=%async_computation.10 | async-start | bytes 655360 | tf_op jit(solution)/shard_map/reduce_scatter | solution.py:574
  17.6 18.6 %collective-permute-start.1 = (bf16[288,512]{1,0:T(8,128)(2,1)}, bf16[288,512]{1,0:T(8,128)(2,1)S(1)}, u32[]{:S(2)}, u32[]{:S(2)}) collective-permute-start(bf16[288,512]{1,0:T(8,128)(2,1)} %pad_maximum_fusion.17), channel_id=1, source_target_pairs={{0,6},{2,0},{4,2},{6,4},{1,7},{3,1},{5,3},{7,5},{8,14},{10,8},{12,... | collective-permute-start | bytes 884744 | tf_op jit(solution)/shard_map/ppermute | solution.py:562
  22.7 28.1 %collective-permute-start.2 = (bf16[288,512]{1,0:T(8,128)(2,1)}, bf16[288,512]{1,0:T(8,128)(2,1)S(1)}, u32[]{:S(2)}, u32[]{:S(2)}) collective-permute-start(bf16[288,512]{1,0:T(8,128)(2,1)} %pad_maximum_fusion.17), channel_id=1, source_target_pairs={{0,4},{2,6},{4,0},{6,2},{1,5},{3,7},{5,1},{7,3},{8,12},{10,14},{12... | collective-permute-start | bytes 884744 | tf_op jit(solution)/shard_map/ppermute | solution.py:562
  22.7 28.1 %collective-permute-start.3 = (bf16[288,512]{1,0:T(8,128)(2,1)}, bf16[288,512]{1,0:T(8,128)(2,1)S(1)}, u32[]{:S(2)}, u32[]{:S(2)}) collective-permute-start(bf16[288,512]{1,0:T(8,128)(2,1)} %pad_maximum_fusion.17), channel_id=1, source_target_pairs={{0,2},{2,4},{4,6},{6,0},{1,3},{3,5},{5,7},{7,1},{8,10},{10,12},{12... | collective-permute-start | bytes 884744 | tf_op jit(solution)/shard_map/ppermute | solution.py:562
  24.3 28.5 %collective-permute-start = (bf16[16,1024]{1,0:T(8,128)(2,1)}, bf16[16,1024]{1,0:T(8,128)(2,1)}, u32[]{:S(2)}, u32[]{:S(2)}) collective-permute-start(bf16[16,1024]{1,0:T(8,128)(2,1)} %slice.313), channel_id=1, source_target_pairs={{0,1},{2,3},{4,5},{6,7},{8,9},{10,11},{12,13},{14,15},{16,17},{18,... | collective-permute-start | bytes 98312 | tf_op jit(solution)/shard_map/ppermute | solution.py:908
  32.3 132.7 %copy-start.140 = (f32[6,64]{1,0:T(8,128)}, f32[6,64]{1,0:T(8,128)S(1)}, u32[]{:S(2)}) copy-start(f32[6,64]{1,0:T(8,128)S(1)} %get-tuple-element.172) | copy-start | bytes 4612
  32.3 132.7 %copy-start.144 = (f32[6,64]{1,0:T(8,128)}, f32[6,64]{1,0:T(8,128)S(1)}, u32[]{:S(2)}) copy-start(f32[6,64]{1,0:T(8,128)S(1)} %get-tuple-element.173) | copy-start | bytes 4612
  51.2 13.6 %collective-permute-start.4 = (bf16[1024,256]{1,0:T(8,128)(2,1)S(1)}, bf16[1024,256]{1,0:T(8,128)(2,1)S(1)}, u32[]{:S(2)}, u32[]{:S(2)}) collective-permute-start(bf16[1024,256]{1,0:T(8,128)(2,1)S(1)} %get-tuple-element.128), channel_id=1, source_target_pairs={{0,1},{1,0},{2,3},{3,2},{4,5},{5,4},{6,7},{7,6},{8,9},{9,8},{10,11... | collective-permute-start | bytes 1572872 | tf_op jit(solution)/shard_map/ppermute | solution.py:524
  53.9 13.0 %collective-permute-start.7 = (bf16[1024,256]{1,0:T(8,128)(2,1)S(1)}, bf16[1024,256]{1,0:T(8,128)(2,1)S(1)}, u32[]{:S(2)}, u32[]{:S(2)}) collective-permute-start(bf16[1024,256]{1,0:T(8,128)(2,1)S(1)} %get-tuple-element.127), channel_id=1, source_target_pairs={{0,16},{16,0},{1,17},{17,1},{2,18},{18,2},{3,19},{19,3},{4,20},{20... | collective-permute-start | bytes 1572872 | tf_op jit(solution)/shard_map/ppermute | solution.py:524
  65.0 31.8 %collective-permute-start.5 = (bf16[1024,512]{1,0:T(8,128)(2,1)S(1)}, bf16[1024,512]{1,0:T(8,128)(2,1)S(1)}, u32[]{:S(2)}, u32[]{:S(2)}) collective-permute-start(bf16[1024,512]{1,0:T(8,128)(2,1)S(1)} %pad_maximum_fusion.2), channel_id=1, source_target_pairs={{0,16},{16,0},{1,17},{17,1},{2,18},{18,2},{3,19},{19,3},{4,20},{20... | collective-permute-start | bytes 3145736 | tf_op jit(solution)/shard_map/ppermute | solution.py:524
  68.0 38.4 %collective-permute-start.8 = (bf16[1024,512]{1,0:T(8,128)(2,1)}, bf16[1024,512]{1,0:T(8,128)(2,1)}, u32[]{:S(2)}, u32[]{:S(2)}) collective-permute-start(bf16[1024,512]{1,0:T(8,128)(2,1)} %pad_maximum_fusion.3), channel_id=1, source_target_pairs={{0,1},{1,0},{2,3},{3,2},{4,5},{5,4},{6,7},{7,6},{8,9},{9,8},{10,11... | collective-permute-start | bytes 3145736 | tf_op jit(solution)/shard_map/ppermute | solution.py:524
  98.4 19.4 %collective-permute-start.6 = (bf16[1024,1024]{1,0:T(8,128)(2,1)}, bf16[1024,1024]{1,0:T(8,128)(2,1)}, u32[]{:S(2)}, u32[]{:S(2)}) collective-permute-start(bf16[1024,1024]{1,0:T(8,128)(2,1)} %pad_maximum_fusion), channel_id=1, source_target_pairs={{0,8},{8,0},{1,9},{9,1},{2,10},{10,2},{3,11},{11,3},{4,12},{12,4},... | collective-permute-start | bytes 6291464 | tf_op jit(solution)/shard_map/ppermute | solution.py:524
  105.0 123.2 %copy-start.4 = (bf16[384,1024]{1,0:T(8,128)(2,1)}, bf16[384,1024]{1,0:T(8,128)(2,1)S(1)}, u32[]{:S(2)}) copy-start(bf16[384,1024]{1,0:T(8,128)(2,1)S(1)} %fusion.15) | copy-start | bytes 2359300
  108.1 13.5 %collective-permute-start.9 = (bf16[1024,1024]{1,0:T(8,128)(2,1)S(1)}, bf16[1024,1024]{1,0:T(8,128)(2,1)S(1)}, u32[]{:S(2)}, u32[]{:S(2)}) collective-permute-start(bf16[1024,1024]{1,0:T(8,128)(2,1)S(1)} %pad_maximum_fusion.1), channel_id=1, source_target_pairs={{0,8},{8,0},{1,9},{9,1},{2,10},{10,2},{3,11},{11,3},{4,12},{12,4},... | collective-permute-start | bytes 6291464 | tf_op jit(solution)/shard_map/ppermute | solution.py:524
  109.4 17.2 %collective-permute-start.10 = (bf16[256,256]{1,0:T(8,128)(2,1)S(1)}, bf16[256,256]{1,0:T(8,128)(2,1)S(1)}, u32[]{:S(2)}, u32[]{:S(2)}) collective-permute-start(bf16[256,256]{1,0:T(8,128)(2,1)S(1)} %copy-done.76), channel_id=1, source_target_pairs={{0,6},{2,0},{4,2},{6,4},{1,7},{3,1},{5,3},{7,5},{8,14},{10,8},{12,... | collective-permute-start | bytes 393224 | tf_op jit(solution)/shard_map/ppermute | solution.py:562
  110.5 20.0 %collective-permute-start.11 = (bf16[256,256]{1,0:T(8,128)(2,1)S(1)}, bf16[256,256]{1,0:T(8,128)(2,1)S(1)}, u32[]{:S(2)}, u32[]{:S(2)}) collective-permute-start(bf16[256,256]{1,0:T(8,128)(2,1)S(1)} %copy-done.76), channel_id=1, source_target_pairs={{0,4},{2,6},{4,0},{6,2},{1,5},{3,7},{5,1},{7,3},{8,12},{10,14},{12... | collective-permute-start | bytes 393224 | tf_op jit(solution)/shard_map/ppermute | solution.py:562
  112.5 18.1 %collective-permute-start.12 = (bf16[256,256]{1,0:T(8,128)(2,1)S(1)}, bf16[256,256]{1,0:T(8,128)(2,1)S(1)}, u32[]{:S(2)}, u32[]{:S(2)}) collective-permute-start(bf16[256,256]{1,0:T(8,128)(2,1)S(1)} %copy-done.76), channel_id=1, source_target_pairs={{0,2},{2,4},{4,6},{6,0},{1,3},{3,5},{5,7},{7,1},{8,10},{10,12},{12... | collective-permute-start | bytes 393224 | tf_op jit(solution)/shard_map/ppermute | solution.py:562
  124.7 21.0 %collective-permute-start.14 = (bf16[704,128]{1,0:T(8,128)(2,1)S(1)}, bf16[704,128]{1,0:T(8,128)(2,1)S(1)}, u32[]{:S(2)}, u32[]{:S(2)}) collective-permute-start(bf16[704,128]{1,0:T(8,128)(2,1)S(1)} %copy-done.75), channel_id=1, source_target_pairs={{0,6},{2,0},{4,2},{6,4},{1,7},{3,1},{5,3},{7,5},{8,14},{10,8},{12,... | collective-permute-start | bytes 540680 | tf_op jit(solution)/shard_map/ppermute | solution.py:562
  126.7 32.8 %collective-permute-start.15 = (bf16[704,128]{1,0:T(8,128)(2,1)S(1)}, bf16[704,128]{1,0:T(8,128)(2,1)S(1)}, u32[]{:S(2)}, u32[]{:S(2)}) collective-permute-start(bf16[704,128]{1,0:T(8,128)(2,1)S(1)} %copy-done.75), channel_id=1, source_target_pairs={{0,4},{2,6},{4,0},{6,2},{1,5},{3,7},{5,1},{7,3},{8,12},{10,14},{12... | collective-permute-start | bytes 540680 | tf_op jit(solution)/shard_map/ppermute | solution.py:562
  126.7 32.8 %collective-permute-start.16 = (bf16[704,128]{1,0:T(8,128)(2,1)S(1)}, bf16[704,128]{1,0:T(8,128)(2,1)S(1)}, u32[]{:S(2)}, u32[]{:S(2)}) collective-permute-start(bf16[704,128]{1,0:T(8,128)(2,1)S(1)} %copy-done.75), channel_id=1, source_target_pairs={{0,2},{2,4},{4,6},{6,0},{1,3},{3,5},{5,7},{7,1},{8,10},{10,12},{12... | collective-permute-start | bytes 540680 | tf_op jit(solution)/shard_map/ppermute | solution.py:562
  130.8 29.0 %collective-permute-start.13 = (bf16[1024,256]{1,0:T(8,128)(2,1)S(1)}, bf16[1024,256]{1,0:T(8,128)(2,1)}, u32[]{:S(2)}, u32[]{:S(2)}) collective-permute-start(bf16[1024,256]{1,0:T(8,128)(2,1)S(1)} %constant_dynamic-slice_fusion.47), channel_id=1, source_target_pairs={{0,1},{1,0},{2,3},{3,2},{4,5},{5,4},{6,7},{7,6},{8,9},{9,8},{10,11... | collective-permute-start | bytes 1572872 | tf_op jit(solution)/shard_map/ppermute | solution.py:524
  160.9 43.5 %collective-permute-start.17 = (bf16[1024,512]{1,0:T(8,128)(2,1)S(1)}, bf16[1024,512]{1,0:T(8,128)(2,1)}, u32[]{:S(2)}, u32[]{:S(2)}) collective-permute-start(bf16[1024,512]{1,0:T(8,128)(2,1)S(1)} %pad_maximum_fusion.4), channel_id=1, source_target_pairs={{0,16},{16,0},{1,17},{17,1},{2,18},{18,2},{3,19},{19,3},{4,20},{20... | collective-permute-start | bytes 3145736 | tf_op jit(solution)/shard_map/ppermute | solution.py:524
  163.7 43.0 %collective-permute-start.18 = (bf16[2816,128]{1,0:T(8,128)(2,1)S(1)}, bf16[2816,128]{1,0:T(8,128)(2,1)}, u32[]{:S(2)}, u32[]{:S(2)}) collective-permute-start(bf16[2816,128]{1,0:T(8,128)(2,1)S(1)} %constant_dynamic-slice_fusion.45), channel_id=1, source_target_pairs={{0,1},{1,0},{2,3},{3,2},{4,5},{5,4},{6,7},{7,6},{8,9},{9,8},{10,11... | collective-permute-start | bytes 2162696 | tf_op jit(solution)/shard_map/ppermute | solution.py:524
  206.7 57.0 %collective-permute-start.20 = (bf16[1024,1024]{1,0:T(8,128)(2,1)}, bf16[1024,1024]{1,0:T(8,128)(2,1)}, u32[]{:S(2)}, u32[]{:S(2)}) collective-permute-start(bf16[1024,1024]{1,0:T(8,128)(2,1)} %constant_dynamic-update-slice_fusion.21), channel_id=1, source_target_pairs={{0,8},{8,0},{1,9},{9,1},{2,10},{10,2},{3,11},{11,3},{4,12},{12,4},... | collective-permute-start | bytes 6291464 | tf_op jit(solution)/shard_map/ppermute | solution.py:524
  208.8 51.2 %collective-permute-start.21 = (bf16[2816,256]{1,0:T(8,128)(2,1)}, bf16[2816,256]{1,0:T(8,128)(2,1)}, u32[]{:S(2)}, u32[]{:S(2)}) collective-permute-start(bf16[2816,256]{1,0:T(8,128)(2,1)} %constant_dynamic-update-slice_fusion.23), channel_id=1, source_target_pairs={{0,16},{16,0},{1,17},{17,1},{2,18},{18,2},{3,19},{19,3},{4,20},{20... | collective-permute-start | bytes 4325384 | tf_op jit(solution)/shard_map/ppermute | solution.py:524
  212.1 126.5 %copy-start.139 = (f32[1,2,4,128]{3,1,2,0:T(2,128)}, f32[1,2,4,128]{3,1,2,0:T(2,128)S(1)}, u32[]{:S(2)}) copy-start(f32[1,2,4,128]{3,1,2,0:T(2,128)S(1)} %copy.255) | copy-start | bytes 12292
  224.6 14.7 %collective-permute-start.19 = (bf16[8,128,256]{2,1,0:T(8,128)(2,1)S(1)}, bf16[8,128,256]{2,1,0:T(8,128)(2,1)S(1)}, u32[]{:S(2)}, u32[]{:S(2)}) collective-permute-start(bf16[8,128,256]{2,1,0:T(8,128)(2,1)S(1)} %convert_element_type.345), channel_id=1, source_target_pairs={{0,1},{2,3},{4,5},{6,7},{8,9},{10,11},{12,13},{14,15},{16,17},{18,... | collective-permute-start | bytes 1572872 | tf_op jit(solution)/shard_map/ppermute | solution.py:453
  263.7 16.2 %collective-permute-start.22 = (bf16[2816,512]{1,0:T(8,128)(2,1)}, bf16[2816,512]{1,0:T(8,128)(2,1)}, u32[]{:S(2)}, u32[]{:S(2)}) collective-permute-start(bf16[2816,512]{1,0:T(8,128)(2,1)} %constant_dynamic-update-slice_fusion.25), channel_id=1, source_target_pairs={{0,8},{8,0},{1,9},{9,1},{2,10},{10,2},{3,11},{11,3},{4,12},{12,4},... | collective-permute-start | bytes 8650760 | tf_op jit(solution)/shard_map/ppermute | solution.py:524
  303.8 22.8 %collective-permute-start.23 = (bf16[2816,512]{1,0:T(8,128)(2,1)}, bf16[2816,512]{1,0:T(8,128)(2,1)}, u32[]{:S(2)}, u32[]{:S(2)}) collective-permute-start(bf16[2816,512]{1,0:T(8,128)(2,1)} %convolution_convert_fusion.1), channel_id=1, source_target_pairs={{0,8},{8,0},{1,9},{9,1},{2,10},{10,2},{3,11},{11,3},{4,12},{12,4},... | collective-permute-start | bytes 8650760 | tf_op jit(solution)/shard_map/ppermute | solution.py:524
  326.6 76.3 %collective-permute-start.24 = (bf16[1024,2816]{1,0:T(8,128)(2,1)}, bf16[1024,2816]{1,0:T(8,128)(2,1)}, u32[]{:S(2)}, u32[]{:S(2)}) collective-permute-start(bf16[1024,2816]{1,0:T(8,128)(2,1)} %convolution_convert_fusion), channel_id=1, source_target_pairs={{0,8},{8,0},{1,9},{9,1},{2,10},{10,2},{3,11},{11,3},{4,12},{12,4},... | collective-permute-start | bytes 17301512 | tf_op jit(solution)/shard_map/ppermute | solution.py:524
  351.4 16.8 %collective-permute-start.25 = (bf16[2048,512]{1,0:T(8,128)(2,1)}, bf16[2048,512]{1,0:T(8,128)(2,1)}, u32[]{:S(2)}, u32[]{:S(2)}) collective-permute-start(bf16[2048,512]{1,0:T(8,128)(2,1)} %convolution_convert_fusion.2), channel_id=1, source_target_pairs={{0,8},{8,0},{1,9},{9,1},{2,10},{10,2},{3,11},{11,3},{4,12},{12,4},... | collective-permute-start | bytes 6291464 | tf_op jit(solution)/shard_map/ppermute | solution.py:524
  362.0 11.7 %collective-permute-start.26 = (bf16[1024,1024]{1,0:T(8,128)(2,1)}, bf16[1024,1024]{1,0:T(8,128)(2,1)}, u32[]{:S(2)}, u32[]{:S(2)}) collective-permute-start(bf16[1024,1024]{1,0:T(8,128)(2,1)} %convolution_convert_fusion.5), channel_id=1, source_target_pairs={{0,8},{8,0},{1,9},{9,1},{2,10},{10,2},{3,11},{11,3},{4,12},{12,4},... | collective-permute-start | bytes 6291464 | tf_op jit(solution)/shard_map/ppermute | solution.py:524
  362.4 34.6 %collective-permute-start.28 = (bf16[2816,256]{1,0:T(8,128)(2,1)}, bf16[2816,256]{1,0:T(8,128)(2,1)S(1)}, u32[]{:S(2)}, u32[]{:S(2)}) collective-permute-start(bf16[2816,256]{1,0:T(8,128)(2,1)} %add_convert_fusion.5), channel_id=1, source_target_pairs={{0,16},{16,0},{1,17},{17,1},{2,18},{18,2},{3,19},{19,3},{4,20},{20... | collective-permute-start | bytes 4325384 | tf_op jit(solution)/shard_map/ppermute | solution.py:524
  371.3 54.1 %collective-permute-start.30 = (bf16[2048,256]{1,0:T(8,128)(2,1)}, bf16[2048,256]{1,0:T(8,128)(2,1)}, u32[]{:S(2)}, u32[]{:S(2)}) collective-permute-start(bf16[2048,256]{1,0:T(8,128)(2,1)} %add_convert_fusion.9), channel_id=1, source_target_pairs={{0,1},{1,0},{2,3},{3,2},{4,5},{5,4},{6,7},{7,6},{8,9},{9,8},{10,11... | collective-permute-start | bytes 3145736 | tf_op jit(solution)/shard_map/ppermute | solution.py:524
  376.9 51.5 %collective-permute-start.32 = (bf16[1024,512]{1,0:T(8,128)(2,1)}, bf16[1024,512]{1,0:T(8,128)(2,1)}, u32[]{:S(2)}, u32[]{:S(2)}) collective-permute-start(bf16[1024,512]{1,0:T(8,128)(2,1)} %add_convert_fusion.8), channel_id=1, source_target_pairs={{0,16},{16,0},{1,17},{17,1},{2,18},{18,2},{3,19},{19,3},{4,20},{20... | collective-permute-start | bytes 3145736 | tf_op jit(solution)/shard_map/ppermute | solution.py:524
  400.4 34.0 %collective-permute-start.29 = (bf16[2816,128]{1,0:T(8,128)(2,1)}, bf16[2816,128]{1,0:T(8,128)(2,1)S(1)}, u32[]{:S(2)}, u32[]{:S(2)}) collective-permute-start(bf16[2816,128]{1,0:T(8,128)(2,1)} %add_convert_fusion.12), channel_id=1, source_target_pairs={{0,1},{1,0},{2,3},{3,2},{4,5},{5,4},{6,7},{7,6},{8,9},{9,8},{10,11... | collective-permute-start | bytes 2162696 | tf_op jit(solution)/shard_map/ppermute | solution.py:524
  424.0 17.1 %collective-permute-start.27 = (bf16[8,128,256]{2,1,0:T(8,128)(2,1)}, bf16[8,128,256]{2,1,0:T(8,128)(2,1)}, u32[]{:S(2)}, u32[]{:S(2)}) collective-permute-start(bf16[8,128,256]{2,1,0:T(8,128)(2,1)} %convert_element_type.372), channel_id=1, source_target_pairs={{1,0},{3,2},{5,4},{7,6},{9,8},{11,10},{13,12},{15,14},{17,16},{19,... | collective-permute-start | bytes 1572872 | tf_op jit(solution)/shard_map/ppermute | solution.py:470
  428.0 37.9 %collective-permute-start.31 = (bf16[2048,128]{1,0:T(8,128)(2,1)}, bf16[2048,128]{1,0:T(8,128)(2,1)}, u32[]{:S(2)}, u32[]{:S(2)}) collective-permute-start(bf16[2048,128]{1,0:T(8,128)(2,1)} %add_convert_fusion.20), channel_id=1, source_target_pairs={{0,16},{16,0},{1,17},{17,1},{2,18},{18,2},{3,19},{19,3},{4,20},{20... | collective-permute-start | bytes 1572872 | tf_op jit(solution)/shard_map/ppermute | solution.py:524
  430.9 35.0 %collective-permute-start.33 = (bf16[1024,256]{1,0:T(8,128)(2,1)}, bf16[1024,256]{1,0:T(8,128)(2,1)}, u32[]{:S(2)}, u32[]{:S(2)}) collective-permute-start(bf16[1024,256]{1,0:T(8,128)(2,1)} %add_convert_fusion.18), channel_id=1, source_target_pairs={{0,1},{1,0},{2,3},{3,2},{4,5},{5,4},{6,7},{7,6},{8,9},{9,8},{10,11... | collective-permute-start | bytes 1572872 | tf_op jit(solution)/shard_map/ppermute | solution.py:524
  494.8 6.9 collective-permute-start.34
  496.1 59.4 %collective-permute-start.49 = (bf16[1024,1408]{1,0:T(8,128)(2,1)}, bf16[1024,1408]{1,0:T(8,128)(2,1)}, u32[]{:S(2)}, u32[]{:S(2)}) collective-permute-start(bf16[1024,1408]{1,0:T(8,128)(2,1)} %add_convert_fusion.2), channel_id=1, source_target_pairs={{0,16},{16,0},{1,17},{17,1},{2,18},{18,2},{3,19},{19,3},{4,20},{20... | collective-permute-start | bytes 8650760 | tf_op jit(solution)/shard_map/ppermute | solution.py:524
  496.6 141.5 %reduce-scatter.8.cloned.1.call-start = ((), (), s32[]{:S(2)}) async-start(), calls=%async_computation.8 | async-start | bytes 901120 | tf_op jit(solution)/shard_map/reduce_scatter | solution.py:574
  507.0 59.0 %collective-permute-start.38 = (bf16[1024,1024]{1,0:T(8,128)(2,1)}, bf16[1024,1024]{1,0:T(8,128)(2,1)}, u32[]{:S(2)}, u32[]{:S(2)}) collective-permute-start(bf16[1024,1024]{1,0:T(8,128)(2,1)} %convolution_convert_fusion.3), channel_id=1, source_target_pairs={{0,8},{8,0},{1,9},{9,1},{2,10},{10,2},{3,11},{11,3},{4,12},{12,4},... | collective-permute-start | bytes 6291464 | tf_op jit(solution)/shard_map/ppermute | solution.py:524
  510.7 58.3 %collective-permute-start.35 = (bf16[1024,1024]{1,0:T(8,128)(2,1)}, bf16[1024,1024]{1,0:T(8,128)(2,1)}, u32[]{:S(2)}, u32[]{:S(2)}) collective-permute-start(bf16[1024,1024]{1,0:T(8,128)(2,1)} %convolution_convert_fusion.4), channel_id=1, source_target_pairs={{0,8},{8,0},{1,9},{9,1},{2,10},{10,2},{3,11},{11,3},{4,12},{12,4},... | collective-permute-start | bytes 6291464 | tf_op jit(solution)/shard_map/ppermute | solution.py:524
  511.3 126.9 %reduce-scatter.10.cloned.1.call-start = ((), (), s32[]{:S(2)}) async-start(), calls=%async_computation.9 | async-start | bytes 655360 | tf_op jit(solution)/shard_map/reduce_scatter | solution.py:574
  559.8 28.1 %collective-permute-start.50 = (bf16[512,1408]{1,0:T(8,128)(2,1)}, bf16[512,1408]{1,0:T(8,128)(2,1)S(1)}, u32[]{:S(2)}, u32[]{:S(2)}) collective-permute-start(bf16[512,1408]{1,0:T(8,128)(2,1)} %add_convert_fusion.4), channel_id=1, source_target_pairs={{0,1},{1,0},{2,3},{3,2},{4,5},{5,4},{6,7},{7,6},{8,9},{9,8},{10,11... | collective-permute-start | bytes 4325384 | tf_op jit(solution)/shard_map/ppermute | solution.py:524
  565.9 99.6 %reduce-scatter.14.cloned.1.call-start = ((), (), s32[]{:S(2)}) async-start(), calls=%async_computation.11 | async-start | bytes 1802240 | tf_op jit(solution)/shard_map/reduce_scatter | solution.py:574
  591.5 113.4 %reduce-scatter.6.cloned.1.call-start = ((), (), s32[]{:S(2)}) async-start(), calls=%async_computation.7 | async-start | bytes 1310720 | tf_op jit(solution)/shard_map/reduce_scatter | solution.py:574
  591.8 20.1 %collective-permute-start.39 = (bf16[1024,512]{1,0:T(8,128)(2,1)}, bf16[1024,512]{1,0:T(8,128)(2,1)S(1)}, u32[]{:S(2)}, u32[]{:S(2)}) collective-permute-start(bf16[1024,512]{1,0:T(8,128)(2,1)} %add_convert_fusion.6), channel_id=1, source_target_pairs={{0,1},{1,0},{2,3},{3,2},{4,5},{5,4},{6,7},{7,6},{8,9},{9,8},{10,11... | collective-permute-start | bytes 3145736 | tf_op jit(solution)/shard_map/ppermute | solution.py:524
  593.9 21.4 %collective-permute-start.36 = (bf16[1024,512]{1,0:T(8,128)(2,1)}, bf16[1024,512]{1,0:T(8,128)(2,1)S(1)}, u32[]{:S(2)}, u32[]{:S(2)}) collective-permute-start(bf16[1024,512]{1,0:T(8,128)(2,1)} %add_convert_fusion.7), channel_id=1, source_target_pairs={{0,16},{16,0},{1,17},{17,1},{2,18},{18,2},{3,19},{19,3},{4,20},{20... | collective-permute-start | bytes 3145736 | tf_op jit(solution)/shard_map/ppermute | solution.py:524
  613.4 9.2 %collective-permute-start.40 = (bf16[1024,256]{1,0:T(8,128)(2,1)S(1)}, bf16[1024,256]{1,0:T(8,128)(2,1)S(1)}, u32[]{:S(2)}, u32[]{:S(2)}) collective-permute-start(bf16[1024,256]{1,0:T(8,128)(2,1)S(1)} %add_convert_fusion.14), channel_id=1, source_target_pairs={{0,16},{16,0},{1,17},{17,1},{2,18},{18,2},{3,19},{19,3},{4,20},{20... | collective-permute-start | bytes 1572872 | tf_op jit(solution)/shard_map/ppermute | solution.py:524
  616.8 9.2 %collective-permute-start.37 = (bf16[1024,256]{1,0:T(8,128)(2,1)S(1)}, bf16[1024,256]{1,0:T(8,128)(2,1)S(1)}, u32[]{:S(2)}, u32[]{:S(2)}) collective-permute-start(bf16[1024,256]{1,0:T(8,128)(2,1)S(1)} %add_convert_fusion.16), channel_id=1, source_target_pairs={{0,1},{1,0},{2,3},{3,2},{4,5},{5,4},{6,7},{7,6},{8,9},{9,8},{10,11... | collective-permute-start | bytes 1572872 | tf_op jit(solution)/shard_map/ppermute | solution.py:524
  628.5 109.7 %all-gather.11.cloned.1.call-start = ((), (), s32[]{:S(2)}) async-start(), calls=%async_computation.12 | async-start | bytes 3981312 | tf_op jit(solution)/shard_map/all_gather | solution.py:675
  640.0 114.5 %all-gather.13.cloned.1.call-start = ((), (), s32[]{:S(2)}) async-start(), calls=%async_computation.13 | async-start | bytes 3244032 | tf_op jit(solution)/shard_map/all_gather | solution.py:675
  682.5 1.6 collective-permute-start.44
  684.2 6.7 collective-permute-start.45
  690.9 5.7 collective-permute-start.46
  696.6 5.2 collective-permute-start.47
  701.8 9.8 %collective-permute-start.48 = (f32[280,128]{1,0:T(8,128)S(1)}, f32[280,128]{1,0:T(8,128)}, u32[]{:S(2)}, u32[]{:S(2)}) collective-permute-start(f32[280,128]{1,0:T(8,128)S(1)} %add.838), channel_id=1, source_target_pairs={{0,4},{2,6},{4,0},{6,2},{1,5},{3,7},{5,1},{7,3},{8,12},{10,14},{12... | collective-permute-start | bytes 430088 | tf_op jit(solution)/shard_map/ppermute | solution.py:802
  705.9 11.7 %collective-permute-start.41 = (bf16[1,1024,128]{2,1,0:T(8,128)(2,1)S(1)}, bf16[1,1024,128]{2,1,0:T(8,128)(2,1)}, u32[]{:S(2)}, u32[]{:S(2)}) collective-permute-start(bf16[1,1024,128]{2,1,0:T(8,128)(2,1)S(1)} %maximum_bitcast_fusion), channel_id=1, source_target_pairs={{0,1},{1,0},{2,3},{3,2},{4,5},{5,4},{6,7},{7,6},{8,9},{9,8},{10,11... | collective-permute-start | bytes 786440 | tf_op jit(solution)/shard_map/ppermute | solution.py:524
  718.7 18.4 %collective-permute-start.42 = (bf16[2,1024,128]{2,1,0:T(8,128)(2,1)S(1)}, bf16[2,1024,128]{2,1,0:T(8,128)(2,1)S(1)}, u32[]{:S(2)}, u32[]{:S(2)}) collective-permute-start(bf16[2,1024,128]{2,1,0:T(8,128)(2,1)S(1)} %pad_maximum_fusion.12), channel_id=1, source_target_pairs={{0,16},{16,0},{1,17},{17,1},{2,18},{18,2},{3,19},{19,3},{4,20},{20... | collective-permute-start | bytes 1572872 | tf_op jit(solution)/shard_map/ppermute | solution.py:524
  738.1 9.3 %collective-permute-start.43 = (bf16[4,1024,128]{2,1,0:T(8,128)(2,1)S(1)}, bf16[4,1024,128]{2,1,0:T(8,128)(2,1)S(1)}, u32[]{:S(2)}, u32[]{:S(2)}) collective-permute-start(bf16[4,1024,128]{2,1,0:T(8,128)(2,1)S(1)} %pad_maximum_fusion.6.refs_0_), channel_id=1, source_target_pairs={{0,8},{8,0},{1,9},{9,1},{2,10},{10,2},{3,11},{11,3},{4,12},{12,4},... | collective-permute-start | bytes 3145736 | tf_op jit(solution)/shard_map/ppermute | solution.py:524
  (173 other events, 1933.0 us)
Sparse Core Ops, SparseCore 0:
  10.9 85.4 all-gather.6
  99.9 119.6 all-gather.8
  496.7 20.9 reduce-scatter.11
  520.4 21.2 reduce-scatter.7
  566.0 18.3 reduce-scatter.9
  591.6 31.7 reduce-scatter.13
  628.6 25.1 reduce-scatter.5
  655.9 34.0 all-gather.10
  692.0 41.6 all-gather.12

commit v6 on v5

--- a/solution.py
+++ b/solution.py
@@ -441,7 +441,6 @@
     cor_shape = ((blocks, groups, ROWS, ROWS), BF16)
     x = points("conv", x)
     (n,) = call(conv_kernel, [n_shape], [], x, weights, masks)
-    n = points("conv_done", n)
     n = points("inverse", n)
     (inv,) = call(inverse_kernel, [inv_shape], [], n, col)
     inv = points("state", inv)
@@ -450,6 +449,7 @@
     behind = [(i + 1, i) for i in range(sp_size - 1)]
     for _ in range(sp_size - 1):
         (state,) = call(state_kernel, [state_shape], [], n, inv, col, start)
+        state = points("state_done", state)
         start = lax.ppermute(state.astype(BF16), "sp", ahead)
     mixed, cor, states = call(
         scan_kernel,
@@ -778,6 +778,13 @@
     )
 
 
+def by_member(value):
+    blocks = value.reshape(lax.axis_size("fsdp"), -1, value.shape[1])
+    return jnp.concatenate(
+        [blocks[:, :, i : i + 128] for i in range(0, value.shape[1], 128)], axis=1
+    )
+
+
 def pack_small(parts, width):
     flat = jnp.concatenate([p.reshape(-1) for p in parts])
     return jnp.pad(flat, (0, -flat.shape[0] % (16 * width))).reshape(-1, width)
@@ -838,7 +845,7 @@
     members = lax.axis_size("fsdp")
     qk_way = ColumnGather(input_weight[:, :qk_cols], "x")
     v_way = ColumnGather(input_weight[:, qk_cols:qkv_cols], "sp")
-    gate_way = ColumnGather(input_weight[:, qkv_cols:], "x")
+    gate_way = ColumnGather(input_weight[:, qkv_cols:], "sp")
     down_way = ColumnGather(down_weight, "x")
     pair_rows, pair_cols = qk_way.piece.shape[0], 2 * qk_way.piece.shape[1]
     smalls = (rate_weight, conv_weight, head_decay, mixer_gain, heads_gain, feed_gain)
@@ -871,34 +878,37 @@
         if name == "conv":
             gate_way.blocks(qkv_third, value)
             gate_way.second()
-            x_ready.append(value)
-            return value
-        if name == "conv_done":
-            down_way.blocks((x_ready[0],), value)
             return value
         if name == "inverse":
-            value = after(value, gate_way.held, down_way.held)
+            value = after(value, gate_way.held)
             gate_way.third(value)
-            down_way.second(value)
+            ready.append(value)
             return value
         if name == "state":
-            value = after(value, gate_way.held, down_way.held)
+            down_way.blocks(ready, value)
+            down_way.second()
+            return after(value, gate_way.held)
+        if name == "state_done":
             down_way.third(value)
             return value
         if name == "sent":
-            for key in ("out", "gate"):
+            for key in ("down", "out", "gate"):
                 sums[key].third(value)
             return value
         if name == "back":
-            return after(value, sums["down"].third())
+            return after(value, sums["down"].outgoing)
         if name == "conv_back":
             for key in ("out", "gate"):
                 sums[key].from_second = after(sums[key].from_second, value)
-            owns.extend(sums[key].own().astype(BF16) for key in ("down", "out", "gate"))
-            return after(value, *owns)
+            packed = jnp.concatenate(
+                [by_member(sums[key].own().astype(BF16)) for key in ("down", "out", "gate")],
+                axis=1,
+            )
+            owns.append(packed.reshape(-1, 128))
+            return after(value, owns[0], sums["up"].third())
         return value
 
-    sums, x_ready, owns = {}, [], []
+    sums, ready, owns = {}, [], []
 
     ends = jnp.cumsum(doc_lengths[0])
     positions = lax.broadcasted_iota(jnp.int32, (length * sp_size, 1), 0)
@@ -922,7 +932,7 @@
     rates = rate_raw.astype(BF16).astype(F32)
     mixed, pull_mix = mixer(qkv, conv_full, rates, decay_full, doc_ids, member, sp_size, points)
     gate_full, down_full = gate_way.full(), down_way.full()
-    gate_raw = reorder(dot_columns(normed_low, gate_full), "x")
+    gate_raw = reorder(dot_columns(normed_low, gate_full), "sp")
     gated, pull_gate = jax.vjp(output_gate, mixed.astype(F32), gate_raw, heads_scale)
     gated_low = gated.astype(BF16)
     attended = jnp.dot(gated_low, out_full, preferred_element_type=F32)
@@ -951,8 +961,8 @@
     d_gated = jnp.einsum("td,ed->te", d_att_low, out_full, preferred_element_type=F32)
     d_mixed, d_gate, heads_grad = pull_gate(d_gated)
     d_gate_low = d_gate.astype(BF16)
-    d_gate_rel = reorder(d_gate_low, "x")
-    sums["gate"] = ColumnSum(normed_low, d_gate_rel, "x")
+    d_gate_rel = reorder(d_gate_low, "sp")
+    sums["gate"] = ColumnSum(normed_low, d_gate_rel, "sp")
     d_mixed_low = after(
         d_mixed.astype(BF16), *(sums[key].second() for key in ("up", "out", "gate"))
     )
@@ -964,14 +974,19 @@
     d_v_rel = reorder(d_qkv[:, qk_cols:], "sp")
     sums["qk"] = ColumnSum(normed_low, d_qk_rel, "x")
     sums["v"] = ColumnSum(normed_low, d_v_rel, "sp")
-    sums["up"].third()
     sums["up"].from_y = after(sums["up"].from_y, sums["qk"].second(), sums["v"].second())
+    d_normed = dot_back(d_qk_rel, qk_full) + dot_back(d_v_rel, v_full)
+    d_normed = d_normed + dot_back(d_gate_rel, gate_full)
+    d_normed = d_normed + jnp.einsum(
+        "tf,df->td", d_rate_low, rate_full, preferred_element_type=F32
+    )
     for key in ("qk", "v"):
         sums[key].third()
+        sums[key].from_second = after(sums[key].from_second, d_normed)
     places = spread_places()
-    blocks = [sum_blocks(own) for own in owns]
-    down_rows, out_rows = blocks[0].shape[0], blocks[1].shape[0]
-    early_sums = spread_aside([narrow(block) for block in blocks])
+    early_block = sum_blocks(owns[0])
+    down_rows, out_rows = down_weight.shape[0], output_weight.shape[0]
+    early_sums = spread_aside([early_block])
     down_shard, output_shard = unpack(
         places,
         [(0, 0, 0, 0, down_rows, 1, 3), (0, down_rows, 1, 0, out_rows, 1, 4)],
@@ -987,23 +1002,18 @@
     )
     late_block = sum_blocks(jnp.concatenate([sums["qk"].own(), sums["v"].own()], axis=1))
     rows, wide = late_block.shape[0], late_block.shape[1] // 256
-    gate_wide = blocks[2].shape[1] // 128
+    gate_wide = H * DV // 8 // 128
     (input_shard,) = unpack(
         places,
         [
             (0, 0, 0, 0, rows, wide, 0),
             (0, wide * rows, 0, qk_cols, rows, wide, 1),
-            (1, down_rows + out_rows, 0, qkv_cols, rows, gate_wide, 3),
+            (1, down_rows + out_rows, 0, qkv_cols, rows, gate_wide, 4),
         ],
         spread([narrow(late_block)]) + early_sums,
         [input_weight.shape],
     )
     rate_grad = jnp.einsum("td,tf->df", normed_low, d_rate_low, preferred_element_type=F32)
-    d_normed = dot_back(d_qk_rel, qk_full) + dot_back(d_v_rel, v_full)
-    d_normed = d_normed + dot_back(d_gate_rel, gate_full)
-    d_normed = d_normed + jnp.einsum(
-        "tf,df->td", d_rate_low, rate_full, preferred_element_type=F32
-    )
     d_front, mixer_grad = pull_norm(d_normed)
     tokens_grad = (d_resid + d_front).astype(BF16)
     rate_sum, conv_sum, decay_sum, mixer_sum, heads_sum, feed_sum = sum_small(

time: 779 us -> 793 us (1.018)
  waiting for transfers between devices: 219 us -> 232 us
    ppermute x1, waiting for transfers between devices: 4.45 us -> 22.1 us  [pull(): dstart = lax.ppermute(points('sent', dstate.astype(BF16)), 'sp', behind)]
    ppermute x9, waiting for transfers between devices: 31.7 us -> 17.3 us  [shifted(): lax.ppermute(value, 'fsdp', [(i, (i + step) % count) for i in range(count)])]
    all_gather x2, waiting for transfers between devices: 0.02 us -> 11.2 us  [spread_aside(): lax.all_gather(jnp.concatenate(blocks, axis=0), ('x', 'core', 'sp'), axis=0)]
    unnamed x401 -> x398, local copies, waits for them, and re-layouts: 36.2 us -> 41.6 us
  transfers between devices with their start and end apart: 60 -> 58, of which waited for: 21 -> 23; matrix products, arithmetic and copies ran while one was open for 37% -> 37% of each run, Pallas kernels for 15% -> 14%
where the time goes in v6:
time: 793 us; the launch traced here: 784 us
  waiting for transfers between devices  232 us (29%)
  matrix products  145 us (18%)
  Pallas kernels  142 us (18%)
  local copies, waits for them, and re-layouts  109 us (14%)
  other arithmetic  80.4 us (10%)
  starting transfers between devices  59.9 us (8%)
  between operations  17.5 us (2%)
    ppermute x36, waiting for transfers between devices, swap(): return lax.ppermute(value, axis, [(0, 1), (1, 0)])  170 us
    pallas_call x7, Pallas kernels, call(): pl.pallas_call(kernel, out_shape=[jax.ShapeDtypeStruct(s, t) for s, t in...  125 us
    dot_general x24, matrix products, grad_dot(): return jnp.einsum('td,tf->df', left, right, preferred_element_type=F32)  67.7 us
    unnamed x398, local copies, waits for them, and re-layouts  41.6 us
    ppermute x36, starting transfers between devices, swap(): return lax.ppermute(value, axis, [(0, 1), (1, 0)])  32 us
    ppermute x1, waiting for transfers between devices, pull(): dstart = lax.ppermute(points('sent', dstate.astype(BF16)), 'sp', behind)  22.1 us
    dot_general x8, matrix products, dot_columns(): parts = [jnp.dot(values, w, preferred_element_type=F32) for w in halves_of]  20.4 us
    dot_general x4, matrix products, dot_back(): jnp.einsum('tf,df->td', grads[:, :half], halves_of[0], preferred_element_...  18.2 us
  transfers between devices with their start and end apart: 58, of which 23 were waited for; matrix products, arithmetic and copies ran while one was open for 37% of the time, Pallas kernels for 14%

profile of v6, /device:TPU:0, one launch (start us, length us, event | category | flops | bytes accessed | tf_op | source)
XLA Modules:
  0.0 784.3 jit_solution(17157308290786437156)
XLA Ops:
  16.8 5.1 collective-permute-start.1
  23.5 4.0 collective-permute-start
  32.5 17.3 %collective-permute-done.2 = bf16[288,512]{1,0:T(8,128)(2,1)S(1)} collective-permute-done((bf16[288,512]{1,0:T(8,128)(2,1)S(1)}, bf16[288,512]{1,0:T(8,128)(2,1)S(1)}, u32[]{:S(2)}, u32[]{:S(2)}) %collective-permute-start.2) | collective-permute-done | bytes 294944 | tf_op jit(solution)/shard_map/ppermute | solution.py:562
  54.6 9.4 %collective-permute-done.4 = bf16[1024,256]{1,0:T(8,128)(2,1)} collective-permute-done((bf16[1024,256]{1,0:T(8,128)(2,1)S(1)}, bf16[1024,256]{1,0:T(8,128)(2,1)}, u32[]{:S(2)}, u32[]{:S(2)}) %collective-permute-start.4) | collective-permute-done | bytes 524320 | tf_op jit(solution)/shard_map/ppermute | solution.py:524
  71.0 40.6 %collective-permute-done.7 = bf16[1024,256]{1,0:T(8,128)(2,1)S(1)} collective-permute-done((bf16[1024,256]{1,0:T(8,128)(2,1)S(1)}, bf16[1024,256]{1,0:T(8,128)(2,1)S(1)}, u32[]{:S(2)}, u32[]{:S(2)}) %collective-permute-start.7) | collective-permute-done | bytes 524320 | tf_op jit(solution)/shard_map/ppermute | solution.py:524
  112.8 2.9 pad_maximum_fusion
  116.4 5.3 reshape_reshape.6
  125.7 15.0 %collective-permute-done.8 = bf16[1024,512]{1,0:T(8,128)(2,1)} collective-permute-done((bf16[1024,512]{1,0:T(8,128)(2,1)}, bf16[1024,512]{1,0:T(8,128)(2,1)}, u32[]{:S(2)}, u32[]{:S(2)}) %collective-permute-start.8) | collective-permute-done | bytes 1048608 | tf_op jit(solution)/shard_map/ppermute | solution.py:524
  143.2 4.7 collective-permute-start.11
  161.0 6.3 collective-permute-start.13
  169.3 13.2 %shard_map.220.n_ref = bf16[384,4096]{1,0:T(8,128)(2,1)} custom-call(bf16[400,4096]{1,0:T(8,128)(2,1)} %copy-done.19, f32[4,4096]{1,0:T(4,128)} %bitcast.256, f32[384,8]{1,0:T(8,128)} %copy.205.mask_ref), custom_call_target="tpu_custom_call" | custom-call | flops 1 | bytes 1 | tf_op jit(solution)/shard_map/pallas_call | solution.py:386
  182.5 7.7 collective-permute-done.13
  194.8 27.3 %shard_map.221.inv_ref = f32[6,2,256,256]{3,2,1,0:T(8,128)} custom-call(bf16[384,4096]{1,0:T(8,128)(2,1)} %shard_map.220.n_ref, f32[384,128]{1,0:T(8,128)} %concatenate.204.col_ref), custom_call_target="tpu_custom_call" | custom-call | flops 1 | bytes 1 | tf_op jit(solution)/shard_map/pallas_call | solution.py:386
  232.9 15.4 %collective-permute-done.14 = bf16[1024,512]{1,0:T(8,128)(2,1)} collective-permute-done((bf16[1024,512]{1,0:T(8,128)(2,1)S(1)}, bf16[1024,512]{1,0:T(8,128)(2,1)}, u32[]{:S(2)}, u32[]{:S(2)}) %collective-permute-start.14) | collective-permute-done | bytes 1048608 | tf_op jit(solution)/shard_map/ppermute | solution.py:524
  250.6 10.1 %collective-permute-done.20 = bf16[2816,128]{1,0:T(8,128)(2,1)} collective-permute-done((bf16[2816,128]{1,0:T(8,128)(2,1)S(1)}, bf16[2816,128]{1,0:T(8,128)(2,1)}, u32[]{:S(2)}, u32[]{:S(2)}) %collective-permute-start.20) | collective-permute-done | bytes 720928 | tf_op jit(solution)/shard_map/ppermute | solution.py:524
  263.8 10.3 %shard_map.222 = f32[8,128,256]{2,1,0:T(8,128)} custom-call(bf16[384,4096]{1,0:T(8,128)(2,1)} %shard_map.220.n_ref, f32[6,2,256,256]{3,2,1,0:T(8,128)} %shard_map.221.inv_ref, f32[384,128]{1,0:T(8,128)} %concatenate.204.col_ref, bf16[8,128,256]{2,1,0:T(8,128)(2,1)} %broadcast_20_start_ref.2.start_ref), custom_call_target="tpu_custom_call" | custom-call | flops 1 | bytes 1 | tf_op jit(solution)/shard_map/pallas_call | solution.py:386
  286.4 2.9 collective-permute-done.15.start_ref
  290.0 13.5 %shard_map.223 = (bf16[384,2048]{1,0:T(8,128)(2,1)}, bf16[6,2,256,256]{3,2,1,0:T(8,128)(2,1)}, bf16[6,8,128,256]{3,2,1,0:T(8,128)(2,1)}) custom-call(bf16[384,4096]{1,0:T(8,128)(2,1)} %shard_map.220.n_ref, f32[6,2,256,256]{3,2,1,0:T(8,128)} %shard_map.221.inv_ref, f32[384,128]{1,0:T(8,128)} %concatenate.204.col_ref, bf16[8,128,256]{2,1,0:T(8,128)(2,1)} %copy-done.71), custom_call_target="tpu_custom_call" | custom-call | flops 1 | bytes 1 | tf_op jit(solution)/shard_map/pallas_call | solution.py:386
  309.9 3.7 constant_dynamic-update-slice_fusion.23
  322.7 4.7 multiply_reduce_fusion.4
  329.7 5.2 fusion.172
  335.0 8.0 %fusion.245 = f32[384,5632]{1,0:T(8,128)S(1)} fusion(bf16[384,1024]{1,0:T(8,128)(2,1)} %multiply_convert_fusion.2, bf16[1024,5632]{1,0:T(8,128)(2,1)} %all-gather.9.cloned.1.call-done), kind=kOutput, calls=%fused_computation.527 | convolution fusion | flops 4429185024 | bytes 20971520 | tf_op jit(solution)/shard_map/dot_general | solution.py:941
  343.0 7.3 fusion.54
  350.3 3.3 convolution_convert_fusion.1
  366.1 4.2 add_convert_fusion
  370.6 5.7 convolution_convert_fusion
  376.5 3.5 add_convert_fusion.5
  380.1 8.4 %multiply_reduce_fusion.2 = (f32[1024]{0:T(1024)}, f32[384]{0:T(512)S(1)}, f32[384,1024]{1,0:T(8,128)S(1)}) fusion(f32[384,1024]{1,0:T(8,128)S(1)} %copy-done.15, f32[384]{0:T(512)S(1)} %copy-done.136, f32[1024]{0:T(1024)S(1)} %bitcast.274, bf16[384,5632]{1,0:T(8,128)(2,1)S(1)} %add_convert_fusion, bf16[1024,5632]{1,0:T(8,128)(2,1)} %all-gather.9.cloned.1.call-done), kind=kOutput, calls=%fused_computation.122 | convolution fusion | flops 4431542784 | bytes 19016704 | tf_op jit(solution)/shard_map/tf,df->td/dot_general | solution.py:956
  402.1 5.7 multiply_reduce_fusion
  415.7 3.9 fusion.25
  422.7 4.0 fusion.165
  426.7 3.0 add_convert_fusion.8
  432.3 3.0 add_convert_fusion.9
  435.4 5.1 add_convert_fusion.2
  442.0 13.4 %shard_map.224 = f32[8,128,256]{2,1,0:T(8,128)} custom-call(bf16[384,4096]{1,0:T(8,128)(2,1)} %shard_map.220.n_ref, f32[6,2,256,256]{3,2,1,0:T(8,128)} %shard_map.221.inv_ref, f32[384,128]{1,0:T(8,128)} %concatenate.204.col_ref, bf16[384,2048]{1,0:T(8,128)(2,1)} %get-tuple-element.60.dout_ref, bf16[8,128,256]{2,1,0:T(8,128)(2,1)} %broadcast_20_start_ref.2.start_ref), custom_call_target="tpu_custom_call" | custom-call | flops 1 | bytes 1 | tf_op jit(solution)/shard_map/pallas_call | solution.py:386
  456.8 3.7 add_convert_fusion.12
  468.5 10.6 %collective-permute-done.30 = bf16[2048,256]{1,0:T(8,128)(2,1)} collective-permute-done((bf16[2048,256]{1,0:T(8,128)(2,1)}, bf16[2048,256]{1,0:T(8,128)(2,1)}, u32[]{:S(2)}, u32[]{:S(2)}) %collective-permute-start.30) | collective-permute-done | bytes 1048608 | tf_op jit(solution)/shard_map/ppermute | solution.py:524
  483.2 22.1 %collective-permute-done.27.start_ref = bf16[8,128,256]{2,1,0:T(8,128)(2,1)S(1)} collective-permute-done((bf16[8,128,256]{2,1,0:T(8,128)(2,1)S(1)}, bf16[8,128,256]{2,1,0:T(8,128)(2,1)S(1)}, u32[]{:S(2)}, u32[]{:S(2)}) %collective-permute-start.27) | collective-permute-done | bytes 524320 | tf_op jit(solution)/shard_map/ppermute | solution.py:470
  506.1 24.7 %shard_map.225 = (f32[384,4096]{1,0:T(8,128)}, f32[384,128]{1,0:T(8,128)}) custom-call(bf16[384,4096]{1,0:T(8,128)(2,1)} %shard_map.220.n_ref, f32[6,2,256,256]{3,2,1,0:T(8,128)} %shard_map.221.inv_ref, f32[384,128]{1,0:T(8,128)} %concatenate.204.col_ref, bf16[384,2048]{1,0:T(8,128)(2,1)} %get-tuple-element.60.dout_ref, ...), custom_call_target="tpu_custom_call" | custom-call | flops 1 | bytes 1 | tf_op jit(solution)/shard_map/pallas_call | solution.py:386
  532.8 6.3 collective-permute-done.31
  543.6 3.9 add_convert_fusion.4
  547.6 23.1 %shard_map.226 = (bf16[400,4096]{1,0:T(8,128)(2,1)}, f32[4,4096]{1,0:T(4,128)}) custom-call(bf16[400,4096]{1,0:T(8,128)(2,1)} %copy-done.19, f32[4,4096]{1,0:T(4,128)} %bitcast.257, f32[384,8]{1,0:T(8,128)} %copy.205.mask_ref, f32[384,4096]{1,0:T(8,128)} %get-tuple-element.70.dn_ref), custom_call_target="tpu_custom_call" | custom-call | flops 1 | bytes 1 | tf_op jit(solution)/shard_map/pallas_call | solution.py:386
  574.2 4.4 collective-permute-done.35
  590.9 3.8 fusion.39
  597.7 3.0 add_convert_fusion.6
  602.7 3.1 add_convert_fusion.7
  606.3 18.9 %collective-permute-done.50 = bf16[512,1408]{1,0:T(8,128)(2,1)S(1)} collective-permute-done((bf16[512,1408]{1,0:T(8,128)(2,1)}, bf16[512,1408]{1,0:T(8,128)(2,1)S(1)}, u32[]{:S(2)}, u32[]{:S(2)}) %collective-permute-start.50) | collective-permute-done | bytes 1441824 | tf_op jit(solution)/shard_map/ppermute | solution.py:524
  625.2 3.7 add_convert_fusion.3
  633.2 2.9 fusion.164
  636.1 10.7 %collective-permute-done.40 = bf16[1024,512]{1,0:T(8,128)(2,1)} collective-permute-done((bf16[1024,512]{1,0:T(8,128)(2,1)}, bf16[1024,512]{1,0:T(8,128)(2,1)}, u32[]{:S(2)}, u32[]{:S(2)}) %collective-permute-start.40) | collective-permute-done | bytes 1048608 | tf_op jit(solution)/shard_map/ppermute | solution.py:524
  651.7 4.4 fusion.16
  656.2 5.7 collective-permute-done.41
  670.7 3.9 fusion.246
  674.6 3.1 fusion.247
  693.8 3.3 collective-permute-done.46
  699.4 3.2 collective-permute-done.47
  711.8 4.4 fusion.18
  728.4 11.3 %collective-permute-done.43 = bf16[2,1024,128]{2,1,0:T(8,128)(2,1)S(1)} collective-permute-done((bf16[2,1024,128]{2,1,0:T(8,128)(2,1)S(1)}, bf16[2,1024,128]{2,1,0:T(8,128)(2,1)S(1)}, u32[]{:S(2)}, u32[]{:S(2)}) %collective-permute-start.43) | collective-permute-done | bytes 524320 | tf_op jit(solution)/shard_map/ppermute | solution.py:524
  740.9 4.3 fusion.230
  745.2 4.9 shard_map.228
  751.1 6.1 shard_map.227
  757.2 11.2 %all-gather.13.cloned.1.call-done = bf16[11264,128]{1,0:T(8,128)(2,1)} async-done(((bf16[1408,128]{1,0:T(8,128)(2,1)}), bf16[11264,128]{1,0:T(8,128)(2,1)}) %all-gather.13.cloned.1.call-update) | async-done | bytes 2883600 | tf_op jit(solution)/shard_map/all_gather | solution.py:675
  768.3 3.6 fusion.233
  771.9 5.1 shard_map.229
  (733 shorter events, 244.2 us)
Async XLA Ops:
  7.2 315.5 %all-gather.7.cloned.1.call-start = ((), (), s32[]{:S(2)}) async-start(), calls=%async_computation.3 | async-start | bytes 4325376 | tf_op jit(solution)/shard_map/all_gather | solution.py:590
  9.0 325.9 %all-gather.9.cloned.1.call-start = ((), (), s32[]{:S(2)}) async-start(), calls=%async_computation.4 | async-start | bytes 11894784 | tf_op jit(solution)/shard_map/all_gather | solution.py:590
  9.9 658.4 %reduce-scatter.6.cloned.1.call-start = ((), (), s32[]{:S(2)}) async-start(), calls=%async_computation.6 | async-start | bytes 2211840 | tf_op jit(solution)/shard_map/reduce_scatter | solution.py:574
  16.8 15.7 %collective-permute-start.1 = (bf16[288,512]{1,0:T(8,128)(2,1)S(1)}, bf16[288,512]{1,0:T(8,128)(2,1)S(1)}, u32[]{:S(2)}, u32[]{:S(2)}) collective-permute-start(bf16[288,512]{1,0:T(8,128)(2,1)S(1)} %pad_maximum_fusion.18), channel_id=1, source_target_pairs={{0,6},{2,0},{4,2},{6,4},{1,7},{3,1},{5,3},{7,5},{8,14},{10,8},{12,... | collective-permute-start | bytes 884744 | tf_op jit(solution)/shard_map/ppermute | solution.py:562
  21.9 27.9 %collective-permute-start.2 = (bf16[288,512]{1,0:T(8,128)(2,1)S(1)}, bf16[288,512]{1,0:T(8,128)(2,1)S(1)}, u32[]{:S(2)}, u32[]{:S(2)}) collective-permute-start(bf16[288,512]{1,0:T(8,128)(2,1)S(1)} %pad_maximum_fusion.18), channel_id=1, source_target_pairs={{0,4},{2,6},{4,0},{6,2},{1,5},{3,7},{5,1},{7,3},{8,12},{10,14},{12... | collective-permute-start | bytes 884744 | tf_op jit(solution)/shard_map/ppermute | solution.py:562
  21.9 27.9 %collective-permute-start.3 = (bf16[288,512]{1,0:T(8,128)(2,1)S(1)}, bf16[288,512]{1,0:T(8,128)(2,1)S(1)}, u32[]{:S(2)}, u32[]{:S(2)}) collective-permute-start(bf16[288,512]{1,0:T(8,128)(2,1)S(1)} %pad_maximum_fusion.18), channel_id=1, source_target_pairs={{0,2},{2,4},{4,6},{6,0},{1,3},{3,5},{5,7},{7,1},{8,10},{10,12},{12... | collective-permute-start | bytes 884744 | tf_op jit(solution)/shard_map/ppermute | solution.py:562
  23.5 30.2 %collective-permute-start = (bf16[16,1024]{1,0:T(8,128)(2,1)}, bf16[16,1024]{1,0:T(8,128)(2,1)}, u32[]{:S(2)}, u32[]{:S(2)}) collective-permute-start(bf16[16,1024]{1,0:T(8,128)(2,1)} %slice.313), channel_id=1, source_target_pairs={{0,1},{2,3},{4,5},{6,7},{8,9},{10,11},{12,13},{14,15},{16,17},{18,... | collective-permute-start | bytes 98312 | tf_op jit(solution)/shard_map/ppermute | solution.py:918
  50.3 97.8 %copy-start.39 = (bf16[1024,256]{1,0:T(8,128)(2,1)}, bf16[1024,256]{1,0:T(8,128)(2,1)S(1)}, u32[]{:S(2)}) copy-start(bf16[1024,256]{1,0:T(8,128)(2,1)S(1)} %get-tuple-element.132) | copy-start | bytes 1572868
  50.3 13.8 %collective-permute-start.4 = (bf16[1024,256]{1,0:T(8,128)(2,1)S(1)}, bf16[1024,256]{1,0:T(8,128)(2,1)}, u32[]{:S(2)}, u32[]{:S(2)}) collective-permute-start(bf16[1024,256]{1,0:T(8,128)(2,1)S(1)} %get-tuple-element.132), channel_id=1, source_target_pairs={{0,1},{1,0},{2,3},{3,2},{4,5},{5,4},{6,7},{7,6},{8,9},{9,8},{10,11... | collective-permute-start | bytes 1572872 | tf_op jit(solution)/shard_map/ppermute | solution.py:524
  52.1 140.2 %copy-start.129 = (f32[6,64]{1,0:T(8,128)}, f32[6,64]{1,0:T(8,128)S(1)}, u32[]{:S(2)}) copy-start(f32[6,64]{1,0:T(8,128)S(1)} %get-tuple-element.176) | copy-start | bytes 4612
  52.1 140.2 %copy-start.133 = (f32[6,64]{1,0:T(8,128)}, f32[6,64]{1,0:T(8,128)S(1)}, u32[]{:S(2)}) copy-start(f32[6,64]{1,0:T(8,128)S(1)} %get-tuple-element.177) | copy-start | bytes 4612
  66.2 46.7 %collective-permute-start.5 = (bf16[1024,512]{1,0:T(8,128)(2,1)}, bf16[1024,512]{1,0:T(8,128)(2,1)}, u32[]{:S(2)}, u32[]{:S(2)}) collective-permute-start(bf16[1024,512]{1,0:T(8,128)(2,1)} %pad_maximum_fusion.4), channel_id=1, source_target_pairs={{0,16},{16,0},{1,17},{17,1},{2,18},{18,2},{3,19},{19,3},{4,20},{20... | collective-permute-start | bytes 3145736 | tf_op jit(solution)/shard_map/ppermute | solution.py:524
  68.3 43.4 %collective-permute-start.7 = (bf16[1024,256]{1,0:T(8,128)(2,1)S(1)}, bf16[1024,256]{1,0:T(8,128)(2,1)S(1)}, u32[]{:S(2)}, u32[]{:S(2)}) collective-permute-start(bf16[1024,256]{1,0:T(8,128)(2,1)S(1)} %get-tuple-element.131), channel_id=1, source_target_pairs={{0,16},{16,0},{1,17},{17,1},{2,18},{18,2},{3,19},{19,3},{4,20},{20... | collective-permute-start | bytes 1572872 | tf_op jit(solution)/shard_map/ppermute | solution.py:524
  69.6 72.7 %copy-start.115 = (f32[1,2,4,128]{3,1,2,0:T(2,128)}, f32[1,2,4,128]{3,1,2,0:T(2,128)S(1)}, u32[]{:S(2)}) copy-start(f32[1,2,4,128]{3,1,2,0:T(2,128)S(1)} %copy.250) | copy-start | bytes 12292
  112.8 27.9 %collective-permute-start.8 = (bf16[1024,512]{1,0:T(8,128)(2,1)}, bf16[1024,512]{1,0:T(8,128)(2,1)}, u32[]{:S(2)}, u32[]{:S(2)}) collective-permute-start(bf16[1024,512]{1,0:T(8,128)(2,1)} %pad_maximum_fusion.5), channel_id=1, source_target_pairs={{0,1},{1,0},{2,3},{3,2},{4,5},{5,4},{6,7},{7,6},{8,9},{9,8},{10,11... | collective-permute-start | bytes 3145736 | tf_op jit(solution)/shard_map/ppermute | solution.py:524
  115.8 36.9 %collective-permute-start.6 = (bf16[1024,1024]{1,0:T(8,128)(2,1)}, bf16[1024,1024]{1,0:T(8,128)(2,1)}, u32[]{:S(2)}, u32[]{:S(2)}) collective-permute-start(bf16[1024,1024]{1,0:T(8,128)(2,1)} %pad_maximum_fusion), channel_id=1, source_target_pairs={{0,8},{8,0},{1,9},{9,1},{2,10},{10,2},{3,11},{11,3},{4,12},{12,4},... | collective-permute-start | bytes 6291464 | tf_op jit(solution)/shard_map/ppermute | solution.py:524
  124.0 157.2 %copy-start.4 = (bf16[384,1024]{1,0:T(8,128)(2,1)}, bf16[384,1024]{1,0:T(8,128)(2,1)S(1)}, u32[]{:S(2)}) copy-start(bf16[384,1024]{1,0:T(8,128)(2,1)S(1)} %fusion.15) | copy-start | bytes 2359300
  142.1 14.3 %collective-permute-start.9 = (bf16[1024,1024]{1,0:T(8,128)(2,1)S(1)}, bf16[1024,1024]{1,0:T(8,128)(2,1)S(1)}, u32[]{:S(2)}, u32[]{:S(2)}) collective-permute-start(bf16[1024,1024]{1,0:T(8,128)(2,1)S(1)} %pad_maximum_fusion.1), channel_id=1, source_target_pairs={{0,8},{8,0},{1,9},{9,1},{2,10},{10,2},{3,11},{11,3},{4,12},{12,4},... | collective-permute-start | bytes 6291464 | tf_op jit(solution)/shard_map/ppermute | solution.py:524
  143.1 17.6 %collective-permute-start.10 = (bf16[256,256]{1,0:T(8,128)(2,1)S(1)}, bf16[256,256]{1,0:T(8,128)(2,1)S(1)}, u32[]{:S(2)}, u32[]{:S(2)}) collective-permute-start(bf16[256,256]{1,0:T(8,128)(2,1)S(1)} %constant_dynamic-slice_fusion.48), channel_id=1, source_target_pairs={{0,6},{2,0},{4,2},{6,4},{1,7},{3,1},{5,3},{7,5},{8,14},{10,8},{12,... | collective-permute-start | bytes 393224 | tf_op jit(solution)/shard_map/ppermute | solution.py:562
  143.2 17.7 %collective-permute-start.11 = (bf16[256,256]{1,0:T(8,128)(2,1)S(1)}, bf16[256,256]{1,0:T(8,128)(2,1)S(1)}, u32[]{:S(2)}, u32[]{:S(2)}) collective-permute-start(bf16[256,256]{1,0:T(8,128)(2,1)S(1)} %constant_dynamic-slice_fusion.48), channel_id=1, source_target_pairs={{0,4},{2,6},{4,0},{6,2},{1,5},{3,7},{5,1},{7,3},{8,12},{10,14},{12... | collective-permute-start | bytes 393224 | tf_op jit(solution)/shard_map/ppermute | solution.py:562
  147.8 13.0 %collective-permute-start.12 = (bf16[256,256]{1,0:T(8,128)(2,1)S(1)}, bf16[256,256]{1,0:T(8,128)(2,1)S(1)}, u32[]{:S(2)}, u32[]{:S(2)}) collective-permute-start(bf16[256,256]{1,0:T(8,128)(2,1)S(1)} %constant_dynamic-slice_fusion.48), channel_id=1, source_target_pairs={{0,2},{2,4},{4,6},{6,0},{1,3},{3,5},{5,7},{7,1},{8,10},{10,12},{12... | collective-permute-start | bytes 393224 | tf_op jit(solution)/shard_map/ppermute | solution.py:562
  161.0 29.2 %collective-permute-start.13 = (bf16[1024,256]{1,0:T(8,128)(2,1)S(1)}, bf16[1024,256]{1,0:T(8,128)(2,1)S(1)}, u32[]{:S(2)}, u32[]{:S(2)}) collective-permute-start(bf16[1024,256]{1,0:T(8,128)(2,1)S(1)} %constant_dynamic-slice_fusion.47), channel_id=1, source_target_pairs={{0,16},{16,0},{1,17},{17,1},{2,18},{18,2},{3,19},{19,3},{4,20},{20... | collective-permute-start | bytes 1572872 | tf_op jit(solution)/shard_map/ppermute | solution.py:524
  190.3 31.8 %collective-permute-start.17 = (bf16[704,128]{1,0:T(8,128)(2,1)}, bf16[704,128]{1,0:T(8,128)(2,1)}, u32[]{:S(2)}, u32[]{:S(2)}) collective-permute-start(bf16[704,128]{1,0:T(8,128)(2,1)} %constant_dynamic-slice_fusion.44), channel_id=1, source_target_pairs={{0,6},{2,0},{4,2},{6,4},{1,7},{3,1},{5,3},{7,5},{8,14},{10,8},{12,... | collective-permute-start | bytes 540680 | tf_op jit(solution)/shard_map/ppermute | solution.py:562
  191.1 31.0 %collective-permute-start.18 = (bf16[704,128]{1,0:T(8,128)(2,1)}, bf16[704,128]{1,0:T(8,128)(2,1)}, u32[]{:S(2)}, u32[]{:S(2)}) collective-permute-start(bf16[704,128]{1,0:T(8,128)(2,1)} %constant_dynamic-slice_fusion.44), channel_id=1, source_target_pairs={{0,4},{2,6},{4,0},{6,2},{1,5},{3,7},{5,1},{7,3},{8,12},{10,14},{12... | collective-permute-start | bytes 540680 | tf_op jit(solution)/shard_map/ppermute | solution.py:562
  191.1 31.0 %collective-permute-start.19 = (bf16[704,128]{1,0:T(8,128)(2,1)}, bf16[704,128]{1,0:T(8,128)(2,1)}, u32[]{:S(2)}, u32[]{:S(2)}) collective-permute-start(bf16[704,128]{1,0:T(8,128)(2,1)} %constant_dynamic-slice_fusion.44), channel_id=1, source_target_pairs={{0,2},{2,4},{4,6},{6,0},{1,3},{3,5},{5,7},{7,1},{8,10},{10,12},{12... | collective-permute-start | bytes 540680 | tf_op jit(solution)/shard_map/ppermute | solution.py:562
  222.1 26.2 %collective-permute-start.14 = (bf16[1024,512]{1,0:T(8,128)(2,1)S(1)}, bf16[1024,512]{1,0:T(8,128)(2,1)}, u32[]{:S(2)}, u32[]{:S(2)}) collective-permute-start(bf16[1024,512]{1,0:T(8,128)(2,1)S(1)} %pad_maximum_fusion.6), channel_id=1, source_target_pairs={{0,1},{1,0},{2,3},{3,2},{4,5},{5,4},{6,7},{7,6},{8,9},{9,8},{10,11... | collective-permute-start | bytes 3145736 | tf_op jit(solution)/shard_map/ppermute | solution.py:524
  228.9 31.7 %collective-permute-start.20 = (bf16[2816,128]{1,0:T(8,128)(2,1)S(1)}, bf16[2816,128]{1,0:T(8,128)(2,1)}, u32[]{:S(2)}, u32[]{:S(2)}) collective-permute-start(bf16[2816,128]{1,0:T(8,128)(2,1)S(1)} %constant_dynamic-slice_fusion.43), channel_id=1, source_target_pairs={{0,1},{1,0},{2,3},{3,2},{4,5},{5,4},{6,7},{7,6},{8,9},{9,8},{10,11... | collective-permute-start | bytes 2162696 | tf_op jit(solution)/shard_map/ppermute | solution.py:524
  250.6 63.1 %collective-permute-start.16 = (bf16[1024,1024]{1,0:T(8,128)(2,1)}, bf16[1024,1024]{1,0:T(8,128)(2,1)}, u32[]{:S(2)}, u32[]{:S(2)}) collective-permute-start(bf16[1024,1024]{1,0:T(8,128)(2,1)} %constant_dynamic-update-slice_fusion.14), channel_id=1, source_target_pairs={{0,8},{8,0},{1,9},{9,1},{2,10},{10,2},{3,11},{11,3},{4,12},{12,4},... | collective-permute-start | bytes 6291464 | tf_op jit(solution)/shard_map/ppermute | solution.py:524
  274.2 35.8 %collective-permute-start.21 = (bf16[2816,256]{1,0:T(8,128)(2,1)}, bf16[2816,256]{1,0:T(8,128)(2,1)}, u32[]{:S(2)}, u32[]{:S(2)}) collective-permute-start(bf16[2816,256]{1,0:T(8,128)(2,1)} %pad_maximum_fusion.3), channel_id=1, source_target_pairs={{0,16},{16,0},{1,17},{17,1},{2,18},{18,2},{3,19},{19,3},{4,20},{20... | collective-permute-start | bytes 4325384 | tf_op jit(solution)/shard_map/ppermute | solution.py:524
  277.3 111.2 %copy-start.127 = (f32[1,2,4,128]{3,1,2,0:T(2,128)}, f32[1,2,4,128]{3,1,2,0:T(2,128)S(1)}, u32[]{:S(2)}) copy-start(f32[1,2,4,128]{3,1,2,0:T(2,128)S(1)} %copy.255) | copy-start | bytes 12292
  278.6 10.6 %collective-permute-start.15 = (bf16[8,128,256]{2,1,0:T(8,128)(2,1)S(1)}, bf16[8,128,256]{2,1,0:T(8,128)(2,1)S(1)}, u32[]{:S(2)}, u32[]{:S(2)}) collective-permute-start(bf16[8,128,256]{2,1,0:T(8,128)(2,1)S(1)} %convert_element_type.345), channel_id=1, source_target_pairs={{0,1},{2,3},{4,5},{6,7},{8,9},{10,11},{12,13},{14,15},{16,17},{18,... | collective-permute-start | bytes 1572872 | tf_op jit(solution)/shard_map/ppermute | solution.py:453
  313.6 16.0 %collective-permute-start.22 = (bf16[2816,512]{1,0:T(8,128)(2,1)}, bf16[2816,512]{1,0:T(8,128)(2,1)}, u32[]{:S(2)}, u32[]{:S(2)}) collective-permute-start(bf16[2816,512]{1,0:T(8,128)(2,1)} %constant_dynamic-update-slice_fusion.23), channel_id=1, source_target_pairs={{0,8},{8,0},{1,9},{9,1},{2,10},{10,2},{3,11},{11,3},{4,12},{12,4},... | collective-permute-start | bytes 8650760 | tf_op jit(solution)/shard_map/ppermute | solution.py:524
  353.6 22.8 %collective-permute-start.23 = (bf16[2816,512]{1,0:T(8,128)(2,1)}, bf16[2816,512]{1,0:T(8,128)(2,1)}, u32[]{:S(2)}, u32[]{:S(2)}) collective-permute-start(bf16[2816,512]{1,0:T(8,128)(2,1)} %convolution_convert_fusion.1), channel_id=1, source_target_pairs={{0,8},{8,0},{1,9},{9,1},{2,10},{10,2},{3,11},{11,3},{4,12},{12,4},... | collective-permute-start | bytes 8650760 | tf_op jit(solution)/shard_map/ppermute | solution.py:524
  376.4 59.0 %collective-permute-start.24 = (bf16[1024,2816]{1,0:T(8,128)(2,1)}, bf16[1024,2816]{1,0:T(8,128)(2,1)}, u32[]{:S(2)}, u32[]{:S(2)}) collective-permute-start(bf16[1024,2816]{1,0:T(8,128)(2,1)} %convolution_convert_fusion), channel_id=1, source_target_pairs={{0,8},{8,0},{1,9},{9,1},{2,10},{10,2},{3,11},{11,3},{4,12},{12,4},... | collective-permute-start | bytes 17301512 | tf_op jit(solution)/shard_map/ppermute | solution.py:524
  411.6 15.0 %collective-permute-start.26 = (bf16[1024,1024]{1,0:T(8,128)(2,1)}, bf16[1024,1024]{1,0:T(8,128)(2,1)}, u32[]{:S(2)}, u32[]{:S(2)}) collective-permute-start(bf16[1024,1024]{1,0:T(8,128)(2,1)} %convolution_convert_fusion.5), channel_id=1, source_target_pairs={{0,8},{8,0},{1,9},{9,1},{2,10},{10,2},{3,11},{11,3},{4,12},{12,4},... | collective-permute-start | bytes 6291464 | tf_op jit(solution)/shard_map/ppermute | solution.py:524
  415.6 16.6 %collective-permute-start.25 = (bf16[2048,512]{1,0:T(8,128)(2,1)}, bf16[2048,512]{1,0:T(8,128)(2,1)}, u32[]{:S(2)}, u32[]{:S(2)}) collective-permute-start(bf16[2048,512]{1,0:T(8,128)(2,1)} %convolution_convert_fusion.2), channel_id=1, source_target_pairs={{0,8},{8,0},{1,9},{9,1},{2,10},{10,2},{3,11},{11,3},{4,12},{12,4},... | collective-permute-start | bytes 6291464 | tf_op jit(solution)/shard_map/ppermute | solution.py:524
  420.5 36.2 %collective-permute-start.28 = (bf16[2816,256]{1,0:T(8,128)(2,1)}, bf16[2816,256]{1,0:T(8,128)(2,1)}, u32[]{:S(2)}, u32[]{:S(2)}) collective-permute-start(bf16[2816,256]{1,0:T(8,128)(2,1)} %add_convert_fusion.5), channel_id=1, source_target_pairs={{0,16},{16,0},{1,17},{17,1},{2,18},{18,2},{3,19},{19,3},{4,20},{20... | collective-permute-start | bytes 4325384 | tf_op jit(solution)/shard_map/ppermute | solution.py:524
  429.8 35.7 %collective-permute-start.32 = (bf16[1024,512]{1,0:T(8,128)(2,1)}, bf16[1024,512]{1,0:T(8,128)(2,1)}, u32[]{:S(2)}, u32[]{:S(2)}) collective-permute-start(bf16[1024,512]{1,0:T(8,128)(2,1)} %add_convert_fusion.8), channel_id=1, source_target_pairs={{0,1},{1,0},{2,3},{3,2},{4,5},{5,4},{6,7},{7,6},{8,9},{9,8},{10,11... | collective-permute-start | bytes 3145736 | tf_op jit(solution)/shard_map/ppermute | solution.py:524
  435.3 43.7 %collective-permute-start.30 = (bf16[2048,256]{1,0:T(8,128)(2,1)}, bf16[2048,256]{1,0:T(8,128)(2,1)}, u32[]{:S(2)}, u32[]{:S(2)}) collective-permute-start(bf16[2048,256]{1,0:T(8,128)(2,1)} %add_convert_fusion.9), channel_id=1, source_target_pairs={{0,1},{1,0},{2,3},{3,2},{4,5},{5,4},{6,7},{7,6},{8,9},{9,8},{10,11... | collective-permute-start | bytes 3145736 | tf_op jit(solution)/shard_map/ppermute | solution.py:524
  440.5 103.1 %collective-permute-start.34 = (bf16[1024,1408]{1,0:T(8,128)(2,1)}, bf16[1024,1408]{1,0:T(8,128)(2,1)}, u32[]{:S(2)}, u32[]{:S(2)}) collective-permute-start(bf16[1024,1408]{1,0:T(8,128)(2,1)} %add_convert_fusion.2), channel_id=1, source_target_pairs={{0,16},{16,0},{1,17},{17,1},{2,18},{18,2},{3,19},{19,3},{4,20},{20... | collective-permute-start | bytes 8650760 | tf_op jit(solution)/shard_map/ppermute | solution.py:524
  460.5 70.3 %collective-permute-start.29 = (bf16[2816,128]{1,0:T(8,128)(2,1)}, bf16[2816,128]{1,0:T(8,128)(2,1)}, u32[]{:S(2)}, u32[]{:S(2)}) collective-permute-start(bf16[2816,128]{1,0:T(8,128)(2,1)} %add_convert_fusion.12), channel_id=1, source_target_pairs={{0,1},{1,0},{2,3},{3,2},{4,5},{5,4},{6,7},{7,6},{8,9},{9,8},{10,11... | collective-permute-start | bytes 2162696 | tf_op jit(solution)/shard_map/ppermute | solution.py:524
  464.0 41.3 %collective-permute-start.27 = (bf16[8,128,256]{2,1,0:T(8,128)(2,1)S(1)}, bf16[8,128,256]{2,1,0:T(8,128)(2,1)S(1)}, u32[]{:S(2)}, u32[]{:S(2)}) collective-permute-start(bf16[8,128,256]{2,1,0:T(8,128)(2,1)S(1)} %convert_element_type.372), channel_id=1, source_target_pairs={{1,0},{3,2},{5,4},{7,6},{9,8},{11,10},{13,12},{15,14},{17,16},{19,... | collective-permute-start | bytes 1572872 | tf_op jit(solution)/shard_map/ppermute | solution.py:470
  467.9 64.8 %collective-permute-start.33 = (bf16[1024,256]{1,0:T(8,128)(2,1)}, bf16[1024,256]{1,0:T(8,128)(2,1)S(1)}, u32[]{:S(2)}, u32[]{:S(2)}) collective-permute-start(bf16[1024,256]{1,0:T(8,128)(2,1)} %add_convert_fusion.18), channel_id=1, source_target_pairs={{0,16},{16,0},{1,17},{17,1},{2,18},{18,2},{3,19},{19,3},{4,20},{20... | collective-permute-start | bytes 1572872 | tf_op jit(solution)/shard_map/ppermute | solution.py:524
  481.7 57.3 %collective-permute-start.31 = (bf16[2048,128]{1,0:T(8,128)(2,1)}, bf16[2048,128]{1,0:T(8,128)(2,1)}, u32[]{:S(2)}, u32[]{:S(2)}) collective-permute-start(bf16[2048,128]{1,0:T(8,128)(2,1)} %add_convert_fusion.20), channel_id=1, source_target_pairs={{0,16},{16,0},{1,17},{17,1},{2,18},{18,2},{3,19},{19,3},{4,20},{20... | collective-permute-start | bytes 1572872 | tf_op jit(solution)/shard_map/ppermute | solution.py:524
  571.6 7.0 collective-permute-start.35
  573.9 105.3 %reduce-scatter.8.cloned.1.call-start = ((), (), s32[]{:S(2)}) async-start(), calls=%async_computation.7 | async-start | bytes 1802240 | tf_op jit(solution)/shard_map/reduce_scatter | solution.py:574
  585.8 11.9 %collective-permute-start.39 = (bf16[1024,1024]{1,0:T(8,128)(2,1)}, bf16[1024,1024]{1,0:T(8,128)(2,1)}, u32[]{:S(2)}, u32[]{:S(2)}) collective-permute-start(bf16[1024,1024]{1,0:T(8,128)(2,1)} %convolution_convert_fusion.3), channel_id=1, source_target_pairs={{0,8},{8,0},{1,9},{9,1},{2,10},{10,2},{3,11},{11,3},{4,12},{12,4},... | collective-permute-start | bytes 6291464 | tf_op jit(solution)/shard_map/ppermute | solution.py:524
  588.6 14.1 %collective-permute-start.36 = (bf16[1024,1024]{1,0:T(8,128)(2,1)}, bf16[1024,1024]{1,0:T(8,128)(2,1)}, u32[]{:S(2)}, u32[]{:S(2)}) collective-permute-start(bf16[1024,1024]{1,0:T(8,128)(2,1)} %convolution_convert_fusion.4), channel_id=1, source_target_pairs={{0,8},{8,0},{1,9},{9,1},{2,10},{10,2},{3,11},{11,3},{4,12},{12,4},... | collective-permute-start | bytes 6291464 | tf_op jit(solution)/shard_map/ppermute | solution.py:524
  590.5 34.7 %collective-permute-start.50 = (bf16[512,1408]{1,0:T(8,128)(2,1)}, bf16[512,1408]{1,0:T(8,128)(2,1)S(1)}, u32[]{:S(2)}, u32[]{:S(2)}) collective-permute-start(bf16[512,1408]{1,0:T(8,128)(2,1)} %add_convert_fusion.4), channel_id=1, source_target_pairs={{0,1},{1,0},{2,3},{3,2},{4,5},{5,4},{6,7},{7,6},{8,9},{9,8},{10,11... | collective-permute-start | bytes 4325384 | tf_op jit(solution)/shard_map/ppermute | solution.py:524
  600.7 46.2 %collective-permute-start.40 = (bf16[1024,512]{1,0:T(8,128)(2,1)}, bf16[1024,512]{1,0:T(8,128)(2,1)}, u32[]{:S(2)}, u32[]{:S(2)}) collective-permute-start(bf16[1024,512]{1,0:T(8,128)(2,1)} %add_convert_fusion.6), channel_id=1, source_target_pairs={{0,1},{1,0},{2,3},{3,2},{4,5},{5,4},{6,7},{7,6},{8,9},{9,8},{10,11... | collective-permute-start | bytes 3145736 | tf_op jit(solution)/shard_map/ppermute | solution.py:524
  605.9 43.5 %collective-permute-start.37 = (bf16[1024,512]{1,0:T(8,128)(2,1)}, bf16[1024,512]{1,0:T(8,128)(2,1)}, u32[]{:S(2)}, u32[]{:S(2)}) collective-permute-start(bf16[1024,512]{1,0:T(8,128)(2,1)} %add_convert_fusion.7), channel_id=1, source_target_pairs={{0,16},{16,0},{1,17},{17,1},{2,18},{18,2},{3,19},{19,3},{4,20},{20... | collective-permute-start | bytes 3145736 | tf_op jit(solution)/shard_map/ppermute | solution.py:524
  628.9 81.1 %reduce-scatter.4.cloned.1.call-start = ((), (), s32[]{:S(2)}) async-start(), calls=%async_computation.5 | async-start | bytes 1310720 | tf_op jit(solution)/shard_map/reduce_scatter | solution.py:574
  648.7 13.1 %collective-permute-start.41 = (bf16[1024,256]{1,0:T(8,128)(2,1)S(1)}, bf16[1024,256]{1,0:T(8,128)(2,1)S(1)}, u32[]{:S(2)}, u32[]{:S(2)}) collective-permute-start(bf16[1024,256]{1,0:T(8,128)(2,1)S(1)} %add_convert_fusion.14), channel_id=1, source_target_pairs={{0,16},{16,0},{1,17},{17,1},{2,18},{18,2},{3,19},{19,3},{4,20},{20... | collective-permute-start | bytes 1572872 | tf_op jit(solution)/shard_map/ppermute | solution.py:524
  651.3 12.7 %collective-permute-start.38 = (bf16[1024,256]{1,0:T(8,128)(2,1)S(1)}, bf16[1024,256]{1,0:T(8,128)(2,1)S(1)}, u32[]{:S(2)}, u32[]{:S(2)}) collective-permute-start(bf16[1024,256]{1,0:T(8,128)(2,1)S(1)} %add_convert_fusion.16), channel_id=1, source_target_pairs={{0,1},{1,0},{2,3},{3,2},{4,5},{5,4},{6,7},{7,6},{8,9},{9,8},{10,11... | collective-permute-start | bytes 1572872 | tf_op jit(solution)/shard_map/ppermute | solution.py:524
  668.2 72.7 %all-gather.11.cloned.1.call-start = ((), (), s32[]{:S(2)}) async-start(), calls=%async_computation.8 | async-start | bytes 3981312 | tf_op jit(solution)/shard_map/all_gather | solution.py:675
  668.8 99.6 %all-gather.13.cloned.1.call-start = ((), (), s32[]{:S(2)}) async-start(), calls=%async_computation.9 | async-start | bytes 3244032 | tf_op jit(solution)/shard_map/all_gather | solution.py:675
  689.3 1.6 collective-permute-start.45
  690.9 6.2 collective-permute-start.46
  697.1 5.4 collective-permute-start.47
  702.6 5.7 collective-permute-start.48
  708.3 8.2 %collective-permute-start.49 = (f32[280,128]{1,0:T(8,128)S(1)}, f32[280,128]{1,0:T(8,128)}, u32[]{:S(2)}, u32[]{:S(2)}) collective-permute-start(f32[280,128]{1,0:T(8,128)S(1)} %add.837), channel_id=1, source_target_pairs={{0,4},{2,6},{4,0},{6,2},{1,5},{3,7},{5,1},{7,3},{8,12},{10,14},{12... | collective-permute-start | bytes 430088 | tf_op jit(solution)/shard_map/ppermute | solution.py:809
  711.0 11.3 %collective-permute-start.42 = (bf16[1,1024,128]{2,1,0:T(8,128)(2,1)S(1)}, bf16[1,1024,128]{2,1,0:T(8,128)(2,1)}, u32[]{:S(2)}, u32[]{:S(2)}) collective-permute-start(bf16[1,1024,128]{2,1,0:T(8,128)(2,1)S(1)} %maximum_bitcast_fusion), channel_id=1, source_target_pairs={{0,1},{1,0},{2,3},{3,2},{4,5},{5,4},{6,7},{7,6},{8,9},{9,8},{10,11... | collective-permute-start | bytes 786440 | tf_op jit(solution)/shard_map/ppermute | solution.py:524
  723.3 16.4 %collective-permute-start.43 = (bf16[2,1024,128]{2,1,0:T(8,128)(2,1)S(1)}, bf16[2,1024,128]{2,1,0:T(8,128)(2,1)S(1)}, u32[]{:S(2)}, u32[]{:S(2)}) collective-permute-start(bf16[2,1024,128]{2,1,0:T(8,128)(2,1)S(1)} %pad_maximum_fusion.14), channel_id=1, source_target_pairs={{0,16},{16,0},{1,17},{17,1},{2,18},{18,2},{3,19},{19,3},{4,20},{20... | collective-permute-start | bytes 1572872 | tf_op jit(solution)/shard_map/ppermute | solution.py:524
  740.8 9.3 %collective-permute-start.44 = (bf16[4,1024,128]{2,1,0:T(8,128)(2,1)S(1)}, bf16[4,1024,128]{2,1,0:T(8,128)(2,1)S(1)}, u32[]{:S(2)}, u32[]{:S(2)}) collective-permute-start(bf16[4,1024,128]{2,1,0:T(8,128)(2,1)S(1)} %pad_maximum_fusion.8.refs_0_), channel_id=1, source_target_pairs={{0,8},{8,0},{1,9},{9,1},{2,10},{10,2},{3,11},{11,3},{4,12},{12,4},... | collective-permute-start | bytes 3145736 | tf_op jit(solution)/shard_map/ppermute | solution.py:524
  (170 other events, 1233.5 us)
Sparse Core Ops, SparseCore 0:
  10.9 82.7 all-gather.6
  97.1 121.9 all-gather.8
  574.1 39.6 reduce-scatter.5
  629.0 32.4 reduce-scatter.7
  668.3 26.9 reduce-scatter.3
  697.0 37.2 all-gather.10
  736.2 32.0 all-gather.12

commit v7 on v6

--- a/solution.py
+++ b/solution.py
@@ -449,7 +449,6 @@
     behind = [(i + 1, i) for i in range(sp_size - 1)]
     for _ in range(sp_size - 1):
         (state,) = call(state_kernel, [state_shape], [], n, inv, col, start)
-        state = points("state_done", state)
         start = lax.ppermute(state.astype(BF16), "sp", ahead)
     mixed, cor, states = call(
         scan_kernel,
@@ -496,6 +495,7 @@
         )
         d_rates, d_decay = pull_small(gfeat[:, : 5 * H])
         from_next = lax.ppermute(dx[:HALO], "sp", behind)
+        dx = points("conv_back_done", dx)
         return dx, from_next, dcw, d_rates, d_decay
 
     return mixed, pull
@@ -845,7 +845,7 @@
     members = lax.axis_size("fsdp")
     qk_way = ColumnGather(input_weight[:, :qk_cols], "x")
     v_way = ColumnGather(input_weight[:, qk_cols:qkv_cols], "sp")
-    gate_way = ColumnGather(input_weight[:, qkv_cols:], "sp")
+    gate_way = ColumnGather(input_weight[:, qkv_cols:], "x")
     down_way = ColumnGather(down_weight, "x")
     pair_rows, pair_cols = qk_way.piece.shape[0], 2 * qk_way.piece.shape[1]
     smalls = (rate_weight, conv_weight, head_decay, mixer_gain, heads_gain, feed_gain)
@@ -863,7 +863,7 @@
         first_all[:, pair_rows:].reshape(members, -1), smalls
     )
     qkv_second = (qk_way.second(), v_way.second())
-    qkv_third = (qk_way.third(), v_way.third())
+    qkv_third = (qk_way.third(*qkv_second), v_way.third(*qkv_second))
     qk_full, v_full = qk_way.full(), v_way.full()
     out_full = gather_rows(output_weight)
     up_full = gather_rows(up_weight)
@@ -878,17 +878,16 @@
         if name == "conv":
             gate_way.blocks(qkv_third, value)
             gate_way.second()
+            ready.append(value)
             return value
         if name == "inverse":
-            value = after(value, gate_way.held)
+            down_way.blocks(ready, value)
+            value = after(value, gate_way.held, down_way.held)
             gate_way.third(value)
-            ready.append(value)
+            down_way.second(value)
             return value
         if name == "state":
-            down_way.blocks(ready, value)
-            down_way.second()
-            return after(value, gate_way.held)
-        if name == "state_done":
+            value = after(value, gate_way.held, down_way.held)
             down_way.third(value)
             return value
         if name == "sent":
@@ -905,7 +904,9 @@
                 axis=1,
             )
             owns.append(packed.reshape(-1, 128))
-            return after(value, owns[0], sums["up"].third())
+            return after(value, owns[0])
+        if name == "conv_back_done":
+            return after(value, sums["up"].third())
         return value
 
     sums, ready, owns = {}, [], []
@@ -932,7 +933,7 @@
     rates = rate_raw.astype(BF16).astype(F32)
     mixed, pull_mix = mixer(qkv, conv_full, rates, decay_full, doc_ids, member, sp_size, points)
     gate_full, down_full = gate_way.full(), down_way.full()
-    gate_raw = reorder(dot_columns(normed_low, gate_full), "sp")
+    gate_raw = reorder(dot_columns(normed_low, gate_full), "x")
     gated, pull_gate = jax.vjp(output_gate, mixed.astype(F32), gate_raw, heads_scale)
     gated_low = gated.astype(BF16)
     attended = jnp.dot(gated_low, out_full, preferred_element_type=F32)
@@ -961,8 +962,8 @@
     d_gated = jnp.einsum("td,ed->te", d_att_low, out_full, preferred_element_type=F32)
     d_mixed, d_gate, heads_grad = pull_gate(d_gated)
     d_gate_low = d_gate.astype(BF16)
-    d_gate_rel = reorder(d_gate_low, "sp")
-    sums["gate"] = ColumnSum(normed_low, d_gate_rel, "sp")
+    d_gate_rel = reorder(d_gate_low, "x")
+    sums["gate"] = ColumnSum(normed_low, d_gate_rel, "x")
     d_mixed_low = after(
         d_mixed.astype(BF16), *(sums[key].second() for key in ("up", "out", "gate"))
     )
@@ -974,7 +975,13 @@
     d_v_rel = reorder(d_qkv[:, qk_cols:], "sp")
     sums["qk"] = ColumnSum(normed_low, d_qk_rel, "x")
     sums["v"] = ColumnSum(normed_low, d_v_rel, "sp")
-    sums["up"].from_y = after(sums["up"].from_y, sums["qk"].second(), sums["v"].second())
+    places = spread_places()
+    early_block = sum_blocks(owns[0])
+    early_sums = spread_aside([early_block])
+    for key in ("qk", "v"):
+        sums[key].from_core = after(sums[key].from_core, early_block)
+        sums[key].second()
+    up_own = sums["up"].own().astype(BF16)
     d_normed = dot_back(d_qk_rel, qk_full) + dot_back(d_v_rel, v_full)
     d_normed = d_normed + dot_back(d_gate_rel, gate_full)
     d_normed = d_normed + jnp.einsum(
@@ -982,18 +989,17 @@
     )
     for key in ("qk", "v"):
         sums[key].third()
-        sums[key].from_second = after(sums[key].from_second, d_normed)
-    places = spread_places()
-    early_block = sum_blocks(owns[0])
+        sums[key].from_second = after(
+            sums[key].from_second, d_normed, up_own, early_sums[0]
+        )
     down_rows, out_rows = down_weight.shape[0], output_weight.shape[0]
-    early_sums = spread_aside([early_block])
     down_shard, output_shard = unpack(
         places,
         [(0, 0, 0, 0, down_rows, 1, 3), (0, down_rows, 1, 0, out_rows, 1, 4)],
         early_sums,
         [down_weight.shape, output_weight.shape],
     )
-    up_block = sum_blocks(sums["up"].own())
+    up_block = sum_blocks(up_own)
     (up_shard,) = unpack(
         places,
         [(0, 0, 0, 0, up_block.shape[0], up_block.shape[1] // 128, 5)],
@@ -1008,7 +1014,7 @@
         [
             (0, 0, 0, 0, rows, wide, 0),
             (0, wide * rows, 0, qk_cols, rows, wide, 1),
-            (1, down_rows + out_rows, 0, qkv_cols, rows, gate_wide, 4),
+            (1, down_rows + out_rows, 0, qkv_cols, rows, gate_wide, 3),
         ],
         spread([narrow(late_block)]) + early_sums,
         [input_weight.shape],

time: 793 us -> 753 us (0.950)
  waiting for transfers between devices: 232 us -> 212 us
  matrix products: 145 us -> 132 us
  other arithmetic: 80.4 us -> 71.1 us
  starting transfers between devices: 59.9 us -> 68.3 us
    ppermute x1, waiting for transfers between devices: 22.1 us -> 2.98 us  [pull(): dstart = lax.ppermute(points('sent', dstate.astype(BF16)), 'sp', behind)]
    dot_general x24, matrix products: 67.7 us -> 53.8 us  [grad_dot(): return jnp.einsum('td,tf->df', left, right, preferred_element_type=F32)]
    all_gather x2, waiting for transfers between devices: 11.2 us -> 0.02 us  [spread_aside(): lax.all_gather(jnp.concatenate(blocks, axis=0), ('x', 'core', 'sp'), axis=0)]
    ppermute x9, waiting for transfers between devices: 17.3 us -> 26.7 us  [shifted(): lax.ppermute(value, 'fsdp', [(i, (i + step) % count) for i in range(count)])]
    ppermute x2, starting transfers between devices: 4.33 us -> 12.8 us  [sum_small(): lax.ppermute(flat, 'fsdp', [(i, i ^ 1 << bit) for i in range(members)])]
    unnamed x398 -> x321, local copies, waits for them, and re-layouts: 41.6 us -> 33.5 us
  transfers between devices with their start and end apart: 58 -> 58, of which waited for: 23 -> 20; matrix products, arithmetic and copies ran while one was open for 37% -> 36% of each run, Pallas kernels for 14% -> 18%
where the time goes in v7:
time: 753 us; the launch traced here: 745 us
  waiting for transfers between devices  212 us (28%)
  Pallas kernels  143 us (19%)
  matrix products  132 us (18%)
  local copies, waits for them, and re-layouts  102 us (14%)
  other arithmetic  71.1 us (9%)
  starting transfers between devices  68.3 us (9%)
  between operations  17.2 us (2%)
    ppermute x36, waiting for transfers between devices, swap(): return lax.ppermute(value, axis, [(0, 1), (1, 0)])  169 us
    pallas_call x7, Pallas kernels, call(): pl.pallas_call(kernel, out_shape=[jax.ShapeDtypeStruct(s, t) for s, t in...  126 us
    dot_general x24, matrix products, grad_dot(): return jnp.einsum('td,tf->df', left, right, preferred_element_type=F32)  53.8 us
    unnamed x321, local copies, waits for them, and re-layouts  33.5 us
    ppermute x36, starting transfers between devices, swap(): return lax.ppermute(value, axis, [(0, 1), (1, 0)])  31.2 us
    ppermute x9, waiting for transfers between devices, shifted(): lax.ppermute(value, 'fsdp', [(i, (i + step) % count) for i in range(count)])  26.7 us
    dot_general x8, matrix products, dot_columns(): parts = [jnp.dot(values, w, preferred_element_type=F32) for w in halves_of]  22.5 us
    dot_general x4, matrix products, dot_back(): jnp.einsum('tf,df->td', grads[:, :half], halves_of[0], preferred_element_...  16.9 us
  transfers between devices with their start and end apart: 58, of which 20 were waited for; matrix products, arithmetic and copies ran while one was open for 36% of the time, Pallas kernels for 18%

profile of v7, /device:TPU:0, one launch (start us, length us, event | category | flops | bytes accessed | tf_op | source)
XLA Modules:
  0.0 744.9 jit_solution(7090350257560145173)
XLA Ops:
  17.5 5.0 collective-permute-start.1
  24.2 4.0 collective-permute-start
  37.0 13.7 %collective-permute-done.2 = bf16[288,512]{1,0:T(8,128)(2,1)S(1)} collective-permute-done((bf16[288,512]{1,0:T(8,128)(2,1)}, bf16[288,512]{1,0:T(8,128)(2,1)S(1)}, u32[]{:S(2)}, u32[]{:S(2)}) %collective-permute-start.2) | collective-permute-done | bytes 294944 | tf_op jit(solution)/shard_map/ppermute | solution.py:562
  54.4 10.4 %collective-permute-done.4 = bf16[1024,256]{1,0:T(8,128)(2,1)S(1)} collective-permute-done((bf16[1024,256]{1,0:T(8,128)(2,1)S(1)}, bf16[1024,256]{1,0:T(8,128)(2,1)S(1)}, u32[]{:S(2)}, u32[]{:S(2)}) %collective-permute-start.4) | collective-permute-done | bytes 524320 | tf_op jit(solution)/shard_map/ppermute | solution.py:524
  71.0 28.6 %collective-permute-done.6 = bf16[1024,512]{1,0:T(8,128)(2,1)S(1)} collective-permute-done((bf16[1024,512]{1,0:T(8,128)(2,1)S(1)}, bf16[1024,512]{1,0:T(8,128)(2,1)S(1)}, u32[]{:S(2)}, u32[]{:S(2)}) %collective-permute-start.6) | collective-permute-done | bytes 1048608 | tf_op jit(solution)/shard_map/ppermute | solution.py:524
  100.7 4.5 reshape_reshape.6
  114.7 3.0 collective-permute-start.11
  117.9 2.6 convolution_convert_fusion.9
  131.2 3.8 collective-permute-start.14
  137.0 13.0 %shard_map.220.n_ref = bf16[384,4096]{1,0:T(8,128)(2,1)} custom-call(bf16[400,4096]{1,0:T(8,128)(2,1)} %copy-done.18, f32[4,4096]{1,0:T(4,128)} %bitcast.258, f32[384,8]{1,0:T(8,128)} %copy.205.mask_ref), custom_call_target="tpu_custom_call" | custom-call | flops 1 | bytes 1 | tf_op jit(solution)/shard_map/pallas_call | solution.py:386
  150.0 13.1 %collective-permute-done.15 = bf16[704,128]{1,0:T(8,128)(2,1)S(1)} collective-permute-done((bf16[704,128]{1,0:T(8,128)(2,1)S(1)}, bf16[704,128]{1,0:T(8,128)(2,1)S(1)}, u32[]{:S(2)}, u32[]{:S(2)}) %collective-permute-start.15) | collective-permute-done | bytes 180256 | tf_op jit(solution)/shard_map/ppermute | solution.py:562
  171.5 27.8 %shard_map.221.inv_ref = f32[6,2,256,256]{3,2,1,0:T(8,128)} custom-call(bf16[384,4096]{1,0:T(8,128)(2,1)} %shard_map.220.n_ref, f32[384,128]{1,0:T(8,128)} %concatenate.203.col_ref), custom_call_target="tpu_custom_call" | custom-call | flops 1 | bytes 1 | tf_op jit(solution)/shard_map/pallas_call | solution.py:386
  209.3 10.4 %shard_map.222 = f32[8,128,256]{2,1,0:T(8,128)} custom-call(bf16[384,4096]{1,0:T(8,128)(2,1)} %shard_map.220.n_ref, f32[6,2,256,256]{3,2,1,0:T(8,128)} %shard_map.221.inv_ref, f32[384,128]{1,0:T(8,128)} %concatenate.203.col_ref, bf16[8,128,256]{2,1,0:T(8,128)(2,1)} %broadcast_20_start_ref.2.start_ref), custom_call_target="tpu_custom_call" | custom-call | flops 1 | bytes 1 | tf_op jit(solution)/shard_map/pallas_call | solution.py:386
  220.9 3.6 collective-permute-start.19
  229.7 6.1 collective-permute-done.19.start_ref
  236.5 13.5 %shard_map.223 = (bf16[384,2048]{1,0:T(8,128)(2,1)}, bf16[6,2,256,256]{3,2,1,0:T(8,128)(2,1)}, bf16[6,8,128,256]{3,2,1,0:T(8,128)(2,1)}) custom-call(bf16[384,4096]{1,0:T(8,128)(2,1)} %shard_map.220.n_ref, f32[6,2,256,256]{3,2,1,0:T(8,128)} %shard_map.221.inv_ref, f32[384,128]{1,0:T(8,128)} %concatenate.203.col_ref, bf16[8,128,256]{2,1,0:T(8,128)(2,1)} %copy-done.58), custom_call_target="tpu_custom_call" | custom-call | flops 1 | bytes 1 | tf_op jit(solution)/shard_map/pallas_call | solution.py:386
  256.4 3.7 constant_dynamic-update-slice_fusion.29
  269.1 4.7 multiply_reduce_fusion.4
  276.2 5.2 fusion.172
  281.4 8.0 %fusion.245 = f32[384,5632]{1,0:T(8,128)S(1)} fusion(bf16[384,1024]{1,0:T(8,128)(2,1)} %multiply_convert_fusion.2, bf16[1024,5632]{1,0:T(8,128)(2,1)} %all-gather.9.cloned.1.call-done), kind=kOutput, calls=%fused_computation.530 | convolution fusion | flops 4429185024 | bytes 20971520 | tf_op jit(solution)/shard_map/dot_general | solution.py:942
  289.4 7.3 fusion.54
  296.7 3.3 convolution_convert_fusion.1
  312.6 4.1 add_convert_fusion
  317.0 5.7 convolution_convert_fusion
  322.8 3.6 add_convert_fusion.5
  326.4 8.4 %multiply_reduce_fusion.2 = (f32[1024]{0:T(1024)}, f32[384]{0:T(512)S(1)}, f32[384,1024]{1,0:T(8,128)S(1)}) fusion(f32[384,1024]{1,0:T(8,128)S(1)} %copy-done.14, f32[384]{0:T(512)S(1)} %copy-done.108, f32[1024]{0:T(1024)S(1)} %bitcast.276, bf16[384,5632]{1,0:T(8,128)(2,1)S(1)} %add_convert_fusion, bf16[1024,5632]{1,0:T(8,128)(2,1)} %all-gather.9.cloned.1.call-done), kind=kOutput, calls=%fused_computation.120 | convolution fusion | flops 4431542784 | bytes 19016704 | tf_op jit(solution)/shard_map/tf,df->td/dot_general | solution.py:957
  348.4 5.8 multiply_reduce_fusion
  359.5 2.7 convolution_convert_fusion.2
  366.7 3.0 add_convert_fusion.8
  370.8 3.0 add_convert_fusion.9
  376.3 5.5 add_convert_fusion.2
  381.7 13.5 %shard_map.224 = f32[8,128,256]{2,1,0:T(8,128)} custom-call(bf16[384,4096]{1,0:T(8,128)(2,1)} %shard_map.220.n_ref, f32[6,2,256,256]{3,2,1,0:T(8,128)} %shard_map.221.inv_ref, f32[384,128]{1,0:T(8,128)} %concatenate.203.col_ref, bf16[384,2048]{1,0:T(8,128)(2,1)} %get-tuple-element.68.dout_ref, bf16[8,128,256]{2,1,0:T(8,128)(2,1)} %broadcast_20_start_ref.2.start_ref), custom_call_target="tpu_custom_call" | custom-call | flops 1 | bytes 1 | tf_op jit(solution)/shard_map/pallas_call | solution.py:386
  397.1 3.0 add_convert_fusion.12
  405.3 14.2 %collective-permute-done.32 = bf16[1024,512]{1,0:T(8,128)(2,1)} collective-permute-done((bf16[1024,512]{1,0:T(8,128)(2,1)}, bf16[1024,512]{1,0:T(8,128)(2,1)}, u32[]{:S(2)}, u32[]{:S(2)}) %collective-permute-start.32) | collective-permute-done | bytes 1048608 | tf_op jit(solution)/shard_map/ppermute | solution.py:524
  424.5 2.6 add_convert_fusion.20
  428.0 3.0 collective-permute-done.27.start_ref
  431.8 25.0 %shard_map.225 = (f32[384,4096]{1,0:T(8,128)}, f32[384,128]{1,0:T(8,128)}) custom-call(bf16[384,4096]{1,0:T(8,128)(2,1)} %shard_map.220.n_ref, f32[6,2,256,256]{3,2,1,0:T(8,128)} %shard_map.221.inv_ref, f32[384,128]{1,0:T(8,128)} %concatenate.203.col_ref, bf16[384,2048]{1,0:T(8,128)(2,1)} %get-tuple-element.68.dout_ref, ...), custom_call_target="tpu_custom_call" | custom-call | flops 1 | bytes 1 | tf_op jit(solution)/shard_map/pallas_call | solution.py:386
  458.8 33.1 %collective-permute-done.31 = bf16[2048,128]{1,0:T(8,128)(2,1)S(1)} collective-permute-done((bf16[2048,128]{1,0:T(8,128)(2,1)}, bf16[2048,128]{1,0:T(8,128)(2,1)S(1)}, u32[]{:S(2)}, u32[]{:S(2)}) %collective-permute-start.31) | collective-permute-done | bytes 524320 | tf_op jit(solution)/shard_map/ppermute | solution.py:524
  496.5 3.1 add_convert_fusion.4
  504.4 29.1 %collective-permute-done.39 = bf16[512,1408]{1,0:T(8,128)(2,1)S(1)} collective-permute-done((bf16[512,1408]{1,0:T(8,128)(2,1)S(1)}, bf16[512,1408]{1,0:T(8,128)(2,1)S(1)}, u32[]{:S(2)}, u32[]{:S(2)}) %collective-permute-start.39) | collective-permute-done | bytes 1441824 | tf_op jit(solution)/shard_map/ppermute | solution.py:524
  533.5 3.7 add_convert_fusion.3
  537.4 3.8 fusion.165
  542.6 23.2 %shard_map.226 = (bf16[400,4096]{1,0:T(8,128)(2,1)}, f32[4,4096]{1,0:T(4,128)}) custom-call(bf16[400,4096]{1,0:T(8,128)(2,1)} %copy-done.18, f32[4,4096]{1,0:T(4,128)} %bitcast.259, f32[384,8]{1,0:T(8,128)} %copy.205.mask_ref, f32[384,4096]{1,0:T(8,128)} %get-tuple-element.78.dn_ref), custom_call_target="tpu_custom_call" | custom-call | flops 1 | bytes 1 | tf_op jit(solution)/shard_map/pallas_call | solution.py:386
  568.7 4.8 collective-permute-done.35
  583.0 2.6 fusion.31
  585.7 2.7 fusion.163
  594.4 4.4 fusion.16
  598.8 27.7 %collective-permute-done.41 = bf16[1024,512]{1,0:T(8,128)(2,1)S(1)} collective-permute-done((bf16[1024,512]{1,0:T(8,128)(2,1)S(1)}, bf16[1024,512]{1,0:T(8,128)(2,1)S(1)}, u32[]{:S(2)}, u32[]{:S(2)}) %collective-permute-start.41) | collective-permute-done | bytes 1048608 | tf_op jit(solution)/shard_map/ppermute | solution.py:524
  633.4 4.1 fusion.230
  637.5 3.8 collective-permute-done.42
  642.1 3.0 collective-permute-done.38
  652.0 3.9 fusion.246
  655.9 3.1 fusion.247
  664.7 4.4 collective-permute-done.47
  671.4 3.3 collective-permute-done.48
  674.7 6.9 collective-permute-start.49
  684.8 5.9 collective-permute-start.50
  692.3 4.4 fusion.18
  697.6 2.6 slice.387
  708.5 4.9 shard_map.228
  713.4 7.9 %collective-permute-done.44 = bf16[2,1024,128]{2,1,0:T(8,128)(2,1)S(1)} collective-permute-done((bf16[2,1024,128]{2,1,0:T(8,128)(2,1)S(1)}, bf16[2,1024,128]{2,1,0:T(8,128)(2,1)S(1)}, u32[]{:S(2)}, u32[]{:S(2)}) %collective-permute-start.44) | collective-permute-done | bytes 524320 | tf_op jit(solution)/shard_map/ppermute | solution.py:524
  722.6 3.9 fusion.233
  726.4 4.9 shard_map.229
  731.3 6.2 shard_map.227
  (655 shorter events, 217.7 us)
Async XLA Ops:
  7.2 261.9 %all-gather.7.cloned.1.call-start = ((), (), s32[]{:S(2)}) async-start(), calls=%async_computation.3 | async-start | bytes 4325376 | tf_op jit(solution)/shard_map/all_gather | solution.py:590
  9.0 272.4 %all-gather.9.cloned.1.call-start = ((), (), s32[]{:S(2)}) async-start(), calls=%async_computation.4 | async-start | bytes 11894784 | tf_op jit(solution)/shard_map/all_gather | solution.py:590
  9.9 558.6 %reduce-scatter.4.cloned.1.call-start = ((), (), s32[]{:S(2)}) async-start(), calls=%async_computation.5 | async-start | bytes 2211840 | tf_op jit(solution)/shard_map/reduce_scatter | solution.py:574
  17.5 19.5 %collective-permute-start.1 = (bf16[288,512]{1,0:T(8,128)(2,1)}, bf16[288,512]{1,0:T(8,128)(2,1)S(1)}, u32[]{:S(2)}, u32[]{:S(2)}) collective-permute-start(bf16[288,512]{1,0:T(8,128)(2,1)} %pad_maximum_fusion.15), channel_id=1, source_target_pairs={{0,6},{2,0},{4,2},{6,4},{1,7},{3,1},{5,3},{7,5},{8,14},{10,8},{12,... | collective-permute-start | bytes 884744 | tf_op jit(solution)/shard_map/ppermute | solution.py:562
  22.6 28.1 %collective-permute-start.2 = (bf16[288,512]{1,0:T(8,128)(2,1)}, bf16[288,512]{1,0:T(8,128)(2,1)S(1)}, u32[]{:S(2)}, u32[]{:S(2)}) collective-permute-start(bf16[288,512]{1,0:T(8,128)(2,1)} %pad_maximum_fusion.15), channel_id=1, source_target_pairs={{0,4},{2,6},{4,0},{6,2},{1,5},{3,7},{5,1},{7,3},{8,12},{10,14},{12... | collective-permute-start | bytes 884744 | tf_op jit(solution)/shard_map/ppermute | solution.py:562
  22.6 28.1 %collective-permute-start.3 = (bf16[288,512]{1,0:T(8,128)(2,1)}, bf16[288,512]{1,0:T(8,128)(2,1)S(1)}, u32[]{:S(2)}, u32[]{:S(2)}) collective-permute-start(bf16[288,512]{1,0:T(8,128)(2,1)} %pad_maximum_fusion.15), channel_id=1, source_target_pairs={{0,2},{2,4},{4,6},{6,0},{1,3},{3,5},{5,7},{7,1},{8,10},{10,12},{12... | collective-permute-start | bytes 884744 | tf_op jit(solution)/shard_map/ppermute | solution.py:562
  24.2 11.9 %collective-permute-start = (bf16[16,1024]{1,0:T(8,128)(2,1)}, bf16[16,1024]{1,0:T(8,128)(2,1)}, u32[]{:S(2)}, u32[]{:S(2)}) collective-permute-start(bf16[16,1024]{1,0:T(8,128)(2,1)} %slice.313), channel_id=1, source_target_pairs={{0,1},{2,3},{4,5},{6,7},{8,9},{10,11},{12,13},{14,15},{16,17},{18,... | collective-permute-start | bytes 98312 | tf_op jit(solution)/shard_map/ppermute | solution.py:919
  33.8 133.5 %copy-start.101 = (f32[6,64]{1,0:T(8,128)}, f32[6,64]{1,0:T(8,128)S(1)}, u32[]{:S(2)}) copy-start(f32[6,64]{1,0:T(8,128)S(1)} %get-tuple-element.186) | copy-start | bytes 4612
  33.8 133.5 %copy-start.105 = (f32[6,64]{1,0:T(8,128)}, f32[6,64]{1,0:T(8,128)S(1)}, u32[]{:S(2)}) copy-start(f32[6,64]{1,0:T(8,128)S(1)} %get-tuple-element.187) | copy-start | bytes 4612
  51.2 13.7 %collective-permute-start.4 = (bf16[1024,256]{1,0:T(8,128)(2,1)S(1)}, bf16[1024,256]{1,0:T(8,128)(2,1)S(1)}, u32[]{:S(2)}, u32[]{:S(2)}) collective-permute-start(bf16[1024,256]{1,0:T(8,128)(2,1)S(1)} %get-tuple-element.142), channel_id=1, source_target_pairs={{0,1},{1,0},{2,3},{3,2},{4,5},{5,4},{6,7},{7,6},{8,9},{9,8},{10,11... | collective-permute-start | bytes 1572872 | tf_op jit(solution)/shard_map/ppermute | solution.py:524
  52.7 14.0 %collective-permute-start.5 = (bf16[1024,256]{1,0:T(8,128)(2,1)S(1)}, bf16[1024,256]{1,0:T(8,128)(2,1)S(1)}, u32[]{:S(2)}, u32[]{:S(2)}) collective-permute-start(bf16[1024,256]{1,0:T(8,128)(2,1)S(1)} %get-tuple-element.141), channel_id=1, source_target_pairs={{0,16},{16,0},{1,17},{17,1},{2,18},{18,2},{3,19},{19,3},{4,20},{20... | collective-permute-start | bytes 1572872 | tf_op jit(solution)/shard_map/ppermute | solution.py:524
  67.8 31.9 %collective-permute-start.6 = (bf16[1024,512]{1,0:T(8,128)(2,1)S(1)}, bf16[1024,512]{1,0:T(8,128)(2,1)S(1)}, u32[]{:S(2)}, u32[]{:S(2)}) collective-permute-start(bf16[1024,512]{1,0:T(8,128)(2,1)S(1)} %pad_maximum_fusion.1), channel_id=1, source_target_pairs={{0,16},{16,0},{1,17},{17,1},{2,18},{18,2},{3,19},{19,3},{4,20},{20... | collective-permute-start | bytes 3145736 | tf_op jit(solution)/shard_map/ppermute | solution.py:524
  68.2 41.7 %collective-permute-start.8 = (bf16[1024,512]{1,0:T(8,128)(2,1)}, bf16[1024,512]{1,0:T(8,128)(2,1)}, u32[]{:S(2)}, u32[]{:S(2)}) collective-permute-start(bf16[1024,512]{1,0:T(8,128)(2,1)} %pad_maximum_fusion.2), channel_id=1, source_target_pairs={{0,1},{1,0},{2,3},{3,2},{4,5},{5,4},{6,7},{7,6},{8,9},{9,8},{10,11... | collective-permute-start | bytes 3145736 | tf_op jit(solution)/shard_map/ppermute | solution.py:524
  100.7 22.4 %collective-permute-start.7 = (bf16[1024,1024]{1,0:T(8,128)(2,1)}, bf16[1024,1024]{1,0:T(8,128)(2,1)}, u32[]{:S(2)}, u32[]{:S(2)}) collective-permute-start(bf16[1024,1024]{1,0:T(8,128)(2,1)} %constant_dynamic-update-slice_fusion.7), channel_id=1, source_target_pairs={{0,8},{8,0},{1,9},{9,1},{2,10},{10,2},{3,11},{11,3},{4,12},{12,4},... | collective-permute-start | bytes 6291464 | tf_op jit(solution)/shard_map/ppermute | solution.py:524
  107.1 117.4 %copy-start.4 = (bf16[384,1024]{1,0:T(8,128)(2,1)}, bf16[384,1024]{1,0:T(8,128)(2,1)S(1)}, u32[]{:S(2)}) copy-start(bf16[384,1024]{1,0:T(8,128)(2,1)S(1)} %fusion.15) | copy-start | bytes 2359300
  112.2 14.6 %collective-permute-start.9 = (bf16[1024,1024]{1,0:T(8,128)(2,1)}, bf16[1024,1024]{1,0:T(8,128)(2,1)}, u32[]{:S(2)}, u32[]{:S(2)}) collective-permute-start(bf16[1024,1024]{1,0:T(8,128)(2,1)} %constant_dynamic-update-slice_fusion.9), channel_id=1, source_target_pairs={{0,8},{8,0},{1,9},{9,1},{2,10},{10,2},{3,11},{11,3},{4,12},{12,4},... | collective-permute-start | bytes 6291464 | tf_op jit(solution)/shard_map/ppermute | solution.py:524
  112.7 51.9 %copy-start.125 = (f32[8]{0:T(128)}, f32[8]{0:T(128)S(1)}, u32[]{:S(2)}) copy-start(f32[8]{0:T(128)S(1)} %negate_bitcast_fusion) | copy-start | bytes 100
  114.6 20.4 %collective-permute-start.10 = (bf16[256,256]{1,0:T(8,128)(2,1)S(1)}, bf16[256,256]{1,0:T(8,128)(2,1)S(1)}, u32[]{:S(2)}, u32[]{:S(2)}) collective-permute-start(bf16[256,256]{1,0:T(8,128)(2,1)S(1)} %copy-done.56), channel_id=1, source_target_pairs={{0,6},{2,0},{4,2},{6,4},{1,7},{3,1},{5,3},{7,5},{8,14},{10,8},{12,... | collective-permute-start | bytes 393224 | tf_op jit(solution)/shard_map/ppermute | solution.py:562
  114.7 20.9 %collective-permute-start.11 = (bf16[256,256]{1,0:T(8,128)(2,1)S(1)}, bf16[256,256]{1,0:T(8,128)(2,1)S(1)}, u32[]{:S(2)}, u32[]{:S(2)}) collective-permute-start(bf16[256,256]{1,0:T(8,128)(2,1)S(1)} %copy-done.56), channel_id=1, source_target_pairs={{0,4},{2,6},{4,0},{6,2},{1,5},{3,7},{5,1},{7,3},{8,12},{10,14},{12... | collective-permute-start | bytes 393224 | tf_op jit(solution)/shard_map/ppermute | solution.py:562
  117.7 17.9 %collective-permute-start.12 = (bf16[256,256]{1,0:T(8,128)(2,1)S(1)}, bf16[256,256]{1,0:T(8,128)(2,1)S(1)}, u32[]{:S(2)}, u32[]{:S(2)}) collective-permute-start(bf16[256,256]{1,0:T(8,128)(2,1)S(1)} %copy-done.56), channel_id=1, source_target_pairs={{0,2},{2,4},{4,6},{6,0},{1,3},{3,5},{5,7},{7,1},{8,10},{10,12},{12... | collective-permute-start | bytes 393224 | tf_op jit(solution)/shard_map/ppermute | solution.py:562
  131.2 18.8 %collective-permute-start.14 = (bf16[704,128]{1,0:T(8,128)(2,1)S(1)}, bf16[704,128]{1,0:T(8,128)(2,1)S(1)}, u32[]{:S(2)}, u32[]{:S(2)}) collective-permute-start(bf16[704,128]{1,0:T(8,128)(2,1)S(1)} %copy-done.54), channel_id=1, source_target_pairs={{0,6},{2,0},{4,2},{6,4},{1,7},{3,1},{5,3},{7,5},{8,14},{10,8},{12,... | collective-permute-start | bytes 540680 | tf_op jit(solution)/shard_map/ppermute | solution.py:562
  135.0 28.0 %collective-permute-start.15 = (bf16[704,128]{1,0:T(8,128)(2,1)S(1)}, bf16[704,128]{1,0:T(8,128)(2,1)S(1)}, u32[]{:S(2)}, u32[]{:S(2)}) collective-permute-start(bf16[704,128]{1,0:T(8,128)(2,1)S(1)} %copy-done.54), channel_id=1, source_target_pairs={{0,4},{2,6},{4,0},{6,2},{1,5},{3,7},{5,1},{7,3},{8,12},{10,14},{12... | collective-permute-start | bytes 540680 | tf_op jit(solution)/shard_map/ppermute | solution.py:562
  135.0 28.0 %collective-permute-start.16 = (bf16[704,128]{1,0:T(8,128)(2,1)S(1)}, bf16[704,128]{1,0:T(8,128)(2,1)S(1)}, u32[]{:S(2)}, u32[]{:S(2)}) collective-permute-start(bf16[704,128]{1,0:T(8,128)(2,1)S(1)} %copy-done.54), channel_id=1, source_target_pairs={{0,2},{2,4},{4,6},{6,0},{1,3},{3,5},{5,7},{7,1},{8,10},{10,12},{12... | collective-permute-start | bytes 540680 | tf_op jit(solution)/shard_map/ppermute | solution.py:562
  135.8 27.6 %collective-permute-start.13 = (bf16[1024,256]{1,0:T(8,128)(2,1)S(1)}, bf16[1024,256]{1,0:T(8,128)(2,1)}, u32[]{:S(2)}, u32[]{:S(2)}) collective-permute-start(bf16[1024,256]{1,0:T(8,128)(2,1)S(1)} %constant_dynamic-slice_fusion.47), channel_id=1, source_target_pairs={{0,1},{1,0},{2,3},{3,2},{4,5},{5,4},{6,7},{7,6},{8,9},{9,8},{10,11... | collective-permute-start | bytes 1572872 | tf_op jit(solution)/shard_map/ppermute | solution.py:524
  164.5 37.8 %collective-permute-start.17 = (bf16[1024,512]{1,0:T(8,128)(2,1)S(1)}, bf16[1024,512]{1,0:T(8,128)(2,1)}, u32[]{:S(2)}, u32[]{:S(2)}) collective-permute-start(bf16[1024,512]{1,0:T(8,128)(2,1)S(1)} %pad_maximum_fusion.3), channel_id=1, source_target_pairs={{0,16},{16,0},{1,17},{17,1},{2,18},{18,2},{3,19},{19,3},{4,20},{20... | collective-permute-start | bytes 3145736 | tf_op jit(solution)/shard_map/ppermute | solution.py:524
  165.9 38.7 %collective-permute-start.18 = (bf16[2816,128]{1,0:T(8,128)(2,1)S(1)}, bf16[2816,128]{1,0:T(8,128)(2,1)}, u32[]{:S(2)}, u32[]{:S(2)}) collective-permute-start(bf16[2816,128]{1,0:T(8,128)(2,1)S(1)} %constant_dynamic-slice_fusion.45), channel_id=1, source_target_pairs={{0,1},{1,0},{2,3},{3,2},{4,5},{5,4},{6,7},{7,6},{8,9},{9,8},{10,11... | collective-permute-start | bytes 2162696 | tf_op jit(solution)/shard_map/ppermute | solution.py:524
  204.6 55.5 %collective-permute-start.20 = (bf16[1024,1024]{1,0:T(8,128)(2,1)}, bf16[1024,1024]{1,0:T(8,128)(2,1)}, u32[]{:S(2)}, u32[]{:S(2)}) collective-permute-start(bf16[1024,1024]{1,0:T(8,128)(2,1)} %constant_dynamic-update-slice_fusion.25), channel_id=1, source_target_pairs={{0,8},{8,0},{1,9},{9,1},{2,10},{10,2},{3,11},{11,3},{4,12},{12,4},... | collective-permute-start | bytes 6291464 | tf_op jit(solution)/shard_map/ppermute | solution.py:524
  206.6 49.7 %collective-permute-start.21 = (bf16[2816,256]{1,0:T(8,128)(2,1)}, bf16[2816,256]{1,0:T(8,128)(2,1)}, u32[]{:S(2)}, u32[]{:S(2)}) collective-permute-start(bf16[2816,256]{1,0:T(8,128)(2,1)} %constant_dynamic-update-slice_fusion.27), channel_id=1, source_target_pairs={{0,16},{16,0},{1,17},{17,1},{2,18},{18,2},{3,19},{19,3},{4,20},{20... | collective-permute-start | bytes 4325384 | tf_op jit(solution)/shard_map/ppermute | solution.py:524
  208.4 56.8 %copy-start.97 = (f32[1,2,8,128]{3,1,2,0:T(2,128)}, f32[1,2,8,128]{3,1,2,0:T(2,128)S(1)}, u32[]{:S(2)}) copy-start(f32[1,2,8,128]{3,1,2,0:T(2,128)S(1)} %copy.254) | copy-start | bytes 24580
  208.4 126.5 %copy-start.99 = (f32[1,2,4,128]{3,1,2,0:T(2,128)}, f32[1,2,4,128]{3,1,2,0:T(2,128)S(1)}, u32[]{:S(2)}) copy-start(f32[1,2,4,128]{3,1,2,0:T(2,128)S(1)} %copy.255) | copy-start | bytes 12292
  220.9 14.8 %collective-permute-start.19 = (bf16[8,128,256]{2,1,0:T(8,128)(2,1)S(1)}, bf16[8,128,256]{2,1,0:T(8,128)(2,1)S(1)}, u32[]{:S(2)}, u32[]{:S(2)}) collective-permute-start(bf16[8,128,256]{2,1,0:T(8,128)(2,1)S(1)} %convert_element_type.345), channel_id=1, source_target_pairs={{0,1},{2,3},{4,5},{6,7},{8,9},{10,11},{12,13},{14,15},{16,17},{18,... | collective-permute-start | bytes 1572872 | tf_op jit(solution)/shard_map/ppermute | solution.py:452
  260.1 16.1 %collective-permute-start.22 = (bf16[2816,512]{1,0:T(8,128)(2,1)}, bf16[2816,512]{1,0:T(8,128)(2,1)}, u32[]{:S(2)}, u32[]{:S(2)}) collective-permute-start(bf16[2816,512]{1,0:T(8,128)(2,1)} %constant_dynamic-update-slice_fusion.29), channel_id=1, source_target_pairs={{0,8},{8,0},{1,9},{9,1},{2,10},{10,2},{3,11},{11,3},{4,12},{12,4},... | collective-permute-start | bytes 8650760 | tf_op jit(solution)/shard_map/ppermute | solution.py:524
  300.1 22.8 %collective-permute-start.23 = (bf16[2816,512]{1,0:T(8,128)(2,1)}, bf16[2816,512]{1,0:T(8,128)(2,1)}, u32[]{:S(2)}, u32[]{:S(2)}) collective-permute-start(bf16[2816,512]{1,0:T(8,128)(2,1)} %convolution_convert_fusion.1), channel_id=1, source_target_pairs={{0,8},{8,0},{1,9},{9,1},{2,10},{10,2},{3,11},{11,3},{4,12},{12,4},... | collective-permute-start | bytes 8650760 | tf_op jit(solution)/shard_map/ppermute | solution.py:524
  322.7 53.6 %collective-permute-start.24 = (bf16[1024,2816]{1,0:T(8,128)(2,1)}, bf16[1024,2816]{1,0:T(8,128)(2,1)}, u32[]{:S(2)}, u32[]{:S(2)}) collective-permute-start(bf16[1024,2816]{1,0:T(8,128)(2,1)} %convolution_convert_fusion), channel_id=1, source_target_pairs={{0,8},{8,0},{1,9},{9,1},{2,10},{10,2},{3,11},{11,3},{4,12},{12,4},... | collective-permute-start | bytes 17301512 | tf_op jit(solution)/shard_map/ppermute | solution.py:524
  358.2 8.1 %collective-permute-start.26 = (bf16[1024,1024]{1,0:T(8,128)(2,1)}, bf16[1024,1024]{1,0:T(8,128)(2,1)}, u32[]{:S(2)}, u32[]{:S(2)}) collective-permute-start(bf16[1024,1024]{1,0:T(8,128)(2,1)} %convolution_convert_fusion.5), channel_id=1, source_target_pairs={{0,8},{8,0},{1,9},{9,1},{2,10},{10,2},{3,11},{11,3},{4,12},{12,4},... | collective-permute-start | bytes 6291464 | tf_op jit(solution)/shard_map/ppermute | solution.py:524
  362.2 8.6 %collective-permute-start.25 = (bf16[2048,512]{1,0:T(8,128)(2,1)}, bf16[2048,512]{1,0:T(8,128)(2,1)}, u32[]{:S(2)}, u32[]{:S(2)}) collective-permute-start(bf16[2048,512]{1,0:T(8,128)(2,1)} %convolution_convert_fusion.2), channel_id=1, source_target_pairs={{0,8},{8,0},{1,9},{9,1},{2,10},{10,2},{3,11},{11,3},{4,12},{12,4},... | collective-permute-start | bytes 6291464 | tf_op jit(solution)/shard_map/ppermute | solution.py:524
  362.3 34.7 %collective-permute-start.28 = (bf16[2816,256]{1,0:T(8,128)(2,1)}, bf16[2816,256]{1,0:T(8,128)(2,1)}, u32[]{:S(2)}, u32[]{:S(2)}) collective-permute-start(bf16[2816,256]{1,0:T(8,128)(2,1)} %add_convert_fusion.5), channel_id=1, source_target_pairs={{0,16},{16,0},{1,17},{17,1},{2,18},{18,2},{3,19},{19,3},{4,20},{20... | collective-permute-start | bytes 4325384 | tf_op jit(solution)/shard_map/ppermute | solution.py:524
  369.6 49.9 %collective-permute-start.32 = (bf16[1024,512]{1,0:T(8,128)(2,1)}, bf16[1024,512]{1,0:T(8,128)(2,1)}, u32[]{:S(2)}, u32[]{:S(2)}) collective-permute-start(bf16[1024,512]{1,0:T(8,128)(2,1)} %add_convert_fusion.8), channel_id=1, source_target_pairs={{0,16},{16,0},{1,17},{17,1},{2,18},{18,2},{3,19},{19,3},{4,20},{20... | collective-permute-start | bytes 3145736 | tf_op jit(solution)/shard_map/ppermute | solution.py:524
  373.8 50.7 %collective-permute-start.30 = (bf16[2048,256]{1,0:T(8,128)(2,1)}, bf16[2048,256]{1,0:T(8,128)(2,1)}, u32[]{:S(2)}, u32[]{:S(2)}) collective-permute-start(bf16[2048,256]{1,0:T(8,128)(2,1)} %add_convert_fusion.9), channel_id=1, source_target_pairs={{0,1},{1,0},{2,3},{3,2},{4,5},{5,4},{6,7},{7,6},{8,9},{9,8},{10,11... | collective-permute-start | bytes 3145736 | tf_op jit(solution)/shard_map/ppermute | solution.py:524
  400.0 56.8 %collective-permute-start.29 = (bf16[2816,128]{1,0:T(8,128)(2,1)}, bf16[2816,128]{1,0:T(8,128)(2,1)}, u32[]{:S(2)}, u32[]{:S(2)}) collective-permute-start(bf16[2816,128]{1,0:T(8,128)(2,1)} %add_convert_fusion.12), channel_id=1, source_target_pairs={{0,1},{1,0},{2,3},{3,2},{4,5},{5,4},{6,7},{7,6},{8,9},{9,8},{10,11... | collective-permute-start | bytes 2162696 | tf_op jit(solution)/shard_map/ppermute | solution.py:524
  403.0 28.0 %collective-permute-start.27 = (bf16[8,128,256]{2,1,0:T(8,128)(2,1)S(1)}, bf16[8,128,256]{2,1,0:T(8,128)(2,1)S(1)}, u32[]{:S(2)}, u32[]{:S(2)}) collective-permute-start(bf16[8,128,256]{2,1,0:T(8,128)(2,1)S(1)} %convert_element_type.372), channel_id=1, source_target_pairs={{1,0},{3,2},{5,4},{7,6},{9,8},{11,10},{13,12},{15,14},{17,16},{19,... | collective-permute-start | bytes 1572872 | tf_op jit(solution)/shard_map/ppermute | solution.py:469
  404.3 92.2 %collective-permute-start.34 = (bf16[1024,1408]{1,0:T(8,128)(2,1)}, bf16[1024,1408]{1,0:T(8,128)(2,1)}, u32[]{:S(2)}, u32[]{:S(2)}) collective-permute-start(bf16[1024,1408]{1,0:T(8,128)(2,1)} %add_convert_fusion.2), channel_id=1, source_target_pairs={{0,16},{16,0},{1,17},{17,1},{2,18},{18,2},{3,19},{19,3},{4,20},{20... | collective-permute-start | bytes 8650760 | tf_op jit(solution)/shard_map/ppermute | solution.py:524
  422.0 36.8 %collective-permute-start.33 = (bf16[1024,256]{1,0:T(8,128)(2,1)}, bf16[1024,256]{1,0:T(8,128)(2,1)}, u32[]{:S(2)}, u32[]{:S(2)}) collective-permute-start(bf16[1024,256]{1,0:T(8,128)(2,1)} %add_convert_fusion.18), channel_id=1, source_target_pairs={{0,1},{1,0},{2,3},{3,2},{4,5},{5,4},{6,7},{7,6},{8,9},{9,8},{10,11... | collective-permute-start | bytes 1572872 | tf_op jit(solution)/shard_map/ppermute | solution.py:524
  427.1 64.8 %collective-permute-start.31 = (bf16[2048,128]{1,0:T(8,128)(2,1)}, bf16[2048,128]{1,0:T(8,128)(2,1)S(1)}, u32[]{:S(2)}, u32[]{:S(2)}) collective-permute-start(bf16[2048,128]{1,0:T(8,128)(2,1)} %add_convert_fusion.20), channel_id=1, source_target_pairs={{0,16},{16,0},{1,17},{17,1},{2,18},{18,2},{3,19},{19,3},{4,20},{20... | collective-permute-start | bytes 1572872 | tf_op jit(solution)/shard_map/ppermute | solution.py:524
  496.4 135.6 %reduce-scatter.8.cloned.1.call-start = ((), (), s32[]{:S(2)}) async-start(), calls=%async_computation.7 | async-start | bytes 1802240 | tf_op jit(solution)/shard_map/reduce_scatter | solution.py:574
  499.6 33.9 %collective-permute-start.39 = (bf16[512,1408]{1,0:T(8,128)(2,1)S(1)}, bf16[512,1408]{1,0:T(8,128)(2,1)S(1)}, u32[]{:S(2)}, u32[]{:S(2)}) collective-permute-start(bf16[512,1408]{1,0:T(8,128)(2,1)S(1)} %add_convert_fusion.4), channel_id=1, source_target_pairs={{0,1},{1,0},{2,3},{3,2},{4,5},{5,4},{6,7},{7,6},{8,9},{9,8},{10,11... | collective-permute-start | bytes 4325384 | tf_op jit(solution)/shard_map/ppermute | solution.py:524
  537.3 96.1 %all-gather.11.cloned.1.call-start = ((), (), s32[]{:S(2)}) async-start(), calls=%async_computation.8 | async-start | bytes 3981312 | tf_op jit(solution)/shard_map/all_gather | solution.py:675
  566.7 6.9 collective-permute-start.35
  568.5 122.2 %reduce-scatter.6.cloned.1.call-start = ((), (), s32[]{:S(2)}) async-start(), calls=%async_computation.6 | async-start | bytes 1310720 | tf_op jit(solution)/shard_map/reduce_scatter | solution.py:574
  577.4 13.6 %collective-permute-start.40 = (bf16[1024,1024]{1,0:T(8,128)(2,1)S(1)}, bf16[1024,1024]{1,0:T(8,128)(2,1)S(1)}, u32[]{:S(2)}, u32[]{:S(2)}) collective-permute-start(bf16[1024,1024]{1,0:T(8,128)(2,1)S(1)} %convolution_convert_fusion.3), channel_id=1, source_target_pairs={{0,8},{8,0},{1,9},{9,1},{2,10},{10,2},{3,11},{11,3},{4,12},{12,4},... | collective-permute-start | bytes 6291464 | tf_op jit(solution)/shard_map/ppermute | solution.py:524
  579.1 12.9 %collective-permute-start.36 = (bf16[1024,1024]{1,0:T(8,128)(2,1)S(1)}, bf16[1024,1024]{1,0:T(8,128)(2,1)S(1)}, u32[]{:S(2)}, u32[]{:S(2)}) collective-permute-start(bf16[1024,1024]{1,0:T(8,128)(2,1)S(1)} %convolution_convert_fusion.4), channel_id=1, source_target_pairs={{0,8},{8,0},{1,9},{9,1},{2,10},{10,2},{3,11},{11,3},{4,12},{12,4},... | collective-permute-start | bytes 6291464 | tf_op jit(solution)/shard_map/ppermute | solution.py:524
  591.9 34.6 %collective-permute-start.41 = (bf16[1024,512]{1,0:T(8,128)(2,1)S(1)}, bf16[1024,512]{1,0:T(8,128)(2,1)S(1)}, u32[]{:S(2)}, u32[]{:S(2)}) collective-permute-start(bf16[1024,512]{1,0:T(8,128)(2,1)S(1)} %add_convert_fusion.6), channel_id=1, source_target_pairs={{0,1},{1,0},{2,3},{3,2},{4,5},{5,4},{6,7},{7,6},{8,9},{9,8},{10,11... | collective-permute-start | bytes 3145736 | tf_op jit(solution)/shard_map/ppermute | solution.py:524
  592.7 36.5 %collective-permute-start.37 = (bf16[1024,512]{1,0:T(8,128)(2,1)S(1)}, bf16[1024,512]{1,0:T(8,128)(2,1)S(1)}, u32[]{:S(2)}, u32[]{:S(2)}) collective-permute-start(bf16[1024,512]{1,0:T(8,128)(2,1)S(1)} %add_convert_fusion.7), channel_id=1, source_target_pairs={{0,16},{16,0},{1,17},{17,1},{2,18},{18,2},{3,19},{19,3},{4,20},{20... | collective-permute-start | bytes 3145736 | tf_op jit(solution)/shard_map/ppermute | solution.py:524
  627.8 13.5 %collective-permute-start.42 = (bf16[1024,256]{1,0:T(8,128)(2,1)}, bf16[1024,256]{1,0:T(8,128)(2,1)S(1)}, u32[]{:S(2)}, u32[]{:S(2)}) collective-permute-start(bf16[1024,256]{1,0:T(8,128)(2,1)} %add_convert_fusion.14), channel_id=1, source_target_pairs={{0,16},{16,0},{1,17},{17,1},{2,18},{18,2},{3,19},{19,3},{4,20},{20... | collective-permute-start | bytes 1572872 | tf_op jit(solution)/shard_map/ppermute | solution.py:524
  631.5 13.7 %collective-permute-start.38 = (bf16[1024,256]{1,0:T(8,128)(2,1)}, bf16[1024,256]{1,0:T(8,128)(2,1)}, u32[]{:S(2)}, u32[]{:S(2)}) collective-permute-start(bf16[1024,256]{1,0:T(8,128)(2,1)} %add_convert_fusion.16), channel_id=1, source_target_pairs={{0,1},{1,0},{2,3},{3,2},{4,5},{5,4},{6,7},{7,6},{8,9},{9,8},{10,11... | collective-permute-start | bytes 1572872 | tf_op jit(solution)/shard_map/ppermute | solution.py:524
  649.4 73.1 %all-gather.13.cloned.1.call-start = ((), (), s32[]{:S(2)}) async-start(), calls=%async_computation.9 | async-start | bytes 3244032 | tf_op jit(solution)/shard_map/all_gather | solution.py:675
  661.4 1.6 collective-permute-start.46
  662.9 6.2 collective-permute-start.47
  669.2 5.5 collective-permute-start.48
  674.7 10.0 %collective-permute-start.49 = (f32[280,128]{1,0:T(8,128)S(1)}, f32[280,128]{1,0:T(8,128)S(1)}, u32[]{:S(2)}, u32[]{:S(2)}) collective-permute-start(f32[280,128]{1,0:T(8,128)S(1)} %add.839), channel_id=1, source_target_pairs={{0,2},{2,0},{4,6},{6,4},{1,3},{3,1},{5,7},{7,5},{8,10},{10,8},{12,... | collective-permute-start | bytes 430088 | tf_op jit(solution)/shard_map/ppermute | solution.py:809
  684.8 11.9 %collective-permute-start.50 = (f32[280,128]{1,0:T(8,128)S(1)}, f32[280,128]{1,0:T(8,128)}, u32[]{:S(2)}, u32[]{:S(2)}) collective-permute-start(f32[280,128]{1,0:T(8,128)S(1)} %add.840), channel_id=1, source_target_pairs={{0,4},{2,6},{4,0},{6,2},{1,5},{3,7},{5,1},{7,3},{8,12},{10,14},{12... | collective-permute-start | bytes 430088 | tf_op jit(solution)/shard_map/ppermute | solution.py:809
  691.6 10.8 %collective-permute-start.43 = (bf16[1,1024,128]{2,1,0:T(8,128)(2,1)S(1)}, bf16[1,1024,128]{2,1,0:T(8,128)(2,1)}, u32[]{:S(2)}, u32[]{:S(2)}) collective-permute-start(bf16[1,1024,128]{2,1,0:T(8,128)(2,1)S(1)} %maximum_bitcast_fusion), channel_id=1, source_target_pairs={{0,1},{1,0},{2,3},{3,2},{4,5},{5,4},{6,7},{7,6},{8,9},{9,8},{10,11... | collective-permute-start | bytes 786440 | tf_op jit(solution)/shard_map/ppermute | solution.py:524
  703.5 17.9 %collective-permute-start.44 = (bf16[2,1024,128]{2,1,0:T(8,128)(2,1)S(1)}, bf16[2,1024,128]{2,1,0:T(8,128)(2,1)S(1)}, u32[]{:S(2)}, u32[]{:S(2)}) collective-permute-start(bf16[2,1024,128]{2,1,0:T(8,128)(2,1)S(1)} %pad_maximum_fusion.11), channel_id=1, source_target_pairs={{0,16},{16,0},{1,17},{17,1},{2,18},{18,2},{3,19},{19,3},{4,20},{20... | collective-permute-start | bytes 1572872 | tf_op jit(solution)/shard_map/ppermute | solution.py:524
  722.4 8.9 %collective-permute-start.45 = (bf16[4,1024,128]{2,1,0:T(8,128)(2,1)S(1)}, bf16[4,1024,128]{2,1,0:T(8,128)(2,1)}, u32[]{:S(2)}, u32[]{:S(2)}) collective-permute-start(bf16[4,1024,128]{2,1,0:T(8,128)(2,1)S(1)} %pad_maximum_fusion.5.refs_0_), channel_id=1, source_target_pairs={{0,8},{8,0},{1,9},{9,1},{2,10},{10,2},{3,11},{11,3},{4,12},{12,4},... | collective-permute-start | bytes 3145736 | tf_op jit(solution)/shard_map/ppermute | solution.py:524
  (130 other events, 1070.1 us)
Sparse Core Ops, SparseCore 0:
  10.9 85.4 all-gather.6
  99.8 126.1 all-gather.8
  496.6 47.0 reduce-scatter.3
  545.9 32.5 reduce-scatter.7
  580.4 47.1 all-gather.10
  649.5 33.2 reduce-scatter.5
  684.7 36.2 all-gather.12
